TPU v7x, 32 devices: a whole 2x2x4 slice. The times are simulated.
32 devices in a mesh: chan: 4 (over y, x), ctx: 8 (over z, core).
Axes of the slice: x: 2, y: 2, z: 4, core: 2. Of those that a mesh axis runs over, the one named last changes fastest.
Arguments:
- inputs: bfloat16 [1024, 4096], P('ctx', 'chan'), may hold values from -0.1875 to 0.1875
- filter_taps: bfloat16 [1024, 4096], P('ctx', 'chan'), may hold values from -0.1875 to 0.1875
- out_grad: bfloat16 [1024, 4096], P('ctx', 'chan')
- skip_gain: float32 [4096], P('chan'), may hold values from 0.5 to 2
Outputs:
- input_grad: float32 [1024, 4096], P('ctx', 'chan')
- filter_grad: float32 [1024, 4096], P('ctx', 'chan')
- skip_grad: float32 [4096], P('chan')
All inputs are finite; a program needn't handle non-finite values.
Results may differ from a plain program's by a relative error of at most 0.0003.
Values may be sent and summed in bfloat16 or wider, within the bound.
No kernel may reach another device: no remote copies, remote signals or barrier semaphores. Data moves between devices by JAX's collectives and lax.ppermute only.
A program may use at most 64 MiB of HBM per device.

v0:
```python
import math

import jax
import jax.numpy as jnp
from jax import lax
from jax.sharding import PartitionSpec as P

epsilon = 1e-06


def shifted(shard, axis, by):
    size = lax.axis_size(axis)
    pairs = [(i, i + by) for i in range(size) if 0 <= i + by < size]
    return lax.ppermute(shard, axis, pairs)


def from_root(shard, axis, root):
    mine = lax.axis_index(axis) == root
    return lax.psum(jnp.where(mine, shard, jnp.zeros_like(shard)), axis)


def tables(length):
    period = 2 * length
    odd_freq = 2 * jnp.arange(length, dtype=jnp.int32) + 1
    sample_ids = jnp.arange(period, dtype=jnp.int32)
    phase_ids = odd_freq[:, None] * sample_ids[None, :] % (2 * period)
    angles = jnp.pi * phase_ids.astype(jnp.float32) / period
    forward = jnp.concatenate([jnp.cos(angles), -jnp.sin(angles)], axis=0)
    back_ids = sample_ids[:length, None] * odd_freq[None, :] % (2 * period)
    back_angles = jnp.pi * back_ids.astype(jnp.float32) / period
    inverse = 2.0 / period * jnp.concatenate([jnp.cos(back_angles), -jnp.sin(back_angles)], axis=1)
    return (forward, inverse)


def transform(matrix, samples):
    return jnp.dot(matrix, samples.astype(jnp.float32), precision=lax.Precision.HIGH)


def correlate(left_spec, right_spec, length):
    real_left, imag_left = (left_spec[:length], left_spec[length:])
    real_right, imag_right = (right_spec[:length], right_spec[length:])
    real_out = real_left * real_right + imag_left * imag_right
    imag_out = imag_left * real_right - real_left * imag_right
    return jnp.concatenate([real_out, imag_out], axis=0)


def per_device(inputs, filter_taps, out_grad, skip_gain):
    length = inputs.shape[0]
    chan_width = inputs.shape[1]
    chain_length = lax.axis_size("ctx")
    forward, inverse = tables(length)
    first_half = forward[:, :length]
    second_half = forward[:, length:]

    def advance(position, carry):
        current, previous, acc_in, acc_fil = carry
        following = shifted(current, "ctx", -1)
        filter_block, input_block = (
            from_root(filter_taps, "ctx", position),
            from_root(inputs, "ctx", position),
        )
        input_spec = transform(forward, jnp.concatenate([previous, input_block], axis=0))
        filter_spec = transform(first_half, filter_block)
        pair_spec = transform(forward, jnp.concatenate([current, following], axis=0))
        lone_spec = transform(second_half, current)
        acc_in = acc_in + correlate(pair_spec, filter_spec, length)
        acc_fil = acc_fil + correlate(lone_spec, input_spec, length)
        return (following, input_block, acc_in, acc_fil)

    zero_spec = jnp.zeros((2 * length, chan_width), jnp.float32)
    zero_input = jnp.zeros((length, chan_width), jnp.bfloat16)
    final = lax.fori_loop(0, chain_length, advance, (out_grad, zero_input, zero_spec, zero_spec))
    acc_in, acc_fil = (final[2], final[3])
    grad_rows = out_grad.astype(jnp.float32)
    input_grad = (
        jnp.dot(inverse, acc_in, precision=lax.Precision.HIGH) + skip_gain[None, :] * grad_rows
    )
    raw_grad = jnp.dot(inverse, acc_fil, precision=lax.Precision.HIGH)
    partial_skip = jnp.sum(grad_rows * inputs.astype(jnp.float32), axis=0)
    skip_grad = lax.psum(partial_skip, "ctx")
    norm_square = lax.psum(jnp.sum(raw_grad * raw_grad), ("chan", "ctx"))
    clip_limit = 0.25 * math.sqrt(length * chain_length * chan_width * lax.axis_size("chan"))
    factor = jnp.minimum(1.0, clip_limit / jnp.sqrt(norm_square + epsilon))
    return (input_grad, raw_grad * factor, skip_grad)


def solution(mesh):
    return jax.shard_map(
        per_device,
        mesh=mesh,
        in_specs=(P("ctx", "chan"), P("ctx", "chan"), P("ctx", "chan"), P("chan")),
        out_specs=(P("ctx", "chan"), P("ctx", "chan"), P("chan")),
        check_vma=False,
    )
```

profile of v0, /device:TPU:0, one launch (start us, length us, event | category | flops | bytes accessed | tf_op | source)
XLA Modules:
  0.0 608.6 jit_solution(3761316563747174442)
XLA Ops:
  11.2 531.4 %while.20 = (s32[]{:T(128)}, bf16[128,1024]{1,0:T(8,128)(2,1)}, bf16[128,1024]{1,0:T(8,128)(2,1)}, f32[256,1024]{1,0:T(8,128)S(1)}, f32[256,1024]{1,0:T(8,128)S(...) while((s32[]{:T(128)}, bf16[128,1024]{1,0:T(8,128)(2,1)}, ...), condition=%wide.region_3.4_spmd.clone, body=%wide.region_0.3_spmd.clone.sunk | while | flops 1213726720 | bytes 31195564 | solution.py:72
  11.2 0.8 broadcast_select_fusion.3
  12.1 1.0 copy.15
  13.0 1.3 collective-permute-start
  14.8 58.7 %all-reduce.5.cloned.1.call-done = (bf16[128,1024]{1,0:T(8,128)(2,1)}, bf16[128,1024]{1,0:T(8,128)(2,1)}) async-done(((bf16[128,1024]{1,0:T(8,128)(2,1)}, bf16[128,1024]{1,0:T(8,128)(2,1)}), (bf16[128,1024]{1,0:T(8,128)(2,1)}, bf16[128,1024]{1,0:T(8,128)(2,1)})) %all-reduce.5.cloned.1.call-update) | async-done | bytes 524304 | tf_op jit(solution)/shard_map/while/body/eval_jaxpr/psum | solution.py:19
  73.4 1.5 convolution_bitcast_fusion.8
  78.0 1.4 convolution_bitcast_fusion.7
  81.0 0.8 broadcast_select_fusion.3
  81.8 1.0 copy.15
  82.8 1.3 collective-permute-start
  84.5 55.0 %all-reduce.5.cloned.1.call-done = (bf16[128,1024]{1,0:T(8,128)(2,1)}, bf16[128,1024]{1,0:T(8,128)(2,1)}) async-done(((bf16[128,1024]{1,0:T(8,128)(2,1)}, bf16[128,1024]{1,0:T(8,128)(2,1)}), (bf16[128,1024]{1,0:T(8,128)(2,1)}, bf16[128,1024]{1,0:T(8,128)(2,1)})) %all-reduce.5.cloned.1.call-update) | async-done | bytes 524304 | tf_op jit(solution)/shard_map/while/body/eval_jaxpr/psum | solution.py:19
  139.5 1.5 convolution_bitcast_fusion.8
  144.1 1.4 convolution_bitcast_fusion.7
  147.9 1.0 copy.15
  148.9 1.3 collective-permute-start
  150.6 55.0 %all-reduce.5.cloned.1.call-done = (bf16[128,1024]{1,0:T(8,128)(2,1)}, bf16[128,1024]{1,0:T(8,128)(2,1)}) async-done(((bf16[128,1024]{1,0:T(8,128)(2,1)}, bf16[128,1024]{1,0:T(8,128)(2,1)}), (bf16[128,1024]{1,0:T(8,128)(2,1)}, bf16[128,1024]{1,0:T(8,128)(2,1)})) %all-reduce.5.cloned.1.call-update) | async-done | bytes 524304 | tf_op jit(solution)/shard_map/while/body/eval_jaxpr/psum | solution.py:19
  205.6 1.5 convolution_bitcast_fusion.8
  210.1 1.4 convolution_bitcast_fusion.7
  214.0 1.0 copy.15
  214.9 1.3 collective-permute-start
  216.7 54.7 %all-reduce.5.cloned.1.call-done = (bf16[128,1024]{1,0:T(8,128)(2,1)}, bf16[128,1024]{1,0:T(8,128)(2,1)}) async-done(((bf16[128,1024]{1,0:T(8,128)(2,1)}, bf16[128,1024]{1,0:T(8,128)(2,1)}), (bf16[128,1024]{1,0:T(8,128)(2,1)}, bf16[128,1024]{1,0:T(8,128)(2,1)})) %all-reduce.5.cloned.1.call-update) | async-done | bytes 524304 | tf_op jit(solution)/shard_map/while/body/eval_jaxpr/psum | solution.py:19
  271.4 1.5 convolution_bitcast_fusion.8
  275.9 1.4 convolution_bitcast_fusion.7
  279.8 1.0 copy.15
  280.7 1.3 collective-permute-start
  282.4 54.7 %all-reduce.5.cloned.1.call-done = (bf16[128,1024]{1,0:T(8,128)(2,1)}, bf16[128,1024]{1,0:T(8,128)(2,1)}) async-done(((bf16[128,1024]{1,0:T(8,128)(2,1)}, bf16[128,1024]{1,0:T(8,128)(2,1)}), (bf16[128,1024]{1,0:T(8,128)(2,1)}, bf16[128,1024]{1,0:T(8,128)(2,1)})) %all-reduce.5.cloned.1.call-update) | async-done | bytes 524304 | tf_op jit(solution)/shard_map/while/body/eval_jaxpr/psum | solution.py:19
  337.1 1.5 convolution_bitcast_fusion.8
  341.7 1.4 convolution_bitcast_fusion.7
  345.5 1.0 copy.15
  346.5 1.3 collective-permute-start
  348.2 54.7 %all-reduce.5.cloned.1.call-done = (bf16[128,1024]{1,0:T(8,128)(2,1)}, bf16[128,1024]{1,0:T(8,128)(2,1)}) async-done(((bf16[128,1024]{1,0:T(8,128)(2,1)}, bf16[128,1024]{1,0:T(8,128)(2,1)}), (bf16[128,1024]{1,0:T(8,128)(2,1)}, bf16[128,1024]{1,0:T(8,128)(2,1)})) %all-reduce.5.cloned.1.call-update) | async-done | bytes 524304 | tf_op jit(solution)/shard_map/while/body/eval_jaxpr/psum | solution.py:19
  402.9 1.5 convolution_bitcast_fusion.8
  407.4 1.4 convolution_bitcast_fusion.7
  411.3 1.0 copy.15
  412.2 1.3 collective-permute-start
  414.0 55.0 %all-reduce.5.cloned.1.call-done = (bf16[128,1024]{1,0:T(8,128)(2,1)}, bf16[128,1024]{1,0:T(8,128)(2,1)}) async-done(((bf16[128,1024]{1,0:T(8,128)(2,1)}, bf16[128,1024]{1,0:T(8,128)(2,1)}), (bf16[128,1024]{1,0:T(8,128)(2,1)}, bf16[128,1024]{1,0:T(8,128)(2,1)})) %all-reduce.5.cloned.1.call-update) | async-done | bytes 524304 | tf_op jit(solution)/shard_map/while/body/eval_jaxpr/psum | solution.py:19
  469.0 1.5 convolution_bitcast_fusion.8
  473.5 1.4 convolution_bitcast_fusion.7
  477.4 1.0 copy.15
  478.3 1.3 collective-permute-start
  480.0 55.0 %all-reduce.5.cloned.1.call-done = (bf16[128,1024]{1,0:T(8,128)(2,1)}, bf16[128,1024]{1,0:T(8,128)(2,1)}) async-done(((bf16[128,1024]{1,0:T(8,128)(2,1)}, bf16[128,1024]{1,0:T(8,128)(2,1)}), (bf16[128,1024]{1,0:T(8,128)(2,1)}, bf16[128,1024]{1,0:T(8,128)(2,1)})) %all-reduce.5.cloned.1.call-update) | async-done | bytes 524304 | tf_op jit(solution)/shard_map/while/body/eval_jaxpr/psum | solution.py:19
  535.1 1.5 convolution_bitcast_fusion.8
  539.6 1.4 convolution_bitcast_fusion.7
  543.0 1.1 multiply_reduce_fusion
  544.1 39.5 %psum.36 = f32[]{:T(128)} all-reduce(f32[]{:T(128)} %get-tuple-element.242), channel_id=1, replica_groups=mesh['chan'=4,'ctx'=8] {'chan','ctx'}, use_global_device_ids=true, to_apply=%region_5.6 | all-reduce | flops 1 | bytes 8 | tf_op jit(solution)/shard_map/psum | solution.py:81
  584.2 0.8 broadcast_multiply_fusion
  585.2 1.2 convolution_add_fusion
  586.5 15.2 %psum.37 = f32[1024]{0:T(1024)} all-reduce(f32[1024]{0:T(1024)S(1)} %fusion.8), channel_id=1, replica_groups=mesh['chan'=4,'ctx'=8] {'ctx'}, use_global_device_ids=true, to_apply=%region_7.8 | all-reduce | flops 1024 | bytes 8192 | tf_op jit(solution)/shard_map/psum | solution.py:80
  (204 shorter events, 49.0 us)
Async XLA Ops:
  8.4 1.0 copy-start.8
  9.5 1.4 copy-start.4
  10.2 1.0 copy-start.2
  11.2 62.2 %all-reduce.5.cloned.1.call-start = ((), (), s32[]{:S(2)}) async-start(), calls=%async_computation | async-start | bytes 1048576 | tf_op jit(solution)/shard_map/while/body/eval_jaxpr/psum | solution.py:19
  13.0 64.4 %collective-permute-start = (bf16[128,1024]{1,0:T(8,128)(2,1)S(1)}, bf16[128,1024]{1,0:T(8,128)(2,1)}, u32[]{:S(2)}, u32[]{:S(2)}) collective-permute-start(bf16[128,1024]{1,0:T(8,128)(2,1)S(1)} %copy.15), channel_id=1, source_target_pairs={{1,0},{2,1},{3,2},{4,3},{5,4},{6,5},{7,6},{9,8},{10,9},{11,10},{12... | collective-permute-start | bytes 786440 | tf_op jit(solution)/shard_map/while/body/eval_jaxpr/ppermute | solution.py:14
  76.0 1.0 copy-start.6
  76.0 1.1 copy-start.7
  79.9 1.0 copy-start.3
  80.0 1.0 copy-start.5
  81.0 58.5 %all-reduce.5.cloned.1.call-start = ((), (), s32[]{:S(2)}) async-start(), calls=%async_computation | async-start | bytes 1048576 | tf_op jit(solution)/shard_map/while/body/eval_jaxpr/psum | solution.py:19
  82.8 60.8 %collective-permute-start = (bf16[128,1024]{1,0:T(8,128)(2,1)S(1)}, bf16[128,1024]{1,0:T(8,128)(2,1)}, u32[]{:S(2)}, u32[]{:S(2)}) collective-permute-start(bf16[128,1024]{1,0:T(8,128)(2,1)S(1)} %copy.15), channel_id=1, source_target_pairs={{1,0},{2,1},{3,2},{4,3},{5,4},{6,5},{7,6},{9,8},{10,9},{11,10},{12... | collective-permute-start | bytes 786440 | tf_op jit(solution)/shard_map/while/body/eval_jaxpr/ppermute | solution.py:14
  142.0 1.0 copy-start.6
  142.0 1.1 copy-start.7
  146.0 1.0 copy-start.3
  146.0 1.0 copy-start.5
  147.1 58.6 %all-reduce.5.cloned.1.call-start = ((), (), s32[]{:S(2)}) async-start(), calls=%async_computation | async-start | bytes 1048576 | tf_op jit(solution)/shard_map/while/body/eval_jaxpr/psum | solution.py:19
  148.9 60.8 %collective-permute-start = (bf16[128,1024]{1,0:T(8,128)(2,1)S(1)}, bf16[128,1024]{1,0:T(8,128)(2,1)}, u32[]{:S(2)}, u32[]{:S(2)}) collective-permute-start(bf16[128,1024]{1,0:T(8,128)(2,1)S(1)} %copy.15), channel_id=1, source_target_pairs={{1,0},{2,1},{3,2},{4,3},{5,4},{6,5},{7,6},{9,8},{10,9},{11,10},{12... | collective-permute-start | bytes 786440 | tf_op jit(solution)/shard_map/while/body/eval_jaxpr/ppermute | solution.py:14
  208.1 1.0 copy-start.6
  208.1 1.1 copy-start.7
  212.1 1.0 copy-start.3
  212.1 1.0 copy-start.5
  213.1 58.3 %all-reduce.5.cloned.1.call-start = ((), (), s32[]{:S(2)}) async-start(), calls=%async_computation | async-start | bytes 1048576 | tf_op jit(solution)/shard_map/while/body/eval_jaxpr/psum | solution.py:19
  214.9 60.5 %collective-permute-start = (bf16[128,1024]{1,0:T(8,128)(2,1)S(1)}, bf16[128,1024]{1,0:T(8,128)(2,1)}, u32[]{:S(2)}, u32[]{:S(2)}) collective-permute-start(bf16[128,1024]{1,0:T(8,128)(2,1)S(1)} %copy.15), channel_id=1, source_target_pairs={{1,0},{2,1},{3,2},{4,3},{5,4},{6,5},{7,6},{9,8},{10,9},{11,10},{12... | collective-permute-start | bytes 786440 | tf_op jit(solution)/shard_map/while/body/eval_jaxpr/ppermute | solution.py:14
  273.9 1.0 copy-start.6
  273.9 1.1 copy-start.7
  277.9 1.0 copy-start.5
  278.9 58.2 %all-reduce.5.cloned.1.call-start = ((), (), s32[]{:S(2)}) async-start(), calls=%async_computation | async-start | bytes 1048576 | tf_op jit(solution)/shard_map/while/body/eval_jaxpr/psum | solution.py:19
  280.7 60.4 %collective-permute-start = (bf16[128,1024]{1,0:T(8,128)(2,1)S(1)}, bf16[128,1024]{1,0:T(8,128)(2,1)}, u32[]{:S(2)}, u32[]{:S(2)}) collective-permute-start(bf16[128,1024]{1,0:T(8,128)(2,1)S(1)} %copy.15), channel_id=1, source_target_pairs={{1,0},{2,1},{3,2},{4,3},{5,4},{6,5},{7,6},{9,8},{10,9},{11,10},{12... | collective-permute-start | bytes 786440 | tf_op jit(solution)/shard_map/while/body/eval_jaxpr/ppermute | solution.py:14
  339.6 1.0 copy-start.6
  339.6 1.1 copy-start.7
  343.6 1.0 copy-start.5
  344.7 58.2 %all-reduce.5.cloned.1.call-start = ((), (), s32[]{:S(2)}) async-start(), calls=%async_computation | async-start | bytes 1048576 | tf_op jit(solution)/shard_map/while/body/eval_jaxpr/psum | solution.py:19
  346.5 60.5 %collective-permute-start = (bf16[128,1024]{1,0:T(8,128)(2,1)S(1)}, bf16[128,1024]{1,0:T(8,128)(2,1)}, u32[]{:S(2)}, u32[]{:S(2)}) collective-permute-start(bf16[128,1024]{1,0:T(8,128)(2,1)S(1)} %copy.15), channel_id=1, source_target_pairs={{1,0},{2,1},{3,2},{4,3},{5,4},{6,5},{7,6},{9,8},{10,9},{11,10},{12... | collective-permute-start | bytes 786440 | tf_op jit(solution)/shard_map/while/body/eval_jaxpr/ppermute | solution.py:14
  405.4 1.0 copy-start.6
  405.4 1.1 copy-start.7
  409.4 1.0 copy-start.5
  410.4 58.5 %all-reduce.5.cloned.1.call-start = ((), (), s32[]{:S(2)}) async-start(), calls=%async_computation | async-start | bytes 1048576 | tf_op jit(solution)/shard_map/while/body/eval_jaxpr/psum | solution.py:19
  412.2 60.8 %collective-permute-start = (bf16[128,1024]{1,0:T(8,128)(2,1)S(1)}, bf16[128,1024]{1,0:T(8,128)(2,1)}, u32[]{:S(2)}, u32[]{:S(2)}) collective-permute-start(bf16[128,1024]{1,0:T(8,128)(2,1)S(1)} %copy.15), channel_id=1, source_target_pairs={{1,0},{2,1},{3,2},{4,3},{5,4},{6,5},{7,6},{9,8},{10,9},{11,10},{12... | collective-permute-start | bytes 786440 | tf_op jit(solution)/shard_map/while/body/eval_jaxpr/ppermute | solution.py:14
  471.5 1.0 copy-start.6
  471.5 1.1 copy-start.7
  475.5 1.0 copy-start.5
  476.5 58.6 %all-reduce.5.cloned.1.call-start = ((), (), s32[]{:S(2)}) async-start(), calls=%async_computation | async-start | bytes 1048576 | tf_op jit(solution)/shard_map/while/body/eval_jaxpr/psum | solution.py:19
  478.3 60.8 %collective-permute-start = (bf16[128,1024]{1,0:T(8,128)(2,1)S(1)}, bf16[128,1024]{1,0:T(8,128)(2,1)}, u32[]{:S(2)}, u32[]{:S(2)}) collective-permute-start(bf16[128,1024]{1,0:T(8,128)(2,1)S(1)} %copy.15), channel_id=1, source_target_pairs={{1,0},{2,1},{3,2},{4,3},{5,4},{6,5},{7,6},{9,8},{10,9},{11,10},{12... | collective-permute-start | bytes 786440 | tf_op jit(solution)/shard_map/while/body/eval_jaxpr/ppermute | solution.py:14
  537.6 1.0 copy-start.6
  537.6 1.1 copy-start.7
  541.6 1.0 copy-start.5
  543.0 42.1 %copy-start.10 = (f32[1024]{0:T(1024)S(1)}, f32[1024]{0:T(1024)}, u32[]{:S(2)}) copy-start(f32[1024]{0:T(1024)} %param.9) | copy-start | bytes 12292
  584.2 1.0 copy-start.9
  (21 other events, 20.0 us)
Sparse Core Ops, SparseCore 0:
  14.4 58.9 all-reduce.4
  84.2 55.3 all-reduce.4
  150.3 55.3 all-reduce.4
  216.0 55.3 all-reduce.4
  281.8 55.2 all-reduce.4
  347.5 55.3 all-reduce.4
  413.6 55.3 all-reduce.4
  479.7 55.3 all-reduce.4
where the time goes:
time: 611 us; the launch traced here: 609 us
  waiting for transfers between devices  443 us (73%)
  blocking collectives  54.7 us (9%)
  local copies, waits for them, and re-layouts  33.8 us (6%)
  matrix products  32.6 us (5%)
  other arithmetic  18.4 us (3%)
  between operations  14.7 us (2%)
  starting transfers between devices  10.3 us (2%)
    psum x8, waiting for transfers between devices, from_root(): return lax.psum(jnp.where(mine, shard, jnp.zeros_like(shard)), axis)  443 us
    psum x1, blocking collectives, per_device(): norm_square = lax.psum(jnp.sum(raw_grad * raw_grad), ('chan', 'ctx'))  39.5 us
    while x112, local copies, waits for them, and re-layouts  31.6 us
    dot_general x32, matrix products, transform(): jnp.dot(matrix, samples.astype(jnp.float32), precision=lax.Precision.HIGH)  30.3 us
    psum x1, blocking collectives, per_device(): skip_grad = lax.psum(partial_skip, 'ctx')  15.2 us
  transfers between devices with their start and end apart: 16, of which 8 were waited for; matrix products, arithmetic and copies ran while one was open for 6% of the time, Pallas kernels for 0%

commit v1 on v0

v1 whole, which is shorter than its diff:
```python
import functools
import math

import jax
import jax.numpy as jnp
import numpy as np
from jax import lax
from jax.experimental import pallas as pl
from jax.experimental.pallas import tpu as pltpu
from jax.sharding import PartitionSpec as P

epsilon = 1e-06
octaves = 246
low_power = 120
top_code = 128 * octaves - 1
tail_rows = 16
vmem_bytes = 48 * 1024 * 1024


def tables(length):
    odd = 2 * np.arange(length) + 1
    phase = odd[:, None] * np.arange(length)[None, :] % (4 * length)
    angles = np.pi * phase / (2 * length)
    forward = np.concatenate([np.cos(angles), -np.sin(angles)], axis=0)
    high = forward.astype(np.float32).astype(jnp.bfloat16)
    low = (forward - high.astype(np.float64)).astype(np.float32).astype(jnp.bfloat16)
    both = np.concatenate([high, low], axis=1)
    scale = np.float32(1.0 / length)
    back_high = (high.astype(np.float32).T * scale).astype(jnp.bfloat16)
    back_low = (low.astype(np.float32).T * scale).astype(jnp.bfloat16)
    return jnp.asarray(both), jnp.asarray(back_high), jnp.asarray(back_low)


def three_parts(value):
    high = value.astype(jnp.bfloat16).astype(jnp.float32)
    rest = value - high
    middle = rest.astype(jnp.bfloat16).astype(jnp.float32)
    return high, middle, rest - middle


def encode(values):
    peak = jnp.max(jnp.abs(values), axis=0, keepdims=True) * (1.0 + 2.0**-7)
    scale = jnp.maximum(peak.astype(jnp.bfloat16).astype(jnp.float32), 2.0**-110)
    units = values * (top_code / scale)
    code = jnp.minimum(jnp.floor(jnp.abs(units) + 0.5), float(top_code))
    octave = jnp.floor(code * (1.0 / 128))
    mantissa = 1.0 + (code - 128.0 * octave) * (1.0 / 128)
    carrier = mantissa * jnp.exp2(octave - float(low_power))
    return jnp.where(units < 0, -carrier, carrier).astype(jnp.bfloat16), scale


def decode(codes, scale):
    carrier = codes.astype(jnp.float32)
    size = jnp.abs(carrier)
    power = jnp.floor(jnp.log2(size) + 0.001)
    mantissa = jnp.floor(size * jnp.exp2(-power) * 128.0 + 0.5)
    units = (power + float(low_power - 1)) * 128.0 + mantissa
    return jnp.where(carrier < 0, -units, units) * (scale * (1.0 / top_code))


def tail_tile(rows, width):
    row_ids = lax.broadcasted_iota(jnp.int32, (tail_rows, width), 0)
    tile = jnp.zeros((tail_rows, width), jnp.float32)
    for i, row in enumerate(rows):
        tile = jnp.where(row_ids == i, jnp.broadcast_to(row, (tail_rows, width)), tile)
    return tile.astype(jnp.bfloat16)


def correlate_rows(pairs, others, size):
    results = []
    for p in range(size):
        real = imag = None
        for q in range(p, size):
            (gr, gi), (fr, fi) = pairs[q], others[q - p]
            real_term = gr * fr + gi * fi
            imag_term = gi * fr - gr * fi
            real = real_term if real is None else real + real_term
            imag = imag_term if imag is None else imag + imag_term
        results.append((real, imag))
    return results


def send_results(position, size, acc, back_high, back_low, emit):
    width = acc.shape[2]
    for k in range(0, size, 2):
        spec = jnp.concatenate([acc[position ^ k], acc[position ^ (k + 1)]], axis=1)
        high = spec.astype(jnp.bfloat16)
        low = (spec - high.astype(jnp.float32)).astype(jnp.bfloat16)
        dot = functools.partial(jnp.dot, preferred_element_type=jnp.float32)
        block = dot(back_high[...], high) + dot(back_high[...], low) + dot(back_low[...], high)
        emit(k, block[:, :width])
        emit(k + 1, block[:, width:])


def first_kernel(size, length, *refs):
    arrived = refs[:size]
    both, back_high, back_low = refs[size : size + 3]
    out = refs[size + 3 : 2 * size + 3]
    pair_spec, squares, spec, acc = refs[2 * size + 3 :]
    width = spec.shape[2] // 2
    position = lax.axis_index("ctx")

    skip = jnp.zeros((1, width), jnp.float32)
    for k in range(size):
        grad, other = arrived[k][:length], arrived[k][length:]
        skip += jnp.sum(grad.astype(jnp.float32) * other.astype(jnp.float32), axis=0, keepdims=True)
        lanes = jnp.concatenate([grad, other], axis=1)
        spec[position ^ k] = jnp.dot(
            both[...], jnp.concatenate([lanes, lanes], axis=0), preferred_element_type=jnp.float32
        )

    flip = jnp.where(lax.broadcasted_iota(jnp.int32, (8, width), 0) % 2 == 0, 1.0, -1.0)

    def rows(r, carry):
        real_rows = pl.ds(pl.multiple_of(r * 8, 8), 8)
        imag_rows = pl.ds(pl.multiple_of(length + r * 8, 8), 8)
        grad = [(spec[q, real_rows, :width], spec[q, imag_rows, :width]) for q in range(size)]
        pairs = []
        for q in range(size):
            if q + 1 < size:
                real = grad[q][0] + flip * grad[q + 1][1]
                imag = grad[q][1] - flip * grad[q + 1][0]
            else:
                real, imag = grad[q]
            pair_spec[q, real_rows, :] = real
            pair_spec[q, imag_rows, :] = imag
            pairs.append((real, imag))
        others = [(spec[q, real_rows, width:], spec[q, imag_rows, width:]) for q in range(size)]
        for p, (real, imag) in enumerate(correlate_rows(pairs, others, size)):
            acc[p, real_rows, :] = real
            acc[p, imag_rows, :] = imag
        return carry

    lax.fori_loop(0, length // 8, rows, 0)
    skip_parts = three_parts(skip)
    squares[...] = jnp.zeros_like(squares)

    def emit(k, block):
        squares[...] += jnp.sum((block * block).reshape(length // 8, 8, width), axis=0)
        codes, scale = encode(block)
        out[k][:length] = codes
        out[k][length:] = tail_tile((scale,) + skip_parts, width)

    send_results(position, size, acc, back_high, back_low, emit)


def second_kernel(size, length, sums, *refs):
    arrived = refs[:size]
    both, back_high, back_low, pair_spec = refs[size : size + 4]
    partial_squares = refs[size + 4 : size + 4 + sums]
    out = refs[size + 4 + sums : 2 * size + 4 + sums]
    spec, acc = refs[2 * size + 4 + sums :]
    width = spec.shape[2]
    position = lax.axis_index("ctx")

    for k in range(0, size, 2):
        lanes = jnp.concatenate([arrived[k][...], arrived[k + 1][...]], axis=1)
        both_specs = jnp.dot(
            both[...], jnp.concatenate([lanes, lanes], axis=0), preferred_element_type=jnp.float32
        )
        spec[position ^ k] = both_specs[:, :width]
        spec[position ^ (k + 1)] = both_specs[:, width:]

    def rows(r, carry):
        real_rows = pl.ds(pl.multiple_of(r * 8, 8), 8)
        imag_rows = pl.ds(pl.multiple_of(length + r * 8, 8), 8)
        pairs = [(pair_spec[q, real_rows, :], pair_spec[q, imag_rows, :]) for q in range(size)]
        others = [(spec[q, real_rows, :], spec[q, imag_rows, :]) for q in range(size)]
        for p, (real, imag) in enumerate(correlate_rows(pairs, others, size)):
            acc[p, real_rows, :] = real
            acc[p, imag_rows, :] = imag
        return carry

    lax.fori_loop(0, length // 8, rows, 0)
    squares = partial_squares[0][...]
    for other in partial_squares[1:]:
        squares += other[...]
    total = jnp.sum(jnp.sum(squares, axis=0, keepdims=True), axis=1, keepdims=True)
    total_parts = three_parts(jnp.broadcast_to(total, (1, width)))

    def emit(k, block):
        codes, scale = encode(block)
        out[k][:length] = codes
        out[k][length:] = tail_tile((scale,) + total_parts, width)

    send_results(position, size, acc, back_high, back_low, emit)


def last_kernel(size, length, part, clip_limit, *refs):
    filter_codes, input_codes = refs[:size], refs[size : 2 * size]
    grad, gain, input_grad, filter_grad, skip_grad = refs[2 * size :]
    position = lax.axis_index("ctx")
    total = jnp.zeros((1, part), jnp.float32)
    for k in range(size):
        tail = input_codes[k][length:].astype(jnp.float32)
        total += tail[1:2] + tail[2:3] + tail[3:4]
    factor = jnp.minimum(1.0, clip_limit / jnp.sqrt(total + epsilon))
    for k in range(size):
        columns = pl.ds(pl.multiple_of((position ^ k) * part, part), part)
        tail = filter_codes[k][length:].astype(jnp.float32)
        filter_grad[:, columns] = decode(filter_codes[k][:length], tail[0:1]) * factor
        skip_grad[:, columns] = tail[1:2] + tail[2:3] + tail[3:4]
        tail = input_codes[k][length:].astype(jnp.float32)
        input_grad[:, columns] = (
            decode(input_codes[k][:length], tail[0:1])
            + gain[:, columns] * grad[:, columns].astype(jnp.float32)
        )


def run(kernel, name, out_shape, scratch=()):
    return pl.pallas_call(
        kernel,
        out_shape=out_shape,
        scratch_shapes=scratch,
        name=name,
        compiler_params=pltpu.CompilerParams(vmem_limit_bytes=vmem_bytes),
    )


def per_device(inputs, filter_taps, out_grad, skip_gain):
    length, chan_width = inputs.shape
    size = lax.axis_size("ctx")
    columns = lax.axis_size("chan")
    part = chan_width // size
    width = -(-part // 128) * 128
    position = lax.axis_index("ctx")
    both, back_high, back_low = tables(length)
    f32, bf16 = jnp.float32, jnp.bfloat16

    def columns_for(array, k):
        block = lax.dynamic_slice_in_dim(array, (position ^ k) * part, part, 1)
        return jnp.pad(block, ((0, 0), (0, width - part)))

    def exchange(blocks):
        return [
            blocks[k] if k == 0 else lax.ppermute(blocks[k], "ctx", [(i, i ^ k) for i in range(size)])
            for k in range(size)
        ]

    grad_input = exchange(
        [
            jnp.concatenate([columns_for(out_grad, k), columns_for(inputs, k)], axis=0)
            for k in range(size)
        ]
    )
    taps = exchange([columns_for(filter_taps, k) for k in range(size)])

    message = jax.ShapeDtypeStruct((length + tail_rows, width), bf16)
    *filter_codes, pair_spec, squares = run(
        functools.partial(first_kernel, size, length),
        "filter_gradient",
        [message] * size
        + [
            jax.ShapeDtypeStruct((size, 2 * length, width), f32),
            jax.ShapeDtypeStruct((8, width), f32),
        ],
        [
            pltpu.VMEM((size, 2 * length, 2 * width), f32),
            pltpu.VMEM((size, 2 * length, width), f32),
        ],
    )(*grad_input, both, back_high, back_low)
    filter_codes = exchange(filter_codes)
    all_squares = [
        squares if k == 0 else lax.ppermute(squares, "chan", [(i, i ^ k) for i in range(columns)])
        for k in range(columns)
    ]
    input_codes = run(
        functools.partial(second_kernel, size, length, columns),
        "input_gradient",
        [message] * size,
        [
            pltpu.VMEM((size, 2 * length, width), f32),
            pltpu.VMEM((size, 2 * length, width), f32),
        ],
    )(*taps, both, back_high, back_low, pair_spec, *all_squares)
    input_codes = exchange(input_codes)

    clip_limit = 0.25 * math.sqrt(length * size * chan_width * columns)
    whole = size * width
    grad_rows, gain = out_grad, skip_gain[None, :]
    if width != part:
        spread = lambda a: jnp.pad(
            a.reshape(a.shape[0], size, part), ((0, 0), (0, 0), (0, width - part))
        ).reshape(a.shape[0], whole)
        grad_rows, gain = spread(grad_rows), spread(gain)
    input_grad, filter_grad, skip_grad = run(
        functools.partial(last_kernel, size, length, width, clip_limit),
        "outputs",
        [
            jax.ShapeDtypeStruct((length, whole), f32),
            jax.ShapeDtypeStruct((length, whole), f32),
            jax.ShapeDtypeStruct((1, whole), f32),
        ],
    )(*filter_codes, *input_codes, grad_rows, gain)
    if width != part:
        gather = lambda a: a.reshape(a.shape[0], size, width)[:, :, :part].reshape(
            a.shape[0], chan_width
        )
        input_grad, filter_grad, skip_grad = gather(input_grad), gather(filter_grad), gather(skip_grad)
    return (input_grad, filter_grad, skip_grad[0])


def solution(mesh):
    return jax.shard_map(
        per_device,
        mesh=mesh,
        in_specs=(P("ctx", "chan"), P("ctx", "chan"), P("ctx", "chan"), P("chan")),
        out_specs=(P("ctx", "chan"), P("ctx", "chan"), P("chan")),
        check_vma=False,
    )
```

time: 611 us -> 63.5 us (0.10)
  waiting for transfers between devices: 443 us -> 10.5 us
  blocking collectives: 54.7 us -> 0 us
  starting transfers between devices: 10.3 us -> 44.4 us
  matrix products: 32.6 us -> 0 us
  local copies, waits for them, and re-layouts: 33.8 us -> 2 us
  other arithmetic: 18.4 us -> 0.05 us
  between operations: 14.7 us -> 0.84 us
    psum x8 -> x0, waiting for transfers between devices: 443 us -> none  [from_root(): return lax.psum(jnp.where(mine, shard, jnp.zeros_like(shard)), axis)]
    psum x2 -> x0, blocking collectives: 54.7 us -> none  [the longest x1 39.5 us: per_device(): norm_square = lax.psum(jnp.sum(raw_grad * raw_grad), ('chan', 'ctx'))]
    ppermute x8 -> x31, starting transfers between devices: 10.2 us -> 44.4 us  [the longest x28 39 us: exchange(): lax.ppermute(blocks[k], 'ctx', [(i, i ^ k) for i in range(size)])]
    dot_general x34 -> x0, matrix products: 32.6 us -> none  [the longest x32 30.3 us: transform(): jnp.dot(matrix, samples.astype(jnp.float32), precision=lax.Precision.HIGH)]
    while x112 -> x0, local copies, waits for them, and re-layouts: 31.6 us -> none
    ppermute x8 -> x31, waiting for transfers between devices: 0.02 us -> 10.5 us  [the longest x3 6.26 us: per_device(): lax.ppermute(squares, 'chan', [(i, i ^ k) for i in range(columns)])]
    add x33 -> x0, other arithmetic: 8.61 us -> none  [the longest x16 2.88 us: correlate(): real_out = real_left * real_right + imag_left * imag_right]
    select_n x8 -> x0, other arithmetic: 6.55 us -> none  [from_root(): return lax.psum(jnp.where(mine, shard, jnp.zeros_like(shard)), axis)]
  transfers between devices with their start and end apart: 16 -> 31, of which waited for: 8 -> 8; matrix products, arithmetic and copies ran while one was open for 6% -> 0% of each run, Pallas kernels for 0% -> 6%
where the time goes in v1:
time: 63.5 us; the launch traced here: 63.2 us
  starting transfers between devices  44.4 us (70%)
  waiting for transfers between devices  10.5 us (17%)
  Pallas kernels  5.43 us (9%)
  local copies, waits for them, and re-layouts  2 us (3%)
  between operations  0.84 us (1%)
    ppermute x28, starting transfers between devices, exchange(): lax.ppermute(blocks[k], 'ctx', [(i, i ^ k) for i in range(size)])  39 us
    ppermute x3, waiting for transfers between devices, per_device(): lax.ppermute(squares, 'chan', [(i, i ^ k) for i in range(columns)])  6.26 us
    ppermute x3, starting transfers between devices, per_device(): lax.ppermute(squares, 'chan', [(i, i ^ k) for i in range(columns)])  5.46 us
    ppermute x28, waiting for transfers between devices, exchange(): lax.ppermute(blocks[k], 'ctx', [(i, i ^ k) for i in range(size)])  4.23 us
    pallas_call x1, Pallas kernels, per_device(): run(functools.partial(first_kernel, size, length), 'filter_gradient', [me...  1.95 us
    pallas_call x1, Pallas kernels, per_device(): run(functools.partial(second_kernel, size, length, columns), 'input_gradi...  1.81 us
    pallas_call x1, Pallas kernels, per_device(): run(functools.partial(last_kernel, size, length, width, clip_limit), 'out...  1.67 us
  transfers between devices with their start and end apart: 31, of which 8 were waited for; matrix products, arithmetic and copies ran while one was open for 0% of the time, Pallas kernels for 6%

profile of v1, /device:TPU:0, one launch (start us, length us, event | category | flops | bytes accessed | tf_op | source)
XLA Modules:
  0.0 63.2 jit_solution(4953663435305648292)
XLA Ops:
  0.7 1.1 %constant_dynamic-slice_fusion.8 = (bf16[128,128]{1,0:T(8,128)(2,1)S(1)}, bf16[128,128]{1,0:T(8,128)(2,1)S(1)}, bf16[128,128]{1,0:T(8,128)(2,1)S(1)}, bf16[128,1...) fusion(bf16[128,1024]{1,0:T(8,128)(2,1)} %param.7, ...), kind=kLoop, calls=%fused_computation.16 | loop fusion | bytes 1048608 | tf_op jit(solution)/shard_map/dynamic_slice | solution.py:231
  1.8 0.0 copy-start.5
  1.8 0.5 collective-permute-start
  2.3 2.7 %collective-permute-start.1 = (bf16[256,128]{1,0:T(8,128)(2,1)S(1)}, bf16[256,128]{1,0:T(8,128)(2,1)S(1)}, u32[]{:S(2)}, u32[]{:S(2)}) collective-permute-start(bf16[256,128]{1,0:T(8,128)(2,1)S(1)} %pad_maximum_fusion.2), channel_id=1, source_target_pairs={{0,2},{1,3},{2,0},{3,1},{4,6},{5,7},{6,4},{7,5},{8,10},{9,11},{10,... | collective-permute-start | bytes 196616 | tf_op jit(solution)/shard_map/ppermute | solution.py:236
  5.0 0.1 collective-permute-start.2
  5.1 0.1 constant_dynamic-slice_fusion
  5.2 0.1 collective-permute-start.14
  5.3 1.9 %collective-permute-start.15 = (bf16[128,128]{1,0:T(8,128)(2,1)S(1)}, bf16[128,128]{1,0:T(8,128)(2,1)S(1)}, u32[]{:S(2)}, u32[]{:S(2)}) collective-permute-start(bf16[128,128]{1,0:T(8,128)(2,1)S(1)} %get-tuple-element.49), channel_id=1, source_target_pairs={{0,2},{1,3},{2,0},{3,1},{4,6},{5,7},{6,4},{7,5},{8,10},{9,11},{10,... | collective-permute-start | bytes 98312 | tf_op jit(solution)/shard_map/ppermute | solution.py:236
  7.3 2.7 %collective-permute-start.3 = (bf16[256,128]{1,0:T(8,128)(2,1)S(1)}, bf16[256,128]{1,0:T(8,128)(2,1)S(1)}, u32[]{:S(2)}, u32[]{:S(2)}) collective-permute-start(bf16[256,128]{1,0:T(8,128)(2,1)S(1)} %pad_maximum_fusion.4), channel_id=1, source_target_pairs={{0,4},{1,5},{2,6},{3,7},{4,0},{5,1},{6,2},{7,3},{8,12},{9,13},{10,... | collective-permute-start | bytes 196616 | tf_op jit(solution)/shard_map/ppermute | solution.py:236
  9.9 0.1 collective-permute-done.15.refs_2_
  10.1 2.0 %collective-permute-start.4 = (bf16[256,128]{1,0:T(8,128)(2,1)S(1)}, bf16[256,128]{1,0:T(8,128)(2,1)S(1)}, u32[]{:S(2)}, u32[]{:S(2)}) collective-permute-start(bf16[256,128]{1,0:T(8,128)(2,1)S(1)} %pad_maximum_fusion.5), channel_id=1, source_target_pairs={{0,5},{1,4},{2,7},{3,6},{4,1},{5,0},{6,3},{7,2},{8,13},{9,12},{10,... | collective-permute-start | bytes 196616 | tf_op jit(solution)/shard_map/ppermute | solution.py:236
  12.0 0.0 collective-permute-done.refs_1_
  12.0 1.5 %collective-permute-start.5 = (bf16[256,128]{1,0:T(8,128)(2,1)S(1)}, bf16[256,128]{1,0:T(8,128)(2,1)S(1)}, u32[]{:S(2)}, u32[]{:S(2)}) collective-permute-start(bf16[256,128]{1,0:T(8,128)(2,1)S(1)} %pad_maximum_fusion.6), channel_id=1, source_target_pairs={{0,6},{1,7},{2,4},{3,5},{4,2},{5,3},{6,0},{7,1},{8,14},{9,15},{10,... | collective-permute-start | bytes 196616 | tf_op jit(solution)/shard_map/ppermute | solution.py:236
  13.6 0.0 collective-permute-done.1.refs_2_
  13.6 2.8 %collective-permute-start.6 = (bf16[256,128]{1,0:T(8,128)(2,1)S(1)}, bf16[256,128]{1,0:T(8,128)(2,1)S(1)}, u32[]{:S(2)}, u32[]{:S(2)}) collective-permute-start(bf16[256,128]{1,0:T(8,128)(2,1)S(1)} %pad_maximum_fusion.7), channel_id=1, source_target_pairs={{0,7},{1,6},{2,5},{3,4},{4,3},{5,2},{6,1},{7,0},{8,15},{9,14},{10,... | collective-permute-start | bytes 196616 | tf_op jit(solution)/shard_map/ppermute | solution.py:236
  16.3 0.0 collective-permute-done.2.refs_3_
  16.3 0.0 collective-permute-start.16
  16.3 0.0 collective-permute-done.3.refs_4_
  16.4 1.4 %collective-permute-start.17 = (bf16[128,128]{1,0:T(8,128)(2,1)S(1)}, bf16[128,128]{1,0:T(8,128)(2,1)S(1)}, u32[]{:S(2)}, u32[]{:S(2)}) collective-permute-start(bf16[128,128]{1,0:T(8,128)(2,1)S(1)} %get-tuple-element.47), channel_id=1, source_target_pairs={{0,4},{1,5},{2,6},{3,7},{4,0},{5,1},{6,2},{7,3},{8,12},{9,13},{10,... | collective-permute-start | bytes 98312 | tf_op jit(solution)/shard_map/ppermute | solution.py:236
  17.7 0.7 %collective-permute-start.18 = (bf16[128,128]{1,0:T(8,128)(2,1)S(1)}, bf16[128,128]{1,0:T(8,128)(2,1)S(1)}, u32[]{:S(2)}, u32[]{:S(2)}) collective-permute-start(bf16[128,128]{1,0:T(8,128)(2,1)S(1)} %get-tuple-element.46), channel_id=1, source_target_pairs={{0,5},{1,4},{2,7},{3,6},{4,1},{5,0},{6,3},{7,2},{8,13},{9,12},{10,... | collective-permute-start | bytes 98312 | tf_op jit(solution)/shard_map/ppermute | solution.py:236
  18.4 0.4 collective-permute-done.5.refs_6_
  18.8 4.9 %collective-permute-start.19 = (bf16[128,128]{1,0:T(8,128)(2,1)S(1)}, bf16[128,128]{1,0:T(8,128)(2,1)S(1)}, u32[]{:S(2)}, u32[]{:S(2)}) collective-permute-start(bf16[128,128]{1,0:T(8,128)(2,1)S(1)} %get-tuple-element.52), channel_id=1, source_target_pairs={{0,6},{1,7},{2,4},{3,5},{4,2},{5,3},{6,0},{7,1},{8,14},{9,15},{10,... | collective-permute-start | bytes 98312 | tf_op jit(solution)/shard_map/ppermute | solution.py:236
  23.7 0.0 copy-start.3
  23.7 0.8 %copy-done.2 = bf16[128,256]{1,0:T(8,128)(2,1)S(1)} copy-done((bf16[128,256]{1,0:T(8,128)(2,1)S(1)}, bf16[128,256]{1,0:T(8,128)(2,1)}, u32[]{:S(2)}) %copy-start.2) | copy-done | bytes 65560
  24.5 0.0 copy-done.3
  24.5 2.0 %filter_gradient.1 = (bf16[144,128]{1,0:T(8,128)(2,1)S(1)}, bf16[144,128]{1,0:T(8,128)(2,1)S(1)}, bf16[144,128]{1,0:T(8,128)(2,1)S(1)}, bf16[144,128]{1,0:T(8,12...) custom-call(bf16[256,128]{1,0:T(8,128)(2,1)S(1)} %pad_maximum_fusion, ...), custom_call_target="tpu_custom_call" | custom-call | tf_op jit(solution)/shard_map/filter_gradient/pallas_call | solution.py:249
  26.5 0.3 collective-permute-start.7
  26.8 3.4 %collective-permute-start.8 = (bf16[144,128]{1,0:T(8,128)(2,1)S(1)}, bf16[144,128]{1,0:T(8,128)(2,1)S(1)}, u32[]{:S(2)}, u32[]{:S(2)}) collective-permute-start(bf16[144,128]{1,0:T(8,128)(2,1)S(1)} %get-tuple-element.26), channel_id=1, source_target_pairs={{0,2},{1,3},{2,0},{3,1},{4,6},{5,7},{6,4},{7,5},{8,10},{9,11},{10,... | collective-permute-start | bytes 110600 | tf_op jit(solution)/shard_map/ppermute | solution.py:236
  30.2 1.2 %collective-permute-start.10 = (bf16[144,128]{1,0:T(8,128)(2,1)S(1)}, bf16[144,128]{1,0:T(8,128)(2,1)S(1)}, u32[]{:S(2)}, u32[]{:S(2)}) collective-permute-start(bf16[144,128]{1,0:T(8,128)(2,1)S(1)} %get-tuple-element.28), channel_id=1, source_target_pairs={{0,4},{1,5},{2,6},{3,7},{4,0},{5,1},{6,2},{7,3},{8,12},{9,13},{10,... | collective-permute-start | bytes 110600 | tf_op jit(solution)/shard_map/ppermute | solution.py:236
  31.4 1.5 %collective-permute-start.21 = (f32[8,128]{1,0:T(8,128)S(1)}, f32[8,128]{1,0:T(8,128)S(1)}, u32[]{:S(2)}, u32[]{:S(2)}) collective-permute-start(f32[8,128]{1,0:T(8,128)S(1)} %get-tuple-element.33.refs_12_), channel_id=1, source_target_pairs={{0,8},{8,0},{16,24},{24,16},{1,9},{9,1},{17,25},{25,17},{2,10},{10... | collective-permute-start | bytes 12296 | tf_op jit(solution)/shard_map/ppermute | solution.py:264
  32.9 2.1 %collective-permute-done.21.refs_13_ = f32[8,128]{1,0:T(8,128)S(1)} collective-permute-done((f32[8,128]{1,0:T(8,128)S(1)}, f32[8,128]{1,0:T(8,128)S(1)}, u32[]{:S(2)}, u32[]{:S(2)}) %collective-permute-start.21) | collective-permute-done | bytes 4128 | tf_op jit(solution)/shard_map/ppermute | solution.py:264
  35.0 1.5 %collective-permute-start.22 = (f32[8,128]{1,0:T(8,128)S(1)}, f32[8,128]{1,0:T(8,128)S(1)}, u32[]{:S(2)}, u32[]{:S(2)}) collective-permute-start(f32[8,128]{1,0:T(8,128)S(1)} %get-tuple-element.33.refs_12_), channel_id=1, source_target_pairs={{0,16},{8,24},{16,0},{24,8},{1,17},{9,25},{17,1},{25,9},{2,18},{10... | collective-permute-start | bytes 12296 | tf_op jit(solution)/shard_map/ppermute | solution.py:264
  36.5 2.1 %collective-permute-done.22.refs_14_ = f32[8,128]{1,0:T(8,128)S(1)} collective-permute-done((f32[8,128]{1,0:T(8,128)S(1)}, f32[8,128]{1,0:T(8,128)S(1)}, u32[]{:S(2)}, u32[]{:S(2)}) %collective-permute-start.22) | collective-permute-done | bytes 4128 | tf_op jit(solution)/shard_map/ppermute | solution.py:264
  38.6 2.4 %collective-permute-start.23 = (f32[8,128]{1,0:T(8,128)S(1)}, f32[8,128]{1,0:T(8,128)S(1)}, u32[]{:S(2)}, u32[]{:S(2)}) collective-permute-start(f32[8,128]{1,0:T(8,128)S(1)} %get-tuple-element.33.refs_12_), channel_id=1, source_target_pairs={{0,24},{8,16},{16,8},{24,0},{1,25},{9,17},{17,9},{25,1},{2,26},{10... | collective-permute-start | bytes 12296 | tf_op jit(solution)/shard_map/ppermute | solution.py:264
  41.1 2.1 %collective-permute-done.23.refs_15_ = f32[8,128]{1,0:T(8,128)S(1)} collective-permute-done((f32[8,128]{1,0:T(8,128)S(1)}, f32[8,128]{1,0:T(8,128)S(1)}, u32[]{:S(2)}, u32[]{:S(2)}) %collective-permute-start.23) | collective-permute-done | bytes 4128 | tf_op jit(solution)/shard_map/ppermute | solution.py:264
  43.1 1.8 %input_gradient.1 = (bf16[144,128]{1,0:T(8,128)(2,1)S(1)}, bf16[144,128]{1,0:T(8,128)(2,1)S(1)}, bf16[144,128]{1,0:T(8,128)(2,1)S(1)}, bf16[144,128]{1,0:T(8,128...) custom-call(bf16[128,128]{1,0:T(8,128)(2,1)S(1)} %get-tuple-element., ...), custom_call_target="tpu_custom_call" | custom-call | tf_op jit(solution)/shard_map/input_gradient/pallas_call | solution.py:267
  45.0 2.7 %collective-permute-start.12 = (bf16[144,128]{1,0:T(8,128)(2,1)S(1)}, bf16[144,128]{1,0:T(8,128)(2,1)S(1)}, u32[]{:S(2)}, u32[]{:S(2)}) collective-permute-start(bf16[144,128]{1,0:T(8,128)(2,1)S(1)} %get-tuple-element.30), channel_id=1, source_target_pairs={{0,6},{1,7},{2,4},{3,5},{4,2},{5,3},{6,0},{7,1},{8,14},{9,15},{10,... | collective-permute-start | bytes 110600 | tf_op jit(solution)/shard_map/ppermute | solution.py:236
  47.6 2.5 %collective-permute-start.13 = (bf16[144,128]{1,0:T(8,128)(2,1)S(1)}, bf16[144,128]{1,0:T(8,128)(2,1)S(1)}, u32[]{:S(2)}, u32[]{:S(2)}) collective-permute-start(bf16[144,128]{1,0:T(8,128)(2,1)S(1)} %get-tuple-element.31), channel_id=1, source_target_pairs={{0,7},{1,6},{2,5},{3,4},{4,3},{5,2},{6,1},{7,0},{8,15},{9,14},{10,... | collective-permute-start | bytes 110600 | tf_op jit(solution)/shard_map/ppermute | solution.py:236
  50.1 0.1 collective-permute-start.25
  50.2 1.8 %collective-permute-start.26 = (bf16[144,128]{1,0:T(8,128)(2,1)S(1)}, bf16[144,128]{1,0:T(8,128)(2,1)S(1)}, u32[]{:S(2)}, u32[]{:S(2)}) collective-permute-start(bf16[144,128]{1,0:T(8,128)(2,1)S(1)} %get-tuple-element.37), channel_id=1, source_target_pairs={{0,3},{1,2},{2,1},{3,0},{4,7},{5,6},{6,5},{7,4},{8,11},{9,10},{10,... | collective-permute-start | bytes 110600 | tf_op jit(solution)/shard_map/ppermute | solution.py:236
  52.0 0.6 collective-permute-start.27
  52.5 0.3 collective-permute-done.13.refs_7_
  52.8 1.8 %collective-permute-start.28 = (bf16[144,128]{1,0:T(8,128)(2,1)S(1)}, bf16[144,128]{1,0:T(8,128)(2,1)S(1)}, u32[]{:S(2)}, u32[]{:S(2)}) collective-permute-start(bf16[144,128]{1,0:T(8,128)(2,1)S(1)} %get-tuple-element.39), channel_id=1, source_target_pairs={{0,5},{1,4},{2,7},{3,6},{4,1},{5,0},{6,3},{7,2},{8,13},{9,12},{10,... | collective-permute-start | bytes 110600 | tf_op jit(solution)/shard_map/ppermute | solution.py:236
  54.6 1.7 %collective-permute-start.29 = (bf16[144,128]{1,0:T(8,128)(2,1)S(1)}, bf16[144,128]{1,0:T(8,128)(2,1)S(1)}, u32[]{:S(2)}, u32[]{:S(2)}) collective-permute-start(bf16[144,128]{1,0:T(8,128)(2,1)S(1)} %get-tuple-element.40), channel_id=1, source_target_pairs={{0,6},{1,7},{2,4},{3,5},{4,2},{5,3},{6,0},{7,1},{8,14},{9,15},{10,... | collective-permute-start | bytes 110600 | tf_op jit(solution)/shard_map/ppermute | solution.py:236
  56.3 1.9 %collective-permute-start.30 = (bf16[144,128]{1,0:T(8,128)(2,1)S(1)}, bf16[144,128]{1,0:T(8,128)(2,1)S(1)}, u32[]{:S(2)}, u32[]{:S(2)}) collective-permute-start(bf16[144,128]{1,0:T(8,128)(2,1)S(1)} %get-tuple-element.41), channel_id=1, source_target_pairs={{0,7},{1,6},{2,5},{3,4},{4,3},{5,2},{6,1},{7,0},{8,15},{9,14},{10,... | collective-permute-start | bytes 110600 | tf_op jit(solution)/shard_map/ppermute | solution.py:236
  58.2 2.2 %collective-permute-done.29.refs_14_ = bf16[144,128]{1,0:T(8,128)(2,1)S(1)} collective-permute-done((bf16[144,128]{1,0:T(8,128)(2,1)S(1)}, bf16[144,128]{1,0:T(8,128)(2,1)S(1)}, u32[]{:S(2)}, u32[]{:S(2)}) %collective-permute-start.29) | collective-permute-done | bytes 36896 | tf_op jit(solution)/shard_map/ppermute | solution.py:236
  60.4 1.2 %collective-permute-done.30.refs_15_ = bf16[144,128]{1,0:T(8,128)(2,1)S(1)} collective-permute-done((bf16[144,128]{1,0:T(8,128)(2,1)S(1)}, bf16[144,128]{1,0:T(8,128)(2,1)S(1)}, u32[]{:S(2)}, u32[]{:S(2)}) %collective-permute-start.30) | collective-permute-done | bytes 36896 | tf_op jit(solution)/shard_map/ppermute | solution.py:236
  61.6 1.7 %outputs.1 = (f32[128,1024]{1,0:T(8,128)}, f32[128,1024]{1,0:T(8,128)}, f32[1,1024]{1,0:T(1,128)}) custom-call(bf16[144,128]{1,0:T(8,128)(2,1)S(1)} %get-tuple-element.24.refs_0_, bf16[144,128]{1,0:T(8,128)(2,1)S(1)} %collective-permute-done.7.refs_1_, bf16[144,128]{1,0:T(8,128)(2,1)S(1)} %collective-permute-done.8.refs_2_, ...), custom_call_target="tpu_custom_call" | custom-call | tf_op jit(solution)/shard_map/outputs/pallas_call | solution.py:286
  (39 shorter events, 0.1 us)
Async XLA Ops:
  1.8 3.3 %copy-start.5 = (bf16[128,1024]{1,0:T(8,128)(2,1)S(1)}, bf16[128,1024]{1,0:T(8,128)(2,1)}, u32[]{:S(2)}) copy-start(bf16[128,1024]{1,0:T(8,128)(2,1)} %param.8) | copy-start | bytes 786436
  1.8 10.3 %collective-permute-start = (bf16[256,128]{1,0:T(8,128)(2,1)S(1)}, bf16[256,128]{1,0:T(8,128)(2,1)S(1)}, u32[]{:S(2)}, u32[]{:S(2)}) collective-permute-start(bf16[256,128]{1,0:T(8,128)(2,1)S(1)} %pad_maximum_fusion.1), channel_id=1, source_target_pairs={{0,1},{1,0},{2,3},{3,2},{4,5},{5,4},{6,7},{7,6},{8,9},{9,8},{10,11... | collective-permute-start | bytes 196616 | tf_op jit(solution)/shard_map/ppermute | solution.py:236
  2.3 11.2 %collective-permute-start.1 = (bf16[256,128]{1,0:T(8,128)(2,1)S(1)}, bf16[256,128]{1,0:T(8,128)(2,1)S(1)}, u32[]{:S(2)}, u32[]{:S(2)}) collective-permute-start(bf16[256,128]{1,0:T(8,128)(2,1)S(1)} %pad_maximum_fusion.2), channel_id=1, source_target_pairs={{0,2},{1,3},{2,0},{3,1},{4,6},{5,7},{6,4},{7,5},{8,10},{9,11},{10,... | collective-permute-start | bytes 196616 | tf_op jit(solution)/shard_map/ppermute | solution.py:236
  5.0 11.4 %collective-permute-start.2 = (bf16[256,128]{1,0:T(8,128)(2,1)S(1)}, bf16[256,128]{1,0:T(8,128)(2,1)S(1)}, u32[]{:S(2)}, u32[]{:S(2)}) collective-permute-start(bf16[256,128]{1,0:T(8,128)(2,1)S(1)} %pad_maximum_fusion.3), channel_id=1, source_target_pairs={{0,3},{1,2},{2,1},{3,0},{4,7},{5,6},{6,5},{7,4},{8,11},{9,10},{10,... | collective-permute-start | bytes 196616 | tf_op jit(solution)/shard_map/ppermute | solution.py:236
  5.2 2.1 %collective-permute-start.14 = (bf16[128,128]{1,0:T(8,128)(2,1)S(1)}, bf16[128,128]{1,0:T(8,128)(2,1)S(1)}, u32[]{:S(2)}, u32[]{:S(2)}) collective-permute-start(bf16[128,128]{1,0:T(8,128)(2,1)S(1)} %get-tuple-element.50), channel_id=1, source_target_pairs={{0,1},{1,0},{2,3},{3,2},{4,5},{5,4},{6,7},{7,6},{8,9},{9,8},{10,11... | collective-permute-start | bytes 98312 | tf_op jit(solution)/shard_map/ppermute | solution.py:236
  5.3 4.8 %collective-permute-start.15 = (bf16[128,128]{1,0:T(8,128)(2,1)S(1)}, bf16[128,128]{1,0:T(8,128)(2,1)S(1)}, u32[]{:S(2)}, u32[]{:S(2)}) collective-permute-start(bf16[128,128]{1,0:T(8,128)(2,1)S(1)} %get-tuple-element.49), channel_id=1, source_target_pairs={{0,2},{1,3},{2,0},{3,1},{4,6},{5,7},{6,4},{7,5},{8,10},{9,11},{10,... | collective-permute-start | bytes 98312 | tf_op jit(solution)/shard_map/ppermute | solution.py:236
  7.3 9.1 %collective-permute-start.3 = (bf16[256,128]{1,0:T(8,128)(2,1)S(1)}, bf16[256,128]{1,0:T(8,128)(2,1)S(1)}, u32[]{:S(2)}, u32[]{:S(2)}) collective-permute-start(bf16[256,128]{1,0:T(8,128)(2,1)S(1)} %pad_maximum_fusion.4), channel_id=1, source_target_pairs={{0,4},{1,5},{2,6},{3,7},{4,0},{5,1},{6,2},{7,3},{8,12},{9,13},{10,... | collective-permute-start | bytes 196616 | tf_op jit(solution)/shard_map/ppermute | solution.py:236
  10.1 7.7 %collective-permute-start.4 = (bf16[256,128]{1,0:T(8,128)(2,1)S(1)}, bf16[256,128]{1,0:T(8,128)(2,1)S(1)}, u32[]{:S(2)}, u32[]{:S(2)}) collective-permute-start(bf16[256,128]{1,0:T(8,128)(2,1)S(1)} %pad_maximum_fusion.5), channel_id=1, source_target_pairs={{0,5},{1,4},{2,7},{3,6},{4,1},{5,0},{6,3},{7,2},{8,13},{9,12},{10,... | collective-permute-start | bytes 196616 | tf_op jit(solution)/shard_map/ppermute | solution.py:236
  12.0 6.8 %collective-permute-start.5 = (bf16[256,128]{1,0:T(8,128)(2,1)S(1)}, bf16[256,128]{1,0:T(8,128)(2,1)S(1)}, u32[]{:S(2)}, u32[]{:S(2)}) collective-permute-start(bf16[256,128]{1,0:T(8,128)(2,1)S(1)} %pad_maximum_fusion.6), channel_id=1, source_target_pairs={{0,6},{1,7},{2,4},{3,5},{4,2},{5,3},{6,0},{7,1},{8,14},{9,15},{10,... | collective-permute-start | bytes 196616 | tf_op jit(solution)/shard_map/ppermute | solution.py:236
  13.5 10.2 %copy-start.1 = (bf16[256,256]{1,0:T(8,128)(2,1)S(1)}, bf16[256,256]{1,0:T(8,128)(2,1)}, u32[]{:S(2)}) copy-start(bf16[256,256]{1,0:T(8,128)(2,1)} %constant.30.clone.refs_8_) | copy-start | bytes 393220
  13.6 10.1 %collective-permute-start.6 = (bf16[256,128]{1,0:T(8,128)(2,1)S(1)}, bf16[256,128]{1,0:T(8,128)(2,1)S(1)}, u32[]{:S(2)}, u32[]{:S(2)}) collective-permute-start(bf16[256,128]{1,0:T(8,128)(2,1)S(1)} %pad_maximum_fusion.7), channel_id=1, source_target_pairs={{0,7},{1,6},{2,5},{3,4},{4,3},{5,2},{6,1},{7,0},{8,15},{9,14},{10,... | collective-permute-start | bytes 196616 | tf_op jit(solution)/shard_map/ppermute | solution.py:236
  16.3 10.2 %collective-permute-start.16 = (bf16[128,128]{1,0:T(8,128)(2,1)S(1)}, bf16[128,128]{1,0:T(8,128)(2,1)S(1)}, u32[]{:S(2)}, u32[]{:S(2)}) collective-permute-start(bf16[128,128]{1,0:T(8,128)(2,1)S(1)} %get-tuple-element.48), channel_id=1, source_target_pairs={{0,3},{1,2},{2,1},{3,0},{4,7},{5,6},{6,5},{7,4},{8,11},{9,10},{10,... | collective-permute-start | bytes 98312 | tf_op jit(solution)/shard_map/ppermute | solution.py:236
  16.4 10.4 %collective-permute-start.17 = (bf16[128,128]{1,0:T(8,128)(2,1)S(1)}, bf16[128,128]{1,0:T(8,128)(2,1)S(1)}, u32[]{:S(2)}, u32[]{:S(2)}) collective-permute-start(bf16[128,128]{1,0:T(8,128)(2,1)S(1)} %get-tuple-element.47), channel_id=1, source_target_pairs={{0,4},{1,5},{2,6},{3,7},{4,0},{5,1},{6,2},{7,3},{8,12},{9,13},{10,... | collective-permute-start | bytes 98312 | tf_op jit(solution)/shard_map/ppermute | solution.py:236
  17.7 12.5 %collective-permute-start.18 = (bf16[128,128]{1,0:T(8,128)(2,1)S(1)}, bf16[128,128]{1,0:T(8,128)(2,1)S(1)}, u32[]{:S(2)}, u32[]{:S(2)}) collective-permute-start(bf16[128,128]{1,0:T(8,128)(2,1)S(1)} %get-tuple-element.46), channel_id=1, source_target_pairs={{0,5},{1,4},{2,7},{3,6},{4,1},{5,0},{6,3},{7,2},{8,13},{9,12},{10,... | collective-permute-start | bytes 98312 | tf_op jit(solution)/shard_map/ppermute | solution.py:236
  18.8 11.4 %collective-permute-start.19 = (bf16[128,128]{1,0:T(8,128)(2,1)S(1)}, bf16[128,128]{1,0:T(8,128)(2,1)S(1)}, u32[]{:S(2)}, u32[]{:S(2)}) collective-permute-start(bf16[128,128]{1,0:T(8,128)(2,1)S(1)} %get-tuple-element.52), channel_id=1, source_target_pairs={{0,6},{1,7},{2,4},{3,5},{4,2},{5,3},{6,0},{7,1},{8,14},{9,15},{10,... | collective-permute-start | bytes 98312 | tf_op jit(solution)/shard_map/ppermute | solution.py:236
  23.7 7.8 %collective-permute-start.20 = (bf16[128,128]{1,0:T(8,128)(2,1)S(1)}, bf16[128,128]{1,0:T(8,128)(2,1)S(1)}, u32[]{:S(2)}, u32[]{:S(2)}) collective-permute-start(bf16[128,128]{1,0:T(8,128)(2,1)S(1)} %get-tuple-element.45), channel_id=1, source_target_pairs={{0,7},{1,6},{2,5},{3,4},{4,3},{5,2},{6,1},{7,0},{8,15},{9,14},{10,... | collective-permute-start | bytes 98312 | tf_op jit(solution)/shard_map/ppermute | solution.py:236
  23.7 0.8 %copy-start.2 = (bf16[128,256]{1,0:T(8,128)(2,1)S(1)}, bf16[128,256]{1,0:T(8,128)(2,1)}, u32[]{:S(2)}) copy-start(bf16[128,256]{1,0:T(8,128)(2,1)} %constant.31.clone.refs_9_) | copy-start | bytes 196612
  23.7 0.9 %copy-start.3 = (bf16[128,256]{1,0:T(8,128)(2,1)S(1)}, bf16[128,256]{1,0:T(8,128)(2,1)}, u32[]{:S(2)}) copy-start(bf16[128,256]{1,0:T(8,128)(2,1)} %constant.32.clone.refs_10_) | copy-start | bytes 196612
  26.5 18.4 %collective-permute-start.7 = (bf16[144,128]{1,0:T(8,128)(2,1)S(1)}, bf16[144,128]{1,0:T(8,128)(2,1)S(1)}, u32[]{:S(2)}, u32[]{:S(2)}) collective-permute-start(bf16[144,128]{1,0:T(8,128)(2,1)S(1)} %get-tuple-element.25), channel_id=1, source_target_pairs={{0,1},{1,0},{2,3},{3,2},{4,5},{5,4},{6,7},{7,6},{8,9},{9,8},{10,11... | collective-permute-start | bytes 110600 | tf_op jit(solution)/shard_map/ppermute | solution.py:236
  26.8 20.9 %collective-permute-start.8 = (bf16[144,128]{1,0:T(8,128)(2,1)S(1)}, bf16[144,128]{1,0:T(8,128)(2,1)S(1)}, u32[]{:S(2)}, u32[]{:S(2)}) collective-permute-start(bf16[144,128]{1,0:T(8,128)(2,1)S(1)} %get-tuple-element.26), channel_id=1, source_target_pairs={{0,2},{1,3},{2,0},{3,1},{4,6},{5,7},{6,4},{7,5},{8,10},{9,11},{10,... | collective-permute-start | bytes 110600 | tf_op jit(solution)/shard_map/ppermute | solution.py:236
  30.2 19.9 %collective-permute-start.9 = (bf16[144,128]{1,0:T(8,128)(2,1)S(1)}, bf16[144,128]{1,0:T(8,128)(2,1)S(1)}, u32[]{:S(2)}, u32[]{:S(2)}) collective-permute-start(bf16[144,128]{1,0:T(8,128)(2,1)S(1)} %get-tuple-element.27), channel_id=1, source_target_pairs={{0,3},{1,2},{2,1},{3,0},{4,7},{5,6},{6,5},{7,4},{8,11},{9,10},{10,... | collective-permute-start | bytes 110600 | tf_op jit(solution)/shard_map/ppermute | solution.py:236
  30.2 19.9 %collective-permute-start.10 = (bf16[144,128]{1,0:T(8,128)(2,1)S(1)}, bf16[144,128]{1,0:T(8,128)(2,1)S(1)}, u32[]{:S(2)}, u32[]{:S(2)}) collective-permute-start(bf16[144,128]{1,0:T(8,128)(2,1)S(1)} %get-tuple-element.28), channel_id=1, source_target_pairs={{0,4},{1,5},{2,6},{3,7},{4,0},{5,1},{6,2},{7,3},{8,12},{9,13},{10,... | collective-permute-start | bytes 110600 | tf_op jit(solution)/shard_map/ppermute | solution.py:236
  31.4 3.6 %collective-permute-start.21 = (f32[8,128]{1,0:T(8,128)S(1)}, f32[8,128]{1,0:T(8,128)S(1)}, u32[]{:S(2)}, u32[]{:S(2)}) collective-permute-start(f32[8,128]{1,0:T(8,128)S(1)} %get-tuple-element.33.refs_12_), channel_id=1, source_target_pairs={{0,8},{8,0},{16,24},{24,16},{1,9},{9,1},{17,25},{25,17},{2,10},{10... | collective-permute-start | bytes 12296 | tf_op jit(solution)/shard_map/ppermute | solution.py:264
  35.0 3.6 %collective-permute-start.22 = (f32[8,128]{1,0:T(8,128)S(1)}, f32[8,128]{1,0:T(8,128)S(1)}, u32[]{:S(2)}, u32[]{:S(2)}) collective-permute-start(f32[8,128]{1,0:T(8,128)S(1)} %get-tuple-element.33.refs_12_), channel_id=1, source_target_pairs={{0,16},{8,24},{16,0},{24,8},{1,17},{9,25},{17,1},{25,9},{2,18},{10... | collective-permute-start | bytes 12296 | tf_op jit(solution)/shard_map/ppermute | solution.py:264
  38.6 4.5 %collective-permute-start.23 = (f32[8,128]{1,0:T(8,128)S(1)}, f32[8,128]{1,0:T(8,128)S(1)}, u32[]{:S(2)}, u32[]{:S(2)}) collective-permute-start(f32[8,128]{1,0:T(8,128)S(1)} %get-tuple-element.33.refs_12_), channel_id=1, source_target_pairs={{0,24},{8,16},{16,8},{24,0},{1,25},{9,17},{17,9},{25,1},{2,26},{10... | collective-permute-start | bytes 12296 | tf_op jit(solution)/shard_map/ppermute | solution.py:264
  43.1 7.0 %collective-permute-start.11 = (bf16[144,128]{1,0:T(8,128)(2,1)S(1)}, bf16[144,128]{1,0:T(8,128)(2,1)S(1)}, u32[]{:S(2)}, u32[]{:S(2)}) collective-permute-start(bf16[144,128]{1,0:T(8,128)(2,1)S(1)} %get-tuple-element.29), channel_id=1, source_target_pairs={{0,5},{1,4},{2,7},{3,6},{4,1},{5,0},{6,3},{7,2},{8,13},{9,12},{10,... | collective-permute-start | bytes 110600 | tf_op jit(solution)/shard_map/ppermute | solution.py:236
  43.1 18.4 %copy-start = (bf16[128,1024]{1,0:T(8,128)(2,1)S(1)}, bf16[128,1024]{1,0:T(8,128)(2,1)}, u32[]{:S(2)}) copy-start(bf16[128,1024]{1,0:T(8,128)(2,1)} %refs_16_.1) | copy-start | bytes 786436
  45.0 7.0 %collective-permute-start.12 = (bf16[144,128]{1,0:T(8,128)(2,1)S(1)}, bf16[144,128]{1,0:T(8,128)(2,1)S(1)}, u32[]{:S(2)}, u32[]{:S(2)}) collective-permute-start(bf16[144,128]{1,0:T(8,128)(2,1)S(1)} %get-tuple-element.30), channel_id=1, source_target_pairs={{0,6},{1,7},{2,4},{3,5},{4,2},{5,3},{6,0},{7,1},{8,14},{9,15},{10,... | collective-permute-start | bytes 110600 | tf_op jit(solution)/shard_map/ppermute | solution.py:236
  47.6 5.2 %collective-permute-start.13 = (bf16[144,128]{1,0:T(8,128)(2,1)S(1)}, bf16[144,128]{1,0:T(8,128)(2,1)S(1)}, u32[]{:S(2)}, u32[]{:S(2)}) collective-permute-start(bf16[144,128]{1,0:T(8,128)(2,1)S(1)} %get-tuple-element.31), channel_id=1, source_target_pairs={{0,7},{1,6},{2,5},{3,4},{4,3},{5,2},{6,1},{7,0},{8,15},{9,14},{10,... | collective-permute-start | bytes 110600 | tf_op jit(solution)/shard_map/ppermute | solution.py:236
  50.1 4.5 %collective-permute-start.24 = (bf16[144,128]{1,0:T(8,128)(2,1)S(1)}, bf16[144,128]{1,0:T(8,128)(2,1)S(1)}, u32[]{:S(2)}, u32[]{:S(2)}) collective-permute-start(bf16[144,128]{1,0:T(8,128)(2,1)S(1)} %get-tuple-element.35), channel_id=1, source_target_pairs={{0,1},{1,0},{2,3},{3,2},{4,5},{5,4},{6,7},{7,6},{8,9},{9,8},{10,11... | collective-permute-start | bytes 110600 | tf_op jit(solution)/shard_map/ppermute | solution.py:236
  50.1 6.2 %collective-permute-start.25 = (bf16[144,128]{1,0:T(8,128)(2,1)S(1)}, bf16[144,128]{1,0:T(8,128)(2,1)S(1)}, u32[]{:S(2)}, u32[]{:S(2)}) collective-permute-start(bf16[144,128]{1,0:T(8,128)(2,1)S(1)} %get-tuple-element.36), channel_id=1, source_target_pairs={{0,2},{1,3},{2,0},{3,1},{4,6},{5,7},{6,4},{7,5},{8,10},{9,11},{10,... | collective-permute-start | bytes 110600 | tf_op jit(solution)/shard_map/ppermute | solution.py:236
  50.2 8.0 %collective-permute-start.26 = (bf16[144,128]{1,0:T(8,128)(2,1)S(1)}, bf16[144,128]{1,0:T(8,128)(2,1)S(1)}, u32[]{:S(2)}, u32[]{:S(2)}) collective-permute-start(bf16[144,128]{1,0:T(8,128)(2,1)S(1)} %get-tuple-element.37), channel_id=1, source_target_pairs={{0,3},{1,2},{2,1},{3,0},{4,7},{5,6},{6,5},{7,4},{8,11},{9,10},{10,... | collective-permute-start | bytes 110600 | tf_op jit(solution)/shard_map/ppermute | solution.py:236
  52.0 6.2 %collective-permute-start.27 = (bf16[144,128]{1,0:T(8,128)(2,1)S(1)}, bf16[144,128]{1,0:T(8,128)(2,1)S(1)}, u32[]{:S(2)}, u32[]{:S(2)}) collective-permute-start(bf16[144,128]{1,0:T(8,128)(2,1)S(1)} %get-tuple-element.38), channel_id=1, source_target_pairs={{0,4},{1,5},{2,6},{3,7},{4,0},{5,1},{6,2},{7,3},{8,12},{9,13},{10,... | collective-permute-start | bytes 110600 | tf_op jit(solution)/shard_map/ppermute | solution.py:236
  52.8 5.4 %collective-permute-start.28 = (bf16[144,128]{1,0:T(8,128)(2,1)S(1)}, bf16[144,128]{1,0:T(8,128)(2,1)S(1)}, u32[]{:S(2)}, u32[]{:S(2)}) collective-permute-start(bf16[144,128]{1,0:T(8,128)(2,1)S(1)} %get-tuple-element.39), channel_id=1, source_target_pairs={{0,5},{1,4},{2,7},{3,6},{4,1},{5,0},{6,3},{7,2},{8,13},{9,12},{10,... | collective-permute-start | bytes 110600 | tf_op jit(solution)/shard_map/ppermute | solution.py:236
  54.6 7.0 %copy-start.4 = (f32[1024]{0:T(1024)S(1)}, f32[1024]{0:T(1024)}, u32[]{:S(2)}) copy-start(f32[1024]{0:T(1024)} %param.10) | copy-start | bytes 12292
  54.6 5.8 %collective-permute-start.29 = (bf16[144,128]{1,0:T(8,128)(2,1)S(1)}, bf16[144,128]{1,0:T(8,128)(2,1)S(1)}, u32[]{:S(2)}, u32[]{:S(2)}) collective-permute-start(bf16[144,128]{1,0:T(8,128)(2,1)S(1)} %get-tuple-element.40), channel_id=1, source_target_pairs={{0,6},{1,7},{2,4},{3,5},{4,2},{5,3},{6,0},{7,1},{8,14},{9,15},{10,... | collective-permute-start | bytes 110600 | tf_op jit(solution)/shard_map/ppermute | solution.py:236
  56.3 5.3 %collective-permute-start.30 = (bf16[144,128]{1,0:T(8,128)(2,1)S(1)}, bf16[144,128]{1,0:T(8,128)(2,1)S(1)}, u32[]{:S(2)}, u32[]{:S(2)}) collective-permute-start(bf16[144,128]{1,0:T(8,128)(2,1)S(1)} %get-tuple-element.41), channel_id=1, source_target_pairs={{0,7},{1,6},{2,5},{3,4},{4,3},{5,2},{6,1},{7,0},{8,15},{9,14},{10,... | collective-permute-start | bytes 110600 | tf_op jit(solution)/shard_map/ppermute | solution.py:236

commit v2 on v1

--- a/solution.py
+++ b/solution.py
@@ -14,7 +14,8 @@
 low_power = 120
 top_code = 128 * octaves - 1
 tail_rows = 16
-vmem_bytes = 48 * 1024 * 1024
+first_flops = 4 * 10**9
+second_flops = 2 * 10**10
 
 
 def tables(length):
@@ -58,12 +59,14 @@
     return jnp.where(carrier < 0, -units, units) * (scale * (1.0 / top_code))
 
 
-def tail_tile(rows, width):
+def tail_tile(first_row, rows, width):
     row_ids = lax.broadcasted_iota(jnp.int32, (tail_rows, width), 0)
     tile = jnp.zeros((tail_rows, width), jnp.float32)
     for i, row in enumerate(rows):
-        tile = jnp.where(row_ids == i, jnp.broadcast_to(row, (tail_rows, width)), tile)
-    return tile.astype(jnp.bfloat16)
+        tile = jnp.where(
+            row_ids == first_row + i, jnp.broadcast_to(row, (tail_rows, width)), tile
+        )
+    return tile
 
 
 def correlate_rows(pairs, others, size):
@@ -80,29 +83,59 @@
     return results
 
 
-def send_results(position, size, acc, back_high, back_low, emit):
+def send_results(position, order, acc, back_high, back_low, emit):
     width = acc.shape[2]
-    for k in range(0, size, 2):
-        spec = jnp.concatenate([acc[position ^ k], acc[position ^ (k + 1)]], axis=1)
+    for i in range(0, len(order), 2):
+        spec = jnp.concatenate([acc[position ^ order[i]], acc[position ^ order[i + 1]]], axis=1)
         high = spec.astype(jnp.bfloat16)
         low = (spec - high.astype(jnp.float32)).astype(jnp.bfloat16)
         dot = functools.partial(jnp.dot, preferred_element_type=jnp.float32)
         block = dot(back_high[...], high) + dot(back_high[...], low) + dot(back_low[...], high)
-        emit(k, block[:, :width])
-        emit(k + 1, block[:, width:])
-
-
-def first_kernel(size, length, *refs):
-    arrived = refs[:size]
-    both, back_high, back_low = refs[size : size + 3]
-    out = refs[size + 3 : 2 * size + 3]
-    pair_spec, squares, spec, acc = refs[2 * size + 3 :]
+        emit(i, block[:, :width])
+        emit(i + 1, block[:, width:])
+
+
+def columns_kernel(chips, far, length, part, arrays, *refs):
+    pairs, (own, other, taps, other_taps) = refs[:-4], refs[-4:]
+    position = lax.axis_index("ctx")
+
+    def put(out, row, j, k):
+        columns = pl.ds(pl.multiple_of((position ^ k) * part, part), part)
+        out[row : row + length] = arrays[j, :, columns]
+
+    for i, chip in enumerate(chips):
+        parts = 2 if i < far else 3
+        here, there, there_row = (pairs[i], pairs[i], parts * length) if chip else (own, other, 0)
+        for j in range(parts):
+            put(here, j * length, j, 2 * chip)
+            put(there, there_row + j * length, j, 2 * chip + 1)
+    for i, chip in enumerate(chips[:far]):
+        put(taps, i * length, 2, 2 * chip)
+        put(other_taps, i * length, 2, 2 * chip + 1)
+
+
+def pass_kernel(*refs):
+    arrived, own, other, kept, passed = refs[:-4], *refs[-4:]
+    row = 0
+    for pair in arrived:
+        rows = pair.shape[0] // 2
+        kept[row : row + rows] = pair[:rows]
+        passed[row : row + rows] = pair[rows:]
+        row += rows
+    kept[row:] = own[...]
+    passed[row:] = other[...]
+
+
+def first_kernel(order, length, places, *refs):
+    size = len(order)
+    both, back_high, back_low, codes_out, tails_out, pair_spec, squares, spec, acc = refs[-9:]
     width = spec.shape[2] // 2
     position = lax.axis_index("ctx")
 
     skip = jnp.zeros((1, width), jnp.float32)
-    for k in range(size):
-        grad, other = arrived[k][:length], arrived[k][length:]
+    for i, k in enumerate(order):
+        ref, row = places[i]
+        grad, other = refs[ref][row : row + length], refs[ref][row + length : row + 2 * length]
         skip += jnp.sum(grad.astype(jnp.float32) * other.astype(jnp.float32), axis=0, keepdims=True)
         lanes = jnp.concatenate([grad, other], axis=1)
         spec[position ^ k] = jnp.dot(
@@ -135,31 +168,29 @@
     skip_parts = three_parts(skip)
     squares[...] = jnp.zeros_like(squares)
 
-    def emit(k, block):
+    def emit(i, block):
         squares[...] += jnp.sum((block * block).reshape(length // 8, 8, width), axis=0)
-        codes, scale = encode(block)
-        out[k][:length] = codes
-        out[k][length:] = tail_tile((scale,) + skip_parts, width)
-
-    send_results(position, size, acc, back_high, back_low, emit)
-
-
-def second_kernel(size, length, sums, *refs):
-    arrived = refs[:size]
-    both, back_high, back_low, pair_spec = refs[size : size + 4]
-    partial_squares = refs[size + 4 : size + 4 + sums]
-    out = refs[size + 4 + sums : 2 * size + 4 + sums]
-    spec, acc = refs[2 * size + 4 + sums :]
+        codes_out[i], scale = encode(block)
+        tails_out[i] = tail_tile(0, (scale,) + skip_parts, width)
+
+    send_results(position, order, acc, back_high, back_low, emit)
+
+
+def second_kernel(order, length, places, *refs):
+    size = len(order)
+    both, back_high, back_low, pair_spec, codes_out, tails_out, spec, acc = refs[-8:]
     width = spec.shape[2]
     position = lax.axis_index("ctx")
 
-    for k in range(0, size, 2):
-        lanes = jnp.concatenate([arrived[k][...], arrived[k + 1][...]], axis=1)
+    for i in range(0, size, 2):
+        lanes = jnp.concatenate(
+            [refs[ref][row : row + length] for ref, row in places[i : i + 2]], axis=1
+        )
         both_specs = jnp.dot(
             both[...], jnp.concatenate([lanes, lanes], axis=0), preferred_element_type=jnp.float32
         )
-        spec[position ^ k] = both_specs[:, :width]
-        spec[position ^ (k + 1)] = both_specs[:, width:]
+        spec[position ^ order[i]] = both_specs[:, :width]
+        spec[position ^ order[i + 1]] = both_specs[:, width:]
 
     def rows(r, carry):
         real_rows = pl.ds(pl.multiple_of(r * 8, 8), 8)
@@ -172,47 +203,59 @@
         return carry
 
     lax.fori_loop(0, length // 8, rows, 0)
+
+    def emit(i, block):
+        codes_out[i], scale = encode(block)
+        tails_out[i] = tail_tile(4, (scale,), width)
+
+    send_results(position, order, acc, back_high, back_low, emit)
+
+
+def message_kernel(size, length, sums, *refs):
+    filter_codes, filter_tails, input_codes, input_tails = refs[:4]
+    partial_squares, out = refs[4 : 4 + sums], refs[4 + sums :]
     squares = partial_squares[0][...]
     for other in partial_squares[1:]:
         squares += other[...]
     total = jnp.sum(jnp.sum(squares, axis=0, keepdims=True), axis=1, keepdims=True)
-    total_parts = three_parts(jnp.broadcast_to(total, (1, width)))
-
-    def emit(k, block):
-        codes, scale = encode(block)
-        out[k][:length] = codes
-        out[k][length:] = tail_tile((scale,) + total_parts, width)
-
-    send_results(position, size, acc, back_high, back_low, emit)
-
-
-def last_kernel(size, length, part, clip_limit, *refs):
-    filter_codes, input_codes = refs[:size], refs[size : 2 * size]
-    grad, gain, input_grad, filter_grad, skip_grad = refs[2 * size :]
+    width = squares.shape[1]
+    total_rows = tail_tile(5, three_parts(jnp.broadcast_to(total, (1, width))), width)
+    for i in range(size):
+        out[i][:length] = filter_codes[i]
+        out[i][length : 2 * length] = input_codes[i]
+        tail = filter_tails[i] + input_tails[i] + total_rows
+        out[i][2 * length :] = tail.astype(jnp.bfloat16)
+
+
+def last_kernel(order, length, part, clip_limit, *refs):
+    size = len(order)
+    messages = refs[:size]
+    grad, gain, input_grad, filter_grad, skip_grad = refs[size:]
     position = lax.axis_index("ctx")
     total = jnp.zeros((1, part), jnp.float32)
-    for k in range(size):
-        tail = input_codes[k][length:].astype(jnp.float32)
-        total += tail[1:2] + tail[2:3] + tail[3:4]
+    for message in messages:
+        tail = message[2 * length :].astype(jnp.float32)
+        total += tail[5:6] + tail[6:7] + tail[7:8]
     factor = jnp.minimum(1.0, clip_limit / jnp.sqrt(total + epsilon))
-    for k in range(size):
+    for k, message in zip(order, messages):
         columns = pl.ds(pl.multiple_of((position ^ k) * part, part), part)
-        tail = filter_codes[k][length:].astype(jnp.float32)
-        filter_grad[:, columns] = decode(filter_codes[k][:length], tail[0:1]) * factor
+        tail = message[2 * length :].astype(jnp.float32)
+        filter_grad[:, columns] = decode(message[:length], tail[0:1]) * factor
         skip_grad[:, columns] = tail[1:2] + tail[2:3] + tail[3:4]
-        tail = input_codes[k][length:].astype(jnp.float32)
         input_grad[:, columns] = (
-            decode(input_codes[k][:length], tail[0:1])
+            decode(message[length : 2 * length], tail[4:5])
             + gain[:, columns] * grad[:, columns].astype(jnp.float32)
         )
 
 
-def run(kernel, name, out_shape, scratch=()):
+def run(kernel, name, vmem_bytes, out_shape, scratch=(), flops=10**9, **specs):
     return pl.pallas_call(
         kernel,
         out_shape=out_shape,
         scratch_shapes=scratch,
         name=name,
+        **specs,
+        cost_estimate=pl.CostEstimate(flops=flops, bytes_accessed=0, transcendentals=0),
         compiler_params=pltpu.CompilerParams(vmem_limit_bytes=vmem_bytes),
     )
 
@@ -226,31 +269,76 @@
     position = lax.axis_index("ctx")
     both, back_high, back_low = tables(length)
     f32, bf16 = jnp.float32, jnp.bfloat16
+    chips = sorted(range(size // 2), key=lambda chip: (-chip.bit_length(), chip))
+    order = [k for chip in chips for k in (2 * chip, 2 * chip + 1)]
+    far = size // 4
+    vmem_bytes = (8 + size) * 2**20
 
     def columns_for(array, k):
         block = lax.dynamic_slice_in_dim(array, (position ^ k) * part, part, 1)
         return jnp.pad(block, ((0, 0), (0, width - part)))
 
-    def exchange(blocks):
-        return [
-            blocks[k] if k == 0 else lax.ppermute(blocks[k], "ctx", [(i, i ^ k) for i in range(size)])
-            for k in range(size)
+    def send(block, k):
+        return lax.ppermute(block, "ctx", [(i, i ^ k) for i in range(size)])
+
+    three = (out_grad, inputs, filter_taps)
+    parts = [2] * far + [3] * (len(chips) - far)
+    if width == part:
+        blocks = [2 * n for n in parts[:-1]] + [3, 3, far, far]
+        *pairs, own, other, taps, other_taps = run(
+            functools.partial(columns_kernel, chips, far, length, part),
+            "columns", vmem_bytes,
+            [jax.ShapeDtypeStruct((n * length, width), bf16) for n in blocks],
+        )(jnp.stack(three))
+    else:
+        cores = [
+            [
+                jnp.concatenate([columns_for(a, 2 * chip + core) for a in three[:n]])
+                for chip, n in zip(chips, parts)
+            ]
+            for core in range(2)
         ]
-
-    grad_input = exchange(
+        pairs = [jnp.concatenate(two) for two in zip(*cores)][:-1]
+        own, other = cores[0][-1], cores[1][-1]
+        taps, other_taps = (
+            jnp.concatenate([columns_for(filter_taps, 2 * chip + core) for chip in chips[:far]])
+            for core in range(2)
+        )
+
+    arrived = [send(pair, 2 * chip) for chip, pair in zip(chips, pairs)]
+    kept, passed_on = run(
+        pass_kernel,
+        "passing", vmem_bytes,
+        [jax.ShapeDtypeStruct((sum(parts) * length, width), bf16)] * 2,
+    )(*arrived, own, other)
+    passed_on = send(passed_on, 1)
+    sibling_taps = send(other_taps, 1)
+    sibling_taps, _ = lax.optimization_barrier((sibling_taps, arrived[-1]))
+    arrived_taps = [
+        send(
+            jnp.concatenate(
+                [held[i * length : (i + 1) * length] for held in (taps, sibling_taps)]
+            ),
+            2 * chip,
+        )
+        for i, chip in enumerate(chips[:far])
+    ]
+    first_places, second_places = [], []
+    row = 0
+    for i, n in enumerate(parts):
+        first_places += [(0, row), (1, row)]
+        taps_row = row + 2 * length
+        second_places += [(i, 0), (i, length)] if i < far else [(far, taps_row), (far + 1, taps_row)]
+        row += n * length
+    first_arrived = [kept, passed_on]
+    second_arrived = [*arrived_taps, kept, passed_on]
+
+    codes, tails, pair_spec, squares = run(
+        functools.partial(first_kernel, order, length, first_places),
+        "filter_gradient", vmem_bytes,
         [
-            jnp.concatenate([columns_for(out_grad, k), columns_for(inputs, k)], axis=0)
-            for k in range(size)
-        ]
-    )
-    taps = exchange([columns_for(filter_taps, k) for k in range(size)])
-
-    message = jax.ShapeDtypeStruct((length + tail_rows, width), bf16)
-    *filter_codes, pair_spec, squares = run(
-        functools.partial(first_kernel, size, length),
-        "filter_gradient",
-        [message] * size
-        + [
+            jax.ShapeDtypeStruct((size, length, width), bf16),
+            jax.ShapeDtypeStruct((size, tail_rows, width), f32),
             jax.ShapeDtypeStruct((size, 2 * length, width), f32),
             jax.ShapeDtypeStruct((8, width), f32),
         ],
@@ -258,22 +346,31 @@
             pltpu.VMEM((size, 2 * length, 2 * width), f32),
             pltpu.VMEM((size, 2 * length, width), f32),
         ],
-    )(*grad_input, both, back_high, back_low)
-    filter_codes = exchange(filter_codes)
+        flops=first_flops,
+    )(*first_arrived, both, back_high, back_low)
     all_squares = [
         squares if k == 0 else lax.ppermute(squares, "chan", [(i, i ^ k) for i in range(columns)])
         for k in range(columns)
     ]
-    input_codes = run(
-        functools.partial(second_kernel, size, length, columns),
-        "input_gradient",
-        [message] * size,
+    input_codes, input_tails = run(
+        functools.partial(second_kernel, order, length, second_places),
+        "input_gradient", vmem_bytes,
+        [
+            jax.ShapeDtypeStruct((size, length, width), bf16),
+            jax.ShapeDtypeStruct((size, tail_rows, width), f32),
+        ],
         [
             pltpu.VMEM((size, 2 * length, width), f32),
             pltpu.VMEM((size, 2 * length, width), f32),
         ],
-    )(*taps, both, back_high, back_low, pair_spec, *all_squares)
-    input_codes = exchange(input_codes)
+        flops=second_flops,
+    )(*second_arrived, both, back_high, back_low, pair_spec)
+    messages = run(
+        functools.partial(message_kernel, size, length, columns),
+        "messages", vmem_bytes,
+        [jax.ShapeDtypeStruct((2 * length + tail_rows, width), bf16)] * size,
+    )(codes, tails, input_codes, input_tails, *all_squares)
+    messages = [send(message, k) if k else message for k, message in zip(order, messages)]
 
     clip_limit = 0.25 * math.sqrt(length * size * chan_width * columns)
     whole = size * width
@@ -284,14 +381,14 @@
         ).reshape(a.shape[0], whole)
         grad_rows, gain = spread(grad_rows), spread(gain)
     input_grad, filter_grad, skip_grad = run(
-        functools.partial(last_kernel, size, length, width, clip_limit),
-        "outputs",
+        functools.partial(last_kernel, order, length, width, clip_limit),
+        "outputs", vmem_bytes,
         [
             jax.ShapeDtypeStruct((length, whole), f32),
             jax.ShapeDtypeStruct((length, whole), f32),
             jax.ShapeDtypeStruct((1, whole), f32),
         ],
-    )(*filter_codes, *input_codes, grad_rows, gain)
+    )(*messages, grad_rows, gain)
     if width != part:
         gather = lambda a: a.reshape(a.shape[0], size, width)[:, :, :part].reshape(
             a.shape[0], chan_width

time: 63.5 us -> 48.1 us (0.76)
  starting transfers between devices: 44.4 us -> 20.4 us
  waiting for transfers between devices: 10.5 us -> 19.7 us
  local copies, waits for them, and re-layouts: 2 us -> 0.03 us
  other arithmetic: 0.05 us -> 1.21 us
    ppermute x28 -> x14, starting transfers between devices: 39 us -> 16.9 us  [send(): return lax.ppermute(block, 'ctx', [(i, i ^ k) for i in range(size)])]
    ppermute x28 -> x14, waiting for transfers between devices: 4.23 us -> 18.4 us  [send(): return lax.ppermute(block, 'ctx', [(i, i ^ k) for i in range(size)])]
    ppermute x3, waiting for transfers between devices: 6.26 us -> 1.28 us  [per_device(): lax.ppermute(squares, 'chan', [(i, i ^ k) for i in range(columns)])]
    ppermute x3, starting transfers between devices: 5.46 us -> 3.55 us  [per_device(): lax.ppermute(squares, 'chan', [(i, i ^ k) for i in range(columns)])]
    another operation x0 -> x1, other arithmetic: none -> 1.2 us  [per_device(): jnp.stack(three)]
    dynamic_slice x2 -> x0, local copies, waits for them, and re-layouts: 1.14 us -> none  [columns_for(): block = lax.dynamic_slice_in_dim(array, (position ^ k) * part, part, 1)]
    unnamed x12 -> x10, local copies, waits for them, and re-layouts: 0.85 us -> 0.02 us
    pallas_call x3 -> x6, Pallas kernels: 5.43 us -> 5.78 us  [the longest x1 1.95 us: per_device(): run(functools.partial(first_kernel, order, length, first_places), 'filter...]
  transfers between devices with their start and end apart: 31 -> 17, of which waited for: 8 -> 6; matrix products, arithmetic and copies ran while one was open for 0% -> 0% of each run, Pallas kernels for 6% -> 8%
where the time goes in v2:
time: 48.1 us; the launch traced here: 47.9 us
  starting transfers between devices  20.4 us (42%)
  waiting for transfers between devices  19.7 us (41%)
  Pallas kernels  5.78 us (12%)
  other arithmetic  1.21 us (3%)
  between operations  0.74 us (2%)
    ppermute x14, waiting for transfers between devices, send(): return lax.ppermute(block, 'ctx', [(i, i ^ k) for i in range(size)])  18.4 us
    ppermute x14, starting transfers between devices, send(): return lax.ppermute(block, 'ctx', [(i, i ^ k) for i in range(size)])  16.9 us
    ppermute x3, starting transfers between devices, per_device(): lax.ppermute(squares, 'chan', [(i, i ^ k) for i in range(columns)])  3.55 us
    pallas_call x1, Pallas kernels, per_device(): run(functools.partial(first_kernel, order, length, first_places), 'filter...  1.95 us
    pallas_call x1, Pallas kernels, per_device(): run(functools.partial(second_kernel, order, length, second_places), 'inpu...  1.76 us
    pallas_call x1, Pallas kernels, per_device(): run(functools.partial(last_kernel, order, length, width, clip_limit), 'ou...  1.72 us
    ppermute x3, waiting for transfers between devices, per_device(): lax.ppermute(squares, 'chan', [(i, i ^ k) for i in range(columns)])  1.28 us
    another operation x1, other arithmetic, per_device(): jnp.stack(three)  1.2 us
  transfers between devices with their start and end apart: 17, of which 6 were waited for; matrix products, arithmetic and copies ran while one was open for 0% of the time, Pallas kernels for 8%

profile of v2, /device:TPU:0, one launch (start us, length us, event | category | flops | bytes accessed | tf_op | source)
XLA Modules:
  0.0 47.9 jit_solution(2640258671736119768)
XLA Ops:
  0.6 1.2 %pad_maximum_fusion.arrays = bf16[3,128,1024]{2,1,0:T(8,128)(2,1)S(1)} fusion(bf16[1,128,1024]{2,1,0:T(8,128)(2,1)} %bitcast.7, bf16[1,128,1024]{2,1,0:T(8,128)(2,1)} %bitcast.8, bf16[1,128,1024]{2,1,0:T(8,128)(2,1)} %bitcast.5), kind=kLoop, calls=%fused_computation | loop fusion | flops 786432 | bytes 1572864 | tf_op jit(solution)/shard_map/stack | solution.py:292
  1.8 0.2 columns.1
  2.1 0.5 %collective-permute-start.4 = (bf16[256,128]{1,0:T(8,128)(2,1)S(1)}, bf16[256,128]{1,0:T(8,128)(2,1)S(1)}, u32[]{:S(2)}, u32[]{:S(2)}) collective-permute-start(bf16[256,128]{1,0:T(8,128)(2,1)S(1)} %get-tuple-element.40), channel_id=1, source_target_pairs={{0,1},{1,0},{2,3},{3,2},{4,5},{5,4},{6,7},{7,6},{8,9},{9,8},{10,11... | collective-permute-start | bytes 196616 | tf_op jit(solution)/shard_map/ppermute | solution.py:282
  2.6 3.7 %collective-permute-start = (bf16[512,128]{1,0:T(8,128)(2,1)S(1)}, bf16[512,128]{1,0:T(8,128)(2,1)S(1)}, u32[]{:S(2)}, u32[]{:S(2)}) collective-permute-start(bf16[512,128]{1,0:T(8,128)(2,1)S(1)} %get-tuple-element.30), channel_id=1, source_target_pairs={{0,4},{1,5},{2,6},{3,7},{4,0},{5,1},{6,2},{7,3},{8,12},{9,13},{10,... | collective-permute-start | bytes 393224 | tf_op jit(solution)/shard_map/ppermute | solution.py:282
  6.2 1.3 %collective-permute-start.1 = (bf16[512,128]{1,0:T(8,128)(2,1)S(1)}, bf16[512,128]{1,0:T(8,128)(2,1)S(1)}, u32[]{:S(2)}, u32[]{:S(2)}) collective-permute-start(bf16[512,128]{1,0:T(8,128)(2,1)S(1)} %get-tuple-element.31), channel_id=1, source_target_pairs={{0,6},{1,7},{2,4},{3,5},{4,2},{5,3},{6,0},{7,1},{8,14},{9,15},{10,... | collective-permute-start | bytes 393224 | tf_op jit(solution)/shard_map/ppermute | solution.py:282
  7.6 0.2 collective-permute-start.2
  7.8 0.0 collective-permute-done.4
  7.8 10.9 %collective-permute-done.2.refs_2_ = bf16[768,128]{1,0:T(8,128)(2,1)S(1)} collective-permute-done((bf16[768,128]{1,0:T(8,128)(2,1)S(1)}, bf16[768,128]{1,0:T(8,128)(2,1)S(1)}, u32[]{:S(2)}, u32[]{:S(2)}) %collective-permute-start.2) | collective-permute-done | bytes 196640 | tf_op jit(solution)/shard_map/ppermute | solution.py:282
  18.7 0.0 collective-permute-done.refs_0_
  18.7 0.0 collective-permute-done.1.refs_1_
  18.8 0.1 collective-permute-start.3
  18.9 0.0 copy-start.2
  18.9 2.8 %collective-permute-start.5 = (bf16[256,128]{1,0:T(8,128)(2,1)S(1)}, bf16[256,128]{1,0:T(8,128)(2,1)S(1)}, u32[]{:S(2)}, u32[]{:S(2)}) collective-permute-start(bf16[256,128]{1,0:T(8,128)(2,1)S(1)} %pad_maximum_fusion.1), channel_id=1, source_target_pairs={{0,4},{1,5},{2,6},{3,7},{4,0},{5,1},{6,2},{7,3},{8,12},{9,13},{10,... | collective-permute-start | bytes 196616 | tf_op jit(solution)/shard_map/ppermute | solution.py:282
  21.7 0.0 copy-start.3
  21.7 0.0 copy-start.4
  21.7 0.9 %collective-permute-start.6 = (bf16[256,128]{1,0:T(8,128)(2,1)S(1)}, bf16[256,128]{1,0:T(8,128)(2,1)S(1)}, u32[]{:S(2)}, u32[]{:S(2)}) collective-permute-start(bf16[256,128]{1,0:T(8,128)(2,1)S(1)} %pad_maximum_fusion.2), channel_id=1, source_target_pairs={{0,6},{1,7},{2,4},{3,5},{4,2},{5,3},{6,0},{7,1},{8,14},{9,15},{10,... | collective-permute-start | bytes 196616 | tf_op jit(solution)/shard_map/ppermute | solution.py:282
  22.6 0.0 collective-permute-done.3.refs_1_.refs_3_
  22.6 0.0 copy-done.2
  22.6 0.0 copy-done.3
  22.6 0.0 copy-done.4
  22.7 1.9 %filter_gradient.1 = (bf16[8,128,128]{2,1,0:T(8,128)(2,1)S(1)}, f32[8,16,128]{2,1,0:T(8,128)S(1)}, f32[8,256,128]{2,1,0:T(8,128)S(1)}, f32[8,128]{1,0:T(8,128)S(1)}) custom-call(bf16[1280,128]{1,0:T(8,128)(2,1)S(1)} %get-tuple-element.35.refs_0_.refs_2_, bf16[1280,128]{1,0:T(8,128)(2,1)S(1)} %collective-permute-done.3.refs_1_.refs_3_, ...), custom_call_target="tpu_custom_call" | custom-call | flops 4000000000 | tf_op jit(solution)/shard_map/filter_gradient/pallas_call | solution.py:336
  24.6 2.5 %collective-permute-start.9 = (f32[8,128]{1,0:T(8,128)S(1)}, f32[8,128]{1,0:T(8,128)S(1)}, u32[]{:S(2)}, u32[]{:S(2)}) collective-permute-start(f32[8,128]{1,0:T(8,128)S(1)} %get-tuple-element.45.refs_4_), channel_id=1, source_target_pairs={{0,24},{8,16},{16,8},{24,0},{1,25},{9,17},{17,9},{25,1},{2,26},{10... | collective-permute-start | bytes 12296 | tf_op jit(solution)/shard_map/ppermute | solution.py:352
  27.1 0.5 %collective-permute-start.8 = (f32[8,128]{1,0:T(8,128)S(1)}, f32[8,128]{1,0:T(8,128)S(1)}, u32[]{:S(2)}, u32[]{:S(2)}) collective-permute-start(f32[8,128]{1,0:T(8,128)S(1)} %get-tuple-element.45.refs_4_), channel_id=1, source_target_pairs={{0,16},{8,24},{16,0},{24,8},{1,17},{9,25},{17,1},{25,9},{2,18},{10... | collective-permute-start | bytes 12296 | tf_op jit(solution)/shard_map/ppermute | solution.py:352
  27.6 0.5 %collective-permute-start.7 = (f32[8,128]{1,0:T(8,128)S(1)}, f32[8,128]{1,0:T(8,128)S(1)}, u32[]{:S(2)}, u32[]{:S(2)}) collective-permute-start(f32[8,128]{1,0:T(8,128)S(1)} %get-tuple-element.45.refs_4_), channel_id=1, source_target_pairs={{0,8},{8,0},{16,24},{24,16},{1,9},{9,1},{17,25},{25,17},{2,10},{10... | collective-permute-start | bytes 12296 | tf_op jit(solution)/shard_map/ppermute | solution.py:352
  28.2 0.0 collective-permute-done.5.refs_0_
  28.2 0.0 collective-permute-done.6.refs_1_
  28.2 1.8 %input_gradient.1 = (bf16[8,128,128]{2,1,0:T(8,128)(2,1)S(1)}, f32[8,16,128]{2,1,0:T(8,128)S(1)}) custom-call(bf16[256,128]{1,0:T(8,128)(2,1)S(1)} %collective-permute-done.5.refs_0_, bf16[256,128]{1,0:T(8,128)(2,1)S(1)} %collective-permute-done.6.refs_1_, bf16[1280,128]{1,0:T(8,128)(2,1)S(1)} %get-tuple-element.35.refs_0_.refs_2_, ...), custom_call_target="tpu_custom_call" | custom-call | flops 20000000000 | tf_op jit(solution)/shard_map/input_gradient/pallas_call | solution.py:355
  29.9 0.0 collective-permute-done.9.refs_7_
  30.0 0.8 %collective-permute-done.8.refs_6_ = f32[8,128]{1,0:T(8,128)S(1)} collective-permute-done((f32[8,128]{1,0:T(8,128)S(1)}, f32[8,128]{1,0:T(8,128)S(1)}, u32[]{:S(2)}, u32[]{:S(2)}) %collective-permute-start.8) | collective-permute-done | bytes 4128 | tf_op jit(solution)/shard_map/ppermute | solution.py:352
  30.7 0.5 %collective-permute-done.7.refs_5_ = f32[8,128]{1,0:T(8,128)S(1)} collective-permute-done((f32[8,128]{1,0:T(8,128)S(1)}, f32[8,128]{1,0:T(8,128)S(1)}, u32[]{:S(2)}, u32[]{:S(2)}) %collective-permute-start.7) | collective-permute-done | bytes 4128 | tf_op jit(solution)/shard_map/ppermute | solution.py:352
  31.2 0.1 messages.1
  31.3 2.0 %collective-permute-start.10 = (bf16[272,128]{1,0:T(8,128)(2,1)S(1)}, bf16[272,128]{1,0:T(8,128)(2,1)S(1)}, u32[]{:S(2)}, u32[]{:S(2)}) collective-permute-start(bf16[272,128]{1,0:T(8,128)(2,1)S(1)} %get-tuple-element.46), channel_id=1, source_target_pairs={{0,4},{1,5},{2,6},{3,7},{4,0},{5,1},{6,2},{7,3},{8,12},{9,13},{10,... | collective-permute-start | bytes 208904 | tf_op jit(solution)/shard_map/ppermute | solution.py:282
  33.4 0.0 collective-permute-start.11
  33.4 1.7 %collective-permute-start.12 = (bf16[272,128]{1,0:T(8,128)(2,1)S(1)}, bf16[272,128]{1,0:T(8,128)(2,1)S(1)}, u32[]{:S(2)}, u32[]{:S(2)}) collective-permute-start(bf16[272,128]{1,0:T(8,128)(2,1)S(1)} %get-tuple-element.48), channel_id=1, source_target_pairs={{0,6},{1,7},{2,4},{3,5},{4,2},{5,3},{6,0},{7,1},{8,14},{9,15},{10,... | collective-permute-start | bytes 208904 | tf_op jit(solution)/shard_map/ppermute | solution.py:282
  35.0 2.5 %collective-permute-start.13 = (bf16[272,128]{1,0:T(8,128)(2,1)S(1)}, bf16[272,128]{1,0:T(8,128)(2,1)S(1)}, u32[]{:S(2)}, u32[]{:S(2)}) collective-permute-start(bf16[272,128]{1,0:T(8,128)(2,1)S(1)} %get-tuple-element.49), channel_id=1, source_target_pairs={{0,7},{1,6},{2,5},{3,4},{4,3},{5,2},{6,1},{7,0},{8,15},{9,14},{10,... | collective-permute-start | bytes 208904 | tf_op jit(solution)/shard_map/ppermute | solution.py:282
  37.6 0.0 collective-permute-start.14
  37.6 0.0 collective-permute-done.10.refs_0_
  37.6 1.1 %collective-permute-start.15 = (bf16[272,128]{1,0:T(8,128)(2,1)S(1)}, bf16[272,128]{1,0:T(8,128)(2,1)S(1)}, u32[]{:S(2)}, u32[]{:S(2)}) collective-permute-start(bf16[272,128]{1,0:T(8,128)(2,1)S(1)} %get-tuple-element.51), channel_id=1, source_target_pairs={{0,3},{1,2},{2,1},{3,0},{4,7},{5,6},{6,5},{7,4},{8,11},{9,10},{10,... | collective-permute-start | bytes 208904 | tf_op jit(solution)/shard_map/ppermute | solution.py:282
  38.7 4.7 %collective-permute-done.11.refs_1_ = bf16[272,128]{1,0:T(8,128)(2,1)S(1)} collective-permute-done((bf16[272,128]{1,0:T(8,128)(2,1)S(1)}, bf16[272,128]{1,0:T(8,128)(2,1)S(1)}, u32[]{:S(2)}, u32[]{:S(2)}) %collective-permute-start.11) | collective-permute-done | bytes 69664 | tf_op jit(solution)/shard_map/ppermute | solution.py:282
  43.4 0.0 collective-permute-start.16
  43.4 0.0 collective-permute-done.12.refs_2_
  43.4 0.0 collective-permute-done.13.refs_3_
  43.4 1.5 %collective-permute-done.14.refs_4_ = bf16[272,128]{1,0:T(8,128)(2,1)S(1)} collective-permute-done((bf16[272,128]{1,0:T(8,128)(2,1)S(1)}, bf16[272,128]{1,0:T(8,128)(2,1)S(1)}, u32[]{:S(2)}, u32[]{:S(2)}) %collective-permute-start.14) | collective-permute-done | bytes 69664 | tf_op jit(solution)/shard_map/ppermute | solution.py:282
  44.9 1.3 %collective-permute-done.15.refs_5_ = bf16[272,128]{1,0:T(8,128)(2,1)S(1)} collective-permute-done((bf16[272,128]{1,0:T(8,128)(2,1)S(1)}, bf16[272,128]{1,0:T(8,128)(2,1)S(1)}, u32[]{:S(2)}, u32[]{:S(2)}) %collective-permute-start.15) | collective-permute-done | bytes 69664 | tf_op jit(solution)/shard_map/ppermute | solution.py:282
  46.2 0.0 collective-permute-done.16.refs_7_
  46.2 0.0 copy-done
  46.2 0.0 copy-done.1
  46.2 1.7 %outputs.1 = (f32[128,1024]{1,0:T(8,128)}, f32[128,1024]{1,0:T(8,128)}, f32[1,1024]{1,0:T(1,128)}) custom-call(bf16[272,128]{1,0:T(8,128)(2,1)S(1)} %collective-permute-done.10.refs_0_, bf16[272,128]{1,0:T(8,128)(2,1)S(1)} %collective-permute-done.11.refs_1_, bf16[272,128]{1,0:T(8,128)(2,1)S(1)} %collective-permute-done.12.refs_2_, ...), custom_call_target="tpu_custom_call" | custom-call | flops 1000000000 | tf_op jit(solution)/shard_map/outputs/pallas_call | solution.py:383
  (7 shorter events, 0.1 us)
Async XLA Ops:
  2.1 5.8 %collective-permute-start.4 = (bf16[256,128]{1,0:T(8,128)(2,1)S(1)}, bf16[256,128]{1,0:T(8,128)(2,1)S(1)}, u32[]{:S(2)}, u32[]{:S(2)}) collective-permute-start(bf16[256,128]{1,0:T(8,128)(2,1)S(1)} %get-tuple-element.40), channel_id=1, source_target_pairs={{0,1},{1,0},{2,3},{3,2},{4,5},{5,4},{6,7},{7,6},{8,9},{9,8},{10,11... | collective-permute-start | bytes 196616 | tf_op jit(solution)/shard_map/ppermute | solution.py:282
  2.6 16.1 %collective-permute-start = (bf16[512,128]{1,0:T(8,128)(2,1)S(1)}, bf16[512,128]{1,0:T(8,128)(2,1)S(1)}, u32[]{:S(2)}, u32[]{:S(2)}) collective-permute-start(bf16[512,128]{1,0:T(8,128)(2,1)S(1)} %get-tuple-element.30), channel_id=1, source_target_pairs={{0,4},{1,5},{2,6},{3,7},{4,0},{5,1},{6,2},{7,3},{8,12},{9,13},{10,... | collective-permute-start | bytes 393224 | tf_op jit(solution)/shard_map/ppermute | solution.py:282
  6.2 12.5 %collective-permute-start.1 = (bf16[512,128]{1,0:T(8,128)(2,1)S(1)}, bf16[512,128]{1,0:T(8,128)(2,1)S(1)}, u32[]{:S(2)}, u32[]{:S(2)}) collective-permute-start(bf16[512,128]{1,0:T(8,128)(2,1)S(1)} %get-tuple-element.31), channel_id=1, source_target_pairs={{0,6},{1,7},{2,4},{3,5},{4,2},{5,3},{6,0},{7,1},{8,14},{9,15},{10,... | collective-permute-start | bytes 393224 | tf_op jit(solution)/shard_map/ppermute | solution.py:282
  7.6 11.1 %collective-permute-start.2 = (bf16[768,128]{1,0:T(8,128)(2,1)S(1)}, bf16[768,128]{1,0:T(8,128)(2,1)S(1)}, u32[]{:S(2)}, u32[]{:S(2)}) collective-permute-start(bf16[768,128]{1,0:T(8,128)(2,1)S(1)} %get-tuple-element.32), channel_id=1, source_target_pairs={{0,2},{1,3},{2,0},{3,1},{4,6},{5,7},{6,4},{7,5},{8,10},{9,11},{10,... | collective-permute-start | bytes 589832 | tf_op jit(solution)/shard_map/ppermute | solution.py:282
  18.8 3.9 %collective-permute-start.3 = (bf16[1280,128]{1,0:T(8,128)(2,1)S(1)}, bf16[1280,128]{1,0:T(8,128)(2,1)S(1)}, u32[]{:S(2)}, u32[]{:S(2)}) collective-permute-start(bf16[1280,128]{1,0:T(8,128)(2,1)S(1)} %get-tuple-element.36), channel_id=1, source_target_pairs={{0,1},{1,0},{2,3},{3,2},{4,5},{5,4},{6,7},{7,6},{8,9},{9,8},{10,11... | collective-permute-start | bytes 983048 | tf_op jit(solution)/shard_map/ppermute | solution.py:282
  18.9 3.8 %copy-start.2 = (bf16[256,256]{1,0:T(8,128)(2,1)S(1)}, bf16[256,256]{1,0:T(8,128)(2,1)}, u32[]{:S(2)}) copy-start(bf16[256,256]{1,0:T(8,128)(2,1)} %constant.6.clone.refs_2_.refs_4_) | copy-start | bytes 393220
  18.9 9.3 %collective-permute-start.5 = (bf16[256,128]{1,0:T(8,128)(2,1)S(1)}, bf16[256,128]{1,0:T(8,128)(2,1)S(1)}, u32[]{:S(2)}, u32[]{:S(2)}) collective-permute-start(bf16[256,128]{1,0:T(8,128)(2,1)S(1)} %pad_maximum_fusion.1), channel_id=1, source_target_pairs={{0,4},{1,5},{2,6},{3,7},{4,0},{5,1},{6,2},{7,3},{8,12},{9,13},{10,... | collective-permute-start | bytes 196616 | tf_op jit(solution)/shard_map/ppermute | solution.py:282
  21.7 0.9 %copy-start.3 = (bf16[128,256]{1,0:T(8,128)(2,1)S(1)}, bf16[128,256]{1,0:T(8,128)(2,1)}, u32[]{:S(2)}) copy-start(bf16[128,256]{1,0:T(8,128)(2,1)} %constant.8.clone.refs_4_.refs_6_) | copy-start | bytes 196612
  21.7 0.9 %copy-start.4 = (bf16[128,256]{1,0:T(8,128)(2,1)S(1)}, bf16[128,256]{1,0:T(8,128)(2,1)}, u32[]{:S(2)}) copy-start(bf16[128,256]{1,0:T(8,128)(2,1)} %constant.7.clone.refs_3_.refs_5_) | copy-start | bytes 196612
  21.7 6.4 %collective-permute-start.6 = (bf16[256,128]{1,0:T(8,128)(2,1)S(1)}, bf16[256,128]{1,0:T(8,128)(2,1)S(1)}, u32[]{:S(2)}, u32[]{:S(2)}) collective-permute-start(bf16[256,128]{1,0:T(8,128)(2,1)S(1)} %pad_maximum_fusion.2), channel_id=1, source_target_pairs={{0,6},{1,7},{2,4},{3,5},{4,2},{5,3},{6,0},{7,1},{8,14},{9,15},{10,... | collective-permute-start | bytes 196616 | tf_op jit(solution)/shard_map/ppermute | solution.py:282
  24.6 5.3 %collective-permute-start.9 = (f32[8,128]{1,0:T(8,128)S(1)}, f32[8,128]{1,0:T(8,128)S(1)}, u32[]{:S(2)}, u32[]{:S(2)}) collective-permute-start(f32[8,128]{1,0:T(8,128)S(1)} %get-tuple-element.45.refs_4_), channel_id=1, source_target_pairs={{0,24},{8,16},{16,8},{24,0},{1,25},{9,17},{17,9},{25,1},{2,26},{10... | collective-permute-start | bytes 12296 | tf_op jit(solution)/shard_map/ppermute | solution.py:352
  27.1 3.6 %collective-permute-start.8 = (f32[8,128]{1,0:T(8,128)S(1)}, f32[8,128]{1,0:T(8,128)S(1)}, u32[]{:S(2)}, u32[]{:S(2)}) collective-permute-start(f32[8,128]{1,0:T(8,128)S(1)} %get-tuple-element.45.refs_4_), channel_id=1, source_target_pairs={{0,16},{8,24},{16,0},{24,8},{1,17},{9,25},{17,1},{25,9},{2,18},{10... | collective-permute-start | bytes 12296 | tf_op jit(solution)/shard_map/ppermute | solution.py:352
  27.6 3.6 %collective-permute-start.7 = (f32[8,128]{1,0:T(8,128)S(1)}, f32[8,128]{1,0:T(8,128)S(1)}, u32[]{:S(2)}, u32[]{:S(2)}) collective-permute-start(f32[8,128]{1,0:T(8,128)S(1)} %get-tuple-element.45.refs_4_), channel_id=1, source_target_pairs={{0,8},{8,0},{16,24},{24,16},{1,9},{9,1},{17,25},{25,17},{2,10},{10... | collective-permute-start | bytes 12296 | tf_op jit(solution)/shard_map/ppermute | solution.py:352
  31.2 15.0 %copy-start = (bf16[128,1024]{1,0:T(8,128)(2,1)S(1)}, bf16[128,1024]{1,0:T(8,128)(2,1)}, u32[]{:S(2)}) copy-start(bf16[128,1024]{1,0:T(8,128)(2,1)} %refs_8_.1) | copy-start | bytes 786436
  31.3 6.2 %collective-permute-start.10 = (bf16[272,128]{1,0:T(8,128)(2,1)S(1)}, bf16[272,128]{1,0:T(8,128)(2,1)S(1)}, u32[]{:S(2)}, u32[]{:S(2)}) collective-permute-start(bf16[272,128]{1,0:T(8,128)(2,1)S(1)} %get-tuple-element.46), channel_id=1, source_target_pairs={{0,4},{1,5},{2,6},{3,7},{4,0},{5,1},{6,2},{7,3},{8,12},{9,13},{10,... | collective-permute-start | bytes 208904 | tf_op jit(solution)/shard_map/ppermute | solution.py:282
  33.4 10.0 %collective-permute-start.11 = (bf16[272,128]{1,0:T(8,128)(2,1)S(1)}, bf16[272,128]{1,0:T(8,128)(2,1)S(1)}, u32[]{:S(2)}, u32[]{:S(2)}) collective-permute-start(bf16[272,128]{1,0:T(8,128)(2,1)S(1)} %get-tuple-element.47), channel_id=1, source_target_pairs={{0,5},{1,4},{2,7},{3,6},{4,1},{5,0},{6,3},{7,2},{8,13},{9,12},{10,... | collective-permute-start | bytes 208904 | tf_op jit(solution)/shard_map/ppermute | solution.py:282
  33.4 10.1 %collective-permute-start.12 = (bf16[272,128]{1,0:T(8,128)(2,1)S(1)}, bf16[272,128]{1,0:T(8,128)(2,1)S(1)}, u32[]{:S(2)}, u32[]{:S(2)}) collective-permute-start(bf16[272,128]{1,0:T(8,128)(2,1)S(1)} %get-tuple-element.48), channel_id=1, source_target_pairs={{0,6},{1,7},{2,4},{3,5},{4,2},{5,3},{6,0},{7,1},{8,14},{9,15},{10,... | collective-permute-start | bytes 208904 | tf_op jit(solution)/shard_map/ppermute | solution.py:282
  35.0 8.4 %collective-permute-start.13 = (bf16[272,128]{1,0:T(8,128)(2,1)S(1)}, bf16[272,128]{1,0:T(8,128)(2,1)S(1)}, u32[]{:S(2)}, u32[]{:S(2)}) collective-permute-start(bf16[272,128]{1,0:T(8,128)(2,1)S(1)} %get-tuple-element.49), channel_id=1, source_target_pairs={{0,7},{1,6},{2,5},{3,4},{4,3},{5,2},{6,1},{7,0},{8,15},{9,14},{10,... | collective-permute-start | bytes 208904 | tf_op jit(solution)/shard_map/ppermute | solution.py:282
  37.6 8.6 %copy-start.1 = (f32[1024]{0:T(1024)S(1)}, f32[1024]{0:T(1024)}, u32[]{:S(2)}) copy-start(f32[1024]{0:T(1024)} %param.10) | copy-start | bytes 12292
  37.6 7.3 %collective-permute-start.14 = (bf16[272,128]{1,0:T(8,128)(2,1)S(1)}, bf16[272,128]{1,0:T(8,128)(2,1)S(1)}, u32[]{:S(2)}, u32[]{:S(2)}) collective-permute-start(bf16[272,128]{1,0:T(8,128)(2,1)S(1)} %get-tuple-element.50), channel_id=1, source_target_pairs={{0,2},{1,3},{2,0},{3,1},{4,6},{5,7},{6,4},{7,5},{8,10},{9,11},{10,... | collective-permute-start | bytes 208904 | tf_op jit(solution)/shard_map/ppermute | solution.py:282
  37.6 8.6 %collective-permute-start.15 = (bf16[272,128]{1,0:T(8,128)(2,1)S(1)}, bf16[272,128]{1,0:T(8,128)(2,1)S(1)}, u32[]{:S(2)}, u32[]{:S(2)}) collective-permute-start(bf16[272,128]{1,0:T(8,128)(2,1)S(1)} %get-tuple-element.51), channel_id=1, source_target_pairs={{0,3},{1,2},{2,1},{3,0},{4,7},{5,6},{6,5},{7,4},{8,11},{9,10},{10,... | collective-permute-start | bytes 208904 | tf_op jit(solution)/shard_map/ppermute | solution.py:282
  43.4 2.8 %collective-permute-start.16 = (bf16[272,128]{1,0:T(8,128)(2,1)S(1)}, bf16[272,128]{1,0:T(8,128)(2,1)S(1)}, u32[]{:S(2)}, u32[]{:S(2)}) collective-permute-start(bf16[272,128]{1,0:T(8,128)(2,1)S(1)} %get-tuple-element.53), channel_id=1, source_target_pairs={{0,1},{1,0},{2,3},{3,2},{4,5},{5,4},{6,7},{7,6},{8,9},{9,8},{10,11... | collective-permute-start | bytes 208904 | tf_op jit(solution)/shard_map/ppermute | solution.py:282

commit v3 on v2

--- a/solution.py
+++ b/solution.py
@@ -96,26 +96,32 @@
 
 
 def columns_kernel(chips, far, length, part, arrays, *refs):
-    pairs, (own, other, taps, other_taps) = refs[:-4], refs[-4:]
+    direct, pairs, (own, other, taps, other_taps) = refs[: 2 * far], refs[2 * far : -4], refs[-4:]
     position = lax.axis_index("ctx")
 
     def put(out, row, j, k):
         columns = pl.ds(pl.multiple_of((position ^ k) * part, part), part)
         out[row : row + length] = arrays[j, :, columns]
 
-    for i, chip in enumerate(chips):
-        parts = 2 if i < far else 3
-        here, there, there_row = (pairs[i], pairs[i], parts * length) if chip else (own, other, 0)
-        for j in range(parts):
+    for i, chip in enumerate(chips[:far]):
+        for j in range(2):
+            put(direct[2 * i], j * length, j, 2 * chip)
+            put(direct[2 * i + 1], j * length, j, 2 * chip + 1)
+        put(taps, i * length, 2, 2 * chip)
+        put(other_taps, i * length, 2, 2 * chip + 1)
+    for i, chip in enumerate(chips[far:]):
+        here, there, there_row = (pairs[i], pairs[i], 3 * length) if chip else (own, other, 0)
+        for j in range(3):
             put(here, j * length, j, 2 * chip)
             put(there, there_row + j * length, j, 2 * chip + 1)
-    for i, chip in enumerate(chips[:far]):
-        put(taps, i * length, 2, 2 * chip)
-        put(other_taps, i * length, 2, 2 * chip + 1)
 
 
 def pass_kernel(*refs):
-    arrived, own, other, kept, passed = refs[:-4], *refs[-4:]
+    arrived, (own, other), tables, (kept, passed), held = refs[:-10], *(
+        refs[i:j] for i, j in ((-10, -8), (-8, -5), (-5, -3), (-3, None))
+    )
+    for table, place in zip(tables, held):
+        place[...] = table[...]
     row = 0
     for pair in arrived:
         rows = pair.shape[0] // 2
@@ -282,38 +288,39 @@
         return lax.ppermute(block, "ctx", [(i, i ^ k) for i in range(size)])
 
     three = (out_grad, inputs, filter_taps)
-    parts = [2] * far + [3] * (len(chips) - far)
+    near = len(chips) - far
     if width == part:
-        blocks = [2 * n for n in parts[:-1]] + [3, 3, far, far]
-        *pairs, own, other, taps, other_taps = run(
+        blocks = [2] * (2 * far) + [6] * (near - 1) + [3, 3, far, far]
+        *sent, own, other, taps, other_taps = run(
             functools.partial(columns_kernel, chips, far, length, part),
             "columns", vmem_bytes,
             [jax.ShapeDtypeStruct((n * length, width), bf16) for n in blocks],
         )(jnp.stack(three))
     else:
-        cores = [
-            [
-                jnp.concatenate([columns_for(a, 2 * chip + core) for a in three[:n]])
-                for chip, n in zip(chips, parts)
-            ]
-            for core in range(2)
+        sent = [
+            jnp.concatenate([columns_for(a, k) for a in three[:2]]) for k in order[: 2 * far]
+        ] + [
+            jnp.concatenate([columns_for(a, 2 * chip + core) for core in range(2) for a in three])
+            for chip in chips[far:-1]
         ]
-        pairs = [jnp.concatenate(two) for two in zip(*cores)][:-1]
-        own, other = cores[0][-1], cores[1][-1]
+        own, other = (jnp.concatenate([columns_for(a, core) for a in three]) for core in range(2))
         taps, other_taps = (
             jnp.concatenate([columns_for(filter_taps, 2 * chip + core) for chip in chips[:far]])
             for core in range(2)
         )
 
-    arrived = [send(pair, 2 * chip) for chip, pair in zip(chips, pairs)]
-    kept, passed_on = run(
+    partners = order[: 2 * far] + [2 * chip for chip in chips[far:-1]]
+    arrived = [send(block, k) for k, block in zip(partners, sent)]
+    kept, passed_on, both, back_high, back_low = run(
         pass_kernel,
         "passing", vmem_bytes,
-        [jax.ShapeDtypeStruct((sum(parts) * length, width), bf16)] * 2,
-    )(*arrived, own, other)
+        [jax.ShapeDtypeStruct((near * 3 * length, width), bf16)] * 2
+        + [jax.ShapeDtypeStruct(t.shape, t.dtype) for t in (both, back_high, back_low)],
+    )(*arrived[2 * far :], own, other, both, back_high, back_low)
     passed_on = send(passed_on, 1)
+    other_taps, _ = lax.optimization_barrier((other_taps, arrived[-1]))
     sibling_taps = send(other_taps, 1)
-    sibling_taps, _ = lax.optimization_barrier((sibling_taps, arrived[-1]))
+    sibling_taps, passed_on = lax.optimization_barrier((sibling_taps, passed_on))
     arrived_taps = [
         send(
             jnp.concatenate(
@@ -323,15 +330,13 @@
         )
         for i, chip in enumerate(chips[:far])
     ]
-    first_places, second_places = [], []
-    row = 0
-    for i, n in enumerate(parts):
-        first_places += [(0, row), (1, row)]
-        taps_row = row + 2 * length
-        second_places += [(i, 0), (i, length)] if i < far else [(far, taps_row), (far + 1, taps_row)]
-        row += n * length
-    first_arrived = [kept, passed_on]
+    first_arrived = [*arrived[: 2 * far], kept, passed_on]
+    first_places = [(i, 0) for i in range(2 * far)]
     second_arrived = [*arrived_taps, kept, passed_on]
+    second_places = [(i, row) for i in range(far) for row in (0, length)]
+    for row in range(0, near * 3 * length, 3 * length):
+        first_places += [(2 * far, row), (2 * far + 1, row)]
+        second_places += [(far, row + 2 * length), (far + 1, row + 2 * length)]
 
     codes, tails, pair_spec, squares = run(
         functools.partial(first_kernel, order, length, first_places),
@@ -370,7 +375,9 @@
         "messages", vmem_bytes,
         [jax.ShapeDtypeStruct((2 * length + tail_rows, width), bf16)] * size,
     )(codes, tails, input_codes, input_tails, *all_squares)
-    messages = [send(message, k) if k else message for k, message in zip(order, messages)]
+    messages = {k: send(message, k) if k else message for k, message in zip(order, messages)}
+    turns = chips[: far // 2] + chips[far:-1] + chips[far // 2 : far] + [0]
+    turns = [k for chip in turns for k in (2 * chip, 2 * chip + 1)]
 
     clip_limit = 0.25 * math.sqrt(length * size * chan_width * columns)
     whole = size * width
@@ -381,14 +388,14 @@
         ).reshape(a.shape[0], whole)
         grad_rows, gain = spread(grad_rows), spread(gain)
     input_grad, filter_grad, skip_grad = run(
-        functools.partial(last_kernel, order, length, width, clip_limit),
+        functools.partial(last_kernel, turns, length, width, clip_limit),
         "outputs", vmem_bytes,
         [
             jax.ShapeDtypeStruct((length, whole), f32),
             jax.ShapeDtypeStruct((length, whole), f32),
             jax.ShapeDtypeStruct((1, whole), f32),
         ],
-    )(*messages, grad_rows, gain)
+    )(*[messages[k] for k in turns], grad_rows, gain)
     if width != part:
         gather = lambda a: a.reshape(a.shape[0], size, width)[:, :, :part].reshape(
             a.shape[0], chan_width

time: 48.1 us -> 45.7 us (0.950)
  waiting for transfers between devices: 19.7 us -> 8.74 us
  starting transfers between devices: 20.4 us -> 29.1 us
    ppermute x14 -> x16, waiting for transfers between devices: 18.4 us -> 7.77 us  [send(): return lax.ppermute(block, 'ctx', [(i, i ^ k) for i in range(size)])]
    ppermute x14 -> x16, starting transfers between devices: 16.9 us -> 25.5 us  [send(): return lax.ppermute(block, 'ctx', [(i, i ^ k) for i in range(size)])]
  transfers between devices with their start and end apart: 17 -> 19, of which waited for: 6 -> 7; matrix products, arithmetic and copies ran while one was open for 0% -> 0% of each run, Pallas kernels for 8% -> 8%
where the time goes in v3:
time: 45.7 us; the launch traced here: 45.6 us
  starting transfers between devices  29.1 us (64%)
  waiting for transfers between devices  8.74 us (19%)
  Pallas kernels  5.78 us (13%)
  other arithmetic  1.21 us (3%)
  between operations  0.77 us (2%)
    ppermute x16, starting transfers between devices, send(): return lax.ppermute(block, 'ctx', [(i, i ^ k) for i in range(size)])  25.5 us
    ppermute x16, waiting for transfers between devices, send(): return lax.ppermute(block, 'ctx', [(i, i ^ k) for i in range(size)])  7.77 us
    ppermute x3, starting transfers between devices, per_device(): lax.ppermute(squares, 'chan', [(i, i ^ k) for i in range(columns)])  3.55 us
    pallas_call x1, Pallas kernels, per_device(): run(functools.partial(first_kernel, order, length, first_places), 'filter...  1.94 us
    pallas_call x1, Pallas kernels, per_device(): run(functools.partial(second_kernel, order, length, second_places), 'inpu...  1.77 us
    pallas_call x1, Pallas kernels, per_device(): run(functools.partial(last_kernel, turns, length, width, clip_limit), 'ou...  1.71 us
    another operation x1, other arithmetic, per_device(): jnp.stack(three)  1.2 us
    ppermute x3, waiting for transfers between devices, per_device(): lax.ppermute(squares, 'chan', [(i, i ^ k) for i in range(columns)])  0.97 us
  transfers between devices with their start and end apart: 19, of which 7 were waited for; matrix products, arithmetic and copies ran while one was open for 0% of the time, Pallas kernels for 8%

profile of v3, /device:TPU:0, one launch (start us, length us, event | category | flops | bytes accessed | tf_op | source)
XLA Modules:
  0.0 45.6 jit_solution(111812719303980349)
XLA Ops:
  0.6 1.2 %pad_maximum_fusion.arrays = bf16[3,128,1024]{2,1,0:T(8,128)(2,1)S(1)} fusion(bf16[1,128,1024]{2,1,0:T(8,128)(2,1)} %bitcast.7, bf16[1,128,1024]{2,1,0:T(8,128)(2,1)} %bitcast.8, bf16[1,128,1024]{2,1,0:T(8,128)(2,1)} %bitcast.5), kind=kLoop, calls=%fused_computation | loop fusion | flops 786432 | bytes 1572864 | tf_op jit(solution)/shard_map/stack | solution.py:298
  1.8 0.0 copy-start.2
  1.8 0.0 copy-start.3
  1.9 0.0 copy-start.4
  1.9 0.2 columns.1
  2.1 3.1 %collective-permute-start.4 = (bf16[768,128]{1,0:T(8,128)(2,1)S(1)}, bf16[768,128]{1,0:T(8,128)(2,1)S(1)}, u32[]{:S(2)}, u32[]{:S(2)}) collective-permute-start(bf16[768,128]{1,0:T(8,128)(2,1)S(1)} %get-tuple-element.41), channel_id=1, source_target_pairs={{0,2},{1,3},{2,0},{3,1},{4,6},{5,7},{6,4},{7,5},{8,10},{9,11},{10,... | collective-permute-start | bytes 589832 | tf_op jit(solution)/shard_map/ppermute | solution.py:288
  5.2 2.6 %collective-permute-start = (bf16[256,128]{1,0:T(8,128)(2,1)S(1)}, bf16[256,128]{1,0:T(8,128)(2,1)S(1)}, u32[]{:S(2)}, u32[]{:S(2)}) collective-permute-start(bf16[256,128]{1,0:T(8,128)(2,1)S(1)} %get-tuple-element.37), channel_id=1, source_target_pairs={{0,4},{1,5},{2,6},{3,7},{4,0},{5,1},{6,2},{7,3},{8,12},{9,13},{10,... | collective-permute-start | bytes 196616 | tf_op jit(solution)/shard_map/ppermute | solution.py:288
  7.8 0.0 collective-permute-start.1
  7.8 1.7 %collective-permute-start.2 = (bf16[256,128]{1,0:T(8,128)(2,1)S(1)}, bf16[256,128]{1,0:T(8,128)(2,1)S(1)}, u32[]{:S(2)}, u32[]{:S(2)}) collective-permute-start(bf16[256,128]{1,0:T(8,128)(2,1)S(1)} %get-tuple-element.39), channel_id=1, source_target_pairs={{0,6},{1,7},{2,4},{3,5},{4,2},{5,3},{6,0},{7,1},{8,14},{9,15},{10,... | collective-permute-start | bytes 196616 | tf_op jit(solution)/shard_map/ppermute | solution.py:288
  9.5 2.4 %collective-permute-done.4.refs_0_ = bf16[768,128]{1,0:T(8,128)(2,1)S(1)} collective-permute-done((bf16[768,128]{1,0:T(8,128)(2,1)S(1)}, bf16[768,128]{1,0:T(8,128)(2,1)S(1)}, u32[]{:S(2)}, u32[]{:S(2)}) %collective-permute-start.4) | collective-permute-done | bytes 196640 | tf_op jit(solution)/shard_map/ppermute | solution.py:288
  11.9 0.0 collective-permute-start.5
  11.9 0.0 copy-done.3
  11.9 0.6 %collective-permute-start.6 = (bf16[768,128]{1,0:T(8,128)(2,1)S(1)}, bf16[768,128]{1,0:T(8,128)(2,1)S(1)}, u32[]{:S(2)}, u32[]{:S(2)}) collective-permute-start(bf16[768,128]{1,0:T(8,128)(2,1)S(1)} %get-tuple-element.47), channel_id=1, source_target_pairs={{0,1},{1,0},{2,3},{3,2},{4,5},{5,4},{6,7},{7,6},{8,9},{9,8},{10,11... | collective-permute-start | bytes 589832 | tf_op jit(solution)/shard_map/ppermute | solution.py:288
  12.5 0.6 %collective-permute-done.5 = bf16[256,128]{1,0:T(8,128)(2,1)S(1)} collective-permute-done((bf16[256,128]{1,0:T(8,128)(2,1)S(1)}, bf16[256,128]{1,0:T(8,128)(2,1)S(1)}, u32[]{:S(2)}, u32[]{:S(2)}) %collective-permute-start.5) | collective-permute-done | bytes 65568 | tf_op jit(solution)/shard_map/ppermute | solution.py:288
  13.1 5.2 %collective-permute-start.3 = (bf16[256,128]{1,0:T(8,128)(2,1)S(1)}, bf16[256,128]{1,0:T(8,128)(2,1)S(1)}, u32[]{:S(2)}, u32[]{:S(2)}) collective-permute-start(bf16[256,128]{1,0:T(8,128)(2,1)S(1)} %get-tuple-element.40), channel_id=1, source_target_pairs={{0,7},{1,6},{2,5},{3,4},{4,3},{5,2},{6,1},{7,0},{8,15},{9,14},{10,... | collective-permute-start | bytes 196616 | tf_op jit(solution)/shard_map/ppermute | solution.py:288
  18.3 0.0 collective-permute-done.6.refs_5_.refs_3_
  18.3 0.1 collective-permute-start.7
  18.4 0.0 collective-permute-done.refs_0_
  18.4 1.1 %collective-permute-start.8 = (bf16[256,128]{1,0:T(8,128)(2,1)S(1)}, bf16[256,128]{1,0:T(8,128)(2,1)S(1)}, u32[]{:S(2)}, u32[]{:S(2)}) collective-permute-start(bf16[256,128]{1,0:T(8,128)(2,1)S(1)} %pad_maximum_fusion.2), channel_id=1, source_target_pairs={{0,6},{1,7},{2,4},{3,5},{4,2},{5,3},{6,0},{7,1},{8,14},{9,15},{10,... | collective-permute-start | bytes 196616 | tf_op jit(solution)/shard_map/ppermute | solution.py:288
  19.5 0.0 collective-permute-done.1.refs_1_
  19.5 0.0 collective-permute-done.2.refs_2_
  19.5 1.3 %collective-permute-done.3.refs_3_ = bf16[256,128]{1,0:T(8,128)(2,1)S(1)} collective-permute-done((bf16[256,128]{1,0:T(8,128)(2,1)S(1)}, bf16[256,128]{1,0:T(8,128)(2,1)S(1)}, u32[]{:S(2)}, u32[]{:S(2)}) %collective-permute-start.3) | collective-permute-done | bytes 65568 | tf_op jit(solution)/shard_map/ppermute | solution.py:288
  20.8 1.9 %filter_gradient.1 = (bf16[8,128,128]{2,1,0:T(8,128)(2,1)S(1)}, f32[8,16,128]{2,1,0:T(8,128)S(1)}, f32[8,256,128]{2,1,0:T(8,128)S(1)}, f32[8,128]{1,0:T(8,128)S(1)}) custom-call(bf16[256,128]{1,0:T(8,128)(2,1)S(1)} %collective-permute-done.refs_0_, bf16[256,128]{1,0:T(8,128)(2,1)S(1)} %collective-permute-done.1.refs_1_, ...), custom_call_target="tpu_custom_call" | custom-call | flops 4000000000 | tf_op jit(solution)/shard_map/filter_gradient/pallas_call | solution.py:341
  22.8 2.2 %collective-permute-start.11 = (f32[8,128]{1,0:T(8,128)S(1)}, f32[8,128]{1,0:T(8,128)S(1)}, u32[]{:S(2)}, u32[]{:S(2)}) collective-permute-start(f32[8,128]{1,0:T(8,128)S(1)} %get-tuple-element.59.refs_4_), channel_id=1, source_target_pairs={{0,24},{8,16},{16,8},{24,0},{1,25},{9,17},{17,9},{25,1},{2,26},{10... | collective-permute-start | bytes 12296 | tf_op jit(solution)/shard_map/ppermute | solution.py:357
  25.0 0.5 %collective-permute-start.10 = (f32[8,128]{1,0:T(8,128)S(1)}, f32[8,128]{1,0:T(8,128)S(1)}, u32[]{:S(2)}, u32[]{:S(2)}) collective-permute-start(f32[8,128]{1,0:T(8,128)S(1)} %get-tuple-element.59.refs_4_), channel_id=1, source_target_pairs={{0,16},{8,24},{16,0},{24,8},{1,17},{9,25},{17,1},{25,9},{2,18},{10... | collective-permute-start | bytes 12296 | tf_op jit(solution)/shard_map/ppermute | solution.py:357
  25.5 0.8 %collective-permute-start.9 = (f32[8,128]{1,0:T(8,128)S(1)}, f32[8,128]{1,0:T(8,128)S(1)}, u32[]{:S(2)}, u32[]{:S(2)}) collective-permute-start(f32[8,128]{1,0:T(8,128)S(1)} %get-tuple-element.59.refs_4_), channel_id=1, source_target_pairs={{0,8},{8,0},{16,24},{24,16},{1,9},{9,1},{17,25},{25,17},{2,10},{10... | collective-permute-start | bytes 12296 | tf_op jit(solution)/shard_map/ppermute | solution.py:357
  26.3 0.0 collective-permute-done.7.refs_0_
  26.3 0.0 collective-permute-done.8.refs_1_
  26.3 1.8 %input_gradient.1 = (bf16[8,128,128]{2,1,0:T(8,128)(2,1)S(1)}, f32[8,16,128]{2,1,0:T(8,128)S(1)}) custom-call(bf16[256,128]{1,0:T(8,128)(2,1)S(1)} %collective-permute-done.7.refs_0_, bf16[256,128]{1,0:T(8,128)(2,1)S(1)} %collective-permute-done.8.refs_1_, bf16[768,128]{1,0:T(8,128)(2,1)S(1)} %get-tuple-element.44.refs_4_.refs_2_, ...), custom_call_target="tpu_custom_call" | custom-call | flops 20000000000 | tf_op jit(solution)/shard_map/input_gradient/pallas_call | solution.py:360
  28.1 0.0 collective-permute-done.11.refs_7_
  28.1 0.5 %collective-permute-done.10.refs_6_ = f32[8,128]{1,0:T(8,128)S(1)} collective-permute-done((f32[8,128]{1,0:T(8,128)S(1)}, f32[8,128]{1,0:T(8,128)S(1)}, u32[]{:S(2)}, u32[]{:S(2)}) %collective-permute-start.10) | collective-permute-done | bytes 4128 | tf_op jit(solution)/shard_map/ppermute | solution.py:357
  28.6 0.5 %collective-permute-done.9.refs_5_ = f32[8,128]{1,0:T(8,128)S(1)} collective-permute-done((f32[8,128]{1,0:T(8,128)S(1)}, f32[8,128]{1,0:T(8,128)S(1)}, u32[]{:S(2)}, u32[]{:S(2)}) %collective-permute-start.9) | collective-permute-done | bytes 4128 | tf_op jit(solution)/shard_map/ppermute | solution.py:357
  29.1 0.1 messages.1
  29.2 1.8 %collective-permute-start.12 = (bf16[272,128]{1,0:T(8,128)(2,1)S(1)}, bf16[272,128]{1,0:T(8,128)(2,1)S(1)}, u32[]{:S(2)}, u32[]{:S(2)}) collective-permute-start(bf16[272,128]{1,0:T(8,128)(2,1)S(1)} %get-tuple-element.60), channel_id=1, source_target_pairs={{0,4},{1,5},{2,6},{3,7},{4,0},{5,1},{6,2},{7,3},{8,12},{9,13},{10,... | collective-permute-start | bytes 208904 | tf_op jit(solution)/shard_map/ppermute | solution.py:288
  31.0 0.0 collective-permute-start.13
  31.0 2.4 %collective-permute-start.14 = (bf16[272,128]{1,0:T(8,128)(2,1)S(1)}, bf16[272,128]{1,0:T(8,128)(2,1)S(1)}, u32[]{:S(2)}, u32[]{:S(2)}) collective-permute-start(bf16[272,128]{1,0:T(8,128)(2,1)S(1)} %get-tuple-element.62), channel_id=1, source_target_pairs={{0,2},{1,3},{2,0},{3,1},{4,6},{5,7},{6,4},{7,5},{8,10},{9,11},{10,... | collective-permute-start | bytes 208904 | tf_op jit(solution)/shard_map/ppermute | solution.py:288
  33.4 0.9 %collective-permute-start.15 = (bf16[272,128]{1,0:T(8,128)(2,1)S(1)}, bf16[272,128]{1,0:T(8,128)(2,1)S(1)}, u32[]{:S(2)}, u32[]{:S(2)}) collective-permute-start(bf16[272,128]{1,0:T(8,128)(2,1)S(1)} %get-tuple-element.63), channel_id=1, source_target_pairs={{0,3},{1,2},{2,1},{3,0},{4,7},{5,6},{6,5},{7,4},{8,11},{9,10},{10,... | collective-permute-start | bytes 208904 | tf_op jit(solution)/shard_map/ppermute | solution.py:288
  34.3 3.0 %collective-permute-start.16 = (bf16[272,128]{1,0:T(8,128)(2,1)S(1)}, bf16[272,128]{1,0:T(8,128)(2,1)S(1)}, u32[]{:S(2)}, u32[]{:S(2)}) collective-permute-start(bf16[272,128]{1,0:T(8,128)(2,1)S(1)} %get-tuple-element.64), channel_id=1, source_target_pairs={{0,6},{1,7},{2,4},{3,5},{4,2},{5,3},{6,0},{7,1},{8,14},{9,15},{10,... | collective-permute-start | bytes 208904 | tf_op jit(solution)/shard_map/ppermute | solution.py:288
  37.3 0.0 collective-permute-done.12.refs_0_
  37.3 1.3 %collective-permute-start.17 = (bf16[272,128]{1,0:T(8,128)(2,1)S(1)}, bf16[272,128]{1,0:T(8,128)(2,1)S(1)}, u32[]{:S(2)}, u32[]{:S(2)}) collective-permute-start(bf16[272,128]{1,0:T(8,128)(2,1)S(1)} %get-tuple-element.65), channel_id=1, source_target_pairs={{0,7},{1,6},{2,5},{3,4},{4,3},{5,2},{6,1},{7,0},{8,15},{9,14},{10,... | collective-permute-start | bytes 208904 | tf_op jit(solution)/shard_map/ppermute | solution.py:288
  38.6 0.0 collective-permute-done.13.refs_1_
  38.6 1.9 %collective-permute-start.18 = (bf16[272,128]{1,0:T(8,128)(2,1)S(1)}, bf16[272,128]{1,0:T(8,128)(2,1)S(1)}, u32[]{:S(2)}, u32[]{:S(2)}) collective-permute-start(bf16[272,128]{1,0:T(8,128)(2,1)S(1)} %get-tuple-element.67), channel_id=1, source_target_pairs={{0,1},{1,0},{2,3},{3,2},{4,5},{5,4},{6,7},{7,6},{8,9},{9,8},{10,11... | collective-permute-start | bytes 208904 | tf_op jit(solution)/shard_map/ppermute | solution.py:288
  40.5 0.0 collective-permute-done.14.refs_2_
  40.5 0.0 collective-permute-done.15.refs_3_
  40.5 1.5 %collective-permute-done.16.refs_4_ = bf16[272,128]{1,0:T(8,128)(2,1)S(1)} collective-permute-done((bf16[272,128]{1,0:T(8,128)(2,1)S(1)}, bf16[272,128]{1,0:T(8,128)(2,1)S(1)}, u32[]{:S(2)}, u32[]{:S(2)}) %collective-permute-start.16) | collective-permute-done | bytes 69664 | tf_op jit(solution)/shard_map/ppermute | solution.py:288
  42.0 1.9 %collective-permute-done.17.refs_5_ = bf16[272,128]{1,0:T(8,128)(2,1)S(1)} collective-permute-done((bf16[272,128]{1,0:T(8,128)(2,1)S(1)}, bf16[272,128]{1,0:T(8,128)(2,1)S(1)}, u32[]{:S(2)}, u32[]{:S(2)}) %collective-permute-start.17) | collective-permute-done | bytes 69664 | tf_op jit(solution)/shard_map/ppermute | solution.py:288
  43.9 0.0 collective-permute-done.18.refs_7_
  43.9 1.7 %outputs.1 = (f32[128,1024]{1,0:T(8,128)}, f32[128,1024]{1,0:T(8,128)}, f32[1,1024]{1,0:T(1,128)}) custom-call(bf16[272,128]{1,0:T(8,128)(2,1)S(1)} %collective-permute-done.12.refs_0_, bf16[272,128]{1,0:T(8,128)(2,1)S(1)} %collective-permute-done.13.refs_1_, bf16[272,128]{1,0:T(8,128)(2,1)S(1)} %collective-permute-done.14.refs_2_, ...), custom_call_target="tpu_custom_call" | custom-call | flops 1000000000 | tf_op jit(solution)/shard_map/outputs/pallas_call | solution.py:390
  (11 shorter events, 0.1 us)
Async XLA Ops:
  1.8 10.0 %copy-start.2 = (bf16[256,256]{1,0:T(8,128)(2,1)S(1)}, bf16[256,256]{1,0:T(8,128)(2,1)}, u32[]{:S(2)}) copy-start(bf16[256,256]{1,0:T(8,128)(2,1)} %constant.6.clone.refs_3_) | copy-start | bytes 393220
  1.8 10.0 %copy-start.3 = (bf16[128,256]{1,0:T(8,128)(2,1)S(1)}, bf16[128,256]{1,0:T(8,128)(2,1)}, u32[]{:S(2)}) copy-start(bf16[128,256]{1,0:T(8,128)(2,1)} %constant.8.clone.refs_5_) | copy-start | bytes 196612
  1.9 10.0 %copy-start.4 = (bf16[128,256]{1,0:T(8,128)(2,1)S(1)}, bf16[128,256]{1,0:T(8,128)(2,1)}, u32[]{:S(2)}) copy-start(bf16[128,256]{1,0:T(8,128)(2,1)} %constant.7.clone.refs_4_) | copy-start | bytes 196612
  2.1 9.8 %collective-permute-start.4 = (bf16[768,128]{1,0:T(8,128)(2,1)S(1)}, bf16[768,128]{1,0:T(8,128)(2,1)S(1)}, u32[]{:S(2)}, u32[]{:S(2)}) collective-permute-start(bf16[768,128]{1,0:T(8,128)(2,1)S(1)} %get-tuple-element.41), channel_id=1, source_target_pairs={{0,2},{1,3},{2,0},{3,1},{4,6},{5,7},{6,4},{7,5},{8,10},{9,11},{10,... | collective-permute-start | bytes 589832 | tf_op jit(solution)/shard_map/ppermute | solution.py:288
  5.2 13.2 %collective-permute-start = (bf16[256,128]{1,0:T(8,128)(2,1)S(1)}, bf16[256,128]{1,0:T(8,128)(2,1)S(1)}, u32[]{:S(2)}, u32[]{:S(2)}) collective-permute-start(bf16[256,128]{1,0:T(8,128)(2,1)S(1)} %get-tuple-element.37), channel_id=1, source_target_pairs={{0,4},{1,5},{2,6},{3,7},{4,0},{5,1},{6,2},{7,3},{8,12},{9,13},{10,... | collective-permute-start | bytes 196616 | tf_op jit(solution)/shard_map/ppermute | solution.py:288
  7.8 11.7 %collective-permute-start.1 = (bf16[256,128]{1,0:T(8,128)(2,1)S(1)}, bf16[256,128]{1,0:T(8,128)(2,1)S(1)}, u32[]{:S(2)}, u32[]{:S(2)}) collective-permute-start(bf16[256,128]{1,0:T(8,128)(2,1)S(1)} %get-tuple-element.38), channel_id=1, source_target_pairs={{0,5},{1,4},{2,7},{3,6},{4,1},{5,0},{6,3},{7,2},{8,13},{9,12},{10,... | collective-permute-start | bytes 196616 | tf_op jit(solution)/shard_map/ppermute | solution.py:288
  7.8 11.7 %collective-permute-start.2 = (bf16[256,128]{1,0:T(8,128)(2,1)S(1)}, bf16[256,128]{1,0:T(8,128)(2,1)S(1)}, u32[]{:S(2)}, u32[]{:S(2)}) collective-permute-start(bf16[256,128]{1,0:T(8,128)(2,1)S(1)} %get-tuple-element.39), channel_id=1, source_target_pairs={{0,6},{1,7},{2,4},{3,5},{4,2},{5,3},{6,0},{7,1},{8,14},{9,15},{10,... | collective-permute-start | bytes 196616 | tf_op jit(solution)/shard_map/ppermute | solution.py:288
  11.9 1.3 %collective-permute-start.5 = (bf16[256,128]{1,0:T(8,128)(2,1)S(1)}, bf16[256,128]{1,0:T(8,128)(2,1)S(1)}, u32[]{:S(2)}, u32[]{:S(2)}) collective-permute-start(bf16[256,128]{1,0:T(8,128)(2,1)S(1)} %get-tuple-element.46), channel_id=1, source_target_pairs={{0,1},{1,0},{2,3},{3,2},{4,5},{5,4},{6,7},{7,6},{8,9},{9,8},{10,11... | collective-permute-start | bytes 196616 | tf_op jit(solution)/shard_map/ppermute | solution.py:288
  11.9 6.3 %collective-permute-start.6 = (bf16[768,128]{1,0:T(8,128)(2,1)S(1)}, bf16[768,128]{1,0:T(8,128)(2,1)S(1)}, u32[]{:S(2)}, u32[]{:S(2)}) collective-permute-start(bf16[768,128]{1,0:T(8,128)(2,1)S(1)} %get-tuple-element.47), channel_id=1, source_target_pairs={{0,1},{1,0},{2,3},{3,2},{4,5},{5,4},{6,7},{7,6},{8,9},{9,8},{10,11... | collective-permute-start | bytes 589832 | tf_op jit(solution)/shard_map/ppermute | solution.py:288
  13.1 7.7 %collective-permute-start.3 = (bf16[256,128]{1,0:T(8,128)(2,1)S(1)}, bf16[256,128]{1,0:T(8,128)(2,1)S(1)}, u32[]{:S(2)}, u32[]{:S(2)}) collective-permute-start(bf16[256,128]{1,0:T(8,128)(2,1)S(1)} %get-tuple-element.40), channel_id=1, source_target_pairs={{0,7},{1,6},{2,5},{3,4},{4,3},{5,2},{6,1},{7,0},{8,15},{9,14},{10,... | collective-permute-start | bytes 196616 | tf_op jit(solution)/shard_map/ppermute | solution.py:288
  18.3 8.0 %collective-permute-start.7 = (bf16[256,128]{1,0:T(8,128)(2,1)S(1)}, bf16[256,128]{1,0:T(8,128)(2,1)S(1)}, u32[]{:S(2)}, u32[]{:S(2)}) collective-permute-start(bf16[256,128]{1,0:T(8,128)(2,1)S(1)} %pad_maximum_fusion.1), channel_id=1, source_target_pairs={{0,4},{1,5},{2,6},{3,7},{4,0},{5,1},{6,2},{7,3},{8,12},{9,13},{10,... | collective-permute-start | bytes 196616 | tf_op jit(solution)/shard_map/ppermute | solution.py:288
  18.4 7.9 %collective-permute-start.8 = (bf16[256,128]{1,0:T(8,128)(2,1)S(1)}, bf16[256,128]{1,0:T(8,128)(2,1)S(1)}, u32[]{:S(2)}, u32[]{:S(2)}) collective-permute-start(bf16[256,128]{1,0:T(8,128)(2,1)S(1)} %pad_maximum_fusion.2), channel_id=1, source_target_pairs={{0,6},{1,7},{2,4},{3,5},{4,2},{5,3},{6,0},{7,1},{8,14},{9,15},{10,... | collective-permute-start | bytes 196616 | tf_op jit(solution)/shard_map/ppermute | solution.py:288
  22.8 5.3 %collective-permute-start.11 = (f32[8,128]{1,0:T(8,128)S(1)}, f32[8,128]{1,0:T(8,128)S(1)}, u32[]{:S(2)}, u32[]{:S(2)}) collective-permute-start(f32[8,128]{1,0:T(8,128)S(1)} %get-tuple-element.59.refs_4_), channel_id=1, source_target_pairs={{0,24},{8,16},{16,8},{24,0},{1,25},{9,17},{17,9},{25,1},{2,26},{10... | collective-permute-start | bytes 12296 | tf_op jit(solution)/shard_map/ppermute | solution.py:357
  25.0 3.6 %collective-permute-start.10 = (f32[8,128]{1,0:T(8,128)S(1)}, f32[8,128]{1,0:T(8,128)S(1)}, u32[]{:S(2)}, u32[]{:S(2)}) collective-permute-start(f32[8,128]{1,0:T(8,128)S(1)} %get-tuple-element.59.refs_4_), channel_id=1, source_target_pairs={{0,16},{8,24},{16,0},{24,8},{1,17},{9,25},{17,1},{25,9},{2,18},{10... | collective-permute-start | bytes 12296 | tf_op jit(solution)/shard_map/ppermute | solution.py:357
  25.5 3.6 %collective-permute-start.9 = (f32[8,128]{1,0:T(8,128)S(1)}, f32[8,128]{1,0:T(8,128)S(1)}, u32[]{:S(2)}, u32[]{:S(2)}) collective-permute-start(f32[8,128]{1,0:T(8,128)S(1)} %get-tuple-element.59.refs_4_), channel_id=1, source_target_pairs={{0,8},{8,0},{16,24},{24,16},{1,9},{9,1},{17,25},{25,17},{2,10},{10... | collective-permute-start | bytes 12296 | tf_op jit(solution)/shard_map/ppermute | solution.py:357
  29.1 14.8 %copy-start = (bf16[128,1024]{1,0:T(8,128)(2,1)S(1)}, bf16[128,1024]{1,0:T(8,128)(2,1)}, u32[]{:S(2)}) copy-start(bf16[128,1024]{1,0:T(8,128)(2,1)} %refs_8_.1) | copy-start | bytes 786436
  29.2 8.1 %collective-permute-start.12 = (bf16[272,128]{1,0:T(8,128)(2,1)S(1)}, bf16[272,128]{1,0:T(8,128)(2,1)S(1)}, u32[]{:S(2)}, u32[]{:S(2)}) collective-permute-start(bf16[272,128]{1,0:T(8,128)(2,1)S(1)} %get-tuple-element.60), channel_id=1, source_target_pairs={{0,4},{1,5},{2,6},{3,7},{4,0},{5,1},{6,2},{7,3},{8,12},{9,13},{10,... | collective-permute-start | bytes 208904 | tf_op jit(solution)/shard_map/ppermute | solution.py:288
  31.0 7.6 %collective-permute-start.13 = (bf16[272,128]{1,0:T(8,128)(2,1)S(1)}, bf16[272,128]{1,0:T(8,128)(2,1)S(1)}, u32[]{:S(2)}, u32[]{:S(2)}) collective-permute-start(bf16[272,128]{1,0:T(8,128)(2,1)S(1)} %get-tuple-element.61), channel_id=1, source_target_pairs={{0,5},{1,4},{2,7},{3,6},{4,1},{5,0},{6,3},{7,2},{8,13},{9,12},{10,... | collective-permute-start | bytes 208904 | tf_op jit(solution)/shard_map/ppermute | solution.py:288
  31.0 9.5 %collective-permute-start.14 = (bf16[272,128]{1,0:T(8,128)(2,1)S(1)}, bf16[272,128]{1,0:T(8,128)(2,1)S(1)}, u32[]{:S(2)}, u32[]{:S(2)}) collective-permute-start(bf16[272,128]{1,0:T(8,128)(2,1)S(1)} %get-tuple-element.62), channel_id=1, source_target_pairs={{0,2},{1,3},{2,0},{3,1},{4,6},{5,7},{6,4},{7,5},{8,10},{9,11},{10,... | collective-permute-start | bytes 208904 | tf_op jit(solution)/shard_map/ppermute | solution.py:288
  33.4 7.0 %collective-permute-start.15 = (bf16[272,128]{1,0:T(8,128)(2,1)S(1)}, bf16[272,128]{1,0:T(8,128)(2,1)S(1)}, u32[]{:S(2)}, u32[]{:S(2)}) collective-permute-start(bf16[272,128]{1,0:T(8,128)(2,1)S(1)} %get-tuple-element.63), channel_id=1, source_target_pairs={{0,3},{1,2},{2,1},{3,0},{4,7},{5,6},{6,5},{7,4},{8,11},{9,10},{10,... | collective-permute-start | bytes 208904 | tf_op jit(solution)/shard_map/ppermute | solution.py:288
  34.3 9.6 %copy-start.1 = (f32[1024]{0:T(1024)S(1)}, f32[1024]{0:T(1024)}, u32[]{:S(2)}) copy-start(f32[1024]{0:T(1024)} %param.10) | copy-start | bytes 12292
  34.3 7.7 %collective-permute-start.16 = (bf16[272,128]{1,0:T(8,128)(2,1)S(1)}, bf16[272,128]{1,0:T(8,128)(2,1)S(1)}, u32[]{:S(2)}, u32[]{:S(2)}) collective-permute-start(bf16[272,128]{1,0:T(8,128)(2,1)S(1)} %get-tuple-element.64), channel_id=1, source_target_pairs={{0,6},{1,7},{2,4},{3,5},{4,2},{5,3},{6,0},{7,1},{8,14},{9,15},{10,... | collective-permute-start | bytes 208904 | tf_op jit(solution)/shard_map/ppermute | solution.py:288
  37.3 6.6 %collective-permute-start.17 = (bf16[272,128]{1,0:T(8,128)(2,1)S(1)}, bf16[272,128]{1,0:T(8,128)(2,1)S(1)}, u32[]{:S(2)}, u32[]{:S(2)}) collective-permute-start(bf16[272,128]{1,0:T(8,128)(2,1)S(1)} %get-tuple-element.65), channel_id=1, source_target_pairs={{0,7},{1,6},{2,5},{3,4},{4,3},{5,2},{6,1},{7,0},{8,15},{9,14},{10,... | collective-permute-start | bytes 208904 | tf_op jit(solution)/shard_map/ppermute | solution.py:288
  38.6 5.3 %collective-permute-start.18 = (bf16[272,128]{1,0:T(8,128)(2,1)S(1)}, bf16[272,128]{1,0:T(8,128)(2,1)S(1)}, u32[]{:S(2)}, u32[]{:S(2)}) collective-permute-start(bf16[272,128]{1,0:T(8,128)(2,1)S(1)} %get-tuple-element.67), channel_id=1, source_target_pairs={{0,1},{1,0},{2,3},{3,2},{4,5},{5,4},{6,7},{7,6},{8,9},{9,8},{10,11... | collective-permute-start | bytes 208904 | tf_op jit(solution)/shard_map/ppermute | solution.py:288

commit v4 on v3

--- a/solution.py
+++ b/solution.py
@@ -42,21 +42,19 @@
 def encode(values):
     peak = jnp.max(jnp.abs(values), axis=0, keepdims=True) * (1.0 + 2.0**-7)
     scale = jnp.maximum(peak.astype(jnp.bfloat16).astype(jnp.float32), 2.0**-110)
-    units = values * (top_code / scale)
-    code = jnp.minimum(jnp.floor(jnp.abs(units) + 0.5), float(top_code))
-    octave = jnp.floor(code * (1.0 / 128))
-    mantissa = 1.0 + (code - 128.0 * octave) * (1.0 / 128)
-    carrier = mantissa * jnp.exp2(octave - float(low_power))
-    return jnp.where(units < 0, -carrier, carrier).astype(jnp.bfloat16), scale
+    size = jnp.abs(values) * (top_code / 128.0 / scale)
+    octave = jnp.floor(size)
+    carrier = (size - octave + 1.0) * jnp.exp2(octave - float(low_power))
+    return jnp.where(values < 0, -carrier, carrier).astype(jnp.bfloat16), scale
 
 
 def decode(codes, scale):
     carrier = codes.astype(jnp.float32)
     size = jnp.abs(carrier)
     power = jnp.floor(jnp.log2(size) + 0.001)
-    mantissa = jnp.floor(size * jnp.exp2(-power) * 128.0 + 0.5)
-    units = (power + float(low_power - 1)) * 128.0 + mantissa
-    return jnp.where(carrier < 0, -units, units) * (scale * (1.0 / top_code))
+    octaves_up = size * jnp.exp2(-power) + (power + float(low_power - 1))
+    scale *= 128.0 / top_code
+    return octaves_up * jnp.where(carrier < 0, -scale, scale)
 
 
 def tail_tile(first_row, rows, width):
@@ -70,16 +68,18 @@
 
 
 def correlate_rows(pairs, others, size):
+    sums = [real + imag for real, imag in pairs]
+    turned = [(real, real - imag, real + imag) for real, imag in others]
     results = []
     for p in range(size):
-        real = imag = None
+        shared = first = second = None
         for q in range(p, size):
-            (gr, gi), (fr, fi) = pairs[q], others[q - p]
-            real_term = gr * fr + gi * fi
-            imag_term = gi * fr - gr * fi
-            real = real_term if real is None else real + real_term
-            imag = imag_term if imag is None else imag + imag_term
-        results.append((real, imag))
+            real, less, more = turned[q - p]
+            terms = sums[q] * real, pairs[q][1] * less, pairs[q][0] * more
+            if q > p:
+                terms = shared + terms[0], first + terms[1], second + terms[2]
+            shared, first, second = terms
+        results.append((shared - first, shared - second))
     return results
 
 
@@ -95,41 +95,32 @@
         emit(i + 1, block[:, width:])
 
 
-def columns_kernel(chips, far, length, part, arrays, *refs):
-    direct, pairs, (own, other, taps, other_taps) = refs[: 2 * far], refs[2 * far : -4], refs[-4:]
+def columns_kernel(chips, direct, length, part, arrays, *refs):
+    blocks, rest = refs[:-2], refs[-2:]
     position = lax.axis_index("ctx")
 
     def put(out, row, j, k):
         columns = pl.ds(pl.multiple_of((position ^ k) * part, part), part)
         out[row : row + length] = arrays[j, :, columns]
 
-    for i, chip in enumerate(chips[:far]):
-        for j in range(2):
-            put(direct[2 * i], j * length, j, 2 * chip)
-            put(direct[2 * i + 1], j * length, j, 2 * chip + 1)
-        put(taps, i * length, 2, 2 * chip)
-        put(other_taps, i * length, 2, 2 * chip + 1)
-    for i, chip in enumerate(chips[far:]):
-        here, there, there_row = (pairs[i], pairs[i], 3 * length) if chip else (own, other, 0)
-        for j in range(3):
-            put(here, j * length, j, 2 * chip)
-            put(there, there_row + j * length, j, 2 * chip + 1)
-
-
-def pass_kernel(*refs):
-    arrived, (own, other), tables, (kept, passed), held = refs[:-10], *(
-        refs[i:j] for i, j in ((-10, -8), (-8, -5), (-5, -3), (-3, None))
-    )
+    for core in range(2):
+        row = 0
+        for i, chip in enumerate(chips):
+            for j in range(3):
+                if i < direct and j < 2:
+                    put(blocks[2 * i + core], j * length, j, 2 * chip + core)
+                else:
+                    put(rest[core], row, j, 2 * chip + core)
+                    row += length
+
+
+def taps_kernel(rows, length, mine, sibling, *refs):
+    tables, messages, held = refs[:3], refs[3:-3], refs[-3:]
     for table, place in zip(tables, held):
         place[...] = table[...]
-    row = 0
-    for pair in arrived:
-        rows = pair.shape[0] // 2
-        kept[row : row + rows] = pair[:rows]
-        passed[row : row + rows] = pair[rows:]
-        row += rows
-    kept[row:] = own[...]
-    passed[row:] = other[...]
+    for row, message in zip(rows, messages):
+        message[:length] = mine[row : row + length]
+        message[length:] = sibling[row : row + length]
 
 
 def first_kernel(order, length, places, *refs):
@@ -288,55 +279,59 @@
         return lax.ppermute(block, "ctx", [(i, i ^ k) for i in range(size)])
 
     three = (out_grad, inputs, filter_taps)
-    near = len(chips) - far
+    direct = size // 8
+    rest_rows = (3 * len(chips) - 2 * direct) * length
     if width == part:
-        blocks = [2] * (2 * far) + [6] * (near - 1) + [3, 3, far, far]
-        *sent, own, other, taps, other_taps = run(
-            functools.partial(columns_kernel, chips, far, length, part),
+        *blocks, mine, others = run(
+            functools.partial(columns_kernel, chips, direct, length, part),
             "columns", vmem_bytes,
-            [jax.ShapeDtypeStruct((n * length, width), bf16) for n in blocks],
+            [jax.ShapeDtypeStruct((2 * length, width), bf16)] * (2 * direct)
+            + [jax.ShapeDtypeStruct((rest_rows, width), bf16)] * 2,
         )(jnp.stack(three))
     else:
-        sent = [
-            jnp.concatenate([columns_for(a, k) for a in three[:2]]) for k in order[: 2 * far]
-        ] + [
-            jnp.concatenate([columns_for(a, 2 * chip + core) for core in range(2) for a in three])
-            for chip in chips[far:-1]
-        ]
-        own, other = (jnp.concatenate([columns_for(a, core) for a in three]) for core in range(2))
-        taps, other_taps = (
-            jnp.concatenate([columns_for(filter_taps, 2 * chip + core) for chip in chips[:far]])
+        blocks = [jnp.concatenate([columns_for(a, k) for a in three[:2]]) for k in order[: 2 * direct]]
+        mine, others = (
+            jnp.concatenate(
+                [
+                    columns_for(a, 2 * chip + core)
+                    for i, chip in enumerate(chips)
+                    for a in (three[2:] if i < direct else three)
+                ]
+            )
             for core in range(2)
         )
 
-    partners = order[: 2 * far] + [2 * chip for chip in chips[far:-1]]
-    arrived = [send(block, k) for k, block in zip(partners, sent)]
-    kept, passed_on, both, back_high, back_low = run(
-        pass_kernel,
-        "passing", vmem_bytes,
-        [jax.ShapeDtypeStruct((near * 3 * length, width), bf16)] * 2
+    sibling = send(others, 1)
+    arrived = [send(block, k) for k, block in zip(order, blocks)]
+    first_places = [(i, 0) for i in range(2 * direct)]
+    taps_rows = [i * length for i in range(direct)]
+    row = direct * length
+    near_places = []
+    for i, chip in enumerate(chips[direct:-1]):
+        here = len(arrived)
+        rows = (2 if i < far - direct else 3) * length
+        pair = jnp.concatenate([held[row : row + rows] for held in (mine, sibling)])
+        first_places += [(here, 0), (here, rows)]
+        arrived.append(send(pair, 2 * chip))
+        if i < far - direct:
+            taps_rows.append(row + 2 * length)
+        else:
+            near_places += [(here, 2 * length), (here, 5 * length)]
+        row += 3 * length
+    first_places += [(len(arrived), row), (len(arrived) + 1, row)]
+    first_arrived = [*arrived, mine, sibling]
+    later = lax.optimization_barrier((mine, sibling, *arrived[: 2 * direct]))[:2]
+    *tap_messages, both, back_high, back_low = run(
+        functools.partial(taps_kernel, taps_rows, length),
+        "taps", vmem_bytes,
+        [jax.ShapeDtypeStruct((2 * length, width), bf16)] * len(taps_rows)
         + [jax.ShapeDtypeStruct(t.shape, t.dtype) for t in (both, back_high, back_low)],
-    )(*arrived[2 * far :], own, other, both, back_high, back_low)
-    passed_on = send(passed_on, 1)
-    other_taps, _ = lax.optimization_barrier((other_taps, arrived[-1]))
-    sibling_taps = send(other_taps, 1)
-    sibling_taps, passed_on = lax.optimization_barrier((sibling_taps, passed_on))
-    arrived_taps = [
-        send(
-            jnp.concatenate(
-                [held[i * length : (i + 1) * length] for held in (taps, sibling_taps)]
-            ),
-            2 * chip,
-        )
-        for i, chip in enumerate(chips[:far])
-    ]
-    first_arrived = [*arrived[: 2 * far], kept, passed_on]
-    first_places = [(i, 0) for i in range(2 * far)]
-    second_arrived = [*arrived_taps, kept, passed_on]
-    second_places = [(i, row) for i in range(far) for row in (0, length)]
-    for row in range(0, near * 3 * length, 3 * length):
-        first_places += [(2 * far, row), (2 * far + 1, row)]
-        second_places += [(far, row + 2 * length), (far + 1, row + 2 * length)]
+    )(*later, both, back_high, back_low)
+    arrived_taps = [send(block, 2 * chip) for chip, block in zip(chips, tap_messages)]
+    second_places = [(i, half) for i in range(far) for half in (0, length)]
+    second_places += [(ref - 2 * direct - (far - direct) + far, at) for ref, at in near_places]
+    second_arrived = [*arrived_taps, *arrived[direct + far :], mine, sibling]
+    second_places += [(len(second_arrived) - 2 + i, row + 2 * length) for i in range(2)]
 
     codes, tails, pair_spec, squares = run(
         functools.partial(first_kernel, order, length, first_places),

time: 45.7 us -> 44.9 us (0.982)
  starting transfers between devices: 29.1 us -> 27.1 us
  waiting for transfers between devices: 8.74 us -> 10.4 us
  Pallas kernels: 5.78 us -> 5.25 us
    ppermute x16 -> x14, starting transfers between devices: 25.5 us -> 23.5 us  [send(): return lax.ppermute(block, 'ctx', [(i, i ^ k) for i in range(size)])]
    ppermute x16 -> x14, waiting for transfers between devices: 7.77 us -> 8.97 us  [send(): return lax.ppermute(block, 'ctx', [(i, i ^ k) for i in range(size)])]
    ppermute x3, waiting for transfers between devices: 0.97 us -> 1.45 us  [per_device(): lax.ppermute(squares, 'chan', [(i, i ^ k) for i in range(columns)])]
  transfers between devices with their start and end apart: 19 -> 17, of which waited for: 7 -> 7; matrix products, arithmetic and copies ran while one was open for 0% -> 0% of each run, Pallas kernels for 8% -> 8%
where the time goes in v4:
time: 44.9 us; the launch traced here: 44.8 us
  starting transfers between devices  27.1 us (60%)
  waiting for transfers between devices  10.4 us (23%)
  Pallas kernels  5.25 us (12%)
  other arithmetic  1.22 us (3%)
  between operations  0.75 us (2%)
    ppermute x14, starting transfers between devices, send(): return lax.ppermute(block, 'ctx', [(i, i ^ k) for i in range(size)])  23.5 us
    ppermute x14, waiting for transfers between devices, send(): return lax.ppermute(block, 'ctx', [(i, i ^ k) for i in range(size)])  8.97 us
    ppermute x3, starting transfers between devices, per_device(): lax.ppermute(squares, 'chan', [(i, i ^ k) for i in range(columns)])  3.55 us
    pallas_call x1, Pallas kernels, per_device(): run(functools.partial(first_kernel, order, length, first_places), 'filter...  1.76 us
    pallas_call x1, Pallas kernels, per_device(): run(functools.partial(second_kernel, order, length, second_places), 'inpu...  1.61 us
    pallas_call x1, Pallas kernels, per_device(): run(functools.partial(last_kernel, turns, length, width, clip_limit), 'ou...  1.54 us
    ppermute x3, waiting for transfers between devices, per_device(): lax.ppermute(squares, 'chan', [(i, i ^ k) for i in range(columns)])  1.45 us
    another operation x1, other arithmetic, per_device(): jnp.stack(three)  1.2 us
  transfers between devices with their start and end apart: 17, of which 7 were waited for; matrix products, arithmetic and copies ran while one was open for 0% of the time, Pallas kernels for 8%

profile of v4, /device:TPU:0, one launch (start us, length us, event | category | flops | bytes accessed | tf_op | source)
XLA Modules:
  0.0 44.8 jit_solution(6192366881591994837)
XLA Ops:
  0.6 1.2 %pad_maximum_fusion.arrays = bf16[3,128,1024]{2,1,0:T(8,128)(2,1)S(1)} fusion(bf16[1,128,1024]{2,1,0:T(8,128)(2,1)} %bitcast.7, bf16[1,128,1024]{2,1,0:T(8,128)(2,1)} %bitcast.8, bf16[1,128,1024]{2,1,0:T(8,128)(2,1)} %bitcast.5), kind=kLoop, calls=%fused_computation | loop fusion | flops 786432 | bytes 1572864 | tf_op jit(solution)/shard_map/stack | solution.py:290
  1.8 0.2 columns.1
  2.1 0.5 %collective-permute-start.2 = (bf16[1280,128]{1,0:T(8,128)(2,1)S(1)}, bf16[1280,128]{1,0:T(8,128)(2,1)S(1)}, u32[]{:S(2)}, u32[]{:S(2)}) collective-permute-start(bf16[1280,128]{1,0:T(8,128)(2,1)S(1)} %get-tuple-element.34), channel_id=1, source_target_pairs={{0,1},{1,0},{2,3},{3,2},{4,5},{5,4},{6,7},{7,6},{8,9},{9,8},{10,11... | collective-permute-start | bytes 983048 | tf_op jit(solution)/shard_map/ppermute | solution.py:279
  2.6 3.7 %collective-permute-start = (bf16[256,128]{1,0:T(8,128)(2,1)S(1)}, bf16[256,128]{1,0:T(8,128)(2,1)S(1)}, u32[]{:S(2)}, u32[]{:S(2)}) collective-permute-start(bf16[256,128]{1,0:T(8,128)(2,1)S(1)} %get-tuple-element.31), channel_id=1, source_target_pairs={{0,4},{1,5},{2,6},{3,7},{4,0},{5,1},{6,2},{7,3},{8,12},{9,13},{10,... | collective-permute-start | bytes 196616 | tf_op jit(solution)/shard_map/ppermute | solution.py:279
  6.2 0.1 collective-permute-start.1
  6.3 0.0 collective-permute-done.2.sibling.refs_5_.refs_4_
  6.4 1.7 %collective-permute-start.4 = (bf16[768,128]{1,0:T(8,128)(2,1)S(1)}, bf16[768,128]{1,0:T(8,128)(2,1)S(1)}, u32[]{:S(2)}, u32[]{:S(2)}) collective-permute-start(bf16[768,128]{1,0:T(8,128)(2,1)S(1)} %pad_maximum_fusion.1), channel_id=1, source_target_pairs={{0,2},{1,3},{2,0},{3,1},{4,6},{5,7},{6,4},{7,5},{8,10},{9,11},{10,... | collective-permute-start | bytes 589832 | tf_op jit(solution)/shard_map/ppermute | solution.py:279
  8.1 0.0 copy-start.2
  8.1 0.0 copy-start.3
  8.1 0.0 copy-start.4
  8.1 2.5 %collective-permute-start.3 = (bf16[512,128]{1,0:T(8,128)(2,1)S(1)}, bf16[512,128]{1,0:T(8,128)(2,1)S(1)}, u32[]{:S(2)}, u32[]{:S(2)}) collective-permute-start(bf16[512,128]{1,0:T(8,128)(2,1)S(1)} %pad_maximum_fusion.2), channel_id=1, source_target_pairs={{0,6},{1,7},{2,4},{3,5},{4,2},{5,3},{6,0},{7,1},{8,14},{9,15},{10,... | collective-permute-start | bytes 393224 | tf_op jit(solution)/shard_map/ppermute | solution.py:279
  10.6 0.0 collective-permute-done.refs_0_
  10.6 2.5 %collective-permute-done.1.refs_1_ = bf16[256,128]{1,0:T(8,128)(2,1)S(1)} collective-permute-done((bf16[256,128]{1,0:T(8,128)(2,1)S(1)}, bf16[256,128]{1,0:T(8,128)(2,1)S(1)}, u32[]{:S(2)}, u32[]{:S(2)}) %collective-permute-start.1) | collective-permute-done | bytes 65568 | tf_op jit(solution)/shard_map/ppermute | solution.py:279
  13.1 0.0 copy-done.2
  13.1 0.0 copy-done.3
  13.1 0.0 copy-done.4
  13.2 0.1 collective-permute-start.5
  13.3 3.7 %collective-permute-start.6 = (bf16[256,128]{1,0:T(8,128)(2,1)S(1)}, bf16[256,128]{1,0:T(8,128)(2,1)S(1)}, u32[]{:S(2)}, u32[]{:S(2)}) collective-permute-start(bf16[256,128]{1,0:T(8,128)(2,1)S(1)} %get-tuple-element.43), channel_id=1, source_target_pairs={{0,6},{1,7},{2,4},{3,5},{4,2},{5,3},{6,0},{7,1},{8,14},{9,15},{10,... | collective-permute-start | bytes 196616 | tf_op jit(solution)/shard_map/ppermute | solution.py:279
  16.9 3.1 %collective-permute-done.3.refs_2_ = bf16[512,128]{1,0:T(8,128)(2,1)S(1)} collective-permute-done((bf16[512,128]{1,0:T(8,128)(2,1)S(1)}, bf16[512,128]{1,0:T(8,128)(2,1)S(1)}, u32[]{:S(2)}, u32[]{:S(2)}) %collective-permute-start.3) | collective-permute-done | bytes 131104 | tf_op jit(solution)/shard_map/ppermute | solution.py:279
  20.0 0.0 collective-permute-done.4.refs_3_.refs_2_
  20.1 1.8 %filter_gradient.1 = (bf16[8,128,128]{2,1,0:T(8,128)(2,1)S(1)}, f32[8,16,128]{2,1,0:T(8,128)S(1)}, f32[8,256,128]{2,1,0:T(8,128)S(1)}, f32[8,128]{1,0:T(8,128)S(1)}) custom-call(bf16[256,128]{1,0:T(8,128)(2,1)S(1)} %collective-permute-done.refs_0_, bf16[256,128]{1,0:T(8,128)(2,1)S(1)} %collective-permute-done.1.refs_1_, ...), custom_call_target="tpu_custom_call" | custom-call | flops 4000000000 | tf_op jit(solution)/shard_map/filter_gradient/pallas_call | solution.py:336
  21.8 2.5 %collective-permute-start.9 = (f32[8,128]{1,0:T(8,128)S(1)}, f32[8,128]{1,0:T(8,128)S(1)}, u32[]{:S(2)}, u32[]{:S(2)}) collective-permute-start(f32[8,128]{1,0:T(8,128)S(1)} %get-tuple-element.47.refs_4_), channel_id=1, source_target_pairs={{0,24},{8,16},{16,8},{24,0},{1,25},{9,17},{17,9},{25,1},{2,26},{10... | collective-permute-start | bytes 12296 | tf_op jit(solution)/shard_map/ppermute | solution.py:352
  24.3 0.5 %collective-permute-start.8 = (f32[8,128]{1,0:T(8,128)S(1)}, f32[8,128]{1,0:T(8,128)S(1)}, u32[]{:S(2)}, u32[]{:S(2)}) collective-permute-start(f32[8,128]{1,0:T(8,128)S(1)} %get-tuple-element.47.refs_4_), channel_id=1, source_target_pairs={{0,16},{8,24},{16,0},{24,8},{1,17},{9,25},{17,1},{25,9},{2,18},{10... | collective-permute-start | bytes 12296 | tf_op jit(solution)/shard_map/ppermute | solution.py:352
  24.8 0.5 %collective-permute-start.7 = (f32[8,128]{1,0:T(8,128)S(1)}, f32[8,128]{1,0:T(8,128)S(1)}, u32[]{:S(2)}, u32[]{:S(2)}) collective-permute-start(f32[8,128]{1,0:T(8,128)S(1)} %get-tuple-element.47.refs_4_), channel_id=1, source_target_pairs={{0,8},{8,0},{16,24},{24,16},{1,9},{9,1},{17,25},{25,17},{2,10},{10... | collective-permute-start | bytes 12296 | tf_op jit(solution)/shard_map/ppermute | solution.py:352
  25.4 0.0 collective-permute-done.5.refs_0_
  25.4 0.0 collective-permute-done.6.refs_1_
  25.4 1.6 %input_gradient.1 = (bf16[8,128,128]{2,1,0:T(8,128)(2,1)S(1)}, f32[8,16,128]{2,1,0:T(8,128)S(1)}) custom-call(bf16[256,128]{1,0:T(8,128)(2,1)S(1)} %collective-permute-done.5.refs_0_, bf16[256,128]{1,0:T(8,128)(2,1)S(1)} %collective-permute-done.6.refs_1_, bf16[768,128]{1,0:T(8,128)(2,1)S(1)} %collective-permute-done.4.refs_3_.refs_2_, ...), custom_call_target="tpu_custom_call" | custom-call | flops 20000000000 | tf_op jit(solution)/shard_map/input_gradient/pallas_call | solution.py:355
  27.0 0.0 collective-permute-done.9.refs_7_
  27.0 0.9 %collective-permute-done.8.refs_6_ = f32[8,128]{1,0:T(8,128)S(1)} collective-permute-done((f32[8,128]{1,0:T(8,128)S(1)}, f32[8,128]{1,0:T(8,128)S(1)}, u32[]{:S(2)}, u32[]{:S(2)}) %collective-permute-start.8) | collective-permute-done | bytes 4128 | tf_op jit(solution)/shard_map/ppermute | solution.py:352
  27.9 0.5 %collective-permute-done.7.refs_5_ = f32[8,128]{1,0:T(8,128)S(1)} collective-permute-done((f32[8,128]{1,0:T(8,128)S(1)}, f32[8,128]{1,0:T(8,128)S(1)}, u32[]{:S(2)}, u32[]{:S(2)}) %collective-permute-start.7) | collective-permute-done | bytes 4128 | tf_op jit(solution)/shard_map/ppermute | solution.py:352
  28.5 0.1 messages.1
  28.6 4.3 %collective-permute-start.10 = (bf16[272,128]{1,0:T(8,128)(2,1)S(1)}, bf16[272,128]{1,0:T(8,128)(2,1)S(1)}, u32[]{:S(2)}, u32[]{:S(2)}) collective-permute-start(bf16[272,128]{1,0:T(8,128)(2,1)S(1)} %get-tuple-element.48), channel_id=1, source_target_pairs={{0,4},{1,5},{2,6},{3,7},{4,0},{5,1},{6,2},{7,3},{8,12},{9,13},{10,... | collective-permute-start | bytes 208904 | tf_op jit(solution)/shard_map/ppermute | solution.py:279
  32.8 0.0 collective-permute-start.11
  32.8 0.4 collective-permute-start.12
  33.3 1.1 %collective-permute-start.13 = (bf16[272,128]{1,0:T(8,128)(2,1)S(1)}, bf16[272,128]{1,0:T(8,128)(2,1)S(1)}, u32[]{:S(2)}, u32[]{:S(2)}) collective-permute-start(bf16[272,128]{1,0:T(8,128)(2,1)S(1)} %get-tuple-element.51), channel_id=1, source_target_pairs={{0,3},{1,2},{2,1},{3,0},{4,7},{5,6},{6,5},{7,4},{8,11},{9,10},{10,... | collective-permute-start | bytes 208904 | tf_op jit(solution)/shard_map/ppermute | solution.py:279
  34.4 2.7 %collective-permute-start.14 = (bf16[272,128]{1,0:T(8,128)(2,1)S(1)}, bf16[272,128]{1,0:T(8,128)(2,1)S(1)}, u32[]{:S(2)}, u32[]{:S(2)}) collective-permute-start(bf16[272,128]{1,0:T(8,128)(2,1)S(1)} %get-tuple-element.52), channel_id=1, source_target_pairs={{0,6},{1,7},{2,4},{3,5},{4,2},{5,3},{6,0},{7,1},{8,14},{9,15},{10,... | collective-permute-start | bytes 208904 | tf_op jit(solution)/shard_map/ppermute | solution.py:279
  37.1 0.0 collective-permute-done.10.refs_0_
  37.1 1.1 %collective-permute-start.15 = (bf16[272,128]{1,0:T(8,128)(2,1)S(1)}, bf16[272,128]{1,0:T(8,128)(2,1)S(1)}, u32[]{:S(2)}, u32[]{:S(2)}) collective-permute-start(bf16[272,128]{1,0:T(8,128)(2,1)S(1)} %get-tuple-element.53), channel_id=1, source_target_pairs={{0,7},{1,6},{2,5},{3,4},{4,3},{5,2},{6,1},{7,0},{8,15},{9,14},{10,... | collective-permute-start | bytes 208904 | tf_op jit(solution)/shard_map/ppermute | solution.py:279
  38.1 0.8 %collective-permute-done.11.refs_1_ = bf16[272,128]{1,0:T(8,128)(2,1)S(1)} collective-permute-done((bf16[272,128]{1,0:T(8,128)(2,1)S(1)}, bf16[272,128]{1,0:T(8,128)(2,1)S(1)}, u32[]{:S(2)}, u32[]{:S(2)}) %collective-permute-start.11) | collective-permute-done | bytes 69664 | tf_op jit(solution)/shard_map/ppermute | solution.py:279
  38.9 1.7 %collective-permute-start.16 = (bf16[272,128]{1,0:T(8,128)(2,1)S(1)}, bf16[272,128]{1,0:T(8,128)(2,1)S(1)}, u32[]{:S(2)}, u32[]{:S(2)}) collective-permute-start(bf16[272,128]{1,0:T(8,128)(2,1)S(1)} %get-tuple-element.55), channel_id=1, source_target_pairs={{0,1},{1,0},{2,3},{3,2},{4,5},{5,4},{6,7},{7,6},{8,9},{9,8},{10,11... | collective-permute-start | bytes 208904 | tf_op jit(solution)/shard_map/ppermute | solution.py:279
  40.6 0.0 collective-permute-done.12.refs_2_
  40.6 0.0 collective-permute-done.13.refs_3_
  40.7 1.1 %collective-permute-done.14.refs_4_ = bf16[272,128]{1,0:T(8,128)(2,1)S(1)} collective-permute-done((bf16[272,128]{1,0:T(8,128)(2,1)S(1)}, bf16[272,128]{1,0:T(8,128)(2,1)S(1)}, u32[]{:S(2)}, u32[]{:S(2)}) %collective-permute-start.14) | collective-permute-done | bytes 69664 | tf_op jit(solution)/shard_map/ppermute | solution.py:279
  41.7 1.5 %collective-permute-done.15.refs_5_ = bf16[272,128]{1,0:T(8,128)(2,1)S(1)} collective-permute-done((bf16[272,128]{1,0:T(8,128)(2,1)S(1)}, bf16[272,128]{1,0:T(8,128)(2,1)S(1)}, u32[]{:S(2)}, u32[]{:S(2)}) %collective-permute-start.15) | collective-permute-done | bytes 69664 | tf_op jit(solution)/shard_map/ppermute | solution.py:279
  43.2 0.0 collective-permute-done.16.refs_7_
  43.2 0.0 copy-done
  43.2 0.0 copy-done.1
  43.2 1.5 %outputs.1 = (f32[128,1024]{1,0:T(8,128)}, f32[128,1024]{1,0:T(8,128)}, f32[1,1024]{1,0:T(1,128)}) custom-call(bf16[272,128]{1,0:T(8,128)(2,1)S(1)} %collective-permute-done.10.refs_0_, bf16[272,128]{1,0:T(8,128)(2,1)S(1)} %collective-permute-done.11.refs_1_, bf16[272,128]{1,0:T(8,128)(2,1)S(1)} %collective-permute-done.12.refs_2_, ...), custom_call_target="tpu_custom_call" | custom-call | flops 1000000000 | tf_op jit(solution)/shard_map/outputs/pallas_call | solution.py:385
  (9 shorter events, 0.1 us)
Async XLA Ops:
  2.1 4.3 %collective-permute-start.2 = (bf16[1280,128]{1,0:T(8,128)(2,1)S(1)}, bf16[1280,128]{1,0:T(8,128)(2,1)S(1)}, u32[]{:S(2)}, u32[]{:S(2)}) collective-permute-start(bf16[1280,128]{1,0:T(8,128)(2,1)S(1)} %get-tuple-element.34), channel_id=1, source_target_pairs={{0,1},{1,0},{2,3},{3,2},{4,5},{5,4},{6,7},{7,6},{8,9},{9,8},{10,11... | collective-permute-start | bytes 983048 | tf_op jit(solution)/shard_map/ppermute | solution.py:279
  2.6 8.1 %collective-permute-start = (bf16[256,128]{1,0:T(8,128)(2,1)S(1)}, bf16[256,128]{1,0:T(8,128)(2,1)S(1)}, u32[]{:S(2)}, u32[]{:S(2)}) collective-permute-start(bf16[256,128]{1,0:T(8,128)(2,1)S(1)} %get-tuple-element.31), channel_id=1, source_target_pairs={{0,4},{1,5},{2,6},{3,7},{4,0},{5,1},{6,2},{7,3},{8,12},{9,13},{10,... | collective-permute-start | bytes 196616 | tf_op jit(solution)/shard_map/ppermute | solution.py:279
  6.2 6.9 %collective-permute-start.1 = (bf16[256,128]{1,0:T(8,128)(2,1)S(1)}, bf16[256,128]{1,0:T(8,128)(2,1)S(1)}, u32[]{:S(2)}, u32[]{:S(2)}) collective-permute-start(bf16[256,128]{1,0:T(8,128)(2,1)S(1)} %get-tuple-element.32), channel_id=1, source_target_pairs={{0,5},{1,4},{2,7},{3,6},{4,1},{5,0},{6,3},{7,2},{8,13},{9,12},{10,... | collective-permute-start | bytes 196616 | tf_op jit(solution)/shard_map/ppermute | solution.py:279
  6.4 13.7 %collective-permute-start.4 = (bf16[768,128]{1,0:T(8,128)(2,1)S(1)}, bf16[768,128]{1,0:T(8,128)(2,1)S(1)}, u32[]{:S(2)}, u32[]{:S(2)}) collective-permute-start(bf16[768,128]{1,0:T(8,128)(2,1)S(1)} %pad_maximum_fusion.1), channel_id=1, source_target_pairs={{0,2},{1,3},{2,0},{3,1},{4,6},{5,7},{6,4},{7,5},{8,10},{9,11},{10,... | collective-permute-start | bytes 589832 | tf_op jit(solution)/shard_map/ppermute | solution.py:279
  8.1 5.1 %copy-start.2 = (bf16[256,256]{1,0:T(8,128)(2,1)S(1)}, bf16[256,256]{1,0:T(8,128)(2,1)}, u32[]{:S(2)}) copy-start(bf16[256,256]{1,0:T(8,128)(2,1)} %constant.6.clone.refs_0_) | copy-start | bytes 393220
  8.1 5.1 %copy-start.3 = (bf16[128,256]{1,0:T(8,128)(2,1)S(1)}, bf16[128,256]{1,0:T(8,128)(2,1)}, u32[]{:S(2)}) copy-start(bf16[128,256]{1,0:T(8,128)(2,1)} %constant.8.clone.refs_2_) | copy-start | bytes 196612
  8.1 5.1 %copy-start.4 = (bf16[128,256]{1,0:T(8,128)(2,1)S(1)}, bf16[128,256]{1,0:T(8,128)(2,1)}, u32[]{:S(2)}) copy-start(bf16[128,256]{1,0:T(8,128)(2,1)} %constant.7.clone.refs_1_) | copy-start | bytes 196612
  8.1 12.0 %collective-permute-start.3 = (bf16[512,128]{1,0:T(8,128)(2,1)S(1)}, bf16[512,128]{1,0:T(8,128)(2,1)S(1)}, u32[]{:S(2)}, u32[]{:S(2)}) collective-permute-start(bf16[512,128]{1,0:T(8,128)(2,1)S(1)} %pad_maximum_fusion.2), channel_id=1, source_target_pairs={{0,6},{1,7},{2,4},{3,5},{4,2},{5,3},{6,0},{7,1},{8,14},{9,15},{10,... | collective-permute-start | bytes 393224 | tf_op jit(solution)/shard_map/ppermute | solution.py:279
  13.2 12.2 %collective-permute-start.5 = (bf16[256,128]{1,0:T(8,128)(2,1)S(1)}, bf16[256,128]{1,0:T(8,128)(2,1)S(1)}, u32[]{:S(2)}, u32[]{:S(2)}) collective-permute-start(bf16[256,128]{1,0:T(8,128)(2,1)S(1)} %get-tuple-element.42), channel_id=1, source_target_pairs={{0,4},{1,5},{2,6},{3,7},{4,0},{5,1},{6,2},{7,3},{8,12},{9,13},{10,... | collective-permute-start | bytes 196616 | tf_op jit(solution)/shard_map/ppermute | solution.py:279
  13.3 12.1 %collective-permute-start.6 = (bf16[256,128]{1,0:T(8,128)(2,1)S(1)}, bf16[256,128]{1,0:T(8,128)(2,1)S(1)}, u32[]{:S(2)}, u32[]{:S(2)}) collective-permute-start(bf16[256,128]{1,0:T(8,128)(2,1)S(1)} %get-tuple-element.43), channel_id=1, source_target_pairs={{0,6},{1,7},{2,4},{3,5},{4,2},{5,3},{6,0},{7,1},{8,14},{9,15},{10,... | collective-permute-start | bytes 196616 | tf_op jit(solution)/shard_map/ppermute | solution.py:279
  21.8 5.2 %collective-permute-start.9 = (f32[8,128]{1,0:T(8,128)S(1)}, f32[8,128]{1,0:T(8,128)S(1)}, u32[]{:S(2)}, u32[]{:S(2)}) collective-permute-start(f32[8,128]{1,0:T(8,128)S(1)} %get-tuple-element.47.refs_4_), channel_id=1, source_target_pairs={{0,24},{8,16},{16,8},{24,0},{1,25},{9,17},{17,9},{25,1},{2,26},{10... | collective-permute-start | bytes 12296 | tf_op jit(solution)/shard_map/ppermute | solution.py:352
  24.3 3.6 %collective-permute-start.8 = (f32[8,128]{1,0:T(8,128)S(1)}, f32[8,128]{1,0:T(8,128)S(1)}, u32[]{:S(2)}, u32[]{:S(2)}) collective-permute-start(f32[8,128]{1,0:T(8,128)S(1)} %get-tuple-element.47.refs_4_), channel_id=1, source_target_pairs={{0,16},{8,24},{16,0},{24,8},{1,17},{9,25},{17,1},{25,9},{2,18},{10... | collective-permute-start | bytes 12296 | tf_op jit(solution)/shard_map/ppermute | solution.py:352
  24.8 3.6 %collective-permute-start.7 = (f32[8,128]{1,0:T(8,128)S(1)}, f32[8,128]{1,0:T(8,128)S(1)}, u32[]{:S(2)}, u32[]{:S(2)}) collective-permute-start(f32[8,128]{1,0:T(8,128)S(1)} %get-tuple-element.47.refs_4_), channel_id=1, source_target_pairs={{0,8},{8,0},{16,24},{24,16},{1,9},{9,1},{17,25},{25,17},{2,10},{10... | collective-permute-start | bytes 12296 | tf_op jit(solution)/shard_map/ppermute | solution.py:352
  28.5 14.8 %copy-start = (bf16[128,1024]{1,0:T(8,128)(2,1)S(1)}, bf16[128,1024]{1,0:T(8,128)(2,1)}, u32[]{:S(2)}) copy-start(bf16[128,1024]{1,0:T(8,128)(2,1)} %refs_8_.1) | copy-start | bytes 786436
  28.6 8.5 %collective-permute-start.10 = (bf16[272,128]{1,0:T(8,128)(2,1)S(1)}, bf16[272,128]{1,0:T(8,128)(2,1)S(1)}, u32[]{:S(2)}, u32[]{:S(2)}) collective-permute-start(bf16[272,128]{1,0:T(8,128)(2,1)S(1)} %get-tuple-element.48), channel_id=1, source_target_pairs={{0,4},{1,5},{2,6},{3,7},{4,0},{5,1},{6,2},{7,3},{8,12},{9,13},{10,... | collective-permute-start | bytes 208904 | tf_op jit(solution)/shard_map/ppermute | solution.py:279
  32.8 6.1 %collective-permute-start.11 = (bf16[272,128]{1,0:T(8,128)(2,1)S(1)}, bf16[272,128]{1,0:T(8,128)(2,1)S(1)}, u32[]{:S(2)}, u32[]{:S(2)}) collective-permute-start(bf16[272,128]{1,0:T(8,128)(2,1)S(1)} %get-tuple-element.49), channel_id=1, source_target_pairs={{0,5},{1,4},{2,7},{3,6},{4,1},{5,0},{6,3},{7,2},{8,13},{9,12},{10,... | collective-permute-start | bytes 208904 | tf_op jit(solution)/shard_map/ppermute | solution.py:279
  32.8 7.8 %collective-permute-start.12 = (bf16[272,128]{1,0:T(8,128)(2,1)S(1)}, bf16[272,128]{1,0:T(8,128)(2,1)S(1)}, u32[]{:S(2)}, u32[]{:S(2)}) collective-permute-start(bf16[272,128]{1,0:T(8,128)(2,1)S(1)} %get-tuple-element.50), channel_id=1, source_target_pairs={{0,2},{1,3},{2,0},{3,1},{4,6},{5,7},{6,4},{7,5},{8,10},{9,11},{10,... | collective-permute-start | bytes 208904 | tf_op jit(solution)/shard_map/ppermute | solution.py:279
  33.3 7.4 %collective-permute-start.13 = (bf16[272,128]{1,0:T(8,128)(2,1)S(1)}, bf16[272,128]{1,0:T(8,128)(2,1)S(1)}, u32[]{:S(2)}, u32[]{:S(2)}) collective-permute-start(bf16[272,128]{1,0:T(8,128)(2,1)S(1)} %get-tuple-element.51), channel_id=1, source_target_pairs={{0,3},{1,2},{2,1},{3,0},{4,7},{5,6},{6,5},{7,4},{8,11},{9,10},{10,... | collective-permute-start | bytes 208904 | tf_op jit(solution)/shard_map/ppermute | solution.py:279
  34.4 8.8 %copy-start.1 = (f32[1024]{0:T(1024)S(1)}, f32[1024]{0:T(1024)}, u32[]{:S(2)}) copy-start(f32[1024]{0:T(1024)} %param.10) | copy-start | bytes 12292
  34.4 7.3 %collective-permute-start.14 = (bf16[272,128]{1,0:T(8,128)(2,1)S(1)}, bf16[272,128]{1,0:T(8,128)(2,1)S(1)}, u32[]{:S(2)}, u32[]{:S(2)}) collective-permute-start(bf16[272,128]{1,0:T(8,128)(2,1)S(1)} %get-tuple-element.52), channel_id=1, source_target_pairs={{0,6},{1,7},{2,4},{3,5},{4,2},{5,3},{6,0},{7,1},{8,14},{9,15},{10,... | collective-permute-start | bytes 208904 | tf_op jit(solution)/shard_map/ppermute | solution.py:279
  37.1 6.1 %collective-permute-start.15 = (bf16[272,128]{1,0:T(8,128)(2,1)S(1)}, bf16[272,128]{1,0:T(8,128)(2,1)S(1)}, u32[]{:S(2)}, u32[]{:S(2)}) collective-permute-start(bf16[272,128]{1,0:T(8,128)(2,1)S(1)} %get-tuple-element.53), channel_id=1, source_target_pairs={{0,7},{1,6},{2,5},{3,4},{4,3},{5,2},{6,1},{7,0},{8,15},{9,14},{10,... | collective-permute-start | bytes 208904 | tf_op jit(solution)/shard_map/ppermute | solution.py:279
  38.9 4.3 %collective-permute-start.16 = (bf16[272,128]{1,0:T(8,128)(2,1)S(1)}, bf16[272,128]{1,0:T(8,128)(2,1)S(1)}, u32[]{:S(2)}, u32[]{:S(2)}) collective-permute-start(bf16[272,128]{1,0:T(8,128)(2,1)S(1)} %get-tuple-element.55), channel_id=1, source_target_pairs={{0,1},{1,0},{2,3},{3,2},{4,5},{5,4},{6,7},{7,6},{8,9},{9,8},{10,11... | collective-permute-start | bytes 208904 | tf_op jit(solution)/shard_map/ppermute | solution.py:279

commit v5 on v4

--- a/solution.py
+++ b/solution.py
@@ -266,7 +266,7 @@
     position = lax.axis_index("ctx")
     both, back_high, back_low = tables(length)
     f32, bf16 = jnp.float32, jnp.bfloat16
-    chips = sorted(range(size // 2), key=lambda chip: (-chip.bit_length(), chip))
+    chips = sorted(range(size // 2), key=lambda chip: (-chip.bit_length(), -chip))
     order = [k for chip in chips for k in (2 * chip, 2 * chip + 1)]
     far = size // 4
     vmem_bytes = (8 + size) * 2**20
@@ -371,7 +371,8 @@
         [jax.ShapeDtypeStruct((2 * length + tail_rows, width), bf16)] * size,
     )(codes, tails, input_codes, input_tails, *all_squares)
     messages = {k: send(message, k) if k else message for k, message in zip(order, messages)}
-    turns = chips[: far // 2] + chips[far:-1] + chips[far // 2 : far] + [0]
+    nearer = sorted(chips[:far])
+    turns = nearer[: far // 2] + chips[far:-1] + nearer[far // 2 :] + [0]
     turns = [k for chip in turns for k in (2 * chip, 2 * chip + 1)]
 
     clip_limit = 0.25 * math.sqrt(length * size * chan_width * columns)

time: 44.9 us -> 44 us (0.980)
  starting transfers between devices: 27.1 us -> 25.3 us
  waiting for transfers between devices: 10.4 us -> 11.2 us
    ppermute x14, starting transfers between devices: 23.5 us -> 21.7 us  [send(): return lax.ppermute(block, 'ctx', [(i, i ^ k) for i in range(size)])]
    ppermute x14, waiting for transfers between devices: 8.97 us -> 10.6 us  [send(): return lax.ppermute(block, 'ctx', [(i, i ^ k) for i in range(size)])]
    ppermute x3, waiting for transfers between devices: 1.45 us -> 0.66 us  [per_device(): lax.ppermute(squares, 'chan', [(i, i ^ k) for i in range(columns)])]
  transfers between devices with their start and end apart: 17 -> 17, of which waited for: 7 -> 9; matrix products, arithmetic and copies ran while one was open for 0% -> 0% of each run, Pallas kernels for 8% -> 8%
where the time goes in v5:
time: 44 us; the launch traced here: 43.8 us
  starting transfers between devices  25.3 us (58%)
  waiting for transfers between devices  11.2 us (25%)
  Pallas kernels  5.25 us (12%)
  other arithmetic  1.22 us (3%)
  between operations  0.77 us (2%)
    ppermute x14, starting transfers between devices, send(): return lax.ppermute(block, 'ctx', [(i, i ^ k) for i in range(size)])  21.7 us
    ppermute x14, waiting for transfers between devices, send(): return lax.ppermute(block, 'ctx', [(i, i ^ k) for i in range(size)])  10.6 us
    ppermute x3, starting transfers between devices, per_device(): lax.ppermute(squares, 'chan', [(i, i ^ k) for i in range(columns)])  3.55 us
    pallas_call x1, Pallas kernels, per_device(): run(functools.partial(first_kernel, order, length, first_places), 'filter...  1.76 us
    pallas_call x1, Pallas kernels, per_device(): run(functools.partial(second_kernel, order, length, second_places), 'inpu...  1.6 us
    pallas_call x1, Pallas kernels, per_device(): run(functools.partial(last_kernel, turns, length, width, clip_limit), 'ou...  1.54 us
    another operation x1, other arithmetic, per_device(): jnp.stack(three)  1.2 us
  transfers between devices with their start and end apart: 17, of which 9 were waited for; matrix products, arithmetic and copies ran while one was open for 0% of the time, Pallas kernels for 8%

profile of v5, /device:TPU:0, one launch (start us, length us, event | category | flops | bytes accessed | tf_op | source)
XLA Modules:
  0.0 43.8 jit_solution(11356766849881068526)
XLA Ops:
  0.6 1.2 %pad_maximum_fusion.arrays = bf16[3,128,1024]{2,1,0:T(8,128)(2,1)S(1)} fusion(bf16[1,128,1024]{2,1,0:T(8,128)(2,1)} %bitcast.7, bf16[1,128,1024]{2,1,0:T(8,128)(2,1)} %bitcast.8, bf16[1,128,1024]{2,1,0:T(8,128)(2,1)} %bitcast.5), kind=kLoop, calls=%fused_computation | loop fusion | flops 786432 | bytes 1572864 | tf_op jit(solution)/shard_map/stack | solution.py:290
  1.8 0.2 columns.1
  2.1 0.5 %collective-permute-start.2 = (bf16[1280,128]{1,0:T(8,128)(2,1)S(1)}, bf16[1280,128]{1,0:T(8,128)(2,1)S(1)}, u32[]{:S(2)}, u32[]{:S(2)}) collective-permute-start(bf16[1280,128]{1,0:T(8,128)(2,1)S(1)} %get-tuple-element.34), channel_id=1, source_target_pairs={{0,1},{1,0},{2,3},{3,2},{4,5},{5,4},{6,7},{7,6},{8,9},{9,8},{10,11... | collective-permute-start | bytes 983048 | tf_op jit(solution)/shard_map/ppermute | solution.py:279
  2.6 4.7 %collective-permute-start = (bf16[256,128]{1,0:T(8,128)(2,1)S(1)}, bf16[256,128]{1,0:T(8,128)(2,1)S(1)}, u32[]{:S(2)}, u32[]{:S(2)}) collective-permute-start(bf16[256,128]{1,0:T(8,128)(2,1)S(1)} %get-tuple-element.31), channel_id=1, source_target_pairs={{0,6},{1,7},{2,4},{3,5},{4,2},{5,3},{6,0},{7,1},{8,14},{9,15},{10,... | collective-permute-start | bytes 196616 | tf_op jit(solution)/shard_map/ppermute | solution.py:279
  7.2 0.1 collective-permute-start.1
  7.3 0.0 collective-permute-done.2.sibling.refs_5_.refs_4_
  7.4 0.1 collective-permute-start.4
  7.5 0.0 copy-start.2
  7.5 0.0 copy-start.3
  7.5 0.0 copy-start.4
  7.5 4.1 %collective-permute-start.3 = (bf16[512,128]{1,0:T(8,128)(2,1)S(1)}, bf16[512,128]{1,0:T(8,128)(2,1)S(1)}, u32[]{:S(2)}, u32[]{:S(2)}) collective-permute-start(bf16[512,128]{1,0:T(8,128)(2,1)S(1)} %pad_maximum_fusion.2), channel_id=1, source_target_pairs={{0,4},{1,5},{2,6},{3,7},{4,0},{5,1},{6,2},{7,3},{8,12},{9,13},{10,... | collective-permute-start | bytes 393224 | tf_op jit(solution)/shard_map/ppermute | solution.py:279
  11.6 0.0 collective-permute-done.refs_0_
  11.7 1.6 %collective-permute-done.1.refs_1_ = bf16[256,128]{1,0:T(8,128)(2,1)S(1)} collective-permute-done((bf16[256,128]{1,0:T(8,128)(2,1)S(1)}, bf16[256,128]{1,0:T(8,128)(2,1)S(1)}, u32[]{:S(2)}, u32[]{:S(2)}) %collective-permute-start.1) | collective-permute-done | bytes 65568 | tf_op jit(solution)/shard_map/ppermute | solution.py:279
  13.2 0.0 copy-done.2
  13.2 0.0 copy-done.3
  13.3 0.0 copy-done.4
  13.3 1.4 %collective-permute-start.5 = (bf16[256,128]{1,0:T(8,128)(2,1)S(1)}, bf16[256,128]{1,0:T(8,128)(2,1)S(1)}, u32[]{:S(2)}, u32[]{:S(2)}) collective-permute-start(bf16[256,128]{1,0:T(8,128)(2,1)S(1)} %get-tuple-element.42), channel_id=1, source_target_pairs={{0,6},{1,7},{2,4},{3,5},{4,2},{5,3},{6,0},{7,1},{8,14},{9,15},{10,... | collective-permute-start | bytes 196616 | tf_op jit(solution)/shard_map/ppermute | solution.py:279
  14.7 0.3 collective-permute-start.6
  15.0 3.2 %collective-permute-done.3.refs_2_ = bf16[512,128]{1,0:T(8,128)(2,1)S(1)} collective-permute-done((bf16[512,128]{1,0:T(8,128)(2,1)S(1)}, bf16[512,128]{1,0:T(8,128)(2,1)S(1)}, u32[]{:S(2)}, u32[]{:S(2)}) %collective-permute-start.3) | collective-permute-done | bytes 131104 | tf_op jit(solution)/shard_map/ppermute | solution.py:279
  18.2 0.4 collective-permute-done.4.refs_3_.refs_2_
  18.6 1.8 %filter_gradient.1 = (bf16[8,128,128]{2,1,0:T(8,128)(2,1)S(1)}, f32[8,16,128]{2,1,0:T(8,128)S(1)}, f32[8,256,128]{2,1,0:T(8,128)S(1)}, f32[8,128]{1,0:T(8,128)S(1)}) custom-call(bf16[256,128]{1,0:T(8,128)(2,1)S(1)} %collective-permute-done.refs_0_, bf16[256,128]{1,0:T(8,128)(2,1)S(1)} %collective-permute-done.1.refs_1_, ...), custom_call_target="tpu_custom_call" | custom-call | flops 4000000000 | tf_op jit(solution)/shard_map/filter_gradient/pallas_call | solution.py:336
  20.4 2.6 %collective-permute-start.9 = (f32[8,128]{1,0:T(8,128)S(1)}, f32[8,128]{1,0:T(8,128)S(1)}, u32[]{:S(2)}, u32[]{:S(2)}) collective-permute-start(f32[8,128]{1,0:T(8,128)S(1)} %get-tuple-element.47.refs_4_), channel_id=1, source_target_pairs={{0,24},{8,16},{16,8},{24,0},{1,25},{9,17},{17,9},{25,1},{2,26},{10... | collective-permute-start | bytes 12296 | tf_op jit(solution)/shard_map/ppermute | solution.py:352
  23.0 0.5 %collective-permute-start.8 = (f32[8,128]{1,0:T(8,128)S(1)}, f32[8,128]{1,0:T(8,128)S(1)}, u32[]{:S(2)}, u32[]{:S(2)}) collective-permute-start(f32[8,128]{1,0:T(8,128)S(1)} %get-tuple-element.47.refs_4_), channel_id=1, source_target_pairs={{0,16},{8,24},{16,0},{24,8},{1,17},{9,25},{17,1},{25,9},{2,18},{10... | collective-permute-start | bytes 12296 | tf_op jit(solution)/shard_map/ppermute | solution.py:352
  23.5 0.4 collective-permute-start.7
  23.9 0.0 collective-permute-done.5.refs_0_
  23.9 0.9 %collective-permute-done.6.refs_1_ = bf16[256,128]{1,0:T(8,128)(2,1)S(1)} collective-permute-done((bf16[256,128]{1,0:T(8,128)(2,1)S(1)}, bf16[256,128]{1,0:T(8,128)(2,1)S(1)}, u32[]{:S(2)}, u32[]{:S(2)}) %collective-permute-start.6) | collective-permute-done | bytes 65568 | tf_op jit(solution)/shard_map/ppermute | solution.py:279
  24.8 1.6 %input_gradient.1 = (bf16[8,128,128]{2,1,0:T(8,128)(2,1)S(1)}, f32[8,16,128]{2,1,0:T(8,128)S(1)}) custom-call(bf16[256,128]{1,0:T(8,128)(2,1)S(1)} %collective-permute-done.5.refs_0_, bf16[256,128]{1,0:T(8,128)(2,1)S(1)} %collective-permute-done.6.refs_1_, bf16[768,128]{1,0:T(8,128)(2,1)S(1)} %collective-permute-done.4.refs_3_.refs_2_, ...), custom_call_target="tpu_custom_call" | custom-call | flops 20000000000 | tf_op jit(solution)/shard_map/input_gradient/pallas_call | solution.py:355
  26.5 0.0 collective-permute-done.9.refs_7_
  26.5 0.2 collective-permute-done.8.refs_6_
  26.6 0.5 %collective-permute-done.7.refs_5_ = f32[8,128]{1,0:T(8,128)S(1)} collective-permute-done((f32[8,128]{1,0:T(8,128)S(1)}, f32[8,128]{1,0:T(8,128)S(1)}, u32[]{:S(2)}, u32[]{:S(2)}) %collective-permute-start.7) | collective-permute-done | bytes 4128 | tf_op jit(solution)/shard_map/ppermute | solution.py:352
  27.1 0.1 messages.1
  27.2 2.9 %collective-permute-start.10 = (bf16[272,128]{1,0:T(8,128)(2,1)S(1)}, bf16[272,128]{1,0:T(8,128)(2,1)S(1)}, u32[]{:S(2)}, u32[]{:S(2)}) collective-permute-start(bf16[272,128]{1,0:T(8,128)(2,1)S(1)} %get-tuple-element.48), channel_id=1, source_target_pairs={{0,4},{1,5},{2,6},{3,7},{4,0},{5,1},{6,2},{7,3},{8,12},{9,13},{10,... | collective-permute-start | bytes 208904 | tf_op jit(solution)/shard_map/ppermute | solution.py:279
  30.1 0.0 collective-permute-start.11
  30.2 1.4 %collective-permute-start.12 = (bf16[272,128]{1,0:T(8,128)(2,1)S(1)}, bf16[272,128]{1,0:T(8,128)(2,1)S(1)}, u32[]{:S(2)}, u32[]{:S(2)}) collective-permute-start(bf16[272,128]{1,0:T(8,128)(2,1)S(1)} %get-tuple-element.50), channel_id=1, source_target_pairs={{0,2},{1,3},{2,0},{3,1},{4,6},{5,7},{6,4},{7,5},{8,10},{9,11},{10,... | collective-permute-start | bytes 208904 | tf_op jit(solution)/shard_map/ppermute | solution.py:279
  31.5 1.2 %collective-permute-start.13 = (bf16[272,128]{1,0:T(8,128)(2,1)S(1)}, bf16[272,128]{1,0:T(8,128)(2,1)S(1)}, u32[]{:S(2)}, u32[]{:S(2)}) collective-permute-start(bf16[272,128]{1,0:T(8,128)(2,1)S(1)} %get-tuple-element.51), channel_id=1, source_target_pairs={{0,3},{1,2},{2,1},{3,0},{4,7},{5,6},{6,5},{7,4},{8,11},{9,10},{10,... | collective-permute-start | bytes 208904 | tf_op jit(solution)/shard_map/ppermute | solution.py:279
  32.7 2.7 %collective-permute-start.14 = (bf16[272,128]{1,0:T(8,128)(2,1)S(1)}, bf16[272,128]{1,0:T(8,128)(2,1)S(1)}, u32[]{:S(2)}, u32[]{:S(2)}) collective-permute-start(bf16[272,128]{1,0:T(8,128)(2,1)S(1)} %get-tuple-element.52), channel_id=1, source_target_pairs={{0,6},{1,7},{2,4},{3,5},{4,2},{5,3},{6,0},{7,1},{8,14},{9,15},{10,... | collective-permute-start | bytes 208904 | tf_op jit(solution)/shard_map/ppermute | solution.py:279
  35.3 0.0 collective-permute-done.10.refs_0_
  35.3 0.6 %collective-permute-start.15 = (bf16[272,128]{1,0:T(8,128)(2,1)S(1)}, bf16[272,128]{1,0:T(8,128)(2,1)S(1)}, u32[]{:S(2)}, u32[]{:S(2)}) collective-permute-start(bf16[272,128]{1,0:T(8,128)(2,1)S(1)} %get-tuple-element.53), channel_id=1, source_target_pairs={{0,7},{1,6},{2,5},{3,4},{4,3},{5,2},{6,1},{7,0},{8,15},{9,14},{10,... | collective-permute-start | bytes 208904 | tf_op jit(solution)/shard_map/ppermute | solution.py:279
  35.9 1.1 %collective-permute-done.11.refs_1_ = bf16[272,128]{1,0:T(8,128)(2,1)S(1)} collective-permute-done((bf16[272,128]{1,0:T(8,128)(2,1)S(1)}, bf16[272,128]{1,0:T(8,128)(2,1)S(1)}, u32[]{:S(2)}, u32[]{:S(2)}) %collective-permute-start.11) | collective-permute-done | bytes 69664 | tf_op jit(solution)/shard_map/ppermute | solution.py:279
  37.0 1.9 %collective-permute-start.16 = (bf16[272,128]{1,0:T(8,128)(2,1)S(1)}, bf16[272,128]{1,0:T(8,128)(2,1)S(1)}, u32[]{:S(2)}, u32[]{:S(2)}) collective-permute-start(bf16[272,128]{1,0:T(8,128)(2,1)S(1)} %get-tuple-element.55), channel_id=1, source_target_pairs={{0,1},{1,0},{2,3},{3,2},{4,5},{5,4},{6,7},{7,6},{8,9},{9,8},{10,11... | collective-permute-start | bytes 208904 | tf_op jit(solution)/shard_map/ppermute | solution.py:279
  38.9 0.0 collective-permute-done.12.refs_2_
  38.9 0.0 collective-permute-done.13.refs_3_
  38.9 1.7 %collective-permute-done.14.refs_4_ = bf16[272,128]{1,0:T(8,128)(2,1)S(1)} collective-permute-done((bf16[272,128]{1,0:T(8,128)(2,1)S(1)}, bf16[272,128]{1,0:T(8,128)(2,1)S(1)}, u32[]{:S(2)}, u32[]{:S(2)}) %collective-permute-start.14) | collective-permute-done | bytes 69664 | tf_op jit(solution)/shard_map/ppermute | solution.py:279
  40.6 1.7 %collective-permute-done.15.refs_5_ = bf16[272,128]{1,0:T(8,128)(2,1)S(1)} collective-permute-done((bf16[272,128]{1,0:T(8,128)(2,1)S(1)}, bf16[272,128]{1,0:T(8,128)(2,1)S(1)}, u32[]{:S(2)}, u32[]{:S(2)}) %collective-permute-start.15) | collective-permute-done | bytes 69664 | tf_op jit(solution)/shard_map/ppermute | solution.py:279
  42.3 0.0 collective-permute-done.16.refs_7_
  42.3 0.0 copy-done
  42.3 0.0 copy-done.1
  42.3 1.5 %outputs.1 = (f32[128,1024]{1,0:T(8,128)}, f32[128,1024]{1,0:T(8,128)}, f32[1,1024]{1,0:T(1,128)}) custom-call(bf16[272,128]{1,0:T(8,128)(2,1)S(1)} %collective-permute-done.10.refs_0_, bf16[272,128]{1,0:T(8,128)(2,1)S(1)} %collective-permute-done.11.refs_1_, bf16[272,128]{1,0:T(8,128)(2,1)S(1)} %collective-permute-done.12.refs_2_, ...), custom_call_target="tpu_custom_call" | custom-call | flops 1000000000 | tf_op jit(solution)/shard_map/outputs/pallas_call | solution.py:386
  (9 shorter events, 0.1 us)
Async XLA Ops:
  2.1 5.3 %collective-permute-start.2 = (bf16[1280,128]{1,0:T(8,128)(2,1)S(1)}, bf16[1280,128]{1,0:T(8,128)(2,1)S(1)}, u32[]{:S(2)}, u32[]{:S(2)}) collective-permute-start(bf16[1280,128]{1,0:T(8,128)(2,1)S(1)} %get-tuple-element.34), channel_id=1, source_target_pairs={{0,1},{1,0},{2,3},{3,2},{4,5},{5,4},{6,7},{7,6},{8,9},{9,8},{10,11... | collective-permute-start | bytes 983048 | tf_op jit(solution)/shard_map/ppermute | solution.py:279
  2.6 9.1 %collective-permute-start = (bf16[256,128]{1,0:T(8,128)(2,1)S(1)}, bf16[256,128]{1,0:T(8,128)(2,1)S(1)}, u32[]{:S(2)}, u32[]{:S(2)}) collective-permute-start(bf16[256,128]{1,0:T(8,128)(2,1)S(1)} %get-tuple-element.31), channel_id=1, source_target_pairs={{0,6},{1,7},{2,4},{3,5},{4,2},{5,3},{6,0},{7,1},{8,14},{9,15},{10,... | collective-permute-start | bytes 196616 | tf_op jit(solution)/shard_map/ppermute | solution.py:279
  7.2 6.0 %collective-permute-start.1 = (bf16[256,128]{1,0:T(8,128)(2,1)S(1)}, bf16[256,128]{1,0:T(8,128)(2,1)S(1)}, u32[]{:S(2)}, u32[]{:S(2)}) collective-permute-start(bf16[256,128]{1,0:T(8,128)(2,1)S(1)} %get-tuple-element.32), channel_id=1, source_target_pairs={{0,7},{1,6},{2,5},{3,4},{4,3},{5,2},{6,1},{7,0},{8,15},{9,14},{10,... | collective-permute-start | bytes 196616 | tf_op jit(solution)/shard_map/ppermute | solution.py:279
  7.4 11.2 %collective-permute-start.4 = (bf16[768,128]{1,0:T(8,128)(2,1)S(1)}, bf16[768,128]{1,0:T(8,128)(2,1)S(1)}, u32[]{:S(2)}, u32[]{:S(2)}) collective-permute-start(bf16[768,128]{1,0:T(8,128)(2,1)S(1)} %pad_maximum_fusion.1), channel_id=1, source_target_pairs={{0,2},{1,3},{2,0},{3,1},{4,6},{5,7},{6,4},{7,5},{8,10},{9,11},{10,... | collective-permute-start | bytes 589832 | tf_op jit(solution)/shard_map/ppermute | solution.py:279
  7.5 5.8 %copy-start.2 = (bf16[256,256]{1,0:T(8,128)(2,1)S(1)}, bf16[256,256]{1,0:T(8,128)(2,1)}, u32[]{:S(2)}) copy-start(bf16[256,256]{1,0:T(8,128)(2,1)} %constant.6.clone.refs_0_) | copy-start | bytes 393220
  7.5 5.8 %copy-start.3 = (bf16[128,256]{1,0:T(8,128)(2,1)S(1)}, bf16[128,256]{1,0:T(8,128)(2,1)}, u32[]{:S(2)}) copy-start(bf16[128,256]{1,0:T(8,128)(2,1)} %constant.8.clone.refs_2_) | copy-start | bytes 196612
  7.5 5.8 %copy-start.4 = (bf16[128,256]{1,0:T(8,128)(2,1)S(1)}, bf16[128,256]{1,0:T(8,128)(2,1)}, u32[]{:S(2)}) copy-start(bf16[128,256]{1,0:T(8,128)(2,1)} %constant.7.clone.refs_1_) | copy-start | bytes 196612
  7.5 10.6 %collective-permute-start.3 = (bf16[512,128]{1,0:T(8,128)(2,1)S(1)}, bf16[512,128]{1,0:T(8,128)(2,1)S(1)}, u32[]{:S(2)}, u32[]{:S(2)}) collective-permute-start(bf16[512,128]{1,0:T(8,128)(2,1)S(1)} %pad_maximum_fusion.2), channel_id=1, source_target_pairs={{0,4},{1,5},{2,6},{3,7},{4,0},{5,1},{6,2},{7,3},{8,12},{9,13},{10,... | collective-permute-start | bytes 393224 | tf_op jit(solution)/shard_map/ppermute | solution.py:279
  13.3 10.6 %collective-permute-start.5 = (bf16[256,128]{1,0:T(8,128)(2,1)S(1)}, bf16[256,128]{1,0:T(8,128)(2,1)S(1)}, u32[]{:S(2)}, u32[]{:S(2)}) collective-permute-start(bf16[256,128]{1,0:T(8,128)(2,1)S(1)} %get-tuple-element.42), channel_id=1, source_target_pairs={{0,6},{1,7},{2,4},{3,5},{4,2},{5,3},{6,0},{7,1},{8,14},{9,15},{10,... | collective-permute-start | bytes 196616 | tf_op jit(solution)/shard_map/ppermute | solution.py:279
  14.7 10.1 %collective-permute-start.6 = (bf16[256,128]{1,0:T(8,128)(2,1)S(1)}, bf16[256,128]{1,0:T(8,128)(2,1)S(1)}, u32[]{:S(2)}, u32[]{:S(2)}) collective-permute-start(bf16[256,128]{1,0:T(8,128)(2,1)S(1)} %get-tuple-element.43), channel_id=1, source_target_pairs={{0,4},{1,5},{2,6},{3,7},{4,0},{5,1},{6,2},{7,3},{8,12},{9,13},{10,... | collective-permute-start | bytes 196616 | tf_op jit(solution)/shard_map/ppermute | solution.py:279
  20.4 6.1 %collective-permute-start.9 = (f32[8,128]{1,0:T(8,128)S(1)}, f32[8,128]{1,0:T(8,128)S(1)}, u32[]{:S(2)}, u32[]{:S(2)}) collective-permute-start(f32[8,128]{1,0:T(8,128)S(1)} %get-tuple-element.47.refs_4_), channel_id=1, source_target_pairs={{0,24},{8,16},{16,8},{24,0},{1,25},{9,17},{17,9},{25,1},{2,26},{10... | collective-permute-start | bytes 12296 | tf_op jit(solution)/shard_map/ppermute | solution.py:352
  23.0 3.6 %collective-permute-start.8 = (f32[8,128]{1,0:T(8,128)S(1)}, f32[8,128]{1,0:T(8,128)S(1)}, u32[]{:S(2)}, u32[]{:S(2)}) collective-permute-start(f32[8,128]{1,0:T(8,128)S(1)} %get-tuple-element.47.refs_4_), channel_id=1, source_target_pairs={{0,16},{8,24},{16,0},{24,8},{1,17},{9,25},{17,1},{25,9},{2,18},{10... | collective-permute-start | bytes 12296 | tf_op jit(solution)/shard_map/ppermute | solution.py:352
  23.5 3.6 %collective-permute-start.7 = (f32[8,128]{1,0:T(8,128)S(1)}, f32[8,128]{1,0:T(8,128)S(1)}, u32[]{:S(2)}, u32[]{:S(2)}) collective-permute-start(f32[8,128]{1,0:T(8,128)S(1)} %get-tuple-element.47.refs_4_), channel_id=1, source_target_pairs={{0,8},{8,0},{16,24},{24,16},{1,9},{9,1},{17,25},{25,17},{2,10},{10... | collective-permute-start | bytes 12296 | tf_op jit(solution)/shard_map/ppermute | solution.py:352
  27.1 15.1 %copy-start = (bf16[128,1024]{1,0:T(8,128)(2,1)S(1)}, bf16[128,1024]{1,0:T(8,128)(2,1)}, u32[]{:S(2)}) copy-start(bf16[128,1024]{1,0:T(8,128)(2,1)} %refs_8_.1) | copy-start | bytes 786436
  27.2 8.1 %collective-permute-start.10 = (bf16[272,128]{1,0:T(8,128)(2,1)S(1)}, bf16[272,128]{1,0:T(8,128)(2,1)S(1)}, u32[]{:S(2)}, u32[]{:S(2)}) collective-permute-start(bf16[272,128]{1,0:T(8,128)(2,1)S(1)} %get-tuple-element.48), channel_id=1, source_target_pairs={{0,4},{1,5},{2,6},{3,7},{4,0},{5,1},{6,2},{7,3},{8,12},{9,13},{10,... | collective-permute-start | bytes 208904 | tf_op jit(solution)/shard_map/ppermute | solution.py:279
  30.1 6.8 %collective-permute-start.11 = (bf16[272,128]{1,0:T(8,128)(2,1)S(1)}, bf16[272,128]{1,0:T(8,128)(2,1)S(1)}, u32[]{:S(2)}, u32[]{:S(2)}) collective-permute-start(bf16[272,128]{1,0:T(8,128)(2,1)S(1)} %get-tuple-element.49), channel_id=1, source_target_pairs={{0,5},{1,4},{2,7},{3,6},{4,1},{5,0},{6,3},{7,2},{8,13},{9,12},{10,... | collective-permute-start | bytes 208904 | tf_op jit(solution)/shard_map/ppermute | solution.py:279
  30.2 8.7 %collective-permute-start.12 = (bf16[272,128]{1,0:T(8,128)(2,1)S(1)}, bf16[272,128]{1,0:T(8,128)(2,1)S(1)}, u32[]{:S(2)}, u32[]{:S(2)}) collective-permute-start(bf16[272,128]{1,0:T(8,128)(2,1)S(1)} %get-tuple-element.50), channel_id=1, source_target_pairs={{0,2},{1,3},{2,0},{3,1},{4,6},{5,7},{6,4},{7,5},{8,10},{9,11},{10,... | collective-permute-start | bytes 208904 | tf_op jit(solution)/shard_map/ppermute | solution.py:279
  31.5 7.4 %collective-permute-start.13 = (bf16[272,128]{1,0:T(8,128)(2,1)S(1)}, bf16[272,128]{1,0:T(8,128)(2,1)S(1)}, u32[]{:S(2)}, u32[]{:S(2)}) collective-permute-start(bf16[272,128]{1,0:T(8,128)(2,1)S(1)} %get-tuple-element.51), channel_id=1, source_target_pairs={{0,3},{1,2},{2,1},{3,0},{4,7},{5,6},{6,5},{7,4},{8,11},{9,10},{10,... | collective-permute-start | bytes 208904 | tf_op jit(solution)/shard_map/ppermute | solution.py:279
  32.7 9.6 %copy-start.1 = (f32[1024]{0:T(1024)S(1)}, f32[1024]{0:T(1024)}, u32[]{:S(2)}) copy-start(f32[1024]{0:T(1024)} %param.10) | copy-start | bytes 12292
  32.7 7.9 %collective-permute-start.14 = (bf16[272,128]{1,0:T(8,128)(2,1)S(1)}, bf16[272,128]{1,0:T(8,128)(2,1)S(1)}, u32[]{:S(2)}, u32[]{:S(2)}) collective-permute-start(bf16[272,128]{1,0:T(8,128)(2,1)S(1)} %get-tuple-element.52), channel_id=1, source_target_pairs={{0,6},{1,7},{2,4},{3,5},{4,2},{5,3},{6,0},{7,1},{8,14},{9,15},{10,... | collective-permute-start | bytes 208904 | tf_op jit(solution)/shard_map/ppermute | solution.py:279
  35.3 6.9 %collective-permute-start.15 = (bf16[272,128]{1,0:T(8,128)(2,1)S(1)}, bf16[272,128]{1,0:T(8,128)(2,1)S(1)}, u32[]{:S(2)}, u32[]{:S(2)}) collective-permute-start(bf16[272,128]{1,0:T(8,128)(2,1)S(1)} %get-tuple-element.53), channel_id=1, source_target_pairs={{0,7},{1,6},{2,5},{3,4},{4,3},{5,2},{6,1},{7,0},{8,15},{9,14},{10,... | collective-permute-start | bytes 208904 | tf_op jit(solution)/shard_map/ppermute | solution.py:279
  37.0 5.3 %collective-permute-start.16 = (bf16[272,128]{1,0:T(8,128)(2,1)S(1)}, bf16[272,128]{1,0:T(8,128)(2,1)S(1)}, u32[]{:S(2)}, u32[]{:S(2)}) collective-permute-start(bf16[272,128]{1,0:T(8,128)(2,1)S(1)} %get-tuple-element.55), channel_id=1, source_target_pairs={{0,1},{1,0},{2,3},{3,2},{4,5},{5,4},{6,7},{7,6},{8,9},{9,8},{10,11... | collective-permute-start | bytes 208904 | tf_op jit(solution)/shard_map/ppermute | solution.py:279

commit v6 on v5

--- a/solution.py
+++ b/solution.py
@@ -125,7 +125,7 @@
 
 def first_kernel(order, length, places, *refs):
     size = len(order)
-    both, back_high, back_low, codes_out, tails_out, pair_spec, squares, spec, acc = refs[-9:]
+    both, back_high, back_low, blocks_out, skip_out, pair_spec, squares, spec, acc = refs[-9:]
     width = spec.shape[2] // 2
     position = lax.axis_index("ctx")
 
@@ -162,20 +162,20 @@
         return carry
 
     lax.fori_loop(0, length // 8, rows, 0)
-    skip_parts = three_parts(skip)
+    skip_out[...] = skip
     squares[...] = jnp.zeros_like(squares)
 
     def emit(i, block):
         squares[...] += jnp.sum((block * block).reshape(length // 8, 8, width), axis=0)
-        codes_out[i], scale = encode(block)
-        tails_out[i] = tail_tile(0, (scale,) + skip_parts, width)
+        blocks_out[i] = block
 
     send_results(position, order, acc, back_high, back_low, emit)
 
 
 def second_kernel(order, length, places, *refs):
     size = len(order)
-    both, back_high, back_low, pair_spec, codes_out, tails_out, spec, acc = refs[-8:]
+    both, back_high, back_low, pair_spec, blocks, skip = refs[-12:-6]
+    filter_codes, filter_tails, input_codes, input_tails, spec, acc = refs[-6:]
     width = spec.shape[2]
     position = lax.axis_index("ctx")
 
@@ -201,9 +201,14 @@
 
     lax.fori_loop(0, length // 8, rows, 0)
 
+    skip_parts = three_parts(skip[...])
+    for i in range(size):
+        filter_codes[i], scale = encode(blocks[i])
+        filter_tails[i] = tail_tile(0, (scale,) + skip_parts, width)
+
     def emit(i, block):
-        codes_out[i], scale = encode(block)
-        tails_out[i] = tail_tile(4, (scale,), width)
+        input_codes[i], scale = encode(block)
+        input_tails[i] = tail_tile(4, (scale,), width)
 
     send_results(position, order, acc, back_high, back_low, emit)
 
@@ -333,12 +338,12 @@
     second_arrived = [*arrived_taps, *arrived[direct + far :], mine, sibling]
     second_places += [(len(second_arrived) - 2 + i, row + 2 * length) for i in range(2)]
 
-    codes, tails, pair_spec, squares = run(
+    filter_blocks, skip, pair_spec, squares = run(
         functools.partial(first_kernel, order, length, first_places),
         "filter_gradient", vmem_bytes,
         [
-            jax.ShapeDtypeStruct((size, length, width), bf16),
-            jax.ShapeDtypeStruct((size, tail_rows, width), f32),
+            jax.ShapeDtypeStruct((size, length, width), f32),
+            jax.ShapeDtypeStruct((1, width), f32),
             jax.ShapeDtypeStruct((size, 2 * length, width), f32),
             jax.ShapeDtypeStruct((8, width), f32),
         ],
@@ -352,24 +357,25 @@
         squares if k == 0 else lax.ppermute(squares, "chan", [(i, i ^ k) for i in range(columns)])
         for k in range(columns)
     ]
-    input_codes, input_tails = run(
+    codes_and_tails = run(
         functools.partial(second_kernel, order, length, second_places),
         "input_gradient", vmem_bytes,
         [
             jax.ShapeDtypeStruct((size, length, width), bf16),
             jax.ShapeDtypeStruct((size, tail_rows, width), f32),
-        ],
+        ]
+        * 2,
         [
             pltpu.VMEM((size, 2 * length, width), f32),
             pltpu.VMEM((size, 2 * length, width), f32),
         ],
         flops=second_flops,
-    )(*second_arrived, both, back_high, back_low, pair_spec)
+    )(*second_arrived, both, back_high, back_low, pair_spec, filter_blocks, skip)
     messages = run(
         functools.partial(message_kernel, size, length, columns),
         "messages", vmem_bytes,
         [jax.ShapeDtypeStruct((2 * length + tail_rows, width), bf16)] * size,
-    )(codes, tails, input_codes, input_tails, *all_squares)
+    )(*codes_and_tails, *all_squares)
     messages = {k: send(message, k) if k else message for k, message in zip(order, messages)}
     nearer = sorted(chips[:far])
     turns = nearer[: far // 2] + chips[far:-1] + nearer[far // 2 :] + [0]

time: 44 us -> 43.8 us (level)
  transfers between devices with their start and end apart: 17 -> 17, of which waited for: 9 -> 8; matrix products, arithmetic and copies ran while one was open for 0% -> 0% of each run, Pallas kernels for 8% -> 8%
where the time goes in v6:
time: 43.8 us; the launch traced here: 43.6 us
  starting transfers between devices  25.3 us (58%)
  waiting for transfers between devices  11 us (25%)
  Pallas kernels  5.3 us (12%)
  other arithmetic  1.22 us (3%)
  between operations  0.78 us (2%)
    ppermute x14, starting transfers between devices, send(): return lax.ppermute(block, 'ctx', [(i, i ^ k) for i in range(size)])  21.7 us
    ppermute x14, waiting for transfers between devices, send(): return lax.ppermute(block, 'ctx', [(i, i ^ k) for i in range(size)])  10.8 us
    ppermute x3, starting transfers between devices, per_device(): lax.ppermute(squares, 'chan', [(i, i ^ k) for i in range(columns)])  3.55 us
    pallas_call x1, Pallas kernels, per_device(): run(functools.partial(second_kernel, order, length, second_places), 'inpu...  1.83 us
    pallas_call x1, Pallas kernels, per_device(): run(functools.partial(first_kernel, order, length, first_places), 'filter...  1.58 us
    pallas_call x1, Pallas kernels, per_device(): run(functools.partial(last_kernel, turns, length, width, clip_limit), 'ou...  1.54 us
    another operation x1, other arithmetic, per_device(): jnp.stack(three)  1.2 us
  transfers between devices with their start and end apart: 17, of which 8 were waited for; matrix products, arithmetic and copies ran while one was open for 0% of the time, Pallas kernels for 8%

profile of v6, /device:TPU:0, one launch (start us, length us, event | category | flops | bytes accessed | tf_op | source)
XLA Modules:
  0.0 43.6 jit_solution(1406668298568846654)
XLA Ops:
  0.6 1.2 %pad_maximum_fusion.arrays = bf16[3,128,1024]{2,1,0:T(8,128)(2,1)S(1)} fusion(bf16[1,128,1024]{2,1,0:T(8,128)(2,1)} %bitcast.7, bf16[1,128,1024]{2,1,0:T(8,128)(2,1)} %bitcast.8, bf16[1,128,1024]{2,1,0:T(8,128)(2,1)} %bitcast.5), kind=kLoop, calls=%fused_computation | loop fusion | flops 786432 | bytes 1572864 | tf_op jit(solution)/shard_map/stack | solution.py:295
  1.8 0.2 columns.1
  2.1 0.5 %collective-permute-start = (bf16[1280,128]{1,0:T(8,128)(2,1)S(1)}, bf16[1280,128]{1,0:T(8,128)(2,1)S(1)}, u32[]{:S(2)}, u32[]{:S(2)}) collective-permute-start(bf16[1280,128]{1,0:T(8,128)(2,1)S(1)} %get-tuple-element.34), channel_id=1, source_target_pairs={{0,1},{1,0},{2,3},{3,2},{4,5},{5,4},{6,7},{7,6},{8,9},{9,8},{10,11... | collective-permute-start | bytes 983048 | tf_op jit(solution)/shard_map/ppermute | solution.py:284
  2.6 4.7 %collective-permute-start.1 = (bf16[256,128]{1,0:T(8,128)(2,1)S(1)}, bf16[256,128]{1,0:T(8,128)(2,1)S(1)}, u32[]{:S(2)}, u32[]{:S(2)}) collective-permute-start(bf16[256,128]{1,0:T(8,128)(2,1)S(1)} %get-tuple-element.35), channel_id=1, source_target_pairs={{0,6},{1,7},{2,4},{3,5},{4,2},{5,3},{6,0},{7,1},{8,14},{9,15},{10,... | collective-permute-start | bytes 196616 | tf_op jit(solution)/shard_map/ppermute | solution.py:284
  7.2 0.1 collective-permute-start.2
  7.3 0.0 collective-permute-done.sibling.refs_5_.refs_4_
  7.4 0.1 collective-permute-start.5
  7.5 0.0 copy-start.2
  7.5 0.0 copy-start.3
  7.5 0.0 copy-start.4
  7.5 4.1 %collective-permute-start.6 = (bf16[512,128]{1,0:T(8,128)(2,1)S(1)}, bf16[512,128]{1,0:T(8,128)(2,1)S(1)}, u32[]{:S(2)}, u32[]{:S(2)}) collective-permute-start(bf16[512,128]{1,0:T(8,128)(2,1)S(1)} %pad_maximum_fusion.2), channel_id=1, source_target_pairs={{0,4},{1,5},{2,6},{3,7},{4,0},{5,1},{6,2},{7,3},{8,12},{9,13},{10,... | collective-permute-start | bytes 393224 | tf_op jit(solution)/shard_map/ppermute | solution.py:284
  11.6 0.0 collective-permute-done.1.refs_0_
  11.7 1.6 %collective-permute-done.2.refs_1_ = bf16[256,128]{1,0:T(8,128)(2,1)S(1)} collective-permute-done((bf16[256,128]{1,0:T(8,128)(2,1)S(1)}, bf16[256,128]{1,0:T(8,128)(2,1)S(1)}, u32[]{:S(2)}, u32[]{:S(2)}) %collective-permute-start.2) | collective-permute-done | bytes 65568 | tf_op jit(solution)/shard_map/ppermute | solution.py:284
  13.2 0.0 copy-done.2
  13.2 0.0 copy-done.3
  13.3 0.0 copy-done.4
  13.3 1.4 %collective-permute-start.3 = (bf16[256,128]{1,0:T(8,128)(2,1)S(1)}, bf16[256,128]{1,0:T(8,128)(2,1)S(1)}, u32[]{:S(2)}, u32[]{:S(2)}) collective-permute-start(bf16[256,128]{1,0:T(8,128)(2,1)S(1)} %get-tuple-element.39), channel_id=1, source_target_pairs={{0,6},{1,7},{2,4},{3,5},{4,2},{5,3},{6,0},{7,1},{8,14},{9,15},{10,... | collective-permute-start | bytes 196616 | tf_op jit(solution)/shard_map/ppermute | solution.py:284
  14.7 0.3 collective-permute-start.4
  15.0 3.2 %collective-permute-done.6.refs_2_ = bf16[512,128]{1,0:T(8,128)(2,1)S(1)} collective-permute-done((bf16[512,128]{1,0:T(8,128)(2,1)S(1)}, bf16[512,128]{1,0:T(8,128)(2,1)S(1)}, u32[]{:S(2)}, u32[]{:S(2)}) %collective-permute-start.6) | collective-permute-done | bytes 131104 | tf_op jit(solution)/shard_map/ppermute | solution.py:284
  18.2 0.4 collective-permute-done.5.refs_3_.refs_2_
  18.6 1.6 %filter_gradient.1 = (f32[8,128,128]{2,1,0:T(8,128)S(1)}, f32[1,128]{1,0:T(1,128)S(1)}, f32[8,256,128]{2,1,0:T(8,128)S(1)}, f32[8,128]{1,0:T(8,128)S(1)}) custom-call(bf16[256,128]{1,0:T(8,128)(2,1)S(1)} %collective-permute-done.1.refs_0_, bf16[256,128]{1,0:T(8,128)(2,1)S(1)} %collective-permute-done.2.refs_1_, ...), custom_call_target="tpu_custom_call" | custom-call | flops 4000000000 | tf_op jit(solution)/shard_map/filter_gradient/pallas_call | solution.py:341
  20.2 2.6 %collective-permute-start.9 = (f32[8,128]{1,0:T(8,128)S(1)}, f32[8,128]{1,0:T(8,128)S(1)}, u32[]{:S(2)}, u32[]{:S(2)}) collective-permute-start(f32[8,128]{1,0:T(8,128)S(1)} %get-tuple-element.51.refs_4_), channel_id=1, source_target_pairs={{0,24},{8,16},{16,8},{24,0},{1,25},{9,17},{17,9},{25,1},{2,26},{10... | collective-permute-start | bytes 12296 | tf_op jit(solution)/shard_map/ppermute | solution.py:357
  22.8 0.5 %collective-permute-start.8 = (f32[8,128]{1,0:T(8,128)S(1)}, f32[8,128]{1,0:T(8,128)S(1)}, u32[]{:S(2)}, u32[]{:S(2)}) collective-permute-start(f32[8,128]{1,0:T(8,128)S(1)} %get-tuple-element.51.refs_4_), channel_id=1, source_target_pairs={{0,16},{8,24},{16,0},{24,8},{1,17},{9,25},{17,1},{25,9},{2,18},{10... | collective-permute-start | bytes 12296 | tf_op jit(solution)/shard_map/ppermute | solution.py:357
  23.3 0.4 collective-permute-start.7
  23.7 0.0 collective-permute-done.3.refs_0_
  23.7 1.1 %collective-permute-done.4.refs_1_ = bf16[256,128]{1,0:T(8,128)(2,1)S(1)} collective-permute-done((bf16[256,128]{1,0:T(8,128)(2,1)S(1)}, bf16[256,128]{1,0:T(8,128)(2,1)S(1)}, u32[]{:S(2)}, u32[]{:S(2)}) %collective-permute-start.4) | collective-permute-done | bytes 65568 | tf_op jit(solution)/shard_map/ppermute | solution.py:284
  24.8 1.8 %input_gradient.1 = (bf16[8,128,128]{2,1,0:T(8,128)(2,1)S(1)}, f32[8,16,128]{2,1,0:T(8,128)S(1)}, bf16[8,128,128]{2,1,0:T(8,128)(2,1)S(1)}, f32[8,16,128]{2,1,0:T(8,128)S(1)}) custom-call(bf16[256,128]{1,0:T(8,128)(2,1)S(1)} %collective-permute-done.3.refs_0_, bf16[256,128]{1,0:T(8,128)(2,1)S(1)} %collective-permute-done.4.refs_1_, ...), custom_call_target="tpu_custom_call" | custom-call | flops 20000000000 | tf_op jit(solution)/shard_map/input_gradient/pallas_call | solution.py:360
  26.7 0.0 collective-permute-done.9.refs_7_
  26.7 0.0 collective-permute-done.8.refs_6_
  26.7 0.2 collective-permute-done.7.refs_5_
  27.0 0.1 messages.1
  27.1 2.9 %collective-permute-start.10 = (bf16[272,128]{1,0:T(8,128)(2,1)S(1)}, bf16[272,128]{1,0:T(8,128)(2,1)S(1)}, u32[]{:S(2)}, u32[]{:S(2)}) collective-permute-start(bf16[272,128]{1,0:T(8,128)(2,1)S(1)} %get-tuple-element.52), channel_id=1, source_target_pairs={{0,4},{1,5},{2,6},{3,7},{4,0},{5,1},{6,2},{7,3},{8,12},{9,13},{10,... | collective-permute-start | bytes 208904 | tf_op jit(solution)/shard_map/ppermute | solution.py:284
  30.0 0.0 collective-permute-start.11
  30.0 1.4 %collective-permute-start.12 = (bf16[272,128]{1,0:T(8,128)(2,1)S(1)}, bf16[272,128]{1,0:T(8,128)(2,1)S(1)}, u32[]{:S(2)}, u32[]{:S(2)}) collective-permute-start(bf16[272,128]{1,0:T(8,128)(2,1)S(1)} %get-tuple-element.54), channel_id=1, source_target_pairs={{0,2},{1,3},{2,0},{3,1},{4,6},{5,7},{6,4},{7,5},{8,10},{9,11},{10,... | collective-permute-start | bytes 208904 | tf_op jit(solution)/shard_map/ppermute | solution.py:284
  31.3 1.2 %collective-permute-start.13 = (bf16[272,128]{1,0:T(8,128)(2,1)S(1)}, bf16[272,128]{1,0:T(8,128)(2,1)S(1)}, u32[]{:S(2)}, u32[]{:S(2)}) collective-permute-start(bf16[272,128]{1,0:T(8,128)(2,1)S(1)} %get-tuple-element.55), channel_id=1, source_target_pairs={{0,3},{1,2},{2,1},{3,0},{4,7},{5,6},{6,5},{7,4},{8,11},{9,10},{10,... | collective-permute-start | bytes 208904 | tf_op jit(solution)/shard_map/ppermute | solution.py:284
  32.5 2.7 %collective-permute-start.14 = (bf16[272,128]{1,0:T(8,128)(2,1)S(1)}, bf16[272,128]{1,0:T(8,128)(2,1)S(1)}, u32[]{:S(2)}, u32[]{:S(2)}) collective-permute-start(bf16[272,128]{1,0:T(8,128)(2,1)S(1)} %get-tuple-element.56), channel_id=1, source_target_pairs={{0,6},{1,7},{2,4},{3,5},{4,2},{5,3},{6,0},{7,1},{8,14},{9,15},{10,... | collective-permute-start | bytes 208904 | tf_op jit(solution)/shard_map/ppermute | solution.py:284
  35.2 0.0 collective-permute-done.10.refs_0_
  35.2 0.6 %collective-permute-start.15 = (bf16[272,128]{1,0:T(8,128)(2,1)S(1)}, bf16[272,128]{1,0:T(8,128)(2,1)S(1)}, u32[]{:S(2)}, u32[]{:S(2)}) collective-permute-start(bf16[272,128]{1,0:T(8,128)(2,1)S(1)} %get-tuple-element.57), channel_id=1, source_target_pairs={{0,7},{1,6},{2,5},{3,4},{4,3},{5,2},{6,1},{7,0},{8,15},{9,14},{10,... | collective-permute-start | bytes 208904 | tf_op jit(solution)/shard_map/ppermute | solution.py:284
  35.7 1.1 %collective-permute-done.11.refs_1_ = bf16[272,128]{1,0:T(8,128)(2,1)S(1)} collective-permute-done((bf16[272,128]{1,0:T(8,128)(2,1)S(1)}, bf16[272,128]{1,0:T(8,128)(2,1)S(1)}, u32[]{:S(2)}, u32[]{:S(2)}) %collective-permute-start.11) | collective-permute-done | bytes 69664 | tf_op jit(solution)/shard_map/ppermute | solution.py:284
  36.8 1.9 %collective-permute-start.16 = (bf16[272,128]{1,0:T(8,128)(2,1)S(1)}, bf16[272,128]{1,0:T(8,128)(2,1)S(1)}, u32[]{:S(2)}, u32[]{:S(2)}) collective-permute-start(bf16[272,128]{1,0:T(8,128)(2,1)S(1)} %get-tuple-element.59), channel_id=1, source_target_pairs={{0,1},{1,0},{2,3},{3,2},{4,5},{5,4},{6,7},{7,6},{8,9},{9,8},{10,11... | collective-permute-start | bytes 208904 | tf_op jit(solution)/shard_map/ppermute | solution.py:284
  38.7 0.0 collective-permute-done.12.refs_2_
  38.7 0.0 collective-permute-done.13.refs_3_
  38.7 1.7 %collective-permute-done.14.refs_4_ = bf16[272,128]{1,0:T(8,128)(2,1)S(1)} collective-permute-done((bf16[272,128]{1,0:T(8,128)(2,1)S(1)}, bf16[272,128]{1,0:T(8,128)(2,1)S(1)}, u32[]{:S(2)}, u32[]{:S(2)}) %collective-permute-start.14) | collective-permute-done | bytes 69664 | tf_op jit(solution)/shard_map/ppermute | solution.py:284
  40.4 1.7 %collective-permute-done.15.refs_5_ = bf16[272,128]{1,0:T(8,128)(2,1)S(1)} collective-permute-done((bf16[272,128]{1,0:T(8,128)(2,1)S(1)}, bf16[272,128]{1,0:T(8,128)(2,1)S(1)}, u32[]{:S(2)}, u32[]{:S(2)}) %collective-permute-start.15) | collective-permute-done | bytes 69664 | tf_op jit(solution)/shard_map/ppermute | solution.py:284
  42.1 0.0 collective-permute-done.16.refs_7_
  42.1 0.0 copy-done
  42.1 0.0 copy-done.1
  42.1 1.5 %outputs.1 = (f32[128,1024]{1,0:T(8,128)}, f32[128,1024]{1,0:T(8,128)}, f32[1,1024]{1,0:T(1,128)}) custom-call(bf16[272,128]{1,0:T(8,128)(2,1)S(1)} %collective-permute-done.10.refs_0_, bf16[272,128]{1,0:T(8,128)(2,1)S(1)} %collective-permute-done.11.refs_1_, bf16[272,128]{1,0:T(8,128)(2,1)S(1)} %collective-permute-done.12.refs_2_, ...), custom_call_target="tpu_custom_call" | custom-call | flops 1000000000 | tf_op jit(solution)/shard_map/outputs/pallas_call | solution.py:392
  (9 shorter events, 0.1 us)
Async XLA Ops:
  2.1 5.3 %collective-permute-start = (bf16[1280,128]{1,0:T(8,128)(2,1)S(1)}, bf16[1280,128]{1,0:T(8,128)(2,1)S(1)}, u32[]{:S(2)}, u32[]{:S(2)}) collective-permute-start(bf16[1280,128]{1,0:T(8,128)(2,1)S(1)} %get-tuple-element.34), channel_id=1, source_target_pairs={{0,1},{1,0},{2,3},{3,2},{4,5},{5,4},{6,7},{7,6},{8,9},{9,8},{10,11... | collective-permute-start | bytes 983048 | tf_op jit(solution)/shard_map/ppermute | solution.py:284
  2.6 9.1 %collective-permute-start.1 = (bf16[256,128]{1,0:T(8,128)(2,1)S(1)}, bf16[256,128]{1,0:T(8,128)(2,1)S(1)}, u32[]{:S(2)}, u32[]{:S(2)}) collective-permute-start(bf16[256,128]{1,0:T(8,128)(2,1)S(1)} %get-tuple-element.35), channel_id=1, source_target_pairs={{0,6},{1,7},{2,4},{3,5},{4,2},{5,3},{6,0},{7,1},{8,14},{9,15},{10,... | collective-permute-start | bytes 196616 | tf_op jit(solution)/shard_map/ppermute | solution.py:284
  7.2 6.0 %collective-permute-start.2 = (bf16[256,128]{1,0:T(8,128)(2,1)S(1)}, bf16[256,128]{1,0:T(8,128)(2,1)S(1)}, u32[]{:S(2)}, u32[]{:S(2)}) collective-permute-start(bf16[256,128]{1,0:T(8,128)(2,1)S(1)} %get-tuple-element.36), channel_id=1, source_target_pairs={{0,7},{1,6},{2,5},{3,4},{4,3},{5,2},{6,1},{7,0},{8,15},{9,14},{10,... | collective-permute-start | bytes 196616 | tf_op jit(solution)/shard_map/ppermute | solution.py:284
  7.4 11.2 %collective-permute-start.5 = (bf16[768,128]{1,0:T(8,128)(2,1)S(1)}, bf16[768,128]{1,0:T(8,128)(2,1)S(1)}, u32[]{:S(2)}, u32[]{:S(2)}) collective-permute-start(bf16[768,128]{1,0:T(8,128)(2,1)S(1)} %pad_maximum_fusion.1), channel_id=1, source_target_pairs={{0,2},{1,3},{2,0},{3,1},{4,6},{5,7},{6,4},{7,5},{8,10},{9,11},{10,... | collective-permute-start | bytes 589832 | tf_op jit(solution)/shard_map/ppermute | solution.py:284
  7.5 5.8 %copy-start.2 = (bf16[256,256]{1,0:T(8,128)(2,1)S(1)}, bf16[256,256]{1,0:T(8,128)(2,1)}, u32[]{:S(2)}) copy-start(bf16[256,256]{1,0:T(8,128)(2,1)} %constant.6.clone.refs_0_) | copy-start | bytes 393220
  7.5 5.8 %copy-start.3 = (bf16[128,256]{1,0:T(8,128)(2,1)S(1)}, bf16[128,256]{1,0:T(8,128)(2,1)}, u32[]{:S(2)}) copy-start(bf16[128,256]{1,0:T(8,128)(2,1)} %constant.8.clone.refs_2_) | copy-start | bytes 196612
  7.5 5.8 %copy-start.4 = (bf16[128,256]{1,0:T(8,128)(2,1)S(1)}, bf16[128,256]{1,0:T(8,128)(2,1)}, u32[]{:S(2)}) copy-start(bf16[128,256]{1,0:T(8,128)(2,1)} %constant.7.clone.refs_1_) | copy-start | bytes 196612
  7.5 10.6 %collective-permute-start.6 = (bf16[512,128]{1,0:T(8,128)(2,1)S(1)}, bf16[512,128]{1,0:T(8,128)(2,1)S(1)}, u32[]{:S(2)}, u32[]{:S(2)}) collective-permute-start(bf16[512,128]{1,0:T(8,128)(2,1)S(1)} %pad_maximum_fusion.2), channel_id=1, source_target_pairs={{0,4},{1,5},{2,6},{3,7},{4,0},{5,1},{6,2},{7,3},{8,12},{9,13},{10,... | collective-permute-start | bytes 393224 | tf_op jit(solution)/shard_map/ppermute | solution.py:284
  13.3 10.5 %collective-permute-start.3 = (bf16[256,128]{1,0:T(8,128)(2,1)S(1)}, bf16[256,128]{1,0:T(8,128)(2,1)S(1)}, u32[]{:S(2)}, u32[]{:S(2)}) collective-permute-start(bf16[256,128]{1,0:T(8,128)(2,1)S(1)} %get-tuple-element.39), channel_id=1, source_target_pairs={{0,6},{1,7},{2,4},{3,5},{4,2},{5,3},{6,0},{7,1},{8,14},{9,15},{10,... | collective-permute-start | bytes 196616 | tf_op jit(solution)/shard_map/ppermute | solution.py:284
  14.7 10.1 %collective-permute-start.4 = (bf16[256,128]{1,0:T(8,128)(2,1)S(1)}, bf16[256,128]{1,0:T(8,128)(2,1)S(1)}, u32[]{:S(2)}, u32[]{:S(2)}) collective-permute-start(bf16[256,128]{1,0:T(8,128)(2,1)S(1)} %get-tuple-element.40), channel_id=1, source_target_pairs={{0,4},{1,5},{2,6},{3,7},{4,0},{5,1},{6,2},{7,3},{8,12},{9,13},{10,... | collective-permute-start | bytes 196616 | tf_op jit(solution)/shard_map/ppermute | solution.py:284
  20.2 6.5 %collective-permute-start.9 = (f32[8,128]{1,0:T(8,128)S(1)}, f32[8,128]{1,0:T(8,128)S(1)}, u32[]{:S(2)}, u32[]{:S(2)}) collective-permute-start(f32[8,128]{1,0:T(8,128)S(1)} %get-tuple-element.51.refs_4_), channel_id=1, source_target_pairs={{0,24},{8,16},{16,8},{24,0},{1,25},{9,17},{17,9},{25,1},{2,26},{10... | collective-permute-start | bytes 12296 | tf_op jit(solution)/shard_map/ppermute | solution.py:357
  22.8 3.9 %collective-permute-start.8 = (f32[8,128]{1,0:T(8,128)S(1)}, f32[8,128]{1,0:T(8,128)S(1)}, u32[]{:S(2)}, u32[]{:S(2)}) collective-permute-start(f32[8,128]{1,0:T(8,128)S(1)} %get-tuple-element.51.refs_4_), channel_id=1, source_target_pairs={{0,16},{8,24},{16,0},{24,8},{1,17},{9,25},{17,1},{25,9},{2,18},{10... | collective-permute-start | bytes 12296 | tf_op jit(solution)/shard_map/ppermute | solution.py:357
  23.3 3.6 %collective-permute-start.7 = (f32[8,128]{1,0:T(8,128)S(1)}, f32[8,128]{1,0:T(8,128)S(1)}, u32[]{:S(2)}, u32[]{:S(2)}) collective-permute-start(f32[8,128]{1,0:T(8,128)S(1)} %get-tuple-element.51.refs_4_), channel_id=1, source_target_pairs={{0,8},{8,0},{16,24},{24,16},{1,9},{9,1},{17,25},{25,17},{2,10},{10... | collective-permute-start | bytes 12296 | tf_op jit(solution)/shard_map/ppermute | solution.py:357
  26.9 15.1 %copy-start = (bf16[128,1024]{1,0:T(8,128)(2,1)S(1)}, bf16[128,1024]{1,0:T(8,128)(2,1)}, u32[]{:S(2)}) copy-start(bf16[128,1024]{1,0:T(8,128)(2,1)} %refs_8_.1) | copy-start | bytes 786436
  27.1 8.1 %collective-permute-start.10 = (bf16[272,128]{1,0:T(8,128)(2,1)S(1)}, bf16[272,128]{1,0:T(8,128)(2,1)S(1)}, u32[]{:S(2)}, u32[]{:S(2)}) collective-permute-start(bf16[272,128]{1,0:T(8,128)(2,1)S(1)} %get-tuple-element.52), channel_id=1, source_target_pairs={{0,4},{1,5},{2,6},{3,7},{4,0},{5,1},{6,2},{7,3},{8,12},{9,13},{10,... | collective-permute-start | bytes 208904 | tf_op jit(solution)/shard_map/ppermute | solution.py:284
  30.0 6.8 %collective-permute-start.11 = (bf16[272,128]{1,0:T(8,128)(2,1)S(1)}, bf16[272,128]{1,0:T(8,128)(2,1)S(1)}, u32[]{:S(2)}, u32[]{:S(2)}) collective-permute-start(bf16[272,128]{1,0:T(8,128)(2,1)S(1)} %get-tuple-element.53), channel_id=1, source_target_pairs={{0,5},{1,4},{2,7},{3,6},{4,1},{5,0},{6,3},{7,2},{8,13},{9,12},{10,... | collective-permute-start | bytes 208904 | tf_op jit(solution)/shard_map/ppermute | solution.py:284
  30.0 8.7 %collective-permute-start.12 = (bf16[272,128]{1,0:T(8,128)(2,1)S(1)}, bf16[272,128]{1,0:T(8,128)(2,1)S(1)}, u32[]{:S(2)}, u32[]{:S(2)}) collective-permute-start(bf16[272,128]{1,0:T(8,128)(2,1)S(1)} %get-tuple-element.54), channel_id=1, source_target_pairs={{0,2},{1,3},{2,0},{3,1},{4,6},{5,7},{6,4},{7,5},{8,10},{9,11},{10,... | collective-permute-start | bytes 208904 | tf_op jit(solution)/shard_map/ppermute | solution.py:284
  31.3 7.4 %collective-permute-start.13 = (bf16[272,128]{1,0:T(8,128)(2,1)S(1)}, bf16[272,128]{1,0:T(8,128)(2,1)S(1)}, u32[]{:S(2)}, u32[]{:S(2)}) collective-permute-start(bf16[272,128]{1,0:T(8,128)(2,1)S(1)} %get-tuple-element.55), channel_id=1, source_target_pairs={{0,3},{1,2},{2,1},{3,0},{4,7},{5,6},{6,5},{7,4},{8,11},{9,10},{10,... | collective-permute-start | bytes 208904 | tf_op jit(solution)/shard_map/ppermute | solution.py:284
  32.5 9.6 %copy-start.1 = (f32[1024]{0:T(1024)S(1)}, f32[1024]{0:T(1024)}, u32[]{:S(2)}) copy-start(f32[1024]{0:T(1024)} %param.10) | copy-start | bytes 12292
  32.5 7.9 %collective-permute-start.14 = (bf16[272,128]{1,0:T(8,128)(2,1)S(1)}, bf16[272,128]{1,0:T(8,128)(2,1)S(1)}, u32[]{:S(2)}, u32[]{:S(2)}) collective-permute-start(bf16[272,128]{1,0:T(8,128)(2,1)S(1)} %get-tuple-element.56), channel_id=1, source_target_pairs={{0,6},{1,7},{2,4},{3,5},{4,2},{5,3},{6,0},{7,1},{8,14},{9,15},{10,... | collective-permute-start | bytes 208904 | tf_op jit(solution)/shard_map/ppermute | solution.py:284
  35.2 6.9 %collective-permute-start.15 = (bf16[272,128]{1,0:T(8,128)(2,1)S(1)}, bf16[272,128]{1,0:T(8,128)(2,1)S(1)}, u32[]{:S(2)}, u32[]{:S(2)}) collective-permute-start(bf16[272,128]{1,0:T(8,128)(2,1)S(1)} %get-tuple-element.57), channel_id=1, source_target_pairs={{0,7},{1,6},{2,5},{3,4},{4,3},{5,2},{6,1},{7,0},{8,15},{9,14},{10,... | collective-permute-start | bytes 208904 | tf_op jit(solution)/shard_map/ppermute | solution.py:284
  36.8 5.3 %collective-permute-start.16 = (bf16[272,128]{1,0:T(8,128)(2,1)S(1)}, bf16[272,128]{1,0:T(8,128)(2,1)S(1)}, u32[]{:S(2)}, u32[]{:S(2)}) collective-permute-start(bf16[272,128]{1,0:T(8,128)(2,1)S(1)} %get-tuple-element.59), channel_id=1, source_target_pairs={{0,1},{1,0},{2,3},{3,2},{4,5},{5,4},{6,7},{7,6},{8,9},{9,8},{10,11... | collective-permute-start | bytes 208904 | tf_op jit(solution)/shard_map/ppermute | solution.py:284

commit v7 on v6

--- a/solution.py
+++ b/solution.py
@@ -229,25 +229,42 @@
         out[i][2 * length :] = tail.astype(jnp.bfloat16)
 
 
-def last_kernel(order, length, part, clip_limit, *refs):
+def early_kernel(order, length, part, *refs):
+    messages, (grad, gain, input_blocks, filter_blocks) = refs[:-4], refs[-4:]
+    position = lax.axis_index("ctx")
+    for i, (k, message) in enumerate(zip(order, messages)):
+        columns = pl.ds(pl.multiple_of((position ^ k) * part, part), part)
+        tail = message[2 * length :].astype(jnp.float32)
+        filter_blocks[i] = decode(message[:length], tail[0:1])
+        input_blocks[i] = (
+            decode(message[length : 2 * length], tail[4:5])
+            + gain[:, columns] * grad[:, columns].astype(jnp.float32)
+        )
+
+
+def last_kernel(order, early, length, part, clip_limit, *refs):
     size = len(order)
     messages = refs[:size]
-    grad, gain, input_grad, filter_grad, skip_grad = refs[size:]
+    input_blocks, filter_blocks, grad, gain, input_grad, filter_grad, skip_grad = refs[size:]
     position = lax.axis_index("ctx")
     total = jnp.zeros((1, part), jnp.float32)
     for message in messages:
         tail = message[2 * length :].astype(jnp.float32)
         total += tail[5:6] + tail[6:7] + tail[7:8]
     factor = jnp.minimum(1.0, clip_limit / jnp.sqrt(total + epsilon))
-    for k, message in zip(order, messages):
+    for i, (k, message) in enumerate(zip(order, messages)):
         columns = pl.ds(pl.multiple_of((position ^ k) * part, part), part)
         tail = message[2 * length :].astype(jnp.float32)
-        filter_grad[:, columns] = decode(message[:length], tail[0:1]) * factor
         skip_grad[:, columns] = tail[1:2] + tail[2:3] + tail[3:4]
-        input_grad[:, columns] = (
-            decode(message[length : 2 * length], tail[4:5])
-            + gain[:, columns] * grad[:, columns].astype(jnp.float32)
-        )
+        if i < early:
+            filter_grad[:, columns] = filter_blocks[i] * factor
+            input_grad[:, columns] = input_blocks[i]
+        else:
+            filter_grad[:, columns] = decode(message[:length], tail[0:1]) * factor
+            input_grad[:, columns] = (
+                decode(message[length : 2 * length], tail[4:5])
+                + gain[:, columns] * grad[:, columns].astype(jnp.float32)
+            )
 
 
 def run(kernel, name, vmem_bytes, out_shape, scratch=(), flops=10**9, **specs):
@@ -389,15 +406,23 @@
             a.reshape(a.shape[0], size, part), ((0, 0), (0, 0), (0, width - part))
         ).reshape(a.shape[0], whole)
         grad_rows, gain = spread(grad_rows), spread(gain)
+    turns = turns[: size // 2] + [0] + [k for k in turns[size // 2 :] if k]
+    early = size // 2 + 1
+    decoded = run(
+        functools.partial(early_kernel, turns[:early], length, width),
+        "early", vmem_bytes,
+        [jax.ShapeDtypeStruct((early, length, width), f32)] * 2,
+        flops=first_flops,
+    )(*[messages[k] for k in turns[:early]], grad_rows, gain)
     input_grad, filter_grad, skip_grad = run(
-        functools.partial(last_kernel, turns, length, width, clip_limit),
+        functools.partial(last_kernel, turns, early, length, width, clip_limit),
         "outputs", vmem_bytes,
         [
             jax.ShapeDtypeStruct((length, whole), f32),
             jax.ShapeDtypeStruct((length, whole), f32),
             jax.ShapeDtypeStruct((1, whole), f32),
         ],
-    )(*[messages[k] for k in turns], grad_rows, gain)
+    )(*[messages[k] for k in turns], *decoded, grad_rows, gain)
     if width != part:
         gather = lambda a: a.reshape(a.shape[0], size, width)[:, :, :part].reshape(
             a.shape[0], chan_width

time: 43.8 us -> 43.4 us (level)
    pallas_call x1 -> x2, Pallas kernels: 1.54 us -> 1.55 us  [the longest x1 1.22 us: per_device(): run(functools.partial(last_kernel, turns, early, length, width, clip_limi...]
  transfers between devices with their start and end apart: 17 -> 17, of which waited for: 8 -> 8; matrix products, arithmetic and copies ran while one was open for 0% -> 0% of each run, Pallas kernels for 8% -> 9%
where the time goes in v7:
time: 43.4 us; the launch traced here: 43.3 us
  starting transfers between devices  25.3 us (58%)
  waiting for transfers between devices  10.7 us (25%)
  Pallas kernels  5.31 us (12%)
  other arithmetic  1.22 us (3%)
  between operations  0.79 us (2%)
    ppermute x14, starting transfers between devices, send(): return lax.ppermute(block, 'ctx', [(i, i ^ k) for i in range(size)])  21.7 us
    ppermute x14, waiting for transfers between devices, send(): return lax.ppermute(block, 'ctx', [(i, i ^ k) for i in range(size)])  10.4 us
    ppermute x3, starting transfers between devices, per_device(): lax.ppermute(squares, 'chan', [(i, i ^ k) for i in range(columns)])  3.55 us
    pallas_call x1, Pallas kernels, per_device(): run(functools.partial(second_kernel, order, length, second_places), 'inpu...  1.83 us
    pallas_call x1, Pallas kernels, per_device(): run(functools.partial(first_kernel, order, length, first_places), 'filter...  1.58 us
    pallas_call x1, Pallas kernels, per_device(): run(functools.partial(last_kernel, turns, early, length, width, clip_limi...  1.22 us
    another operation x1, other arithmetic, per_device(): jnp.stack(three)  1.2 us
  transfers between devices with their start and end apart: 17, of which 8 were waited for; matrix products, arithmetic and copies ran while one was open for 0% of the time, Pallas kernels for 9%

profile of v7, /device:TPU:0, one launch (start us, length us, event | category | flops | bytes accessed | tf_op | source)
XLA Modules:
  0.0 43.3 jit_solution(253746443551143227)
XLA Ops:
  0.6 1.2 %pad_maximum_fusion.arrays = bf16[3,128,1024]{2,1,0:T(8,128)(2,1)S(1)} fusion(bf16[1,128,1024]{2,1,0:T(8,128)(2,1)} %bitcast.8, bf16[1,128,1024]{2,1,0:T(8,128)(2,1)} %bitcast.9, bf16[1,128,1024]{2,1,0:T(8,128)(2,1)} %bitcast.5), kind=kLoop, calls=%fused_computation | loop fusion | flops 786432 | bytes 1572864 | tf_op jit(solution)/shard_map/stack | solution.py:312
  1.8 0.2 columns.1
  2.1 0.5 %collective-permute-start = (bf16[1280,128]{1,0:T(8,128)(2,1)S(1)}, bf16[1280,128]{1,0:T(8,128)(2,1)S(1)}, u32[]{:S(2)}, u32[]{:S(2)}) collective-permute-start(bf16[1280,128]{1,0:T(8,128)(2,1)S(1)} %get-tuple-element.36), channel_id=1, source_target_pairs={{0,1},{1,0},{2,3},{3,2},{4,5},{5,4},{6,7},{7,6},{8,9},{9,8},{10,11... | collective-permute-start | bytes 983048 | tf_op jit(solution)/shard_map/ppermute | solution.py:301
  2.6 4.7 %collective-permute-start.1 = (bf16[256,128]{1,0:T(8,128)(2,1)S(1)}, bf16[256,128]{1,0:T(8,128)(2,1)S(1)}, u32[]{:S(2)}, u32[]{:S(2)}) collective-permute-start(bf16[256,128]{1,0:T(8,128)(2,1)S(1)} %get-tuple-element.37), channel_id=1, source_target_pairs={{0,6},{1,7},{2,4},{3,5},{4,2},{5,3},{6,0},{7,1},{8,14},{9,15},{10,... | collective-permute-start | bytes 196616 | tf_op jit(solution)/shard_map/ppermute | solution.py:301
  7.2 0.1 collective-permute-start.2
  7.3 0.0 collective-permute-done.sibling.refs_5_.refs_4_
  7.4 0.1 collective-permute-start.5
  7.5 0.0 copy-start.2
  7.5 0.0 copy-start.3
  7.5 0.0 copy-start.4
  7.5 4.1 %collective-permute-start.6 = (bf16[512,128]{1,0:T(8,128)(2,1)S(1)}, bf16[512,128]{1,0:T(8,128)(2,1)S(1)}, u32[]{:S(2)}, u32[]{:S(2)}) collective-permute-start(bf16[512,128]{1,0:T(8,128)(2,1)S(1)} %pad_maximum_fusion.2), channel_id=1, source_target_pairs={{0,4},{1,5},{2,6},{3,7},{4,0},{5,1},{6,2},{7,3},{8,12},{9,13},{10,... | collective-permute-start | bytes 393224 | tf_op jit(solution)/shard_map/ppermute | solution.py:301
  11.6 0.0 collective-permute-done.1.refs_0_
  11.7 1.6 %collective-permute-done.2.refs_1_ = bf16[256,128]{1,0:T(8,128)(2,1)S(1)} collective-permute-done((bf16[256,128]{1,0:T(8,128)(2,1)S(1)}, bf16[256,128]{1,0:T(8,128)(2,1)S(1)}, u32[]{:S(2)}, u32[]{:S(2)}) %collective-permute-start.2) | collective-permute-done | bytes 65568 | tf_op jit(solution)/shard_map/ppermute | solution.py:301
  13.2 0.0 copy-done.2
  13.2 0.0 copy-done.3
  13.3 0.0 copy-done.4
  13.3 1.4 %collective-permute-start.3 = (bf16[256,128]{1,0:T(8,128)(2,1)S(1)}, bf16[256,128]{1,0:T(8,128)(2,1)S(1)}, u32[]{:S(2)}, u32[]{:S(2)}) collective-permute-start(bf16[256,128]{1,0:T(8,128)(2,1)S(1)} %get-tuple-element.41), channel_id=1, source_target_pairs={{0,6},{1,7},{2,4},{3,5},{4,2},{5,3},{6,0},{7,1},{8,14},{9,15},{10,... | collective-permute-start | bytes 196616 | tf_op jit(solution)/shard_map/ppermute | solution.py:301
  14.7 0.3 collective-permute-start.4
  15.0 3.2 %collective-permute-done.6.refs_2_ = bf16[512,128]{1,0:T(8,128)(2,1)S(1)} collective-permute-done((bf16[512,128]{1,0:T(8,128)(2,1)S(1)}, bf16[512,128]{1,0:T(8,128)(2,1)S(1)}, u32[]{:S(2)}, u32[]{:S(2)}) %collective-permute-start.6) | collective-permute-done | bytes 131104 | tf_op jit(solution)/shard_map/ppermute | solution.py:301
  18.2 0.4 collective-permute-done.5.refs_3_.refs_2_
  18.6 1.6 %filter_gradient.1 = (f32[8,128,128]{2,1,0:T(8,128)S(1)}, f32[1,128]{1,0:T(1,128)S(1)}, f32[8,256,128]{2,1,0:T(8,128)S(1)}, f32[8,128]{1,0:T(8,128)S(1)}) custom-call(bf16[256,128]{1,0:T(8,128)(2,1)S(1)} %collective-permute-done.1.refs_0_, bf16[256,128]{1,0:T(8,128)(2,1)S(1)} %collective-permute-done.2.refs_1_, ...), custom_call_target="tpu_custom_call" | custom-call | flops 4000000000 | tf_op jit(solution)/shard_map/filter_gradient/pallas_call | solution.py:358
  20.2 2.6 %collective-permute-start.9 = (f32[8,128]{1,0:T(8,128)S(1)}, f32[8,128]{1,0:T(8,128)S(1)}, u32[]{:S(2)}, u32[]{:S(2)}) collective-permute-start(f32[8,128]{1,0:T(8,128)S(1)} %get-tuple-element.53.refs_4_), channel_id=1, source_target_pairs={{0,24},{8,16},{16,8},{24,0},{1,25},{9,17},{17,9},{25,1},{2,26},{10... | collective-permute-start | bytes 12296 | tf_op jit(solution)/shard_map/ppermute | solution.py:374
  22.8 0.5 %collective-permute-start.8 = (f32[8,128]{1,0:T(8,128)S(1)}, f32[8,128]{1,0:T(8,128)S(1)}, u32[]{:S(2)}, u32[]{:S(2)}) collective-permute-start(f32[8,128]{1,0:T(8,128)S(1)} %get-tuple-element.53.refs_4_), channel_id=1, source_target_pairs={{0,16},{8,24},{16,0},{24,8},{1,17},{9,25},{17,1},{25,9},{2,18},{10... | collective-permute-start | bytes 12296 | tf_op jit(solution)/shard_map/ppermute | solution.py:374
  23.3 0.4 collective-permute-start.7
  23.7 0.0 collective-permute-done.3.refs_0_
  23.7 1.1 %collective-permute-done.4.refs_1_ = bf16[256,128]{1,0:T(8,128)(2,1)S(1)} collective-permute-done((bf16[256,128]{1,0:T(8,128)(2,1)S(1)}, bf16[256,128]{1,0:T(8,128)(2,1)S(1)}, u32[]{:S(2)}, u32[]{:S(2)}) %collective-permute-start.4) | collective-permute-done | bytes 65568 | tf_op jit(solution)/shard_map/ppermute | solution.py:301
  24.8 1.8 %input_gradient.1 = (bf16[8,128,128]{2,1,0:T(8,128)(2,1)S(1)}, f32[8,16,128]{2,1,0:T(8,128)S(1)}, bf16[8,128,128]{2,1,0:T(8,128)(2,1)S(1)}, f32[8,16,128]{2,1,0:T(8,128)S(1)}) custom-call(bf16[256,128]{1,0:T(8,128)(2,1)S(1)} %collective-permute-done.3.refs_0_, bf16[256,128]{1,0:T(8,128)(2,1)S(1)} %collective-permute-done.4.refs_1_, ...), custom_call_target="tpu_custom_call" | custom-call | flops 20000000000 | tf_op jit(solution)/shard_map/input_gradient/pallas_call | solution.py:377
  26.7 0.0 collective-permute-done.9.refs_7_
  26.7 0.0 collective-permute-done.8.refs_6_
  26.7 0.2 collective-permute-done.7.refs_5_
  27.0 0.1 messages.1
  27.1 2.9 %collective-permute-start.10 = (bf16[272,128]{1,0:T(8,128)(2,1)S(1)}, bf16[272,128]{1,0:T(8,128)(2,1)S(1)}, u32[]{:S(2)}, u32[]{:S(2)}) collective-permute-start(bf16[272,128]{1,0:T(8,128)(2,1)S(1)} %get-tuple-element.54), channel_id=1, source_target_pairs={{0,4},{1,5},{2,6},{3,7},{4,0},{5,1},{6,2},{7,3},{8,12},{9,13},{10,... | collective-permute-start | bytes 208904 | tf_op jit(solution)/shard_map/ppermute | solution.py:301
  30.0 0.0 collective-permute-start.11
  30.0 1.4 %collective-permute-start.12 = (bf16[272,128]{1,0:T(8,128)(2,1)S(1)}, bf16[272,128]{1,0:T(8,128)(2,1)S(1)}, u32[]{:S(2)}, u32[]{:S(2)}) collective-permute-start(bf16[272,128]{1,0:T(8,128)(2,1)S(1)} %get-tuple-element.56), channel_id=1, source_target_pairs={{0,2},{1,3},{2,0},{3,1},{4,6},{5,7},{6,4},{7,5},{8,10},{9,11},{10,... | collective-permute-start | bytes 208904 | tf_op jit(solution)/shard_map/ppermute | solution.py:301
  31.3 1.2 %collective-permute-start.13 = (bf16[272,128]{1,0:T(8,128)(2,1)S(1)}, bf16[272,128]{1,0:T(8,128)(2,1)S(1)}, u32[]{:S(2)}, u32[]{:S(2)}) collective-permute-start(bf16[272,128]{1,0:T(8,128)(2,1)S(1)} %get-tuple-element.57), channel_id=1, source_target_pairs={{0,3},{1,2},{2,1},{3,0},{4,7},{5,6},{6,5},{7,4},{8,11},{9,10},{10,... | collective-permute-start | bytes 208904 | tf_op jit(solution)/shard_map/ppermute | solution.py:301
  32.5 2.7 %collective-permute-start.14 = (bf16[272,128]{1,0:T(8,128)(2,1)S(1)}, bf16[272,128]{1,0:T(8,128)(2,1)S(1)}, u32[]{:S(2)}, u32[]{:S(2)}) collective-permute-start(bf16[272,128]{1,0:T(8,128)(2,1)S(1)} %get-tuple-element.59), channel_id=1, source_target_pairs={{0,6},{1,7},{2,4},{3,5},{4,2},{5,3},{6,0},{7,1},{8,14},{9,15},{10,... | collective-permute-start | bytes 208904 | tf_op jit(solution)/shard_map/ppermute | solution.py:301
  35.2 0.0 collective-permute-done.10.refs_0_
  35.2 0.6 %collective-permute-start.15 = (bf16[272,128]{1,0:T(8,128)(2,1)S(1)}, bf16[272,128]{1,0:T(8,128)(2,1)S(1)}, u32[]{:S(2)}, u32[]{:S(2)}) collective-permute-start(bf16[272,128]{1,0:T(8,128)(2,1)S(1)} %get-tuple-element.60), channel_id=1, source_target_pairs={{0,7},{1,6},{2,5},{3,4},{4,3},{5,2},{6,1},{7,0},{8,15},{9,14},{10,... | collective-permute-start | bytes 208904 | tf_op jit(solution)/shard_map/ppermute | solution.py:301
  35.7 1.1 %collective-permute-done.11.refs_1_ = bf16[272,128]{1,0:T(8,128)(2,1)S(1)} collective-permute-done((bf16[272,128]{1,0:T(8,128)(2,1)S(1)}, bf16[272,128]{1,0:T(8,128)(2,1)S(1)}, u32[]{:S(2)}, u32[]{:S(2)}) %collective-permute-start.11) | collective-permute-done | bytes 69664 | tf_op jit(solution)/shard_map/ppermute | solution.py:301
  36.8 1.9 %collective-permute-start.16 = (bf16[272,128]{1,0:T(8,128)(2,1)S(1)}, bf16[272,128]{1,0:T(8,128)(2,1)S(1)}, u32[]{:S(2)}, u32[]{:S(2)}) collective-permute-start(bf16[272,128]{1,0:T(8,128)(2,1)S(1)} %get-tuple-element.61), channel_id=1, source_target_pairs={{0,1},{1,0},{2,3},{3,2},{4,5},{5,4},{6,7},{7,6},{8,9},{9,8},{10,11... | collective-permute-start | bytes 208904 | tf_op jit(solution)/shard_map/ppermute | solution.py:301
  38.7 0.0 collective-permute-done.12.refs_2_
  38.7 0.0 collective-permute-done.13.refs_3_
  38.7 0.0 copy-done.1
  38.7 0.3 early.1
  39.1 1.3 %collective-permute-done.14.refs_5_ = bf16[272,128]{1,0:T(8,128)(2,1)S(1)} collective-permute-done((bf16[272,128]{1,0:T(8,128)(2,1)S(1)}, bf16[272,128]{1,0:T(8,128)(2,1)S(1)}, u32[]{:S(2)}, u32[]{:S(2)}) %collective-permute-start.14) | collective-permute-done | bytes 69664 | tf_op jit(solution)/shard_map/ppermute | solution.py:301
  40.4 1.7 %collective-permute-done.15.refs_6_ = bf16[272,128]{1,0:T(8,128)(2,1)S(1)} collective-permute-done((bf16[272,128]{1,0:T(8,128)(2,1)S(1)}, bf16[272,128]{1,0:T(8,128)(2,1)S(1)}, u32[]{:S(2)}, u32[]{:S(2)}) %collective-permute-start.15) | collective-permute-done | bytes 69664 | tf_op jit(solution)/shard_map/ppermute | solution.py:301
  42.1 0.0 collective-permute-done.16.refs_7_
  42.1 1.2 %outputs.1 = (f32[128,1024]{1,0:T(8,128)}, f32[128,1024]{1,0:T(8,128)}, f32[1,1024]{1,0:T(1,128)}) custom-call(bf16[272,128]{1,0:T(8,128)(2,1)S(1)} %collective-permute-done.10.refs_0_, bf16[272,128]{1,0:T(8,128)(2,1)S(1)} %collective-permute-done.11.refs_1_, bf16[272,128]{1,0:T(8,128)(2,1)S(1)} %collective-permute-done.12.refs_2_, ...), custom_call_target="tpu_custom_call" | custom-call | flops 1000000000 | tf_op jit(solution)/shard_map/outputs/pallas_call | solution.py:417
  (10 shorter events, 0.1 us)
Async XLA Ops:
  2.1 5.3 %collective-permute-start = (bf16[1280,128]{1,0:T(8,128)(2,1)S(1)}, bf16[1280,128]{1,0:T(8,128)(2,1)S(1)}, u32[]{:S(2)}, u32[]{:S(2)}) collective-permute-start(bf16[1280,128]{1,0:T(8,128)(2,1)S(1)} %get-tuple-element.36), channel_id=1, source_target_pairs={{0,1},{1,0},{2,3},{3,2},{4,5},{5,4},{6,7},{7,6},{8,9},{9,8},{10,11... | collective-permute-start | bytes 983048 | tf_op jit(solution)/shard_map/ppermute | solution.py:301
  2.6 9.1 %collective-permute-start.1 = (bf16[256,128]{1,0:T(8,128)(2,1)S(1)}, bf16[256,128]{1,0:T(8,128)(2,1)S(1)}, u32[]{:S(2)}, u32[]{:S(2)}) collective-permute-start(bf16[256,128]{1,0:T(8,128)(2,1)S(1)} %get-tuple-element.37), channel_id=1, source_target_pairs={{0,6},{1,7},{2,4},{3,5},{4,2},{5,3},{6,0},{7,1},{8,14},{9,15},{10,... | collective-permute-start | bytes 196616 | tf_op jit(solution)/shard_map/ppermute | solution.py:301
  7.2 6.0 %collective-permute-start.2 = (bf16[256,128]{1,0:T(8,128)(2,1)S(1)}, bf16[256,128]{1,0:T(8,128)(2,1)S(1)}, u32[]{:S(2)}, u32[]{:S(2)}) collective-permute-start(bf16[256,128]{1,0:T(8,128)(2,1)S(1)} %get-tuple-element.38), channel_id=1, source_target_pairs={{0,7},{1,6},{2,5},{3,4},{4,3},{5,2},{6,1},{7,0},{8,15},{9,14},{10,... | collective-permute-start | bytes 196616 | tf_op jit(solution)/shard_map/ppermute | solution.py:301
  7.4 11.2 %collective-permute-start.5 = (bf16[768,128]{1,0:T(8,128)(2,1)S(1)}, bf16[768,128]{1,0:T(8,128)(2,1)S(1)}, u32[]{:S(2)}, u32[]{:S(2)}) collective-permute-start(bf16[768,128]{1,0:T(8,128)(2,1)S(1)} %pad_maximum_fusion.1), channel_id=1, source_target_pairs={{0,2},{1,3},{2,0},{3,1},{4,6},{5,7},{6,4},{7,5},{8,10},{9,11},{10,... | collective-permute-start | bytes 589832 | tf_op jit(solution)/shard_map/ppermute | solution.py:301
  7.5 5.8 %copy-start.2 = (bf16[256,256]{1,0:T(8,128)(2,1)S(1)}, bf16[256,256]{1,0:T(8,128)(2,1)}, u32[]{:S(2)}) copy-start(bf16[256,256]{1,0:T(8,128)(2,1)} %constant.6.clone.refs_0_) | copy-start | bytes 393220
  7.5 5.8 %copy-start.3 = (bf16[128,256]{1,0:T(8,128)(2,1)S(1)}, bf16[128,256]{1,0:T(8,128)(2,1)}, u32[]{:S(2)}) copy-start(bf16[128,256]{1,0:T(8,128)(2,1)} %constant.8.clone.refs_2_) | copy-start | bytes 196612
  7.5 5.8 %copy-start.4 = (bf16[128,256]{1,0:T(8,128)(2,1)S(1)}, bf16[128,256]{1,0:T(8,128)(2,1)}, u32[]{:S(2)}) copy-start(bf16[128,256]{1,0:T(8,128)(2,1)} %constant.7.clone.refs_1_) | copy-start | bytes 196612
  7.5 10.6 %collective-permute-start.6 = (bf16[512,128]{1,0:T(8,128)(2,1)S(1)}, bf16[512,128]{1,0:T(8,128)(2,1)S(1)}, u32[]{:S(2)}, u32[]{:S(2)}) collective-permute-start(bf16[512,128]{1,0:T(8,128)(2,1)S(1)} %pad_maximum_fusion.2), channel_id=1, source_target_pairs={{0,4},{1,5},{2,6},{3,7},{4,0},{5,1},{6,2},{7,3},{8,12},{9,13},{10,... | collective-permute-start | bytes 393224 | tf_op jit(solution)/shard_map/ppermute | solution.py:301
  13.3 10.5 %collective-permute-start.3 = (bf16[256,128]{1,0:T(8,128)(2,1)S(1)}, bf16[256,128]{1,0:T(8,128)(2,1)S(1)}, u32[]{:S(2)}, u32[]{:S(2)}) collective-permute-start(bf16[256,128]{1,0:T(8,128)(2,1)S(1)} %get-tuple-element.41), channel_id=1, source_target_pairs={{0,6},{1,7},{2,4},{3,5},{4,2},{5,3},{6,0},{7,1},{8,14},{9,15},{10,... | collective-permute-start | bytes 196616 | tf_op jit(solution)/shard_map/ppermute | solution.py:301
  14.7 10.1 %collective-permute-start.4 = (bf16[256,128]{1,0:T(8,128)(2,1)S(1)}, bf16[256,128]{1,0:T(8,128)(2,1)S(1)}, u32[]{:S(2)}, u32[]{:S(2)}) collective-permute-start(bf16[256,128]{1,0:T(8,128)(2,1)S(1)} %get-tuple-element.42), channel_id=1, source_target_pairs={{0,4},{1,5},{2,6},{3,7},{4,0},{5,1},{6,2},{7,3},{8,12},{9,13},{10,... | collective-permute-start | bytes 196616 | tf_op jit(solution)/shard_map/ppermute | solution.py:301
  20.2 6.5 %collective-permute-start.9 = (f32[8,128]{1,0:T(8,128)S(1)}, f32[8,128]{1,0:T(8,128)S(1)}, u32[]{:S(2)}, u32[]{:S(2)}) collective-permute-start(f32[8,128]{1,0:T(8,128)S(1)} %get-tuple-element.53.refs_4_), channel_id=1, source_target_pairs={{0,24},{8,16},{16,8},{24,0},{1,25},{9,17},{17,9},{25,1},{2,26},{10... | collective-permute-start | bytes 12296 | tf_op jit(solution)/shard_map/ppermute | solution.py:374
  22.8 3.9 %collective-permute-start.8 = (f32[8,128]{1,0:T(8,128)S(1)}, f32[8,128]{1,0:T(8,128)S(1)}, u32[]{:S(2)}, u32[]{:S(2)}) collective-permute-start(f32[8,128]{1,0:T(8,128)S(1)} %get-tuple-element.53.refs_4_), channel_id=1, source_target_pairs={{0,16},{8,24},{16,0},{24,8},{1,17},{9,25},{17,1},{25,9},{2,18},{10... | collective-permute-start | bytes 12296 | tf_op jit(solution)/shard_map/ppermute | solution.py:374
  23.3 3.6 %collective-permute-start.7 = (f32[8,128]{1,0:T(8,128)S(1)}, f32[8,128]{1,0:T(8,128)S(1)}, u32[]{:S(2)}, u32[]{:S(2)}) collective-permute-start(f32[8,128]{1,0:T(8,128)S(1)} %get-tuple-element.53.refs_4_), channel_id=1, source_target_pairs={{0,8},{8,0},{16,24},{24,16},{1,9},{9,1},{17,25},{25,17},{2,10},{10... | collective-permute-start | bytes 12296 | tf_op jit(solution)/shard_map/ppermute | solution.py:374
  26.9 11.8 %copy-start = (bf16[128,1024]{1,0:T(8,128)(2,1)S(1)}, bf16[128,1024]{1,0:T(8,128)(2,1)}, u32[]{:S(2)}) copy-start(bf16[128,1024]{1,0:T(8,128)(2,1)} %refs_10_.1) | copy-start | bytes 786436
  27.1 8.1 %collective-permute-start.10 = (bf16[272,128]{1,0:T(8,128)(2,1)S(1)}, bf16[272,128]{1,0:T(8,128)(2,1)S(1)}, u32[]{:S(2)}, u32[]{:S(2)}) collective-permute-start(bf16[272,128]{1,0:T(8,128)(2,1)S(1)} %get-tuple-element.54), channel_id=1, source_target_pairs={{0,4},{1,5},{2,6},{3,7},{4,0},{5,1},{6,2},{7,3},{8,12},{9,13},{10,... | collective-permute-start | bytes 208904 | tf_op jit(solution)/shard_map/ppermute | solution.py:301
  30.0 6.8 %collective-permute-start.11 = (bf16[272,128]{1,0:T(8,128)(2,1)S(1)}, bf16[272,128]{1,0:T(8,128)(2,1)S(1)}, u32[]{:S(2)}, u32[]{:S(2)}) collective-permute-start(bf16[272,128]{1,0:T(8,128)(2,1)S(1)} %get-tuple-element.55), channel_id=1, source_target_pairs={{0,5},{1,4},{2,7},{3,6},{4,1},{5,0},{6,3},{7,2},{8,13},{9,12},{10,... | collective-permute-start | bytes 208904 | tf_op jit(solution)/shard_map/ppermute | solution.py:301
  30.0 8.7 %collective-permute-start.12 = (bf16[272,128]{1,0:T(8,128)(2,1)S(1)}, bf16[272,128]{1,0:T(8,128)(2,1)S(1)}, u32[]{:S(2)}, u32[]{:S(2)}) collective-permute-start(bf16[272,128]{1,0:T(8,128)(2,1)S(1)} %get-tuple-element.56), channel_id=1, source_target_pairs={{0,2},{1,3},{2,0},{3,1},{4,6},{5,7},{6,4},{7,5},{8,10},{9,11},{10,... | collective-permute-start | bytes 208904 | tf_op jit(solution)/shard_map/ppermute | solution.py:301
  31.3 7.4 %collective-permute-start.13 = (bf16[272,128]{1,0:T(8,128)(2,1)S(1)}, bf16[272,128]{1,0:T(8,128)(2,1)S(1)}, u32[]{:S(2)}, u32[]{:S(2)}) collective-permute-start(bf16[272,128]{1,0:T(8,128)(2,1)S(1)} %get-tuple-element.57), channel_id=1, source_target_pairs={{0,3},{1,2},{2,1},{3,0},{4,7},{5,6},{6,5},{7,4},{8,11},{9,10},{10,... | collective-permute-start | bytes 208904 | tf_op jit(solution)/shard_map/ppermute | solution.py:301
  32.5 6.2 %copy-start.1 = (f32[1024]{0:T(1024)S(1)}, f32[1024]{0:T(1024)}, u32[]{:S(2)}) copy-start(f32[1024]{0:T(1024)} %param.10) | copy-start | bytes 12292
  32.5 7.9 %collective-permute-start.14 = (bf16[272,128]{1,0:T(8,128)(2,1)S(1)}, bf16[272,128]{1,0:T(8,128)(2,1)S(1)}, u32[]{:S(2)}, u32[]{:S(2)}) collective-permute-start(bf16[272,128]{1,0:T(8,128)(2,1)S(1)} %get-tuple-element.59), channel_id=1, source_target_pairs={{0,6},{1,7},{2,4},{3,5},{4,2},{5,3},{6,0},{7,1},{8,14},{9,15},{10,... | collective-permute-start | bytes 208904 | tf_op jit(solution)/shard_map/ppermute | solution.py:301
  35.2 6.9 %collective-permute-start.15 = (bf16[272,128]{1,0:T(8,128)(2,1)S(1)}, bf16[272,128]{1,0:T(8,128)(2,1)S(1)}, u32[]{:S(2)}, u32[]{:S(2)}) collective-permute-start(bf16[272,128]{1,0:T(8,128)(2,1)S(1)} %get-tuple-element.60), channel_id=1, source_target_pairs={{0,7},{1,6},{2,5},{3,4},{4,3},{5,2},{6,1},{7,0},{8,15},{9,14},{10,... | collective-permute-start | bytes 208904 | tf_op jit(solution)/shard_map/ppermute | solution.py:301
  36.8 5.3 %collective-permute-start.16 = (bf16[272,128]{1,0:T(8,128)(2,1)S(1)}, bf16[272,128]{1,0:T(8,128)(2,1)S(1)}, u32[]{:S(2)}, u32[]{:S(2)}) collective-permute-start(bf16[272,128]{1,0:T(8,128)(2,1)S(1)} %get-tuple-element.61), channel_id=1, source_target_pairs={{0,1},{1,0},{2,3},{3,2},{4,5},{5,4},{6,7},{7,6},{8,9},{9,8},{10,11... | collective-permute-start | bytes 208904 | tf_op jit(solution)/shard_map/ppermute | solution.py:301

commit v8 on v7

--- a/solution.py
+++ b/solution.py
@@ -41,7 +41,7 @@
 
 def encode(values):
     peak = jnp.max(jnp.abs(values), axis=0, keepdims=True) * (1.0 + 2.0**-7)
-    scale = jnp.maximum(peak.astype(jnp.bfloat16).astype(jnp.float32), 2.0**-110)
+    scale = jnp.maximum(peak.astype(jnp.bfloat16).astype(jnp.float32), 2.0**-116)
     size = jnp.abs(values) * (top_code / 128.0 / scale)
     octave = jnp.floor(size)
     carrier = (size - octave + 1.0) * jnp.exp2(octave - float(low_power))
@@ -220,6 +220,7 @@
     for other in partial_squares[1:]:
         squares += other[...]
     total = jnp.sum(jnp.sum(squares, axis=0, keepdims=True), axis=1, keepdims=True)
+    total = jnp.minimum(total, 3.38e38)
     width = squares.shape[1]
     total_rows = tail_tile(5, three_parts(jnp.broadcast_to(total, (1, width))), width)
     for i in range(size):

time: 43.4 us -> 43.5 us (level)
  no operation moved by 1% of the time
where the time goes in v8:
time: 43.5 us; the launch traced here: 43.3 us
  starting transfers between devices  25.3 us (58%)
  waiting for transfers between devices  10.7 us (25%)
  Pallas kernels  5.31 us (12%)
  other arithmetic  1.22 us (3%)
  between operations  0.79 us (2%)
    ppermute x14, starting transfers between devices, send(): return lax.ppermute(block, 'ctx', [(i, i ^ k) for i in range(size)])  21.7 us
    ppermute x14, waiting for transfers between devices, send(): return lax.ppermute(block, 'ctx', [(i, i ^ k) for i in range(size)])  10.4 us
    ppermute x3, starting transfers between devices, per_device(): lax.ppermute(squares, 'chan', [(i, i ^ k) for i in range(columns)])  3.55 us
    pallas_call x1, Pallas kernels, per_device(): run(functools.partial(second_kernel, order, length, second_places), 'inpu...  1.83 us
    pallas_call x1, Pallas kernels, per_device(): run(functools.partial(first_kernel, order, length, first_places), 'filter...  1.58 us
    pallas_call x1, Pallas kernels, per_device(): run(functools.partial(last_kernel, turns, early, length, width, clip_limi...  1.22 us
    another operation x1, other arithmetic, per_device(): jnp.stack(three)  1.2 us
  transfers between devices with their start and end apart: 17, of which 8 were waited for; matrix products, arithmetic and copies ran while one was open for 0% of the time, Pallas kernels for 9%

profile of v8, /device:TPU:0, one launch (start us, length us, event | category | flops | bytes accessed | tf_op | source)
XLA Modules:
  0.0 43.3 jit_solution(1205256686115299459)
XLA Ops:
  0.6 1.2 %pad_maximum_fusion.arrays = bf16[3,128,1024]{2,1,0:T(8,128)(2,1)S(1)} fusion(bf16[1,128,1024]{2,1,0:T(8,128)(2,1)} %bitcast.8, bf16[1,128,1024]{2,1,0:T(8,128)(2,1)} %bitcast.9, bf16[1,128,1024]{2,1,0:T(8,128)(2,1)} %bitcast.5), kind=kLoop, calls=%fused_computation | loop fusion | flops 786432 | bytes 1572864 | tf_op jit(solution)/shard_map/stack | solution.py:313
  1.8 0.2 columns.1
  2.1 0.5 %collective-permute-start = (bf16[1280,128]{1,0:T(8,128)(2,1)S(1)}, bf16[1280,128]{1,0:T(8,128)(2,1)S(1)}, u32[]{:S(2)}, u32[]{:S(2)}) collective-permute-start(bf16[1280,128]{1,0:T(8,128)(2,1)S(1)} %get-tuple-element.36), channel_id=1, source_target_pairs={{0,1},{1,0},{2,3},{3,2},{4,5},{5,4},{6,7},{7,6},{8,9},{9,8},{10,11... | collective-permute-start | bytes 983048 | tf_op jit(solution)/shard_map/ppermute | solution.py:302
  2.6 4.7 %collective-permute-start.1 = (bf16[256,128]{1,0:T(8,128)(2,1)S(1)}, bf16[256,128]{1,0:T(8,128)(2,1)S(1)}, u32[]{:S(2)}, u32[]{:S(2)}) collective-permute-start(bf16[256,128]{1,0:T(8,128)(2,1)S(1)} %get-tuple-element.37), channel_id=1, source_target_pairs={{0,6},{1,7},{2,4},{3,5},{4,2},{5,3},{6,0},{7,1},{8,14},{9,15},{10,... | collective-permute-start | bytes 196616 | tf_op jit(solution)/shard_map/ppermute | solution.py:302
  7.2 0.1 collective-permute-start.2
  7.3 0.0 collective-permute-done.sibling.refs_5_.refs_4_
  7.4 0.1 collective-permute-start.5
  7.5 0.0 copy-start.2
  7.5 0.0 copy-start.3
  7.5 0.0 copy-start.4
  7.5 4.1 %collective-permute-start.6 = (bf16[512,128]{1,0:T(8,128)(2,1)S(1)}, bf16[512,128]{1,0:T(8,128)(2,1)S(1)}, u32[]{:S(2)}, u32[]{:S(2)}) collective-permute-start(bf16[512,128]{1,0:T(8,128)(2,1)S(1)} %pad_maximum_fusion.2), channel_id=1, source_target_pairs={{0,4},{1,5},{2,6},{3,7},{4,0},{5,1},{6,2},{7,3},{8,12},{9,13},{10,... | collective-permute-start | bytes 393224 | tf_op jit(solution)/shard_map/ppermute | solution.py:302
  11.6 0.0 collective-permute-done.1.refs_0_
  11.7 1.6 %collective-permute-done.2.refs_1_ = bf16[256,128]{1,0:T(8,128)(2,1)S(1)} collective-permute-done((bf16[256,128]{1,0:T(8,128)(2,1)S(1)}, bf16[256,128]{1,0:T(8,128)(2,1)S(1)}, u32[]{:S(2)}, u32[]{:S(2)}) %collective-permute-start.2) | collective-permute-done | bytes 65568 | tf_op jit(solution)/shard_map/ppermute | solution.py:302
  13.2 0.0 copy-done.2
  13.2 0.0 copy-done.3
  13.3 0.0 copy-done.4
  13.3 1.4 %collective-permute-start.3 = (bf16[256,128]{1,0:T(8,128)(2,1)S(1)}, bf16[256,128]{1,0:T(8,128)(2,1)S(1)}, u32[]{:S(2)}, u32[]{:S(2)}) collective-permute-start(bf16[256,128]{1,0:T(8,128)(2,1)S(1)} %get-tuple-element.41), channel_id=1, source_target_pairs={{0,6},{1,7},{2,4},{3,5},{4,2},{5,3},{6,0},{7,1},{8,14},{9,15},{10,... | collective-permute-start | bytes 196616 | tf_op jit(solution)/shard_map/ppermute | solution.py:302
  14.7 0.3 collective-permute-start.4
  15.0 3.2 %collective-permute-done.6.refs_2_ = bf16[512,128]{1,0:T(8,128)(2,1)S(1)} collective-permute-done((bf16[512,128]{1,0:T(8,128)(2,1)S(1)}, bf16[512,128]{1,0:T(8,128)(2,1)S(1)}, u32[]{:S(2)}, u32[]{:S(2)}) %collective-permute-start.6) | collective-permute-done | bytes 131104 | tf_op jit(solution)/shard_map/ppermute | solution.py:302
  18.2 0.4 collective-permute-done.5.refs_3_.refs_2_
  18.6 1.6 %filter_gradient.1 = (f32[8,128,128]{2,1,0:T(8,128)S(1)}, f32[1,128]{1,0:T(1,128)S(1)}, f32[8,256,128]{2,1,0:T(8,128)S(1)}, f32[8,128]{1,0:T(8,128)S(1)}) custom-call(bf16[256,128]{1,0:T(8,128)(2,1)S(1)} %collective-permute-done.1.refs_0_, bf16[256,128]{1,0:T(8,128)(2,1)S(1)} %collective-permute-done.2.refs_1_, ...), custom_call_target="tpu_custom_call" | custom-call | flops 4000000000 | tf_op jit(solution)/shard_map/filter_gradient/pallas_call | solution.py:359
  20.2 2.6 %collective-permute-start.9 = (f32[8,128]{1,0:T(8,128)S(1)}, f32[8,128]{1,0:T(8,128)S(1)}, u32[]{:S(2)}, u32[]{:S(2)}) collective-permute-start(f32[8,128]{1,0:T(8,128)S(1)} %get-tuple-element.53.refs_4_), channel_id=1, source_target_pairs={{0,24},{8,16},{16,8},{24,0},{1,25},{9,17},{17,9},{25,1},{2,26},{10... | collective-permute-start | bytes 12296 | tf_op jit(solution)/shard_map/ppermute | solution.py:375
  22.8 0.5 %collective-permute-start.8 = (f32[8,128]{1,0:T(8,128)S(1)}, f32[8,128]{1,0:T(8,128)S(1)}, u32[]{:S(2)}, u32[]{:S(2)}) collective-permute-start(f32[8,128]{1,0:T(8,128)S(1)} %get-tuple-element.53.refs_4_), channel_id=1, source_target_pairs={{0,16},{8,24},{16,0},{24,8},{1,17},{9,25},{17,1},{25,9},{2,18},{10... | collective-permute-start | bytes 12296 | tf_op jit(solution)/shard_map/ppermute | solution.py:375
  23.3 0.4 collective-permute-start.7
  23.7 0.0 collective-permute-done.3.refs_0_
  23.7 1.1 %collective-permute-done.4.refs_1_ = bf16[256,128]{1,0:T(8,128)(2,1)S(1)} collective-permute-done((bf16[256,128]{1,0:T(8,128)(2,1)S(1)}, bf16[256,128]{1,0:T(8,128)(2,1)S(1)}, u32[]{:S(2)}, u32[]{:S(2)}) %collective-permute-start.4) | collective-permute-done | bytes 65568 | tf_op jit(solution)/shard_map/ppermute | solution.py:302
  24.8 1.8 %input_gradient.1 = (bf16[8,128,128]{2,1,0:T(8,128)(2,1)S(1)}, f32[8,16,128]{2,1,0:T(8,128)S(1)}, bf16[8,128,128]{2,1,0:T(8,128)(2,1)S(1)}, f32[8,16,128]{2,1,0:T(8,128)S(1)}) custom-call(bf16[256,128]{1,0:T(8,128)(2,1)S(1)} %collective-permute-done.3.refs_0_, bf16[256,128]{1,0:T(8,128)(2,1)S(1)} %collective-permute-done.4.refs_1_, ...), custom_call_target="tpu_custom_call" | custom-call | flops 20000000000 | tf_op jit(solution)/shard_map/input_gradient/pallas_call | solution.py:378
  26.7 0.0 collective-permute-done.9.refs_7_
  26.7 0.0 collective-permute-done.8.refs_6_
  26.7 0.2 collective-permute-done.7.refs_5_
  27.0 0.1 messages.1
  27.1 2.9 %collective-permute-start.10 = (bf16[272,128]{1,0:T(8,128)(2,1)S(1)}, bf16[272,128]{1,0:T(8,128)(2,1)S(1)}, u32[]{:S(2)}, u32[]{:S(2)}) collective-permute-start(bf16[272,128]{1,0:T(8,128)(2,1)S(1)} %get-tuple-element.54), channel_id=1, source_target_pairs={{0,4},{1,5},{2,6},{3,7},{4,0},{5,1},{6,2},{7,3},{8,12},{9,13},{10,... | collective-permute-start | bytes 208904 | tf_op jit(solution)/shard_map/ppermute | solution.py:302
  30.0 0.0 collective-permute-start.11
  30.0 1.4 %collective-permute-start.12 = (bf16[272,128]{1,0:T(8,128)(2,1)S(1)}, bf16[272,128]{1,0:T(8,128)(2,1)S(1)}, u32[]{:S(2)}, u32[]{:S(2)}) collective-permute-start(bf16[272,128]{1,0:T(8,128)(2,1)S(1)} %get-tuple-element.56), channel_id=1, source_target_pairs={{0,2},{1,3},{2,0},{3,1},{4,6},{5,7},{6,4},{7,5},{8,10},{9,11},{10,... | collective-permute-start | bytes 208904 | tf_op jit(solution)/shard_map/ppermute | solution.py:302
  31.3 1.2 %collective-permute-start.13 = (bf16[272,128]{1,0:T(8,128)(2,1)S(1)}, bf16[272,128]{1,0:T(8,128)(2,1)S(1)}, u32[]{:S(2)}, u32[]{:S(2)}) collective-permute-start(bf16[272,128]{1,0:T(8,128)(2,1)S(1)} %get-tuple-element.57), channel_id=1, source_target_pairs={{0,3},{1,2},{2,1},{3,0},{4,7},{5,6},{6,5},{7,4},{8,11},{9,10},{10,... | collective-permute-start | bytes 208904 | tf_op jit(solution)/shard_map/ppermute | solution.py:302
  32.5 2.7 %collective-permute-start.14 = (bf16[272,128]{1,0:T(8,128)(2,1)S(1)}, bf16[272,128]{1,0:T(8,128)(2,1)S(1)}, u32[]{:S(2)}, u32[]{:S(2)}) collective-permute-start(bf16[272,128]{1,0:T(8,128)(2,1)S(1)} %get-tuple-element.59), channel_id=1, source_target_pairs={{0,6},{1,7},{2,4},{3,5},{4,2},{5,3},{6,0},{7,1},{8,14},{9,15},{10,... | collective-permute-start | bytes 208904 | tf_op jit(solution)/shard_map/ppermute | solution.py:302
  35.2 0.0 collective-permute-done.10.refs_0_
  35.2 0.6 %collective-permute-start.15 = (bf16[272,128]{1,0:T(8,128)(2,1)S(1)}, bf16[272,128]{1,0:T(8,128)(2,1)S(1)}, u32[]{:S(2)}, u32[]{:S(2)}) collective-permute-start(bf16[272,128]{1,0:T(8,128)(2,1)S(1)} %get-tuple-element.60), channel_id=1, source_target_pairs={{0,7},{1,6},{2,5},{3,4},{4,3},{5,2},{6,1},{7,0},{8,15},{9,14},{10,... | collective-permute-start | bytes 208904 | tf_op jit(solution)/shard_map/ppermute | solution.py:302
  35.7 1.1 %collective-permute-done.11.refs_1_ = bf16[272,128]{1,0:T(8,128)(2,1)S(1)} collective-permute-done((bf16[272,128]{1,0:T(8,128)(2,1)S(1)}, bf16[272,128]{1,0:T(8,128)(2,1)S(1)}, u32[]{:S(2)}, u32[]{:S(2)}) %collective-permute-start.11) | collective-permute-done | bytes 69664 | tf_op jit(solution)/shard_map/ppermute | solution.py:302
  36.8 1.9 %collective-permute-start.16 = (bf16[272,128]{1,0:T(8,128)(2,1)S(1)}, bf16[272,128]{1,0:T(8,128)(2,1)S(1)}, u32[]{:S(2)}, u32[]{:S(2)}) collective-permute-start(bf16[272,128]{1,0:T(8,128)(2,1)S(1)} %get-tuple-element.61), channel_id=1, source_target_pairs={{0,1},{1,0},{2,3},{3,2},{4,5},{5,4},{6,7},{7,6},{8,9},{9,8},{10,11... | collective-permute-start | bytes 208904 | tf_op jit(solution)/shard_map/ppermute | solution.py:302
  38.7 0.0 collective-permute-done.12.refs_2_
  38.7 0.0 collective-permute-done.13.refs_3_
  38.7 0.0 copy-done
  38.7 0.3 early.1
  39.1 1.3 %collective-permute-done.14.refs_5_ = bf16[272,128]{1,0:T(8,128)(2,1)S(1)} collective-permute-done((bf16[272,128]{1,0:T(8,128)(2,1)S(1)}, bf16[272,128]{1,0:T(8,128)(2,1)S(1)}, u32[]{:S(2)}, u32[]{:S(2)}) %collective-permute-start.14) | collective-permute-done | bytes 69664 | tf_op jit(solution)/shard_map/ppermute | solution.py:302
  40.4 1.7 %collective-permute-done.15.refs_6_ = bf16[272,128]{1,0:T(8,128)(2,1)S(1)} collective-permute-done((bf16[272,128]{1,0:T(8,128)(2,1)S(1)}, bf16[272,128]{1,0:T(8,128)(2,1)S(1)}, u32[]{:S(2)}, u32[]{:S(2)}) %collective-permute-start.15) | collective-permute-done | bytes 69664 | tf_op jit(solution)/shard_map/ppermute | solution.py:302
  42.1 0.0 collective-permute-done.16.refs_7_
  42.1 1.2 %outputs.1 = (f32[128,1024]{1,0:T(8,128)}, f32[128,1024]{1,0:T(8,128)}, f32[1,1024]{1,0:T(1,128)}) custom-call(bf16[272,128]{1,0:T(8,128)(2,1)S(1)} %collective-permute-done.10.refs_0_, bf16[272,128]{1,0:T(8,128)(2,1)S(1)} %collective-permute-done.11.refs_1_, bf16[272,128]{1,0:T(8,128)(2,1)S(1)} %collective-permute-done.12.refs_2_, ...), custom_call_target="tpu_custom_call" | custom-call | flops 1000000000 | tf_op jit(solution)/shard_map/outputs/pallas_call | solution.py:418
  (10 shorter events, 0.1 us)
Async XLA Ops:
  2.1 5.3 %collective-permute-start = (bf16[1280,128]{1,0:T(8,128)(2,1)S(1)}, bf16[1280,128]{1,0:T(8,128)(2,1)S(1)}, u32[]{:S(2)}, u32[]{:S(2)}) collective-permute-start(bf16[1280,128]{1,0:T(8,128)(2,1)S(1)} %get-tuple-element.36), channel_id=1, source_target_pairs={{0,1},{1,0},{2,3},{3,2},{4,5},{5,4},{6,7},{7,6},{8,9},{9,8},{10,11... | collective-permute-start | bytes 983048 | tf_op jit(solution)/shard_map/ppermute | solution.py:302
  2.6 9.1 %collective-permute-start.1 = (bf16[256,128]{1,0:T(8,128)(2,1)S(1)}, bf16[256,128]{1,0:T(8,128)(2,1)S(1)}, u32[]{:S(2)}, u32[]{:S(2)}) collective-permute-start(bf16[256,128]{1,0:T(8,128)(2,1)S(1)} %get-tuple-element.37), channel_id=1, source_target_pairs={{0,6},{1,7},{2,4},{3,5},{4,2},{5,3},{6,0},{7,1},{8,14},{9,15},{10,... | collective-permute-start | bytes 196616 | tf_op jit(solution)/shard_map/ppermute | solution.py:302
  7.2 6.0 %collective-permute-start.2 = (bf16[256,128]{1,0:T(8,128)(2,1)S(1)}, bf16[256,128]{1,0:T(8,128)(2,1)S(1)}, u32[]{:S(2)}, u32[]{:S(2)}) collective-permute-start(bf16[256,128]{1,0:T(8,128)(2,1)S(1)} %get-tuple-element.38), channel_id=1, source_target_pairs={{0,7},{1,6},{2,5},{3,4},{4,3},{5,2},{6,1},{7,0},{8,15},{9,14},{10,... | collective-permute-start | bytes 196616 | tf_op jit(solution)/shard_map/ppermute | solution.py:302
  7.4 11.2 %collective-permute-start.5 = (bf16[768,128]{1,0:T(8,128)(2,1)S(1)}, bf16[768,128]{1,0:T(8,128)(2,1)S(1)}, u32[]{:S(2)}, u32[]{:S(2)}) collective-permute-start(bf16[768,128]{1,0:T(8,128)(2,1)S(1)} %pad_maximum_fusion.1), channel_id=1, source_target_pairs={{0,2},{1,3},{2,0},{3,1},{4,6},{5,7},{6,4},{7,5},{8,10},{9,11},{10,... | collective-permute-start | bytes 589832 | tf_op jit(solution)/shard_map/ppermute | solution.py:302
  7.5 5.8 %copy-start.2 = (bf16[256,256]{1,0:T(8,128)(2,1)S(1)}, bf16[256,256]{1,0:T(8,128)(2,1)}, u32[]{:S(2)}) copy-start(bf16[256,256]{1,0:T(8,128)(2,1)} %constant.6.clone.refs_0_) | copy-start | bytes 393220
  7.5 5.8 %copy-start.3 = (bf16[128,256]{1,0:T(8,128)(2,1)S(1)}, bf16[128,256]{1,0:T(8,128)(2,1)}, u32[]{:S(2)}) copy-start(bf16[128,256]{1,0:T(8,128)(2,1)} %constant.8.clone.refs_2_) | copy-start | bytes 196612
  7.5 5.8 %copy-start.4 = (bf16[128,256]{1,0:T(8,128)(2,1)S(1)}, bf16[128,256]{1,0:T(8,128)(2,1)}, u32[]{:S(2)}) copy-start(bf16[128,256]{1,0:T(8,128)(2,1)} %constant.7.clone.refs_1_) | copy-start | bytes 196612
  7.5 10.6 %collective-permute-start.6 = (bf16[512,128]{1,0:T(8,128)(2,1)S(1)}, bf16[512,128]{1,0:T(8,128)(2,1)S(1)}, u32[]{:S(2)}, u32[]{:S(2)}) collective-permute-start(bf16[512,128]{1,0:T(8,128)(2,1)S(1)} %pad_maximum_fusion.2), channel_id=1, source_target_pairs={{0,4},{1,5},{2,6},{3,7},{4,0},{5,1},{6,2},{7,3},{8,12},{9,13},{10,... | collective-permute-start | bytes 393224 | tf_op jit(solution)/shard_map/ppermute | solution.py:302
  13.3 10.5 %collective-permute-start.3 = (bf16[256,128]{1,0:T(8,128)(2,1)S(1)}, bf16[256,128]{1,0:T(8,128)(2,1)S(1)}, u32[]{:S(2)}, u32[]{:S(2)}) collective-permute-start(bf16[256,128]{1,0:T(8,128)(2,1)S(1)} %get-tuple-element.41), channel_id=1, source_target_pairs={{0,6},{1,7},{2,4},{3,5},{4,2},{5,3},{6,0},{7,1},{8,14},{9,15},{10,... | collective-permute-start | bytes 196616 | tf_op jit(solution)/shard_map/ppermute | solution.py:302
  14.7 10.1 %collective-permute-start.4 = (bf16[256,128]{1,0:T(8,128)(2,1)S(1)}, bf16[256,128]{1,0:T(8,128)(2,1)S(1)}, u32[]{:S(2)}, u32[]{:S(2)}) collective-permute-start(bf16[256,128]{1,0:T(8,128)(2,1)S(1)} %get-tuple-element.42), channel_id=1, source_target_pairs={{0,4},{1,5},{2,6},{3,7},{4,0},{5,1},{6,2},{7,3},{8,12},{9,13},{10,... | collective-permute-start | bytes 196616 | tf_op jit(solution)/shard_map/ppermute | solution.py:302
  20.2 6.5 %collective-permute-start.9 = (f32[8,128]{1,0:T(8,128)S(1)}, f32[8,128]{1,0:T(8,128)S(1)}, u32[]{:S(2)}, u32[]{:S(2)}) collective-permute-start(f32[8,128]{1,0:T(8,128)S(1)} %get-tuple-element.53.refs_4_), channel_id=1, source_target_pairs={{0,24},{8,16},{16,8},{24,0},{1,25},{9,17},{17,9},{25,1},{2,26},{10... | collective-permute-start | bytes 12296 | tf_op jit(solution)/shard_map/ppermute | solution.py:375
  22.8 3.9 %collective-permute-start.8 = (f32[8,128]{1,0:T(8,128)S(1)}, f32[8,128]{1,0:T(8,128)S(1)}, u32[]{:S(2)}, u32[]{:S(2)}) collective-permute-start(f32[8,128]{1,0:T(8,128)S(1)} %get-tuple-element.53.refs_4_), channel_id=1, source_target_pairs={{0,16},{8,24},{16,0},{24,8},{1,17},{9,25},{17,1},{25,9},{2,18},{10... | collective-permute-start | bytes 12296 | tf_op jit(solution)/shard_map/ppermute | solution.py:375
  23.3 3.6 %collective-permute-start.7 = (f32[8,128]{1,0:T(8,128)S(1)}, f32[8,128]{1,0:T(8,128)S(1)}, u32[]{:S(2)}, u32[]{:S(2)}) collective-permute-start(f32[8,128]{1,0:T(8,128)S(1)} %get-tuple-element.53.refs_4_), channel_id=1, source_target_pairs={{0,8},{8,0},{16,24},{24,16},{1,9},{9,1},{17,25},{25,17},{2,10},{10... | collective-permute-start | bytes 12296 | tf_op jit(solution)/shard_map/ppermute | solution.py:375
  26.9 11.8 %copy-start = (bf16[128,1024]{1,0:T(8,128)(2,1)S(1)}, bf16[128,1024]{1,0:T(8,128)(2,1)}, u32[]{:S(2)}) copy-start(bf16[128,1024]{1,0:T(8,128)(2,1)} %refs_10_.1) | copy-start | bytes 786436
  27.1 8.1 %collective-permute-start.10 = (bf16[272,128]{1,0:T(8,128)(2,1)S(1)}, bf16[272,128]{1,0:T(8,128)(2,1)S(1)}, u32[]{:S(2)}, u32[]{:S(2)}) collective-permute-start(bf16[272,128]{1,0:T(8,128)(2,1)S(1)} %get-tuple-element.54), channel_id=1, source_target_pairs={{0,4},{1,5},{2,6},{3,7},{4,0},{5,1},{6,2},{7,3},{8,12},{9,13},{10,... | collective-permute-start | bytes 208904 | tf_op jit(solution)/shard_map/ppermute | solution.py:302
  30.0 6.8 %collective-permute-start.11 = (bf16[272,128]{1,0:T(8,128)(2,1)S(1)}, bf16[272,128]{1,0:T(8,128)(2,1)S(1)}, u32[]{:S(2)}, u32[]{:S(2)}) collective-permute-start(bf16[272,128]{1,0:T(8,128)(2,1)S(1)} %get-tuple-element.55), channel_id=1, source_target_pairs={{0,5},{1,4},{2,7},{3,6},{4,1},{5,0},{6,3},{7,2},{8,13},{9,12},{10,... | collective-permute-start | bytes 208904 | tf_op jit(solution)/shard_map/ppermute | solution.py:302
  30.0 8.7 %collective-permute-start.12 = (bf16[272,128]{1,0:T(8,128)(2,1)S(1)}, bf16[272,128]{1,0:T(8,128)(2,1)S(1)}, u32[]{:S(2)}, u32[]{:S(2)}) collective-permute-start(bf16[272,128]{1,0:T(8,128)(2,1)S(1)} %get-tuple-element.56), channel_id=1, source_target_pairs={{0,2},{1,3},{2,0},{3,1},{4,6},{5,7},{6,4},{7,5},{8,10},{9,11},{10,... | collective-permute-start | bytes 208904 | tf_op jit(solution)/shard_map/ppermute | solution.py:302
  31.3 7.4 %collective-permute-start.13 = (bf16[272,128]{1,0:T(8,128)(2,1)S(1)}, bf16[272,128]{1,0:T(8,128)(2,1)S(1)}, u32[]{:S(2)}, u32[]{:S(2)}) collective-permute-start(bf16[272,128]{1,0:T(8,128)(2,1)S(1)} %get-tuple-element.57), channel_id=1, source_target_pairs={{0,3},{1,2},{2,1},{3,0},{4,7},{5,6},{6,5},{7,4},{8,11},{9,10},{10,... | collective-permute-start | bytes 208904 | tf_op jit(solution)/shard_map/ppermute | solution.py:302
  32.5 6.2 %copy-start.1 = (f32[1024]{0:T(1024)S(1)}, f32[1024]{0:T(1024)}, u32[]{:S(2)}) copy-start(f32[1024]{0:T(1024)} %param.10) | copy-start | bytes 12292
  32.5 7.9 %collective-permute-start.14 = (bf16[272,128]{1,0:T(8,128)(2,1)S(1)}, bf16[272,128]{1,0:T(8,128)(2,1)S(1)}, u32[]{:S(2)}, u32[]{:S(2)}) collective-permute-start(bf16[272,128]{1,0:T(8,128)(2,1)S(1)} %get-tuple-element.59), channel_id=1, source_target_pairs={{0,6},{1,7},{2,4},{3,5},{4,2},{5,3},{6,0},{7,1},{8,14},{9,15},{10,... | collective-permute-start | bytes 208904 | tf_op jit(solution)/shard_map/ppermute | solution.py:302
  35.2 6.9 %collective-permute-start.15 = (bf16[272,128]{1,0:T(8,128)(2,1)S(1)}, bf16[272,128]{1,0:T(8,128)(2,1)S(1)}, u32[]{:S(2)}, u32[]{:S(2)}) collective-permute-start(bf16[272,128]{1,0:T(8,128)(2,1)S(1)} %get-tuple-element.60), channel_id=1, source_target_pairs={{0,7},{1,6},{2,5},{3,4},{4,3},{5,2},{6,1},{7,0},{8,15},{9,14},{10,... | collective-permute-start | bytes 208904 | tf_op jit(solution)/shard_map/ppermute | solution.py:302
  36.8 5.3 %collective-permute-start.16 = (bf16[272,128]{1,0:T(8,128)(2,1)S(1)}, bf16[272,128]{1,0:T(8,128)(2,1)S(1)}, u32[]{:S(2)}, u32[]{:S(2)}) collective-permute-start(bf16[272,128]{1,0:T(8,128)(2,1)S(1)} %get-tuple-element.61), channel_id=1, source_target_pairs={{0,1},{1,0},{2,3},{3,2},{4,5},{5,4},{6,7},{7,6},{8,9},{9,8},{10,11... | collective-permute-start | bytes 208904 | tf_op jit(solution)/shard_map/ppermute | solution.py:302

commit v9 on v8

--- a/solution.py
+++ b/solution.py
@@ -95,13 +95,14 @@
         emit(i + 1, block[:, width:])
 
 
-def columns_kernel(chips, direct, length, part, arrays, *refs):
-    blocks, rest = refs[:-2], refs[-2:]
-    position = lax.axis_index("ctx")
+def columns_kernel(chips, direct, length, part, *refs):
+    halves, blocks, rest = refs[:6], refs[6:-2], refs[-2:]
+    position = lax.axis_index("ctx")
+    half = len(chips)
 
     def put(out, row, j, k):
-        columns = pl.ds(pl.multiple_of((position ^ k) * part, part), part)
-        out[row : row + length] = arrays[j, :, columns]
+        columns = pl.ds(pl.multiple_of((position ^ k) % half * part, part), part)
+        out[row : row + length] = halves[2 * j + k // half][:, columns]
 
     for core in range(2):
         row = 0
@@ -161,7 +162,7 @@
             acc[p, imag_rows, :] = imag
         return carry
 
-    lax.fori_loop(0, length // 8, rows, 0)
+    lax.fori_loop(0, length // 8, rows, 0, unroll=2)
     skip_out[...] = skip
     squares[...] = jnp.zeros_like(squares)
 
@@ -199,7 +200,7 @@
             acc[p, imag_rows, :] = imag
         return carry
 
-    lax.fori_loop(0, length // 8, rows, 0)
+    lax.fori_loop(0, length // 8, rows, 0, unroll=2)
 
     skip_parts = three_parts(skip[...])
     for i in range(size):
@@ -304,13 +305,18 @@
     three = (out_grad, inputs, filter_taps)
     direct = size // 8
     rest_rows = (3 * len(chips) - 2 * direct) * length
+    half = size // 2
     if width == part:
         *blocks, mine, others = run(
             functools.partial(columns_kernel, chips, direct, length, part),
             "columns", vmem_bytes,
             [jax.ShapeDtypeStruct((2 * length, width), bf16)] * (2 * direct)
             + [jax.ShapeDtypeStruct((rest_rows, width), bf16)] * 2,
-        )(jnp.stack(three))
+        )(*[
+            lax.dynamic_slice_in_dim(array, (position // half * half ^ other) * part, half * part, 1)
+            for array in three
+            for other in (0, half)
+        ])
     else:
         blocks = [jnp.concatenate([columns_for(a, k) for a in three[:2]]) for k in order[: 2 * direct]]
         mine, others = (

time: 43.5 us -> 43.4 us (level)
  other arithmetic: 1.22 us -> 0.03 us
  local copies, waits for them, and re-layouts: 0.06 us -> 1.22 us
    another operation x1 -> x0, other arithmetic: 1.2 us -> none  [per_device(): jnp.stack(three)]
    dynamic_slice x0 -> x2, local copies, waits for them, and re-layouts: none -> 1.08 us  [per_device(): lax.dynamic_slice_in_dim(array, (position // half * half ^ other) * part,...]
  transfers between devices with their start and end apart: 17 -> 17, of which waited for: 8 -> 8; matrix products, arithmetic and copies ran while one was open for 0% -> 0% of each run, Pallas kernels for 9% -> 8%
where the time goes in v9:
time: 43.4 us; the launch traced here: 43.2 us
  starting transfers between devices  25.3 us (58%)
  waiting for transfers between devices  10.7 us (25%)
  Pallas kernels  5.15 us (12%)
  local copies, waits for them, and re-layouts  1.22 us (3%)
  between operations  0.84 us (2%)
    ppermute x14, starting transfers between devices, send(): return lax.ppermute(block, 'ctx', [(i, i ^ k) for i in range(size)])  21.7 us
    ppermute x14, waiting for transfers between devices, send(): return lax.ppermute(block, 'ctx', [(i, i ^ k) for i in range(size)])  10.4 us
    ppermute x3, starting transfers between devices, per_device(): lax.ppermute(squares, 'chan', [(i, i ^ k) for i in range(columns)])  3.55 us
    pallas_call x1, Pallas kernels, per_device(): run(functools.partial(second_kernel, order, length, second_places), 'inpu...  1.75 us
    pallas_call x1, Pallas kernels, per_device(): run(functools.partial(first_kernel, order, length, first_places), 'filter...  1.54 us
    pallas_call x1, Pallas kernels, per_device(): run(functools.partial(last_kernel, turns, early, length, width, clip_limi...  1.22 us
    dynamic_slice x2, local copies, waits for them, and re-layouts, per_device(): lax.dynamic_slice_in_dim(array, (position // half * half ^ other) * part,...  1.08 us
  transfers between devices with their start and end apart: 17, of which 8 were waited for; matrix products, arithmetic and copies ran while one was open for 0% of the time, Pallas kernels for 8%

profile of v9, /device:TPU:0, one launch (start us, length us, event | category | flops | bytes accessed | tf_op | source)
XLA Modules:
  0.0 43.2 jit_solution(15016459096781819944)
XLA Ops:
  0.7 0.0 copy-start.5
  0.7 0.0 copy-start.6
  0.7 1.0 %constant_dynamic-slice_fusion.4 = (bf16[128,512]{1,0:T(8,128)(2,1)S(1)}, bf16[128,512]{1,0:T(8,128)(2,1)S(1)}) fusion(bf16[128,1024]{1,0:T(8,128)(2,1)} %refs_10_.1, s32[]{:T(128)S(6)} %select_n.22, s32[]{:T(128)S(6)} %select_n.21), kind=kLoop, calls=%fused_computation.6 | loop fusion | bytes 524296 | tf_op jit(solution)/shard_map/dynamic_slice | solution.py:316
  1.7 0.0 copy-done.5
  1.7 0.1 copy-done.6
  1.9 0.2 columns.1
  2.0 0.5 %collective-permute-start = (bf16[1280,128]{1,0:T(8,128)(2,1)S(1)}, bf16[1280,128]{1,0:T(8,128)(2,1)S(1)}, u32[]{:S(2)}, u32[]{:S(2)}) collective-permute-start(bf16[1280,128]{1,0:T(8,128)(2,1)S(1)} %get-tuple-element.36), channel_id=1, source_target_pairs={{0,1},{1,0},{2,3},{3,2},{4,5},{5,4},{6,7},{7,6},{8,9},{9,8},{10,11... | collective-permute-start | bytes 983048 | tf_op jit(solution)/shard_map/ppermute | solution.py:303
  2.5 4.7 %collective-permute-start.1 = (bf16[256,128]{1,0:T(8,128)(2,1)S(1)}, bf16[256,128]{1,0:T(8,128)(2,1)S(1)}, u32[]{:S(2)}, u32[]{:S(2)}) collective-permute-start(bf16[256,128]{1,0:T(8,128)(2,1)S(1)} %get-tuple-element.37), channel_id=1, source_target_pairs={{0,6},{1,7},{2,4},{3,5},{4,2},{5,3},{6,0},{7,1},{8,14},{9,15},{10,... | collective-permute-start | bytes 196616 | tf_op jit(solution)/shard_map/ppermute | solution.py:303
  7.2 0.1 collective-permute-start.2
  7.3 0.0 collective-permute-done.sibling.refs_5_.refs_4_
  7.4 0.1 collective-permute-start.5
  7.5 0.0 copy-start.2
  7.5 0.0 copy-start.3
  7.5 0.0 copy-start.4
  7.5 4.1 %collective-permute-start.6 = (bf16[512,128]{1,0:T(8,128)(2,1)S(1)}, bf16[512,128]{1,0:T(8,128)(2,1)S(1)}, u32[]{:S(2)}, u32[]{:S(2)}) collective-permute-start(bf16[512,128]{1,0:T(8,128)(2,1)S(1)} %pad_maximum_fusion.1), channel_id=1, source_target_pairs={{0,4},{1,5},{2,6},{3,7},{4,0},{5,1},{6,2},{7,3},{8,12},{9,13},{10,... | collective-permute-start | bytes 393224 | tf_op jit(solution)/shard_map/ppermute | solution.py:303
  11.6 0.0 collective-permute-done.1.refs_0_
  11.6 1.6 %collective-permute-done.2.refs_1_ = bf16[256,128]{1,0:T(8,128)(2,1)S(1)} collective-permute-done((bf16[256,128]{1,0:T(8,128)(2,1)S(1)}, bf16[256,128]{1,0:T(8,128)(2,1)S(1)}, u32[]{:S(2)}, u32[]{:S(2)}) %collective-permute-start.2) | collective-permute-done | bytes 65568 | tf_op jit(solution)/shard_map/ppermute | solution.py:303
  13.3 1.4 %collective-permute-start.3 = (bf16[256,128]{1,0:T(8,128)(2,1)S(1)}, bf16[256,128]{1,0:T(8,128)(2,1)S(1)}, u32[]{:S(2)}, u32[]{:S(2)}) collective-permute-start(bf16[256,128]{1,0:T(8,128)(2,1)S(1)} %get-tuple-element.41), channel_id=1, source_target_pairs={{0,6},{1,7},{2,4},{3,5},{4,2},{5,3},{6,0},{7,1},{8,14},{9,15},{10,... | collective-permute-start | bytes 196616 | tf_op jit(solution)/shard_map/ppermute | solution.py:303
  14.7 0.3 collective-permute-start.4
  15.0 3.2 %collective-permute-done.6.refs_2_ = bf16[512,128]{1,0:T(8,128)(2,1)S(1)} collective-permute-done((bf16[512,128]{1,0:T(8,128)(2,1)S(1)}, bf16[512,128]{1,0:T(8,128)(2,1)S(1)}, u32[]{:S(2)}, u32[]{:S(2)}) %collective-permute-start.6) | collective-permute-done | bytes 131104 | tf_op jit(solution)/shard_map/ppermute | solution.py:303
  18.2 0.4 collective-permute-done.5.refs_3_.refs_2_
  18.6 1.5 %filter_gradient.1 = (f32[8,128,128]{2,1,0:T(8,128)S(1)}, f32[1,128]{1,0:T(1,128)S(1)}, f32[8,256,128]{2,1,0:T(8,128)S(1)}, f32[8,128]{1,0:T(8,128)S(1)}) custom-call(bf16[256,128]{1,0:T(8,128)(2,1)S(1)} %collective-permute-done.1.refs_0_, bf16[256,128]{1,0:T(8,128)(2,1)S(1)} %collective-permute-done.2.refs_1_, ...), custom_call_target="tpu_custom_call" | custom-call | flops 4000000000 | tf_op jit(solution)/shard_map/filter_gradient/pallas_call | solution.py:365
  20.1 2.6 %collective-permute-start.9 = (f32[8,128]{1,0:T(8,128)S(1)}, f32[8,128]{1,0:T(8,128)S(1)}, u32[]{:S(2)}, u32[]{:S(2)}) collective-permute-start(f32[8,128]{1,0:T(8,128)S(1)} %get-tuple-element.53.refs_4_), channel_id=1, source_target_pairs={{0,24},{8,16},{16,8},{24,0},{1,25},{9,17},{17,9},{25,1},{2,26},{10... | collective-permute-start | bytes 12296 | tf_op jit(solution)/shard_map/ppermute | solution.py:381
  22.8 0.5 %collective-permute-start.8 = (f32[8,128]{1,0:T(8,128)S(1)}, f32[8,128]{1,0:T(8,128)S(1)}, u32[]{:S(2)}, u32[]{:S(2)}) collective-permute-start(f32[8,128]{1,0:T(8,128)S(1)} %get-tuple-element.53.refs_4_), channel_id=1, source_target_pairs={{0,16},{8,24},{16,0},{24,8},{1,17},{9,25},{17,1},{25,9},{2,18},{10... | collective-permute-start | bytes 12296 | tf_op jit(solution)/shard_map/ppermute | solution.py:381
  23.3 0.4 collective-permute-start.7
  23.7 0.0 collective-permute-done.3.refs_0_
  23.7 1.1 %collective-permute-done.4.refs_1_ = bf16[256,128]{1,0:T(8,128)(2,1)S(1)} collective-permute-done((bf16[256,128]{1,0:T(8,128)(2,1)S(1)}, bf16[256,128]{1,0:T(8,128)(2,1)S(1)}, u32[]{:S(2)}, u32[]{:S(2)}) %collective-permute-start.4) | collective-permute-done | bytes 65568 | tf_op jit(solution)/shard_map/ppermute | solution.py:303
  24.8 1.8 %input_gradient.1 = (bf16[8,128,128]{2,1,0:T(8,128)(2,1)S(1)}, f32[8,16,128]{2,1,0:T(8,128)S(1)}, bf16[8,128,128]{2,1,0:T(8,128)(2,1)S(1)}, f32[8,16,128]{2,1,0:T(8,128)S(1)}) custom-call(bf16[256,128]{1,0:T(8,128)(2,1)S(1)} %collective-permute-done.3.refs_0_, bf16[256,128]{1,0:T(8,128)(2,1)S(1)} %collective-permute-done.4.refs_1_, ...), custom_call_target="tpu_custom_call" | custom-call | flops 20000000000 | tf_op jit(solution)/shard_map/input_gradient/pallas_call | solution.py:384
  26.6 0.0 collective-permute-done.9.refs_7_
  26.6 0.0 collective-permute-done.8.refs_6_
  26.6 0.3 collective-permute-done.7.refs_5_
  26.9 0.1 messages.1
  27.0 2.9 %collective-permute-start.10 = (bf16[272,128]{1,0:T(8,128)(2,1)S(1)}, bf16[272,128]{1,0:T(8,128)(2,1)S(1)}, u32[]{:S(2)}, u32[]{:S(2)}) collective-permute-start(bf16[272,128]{1,0:T(8,128)(2,1)S(1)} %get-tuple-element.54), channel_id=1, source_target_pairs={{0,4},{1,5},{2,6},{3,7},{4,0},{5,1},{6,2},{7,3},{8,12},{9,13},{10,... | collective-permute-start | bytes 208904 | tf_op jit(solution)/shard_map/ppermute | solution.py:303
  29.9 0.0 collective-permute-start.11
  29.9 1.4 %collective-permute-start.12 = (bf16[272,128]{1,0:T(8,128)(2,1)S(1)}, bf16[272,128]{1,0:T(8,128)(2,1)S(1)}, u32[]{:S(2)}, u32[]{:S(2)}) collective-permute-start(bf16[272,128]{1,0:T(8,128)(2,1)S(1)} %get-tuple-element.56), channel_id=1, source_target_pairs={{0,2},{1,3},{2,0},{3,1},{4,6},{5,7},{6,4},{7,5},{8,10},{9,11},{10,... | collective-permute-start | bytes 208904 | tf_op jit(solution)/shard_map/ppermute | solution.py:303
  31.3 1.2 %collective-permute-start.13 = (bf16[272,128]{1,0:T(8,128)(2,1)S(1)}, bf16[272,128]{1,0:T(8,128)(2,1)S(1)}, u32[]{:S(2)}, u32[]{:S(2)}) collective-permute-start(bf16[272,128]{1,0:T(8,128)(2,1)S(1)} %get-tuple-element.57), channel_id=1, source_target_pairs={{0,3},{1,2},{2,1},{3,0},{4,7},{5,6},{6,5},{7,4},{8,11},{9,10},{10,... | collective-permute-start | bytes 208904 | tf_op jit(solution)/shard_map/ppermute | solution.py:303
  32.4 2.7 %collective-permute-start.14 = (bf16[272,128]{1,0:T(8,128)(2,1)S(1)}, bf16[272,128]{1,0:T(8,128)(2,1)S(1)}, u32[]{:S(2)}, u32[]{:S(2)}) collective-permute-start(bf16[272,128]{1,0:T(8,128)(2,1)S(1)} %get-tuple-element.59), channel_id=1, source_target_pairs={{0,6},{1,7},{2,4},{3,5},{4,2},{5,3},{6,0},{7,1},{8,14},{9,15},{10,... | collective-permute-start | bytes 208904 | tf_op jit(solution)/shard_map/ppermute | solution.py:303
  35.1 0.0 collective-permute-done.10.refs_0_
  35.1 0.6 %collective-permute-start.15 = (bf16[272,128]{1,0:T(8,128)(2,1)S(1)}, bf16[272,128]{1,0:T(8,128)(2,1)S(1)}, u32[]{:S(2)}, u32[]{:S(2)}) collective-permute-start(bf16[272,128]{1,0:T(8,128)(2,1)S(1)} %get-tuple-element.60), channel_id=1, source_target_pairs={{0,7},{1,6},{2,5},{3,4},{4,3},{5,2},{6,1},{7,0},{8,15},{9,14},{10,... | collective-permute-start | bytes 208904 | tf_op jit(solution)/shard_map/ppermute | solution.py:303
  35.7 1.1 %collective-permute-done.11.refs_1_ = bf16[272,128]{1,0:T(8,128)(2,1)S(1)} collective-permute-done((bf16[272,128]{1,0:T(8,128)(2,1)S(1)}, bf16[272,128]{1,0:T(8,128)(2,1)S(1)}, u32[]{:S(2)}, u32[]{:S(2)}) %collective-permute-start.11) | collective-permute-done | bytes 69664 | tf_op jit(solution)/shard_map/ppermute | solution.py:303
  36.8 1.9 %collective-permute-start.16 = (bf16[272,128]{1,0:T(8,128)(2,1)S(1)}, bf16[272,128]{1,0:T(8,128)(2,1)S(1)}, u32[]{:S(2)}, u32[]{:S(2)}) collective-permute-start(bf16[272,128]{1,0:T(8,128)(2,1)S(1)} %get-tuple-element.61), channel_id=1, source_target_pairs={{0,1},{1,0},{2,3},{3,2},{4,5},{5,4},{6,7},{7,6},{8,9},{9,8},{10,11... | collective-permute-start | bytes 208904 | tf_op jit(solution)/shard_map/ppermute | solution.py:303
  38.6 0.0 collective-permute-done.12.refs_2_
  38.7 0.0 collective-permute-done.13.refs_3_
  38.7 0.3 early.1
  39.0 1.3 %collective-permute-done.14.refs_5_ = bf16[272,128]{1,0:T(8,128)(2,1)S(1)} collective-permute-done((bf16[272,128]{1,0:T(8,128)(2,1)S(1)}, bf16[272,128]{1,0:T(8,128)(2,1)S(1)}, u32[]{:S(2)}, u32[]{:S(2)}) %collective-permute-start.14) | collective-permute-done | bytes 69664 | tf_op jit(solution)/shard_map/ppermute | solution.py:303
  40.3 1.7 %collective-permute-done.15.refs_6_ = bf16[272,128]{1,0:T(8,128)(2,1)S(1)} collective-permute-done((bf16[272,128]{1,0:T(8,128)(2,1)S(1)}, bf16[272,128]{1,0:T(8,128)(2,1)S(1)}, u32[]{:S(2)}, u32[]{:S(2)}) %collective-permute-start.15) | collective-permute-done | bytes 69664 | tf_op jit(solution)/shard_map/ppermute | solution.py:303
  42.0 0.0 collective-permute-done.16.refs_7_
  42.0 1.2 %outputs.1 = (f32[128,1024]{1,0:T(8,128)}, f32[128,1024]{1,0:T(8,128)}, f32[1,1024]{1,0:T(1,128)}) custom-call(bf16[272,128]{1,0:T(8,128)(2,1)S(1)} %collective-permute-done.10.refs_0_, bf16[272,128]{1,0:T(8,128)(2,1)S(1)} %collective-permute-done.11.refs_1_, bf16[272,128]{1,0:T(8,128)(2,1)S(1)} %collective-permute-done.12.refs_2_, ...), custom_call_target="tpu_custom_call" | custom-call | flops 1000000000 | tf_op jit(solution)/shard_map/outputs/pallas_call | solution.py:424
  (15 shorter events, 0.1 us)
Async XLA Ops:
  0.7 1.1 %copy-start.5 = (bf16[128,1024]{1,0:T(8,128)(2,1)S(1)}, bf16[128,1024]{1,0:T(8,128)(2,1)}, u32[]{:S(2)}) copy-start(bf16[128,1024]{1,0:T(8,128)(2,1)} %param.8) | copy-start | bytes 786436
  0.7 1.1 %copy-start.6 = (bf16[128,1024]{1,0:T(8,128)(2,1)S(1)}, bf16[128,1024]{1,0:T(8,128)(2,1)}, u32[]{:S(2)}) copy-start(bf16[128,1024]{1,0:T(8,128)(2,1)} %param.7) | copy-start | bytes 786436
  2.0 5.3 %collective-permute-start = (bf16[1280,128]{1,0:T(8,128)(2,1)S(1)}, bf16[1280,128]{1,0:T(8,128)(2,1)S(1)}, u32[]{:S(2)}, u32[]{:S(2)}) collective-permute-start(bf16[1280,128]{1,0:T(8,128)(2,1)S(1)} %get-tuple-element.36), channel_id=1, source_target_pairs={{0,1},{1,0},{2,3},{3,2},{4,5},{5,4},{6,7},{7,6},{8,9},{9,8},{10,11... | collective-permute-start | bytes 983048 | tf_op jit(solution)/shard_map/ppermute | solution.py:303
  2.5 9.1 %collective-permute-start.1 = (bf16[256,128]{1,0:T(8,128)(2,1)S(1)}, bf16[256,128]{1,0:T(8,128)(2,1)S(1)}, u32[]{:S(2)}, u32[]{:S(2)}) collective-permute-start(bf16[256,128]{1,0:T(8,128)(2,1)S(1)} %get-tuple-element.37), channel_id=1, source_target_pairs={{0,6},{1,7},{2,4},{3,5},{4,2},{5,3},{6,0},{7,1},{8,14},{9,15},{10,... | collective-permute-start | bytes 196616 | tf_op jit(solution)/shard_map/ppermute | solution.py:303
  7.2 6.0 %collective-permute-start.2 = (bf16[256,128]{1,0:T(8,128)(2,1)S(1)}, bf16[256,128]{1,0:T(8,128)(2,1)S(1)}, u32[]{:S(2)}, u32[]{:S(2)}) collective-permute-start(bf16[256,128]{1,0:T(8,128)(2,1)S(1)} %get-tuple-element.38), channel_id=1, source_target_pairs={{0,7},{1,6},{2,5},{3,4},{4,3},{5,2},{6,1},{7,0},{8,15},{9,14},{10,... | collective-permute-start | bytes 196616 | tf_op jit(solution)/shard_map/ppermute | solution.py:303
  7.4 11.2 %collective-permute-start.5 = (bf16[768,128]{1,0:T(8,128)(2,1)S(1)}, bf16[768,128]{1,0:T(8,128)(2,1)S(1)}, u32[]{:S(2)}, u32[]{:S(2)}) collective-permute-start(bf16[768,128]{1,0:T(8,128)(2,1)S(1)} %pad_maximum_fusion), channel_id=1, source_target_pairs={{0,2},{1,3},{2,0},{3,1},{4,6},{5,7},{6,4},{7,5},{8,10},{9,11},{10,... | collective-permute-start | bytes 589832 | tf_op jit(solution)/shard_map/ppermute | solution.py:303
  7.5 5.8 %copy-start.2 = (bf16[256,256]{1,0:T(8,128)(2,1)S(1)}, bf16[256,256]{1,0:T(8,128)(2,1)}, u32[]{:S(2)}) copy-start(bf16[256,256]{1,0:T(8,128)(2,1)} %constant.44.clone.refs_0_) | copy-start | bytes 393220
  7.5 5.8 %copy-start.3 = (bf16[128,256]{1,0:T(8,128)(2,1)S(1)}, bf16[128,256]{1,0:T(8,128)(2,1)}, u32[]{:S(2)}) copy-start(bf16[128,256]{1,0:T(8,128)(2,1)} %constant.46.clone.refs_2_) | copy-start | bytes 196612
  7.5 5.8 %copy-start.4 = (bf16[128,256]{1,0:T(8,128)(2,1)S(1)}, bf16[128,256]{1,0:T(8,128)(2,1)}, u32[]{:S(2)}) copy-start(bf16[128,256]{1,0:T(8,128)(2,1)} %constant.45.clone.refs_1_) | copy-start | bytes 196612
  7.5 10.6 %collective-permute-start.6 = (bf16[512,128]{1,0:T(8,128)(2,1)S(1)}, bf16[512,128]{1,0:T(8,128)(2,1)S(1)}, u32[]{:S(2)}, u32[]{:S(2)}) collective-permute-start(bf16[512,128]{1,0:T(8,128)(2,1)S(1)} %pad_maximum_fusion.1), channel_id=1, source_target_pairs={{0,4},{1,5},{2,6},{3,7},{4,0},{5,1},{6,2},{7,3},{8,12},{9,13},{10,... | collective-permute-start | bytes 393224 | tf_op jit(solution)/shard_map/ppermute | solution.py:303
  13.3 10.4 %collective-permute-start.3 = (bf16[256,128]{1,0:T(8,128)(2,1)S(1)}, bf16[256,128]{1,0:T(8,128)(2,1)S(1)}, u32[]{:S(2)}, u32[]{:S(2)}) collective-permute-start(bf16[256,128]{1,0:T(8,128)(2,1)S(1)} %get-tuple-element.41), channel_id=1, source_target_pairs={{0,6},{1,7},{2,4},{3,5},{4,2},{5,3},{6,0},{7,1},{8,14},{9,15},{10,... | collective-permute-start | bytes 196616 | tf_op jit(solution)/shard_map/ppermute | solution.py:303
  14.7 10.1 %collective-permute-start.4 = (bf16[256,128]{1,0:T(8,128)(2,1)S(1)}, bf16[256,128]{1,0:T(8,128)(2,1)S(1)}, u32[]{:S(2)}, u32[]{:S(2)}) collective-permute-start(bf16[256,128]{1,0:T(8,128)(2,1)S(1)} %get-tuple-element.42), channel_id=1, source_target_pairs={{0,4},{1,5},{2,6},{3,7},{4,0},{5,1},{6,2},{7,3},{8,12},{9,13},{10,... | collective-permute-start | bytes 196616 | tf_op jit(solution)/shard_map/ppermute | solution.py:303
  20.1 6.5 %collective-permute-start.9 = (f32[8,128]{1,0:T(8,128)S(1)}, f32[8,128]{1,0:T(8,128)S(1)}, u32[]{:S(2)}, u32[]{:S(2)}) collective-permute-start(f32[8,128]{1,0:T(8,128)S(1)} %get-tuple-element.53.refs_4_), channel_id=1, source_target_pairs={{0,24},{8,16},{16,8},{24,0},{1,25},{9,17},{17,9},{25,1},{2,26},{10... | collective-permute-start | bytes 12296 | tf_op jit(solution)/shard_map/ppermute | solution.py:381
  22.8 3.8 %collective-permute-start.8 = (f32[8,128]{1,0:T(8,128)S(1)}, f32[8,128]{1,0:T(8,128)S(1)}, u32[]{:S(2)}, u32[]{:S(2)}) collective-permute-start(f32[8,128]{1,0:T(8,128)S(1)} %get-tuple-element.53.refs_4_), channel_id=1, source_target_pairs={{0,16},{8,24},{16,0},{24,8},{1,17},{9,25},{17,1},{25,9},{2,18},{10... | collective-permute-start | bytes 12296 | tf_op jit(solution)/shard_map/ppermute | solution.py:381
  23.3 3.6 %collective-permute-start.7 = (f32[8,128]{1,0:T(8,128)S(1)}, f32[8,128]{1,0:T(8,128)S(1)}, u32[]{:S(2)}, u32[]{:S(2)}) collective-permute-start(f32[8,128]{1,0:T(8,128)S(1)} %get-tuple-element.53.refs_4_), channel_id=1, source_target_pairs={{0,8},{8,0},{16,24},{24,16},{1,9},{9,1},{17,25},{25,17},{2,10},{10... | collective-permute-start | bytes 12296 | tf_op jit(solution)/shard_map/ppermute | solution.py:381
  26.9 11.8 %copy-start = (bf16[128,1024]{1,0:T(8,128)(2,1)S(1)}, bf16[128,1024]{1,0:T(8,128)(2,1)}, u32[]{:S(2)}) copy-start(bf16[128,1024]{1,0:T(8,128)(2,1)} %refs_10_.1) | copy-start | bytes 786436
  27.0 8.1 %collective-permute-start.10 = (bf16[272,128]{1,0:T(8,128)(2,1)S(1)}, bf16[272,128]{1,0:T(8,128)(2,1)S(1)}, u32[]{:S(2)}, u32[]{:S(2)}) collective-permute-start(bf16[272,128]{1,0:T(8,128)(2,1)S(1)} %get-tuple-element.54), channel_id=1, source_target_pairs={{0,4},{1,5},{2,6},{3,7},{4,0},{5,1},{6,2},{7,3},{8,12},{9,13},{10,... | collective-permute-start | bytes 208904 | tf_op jit(solution)/shard_map/ppermute | solution.py:303
  29.9 6.8 %collective-permute-start.11 = (bf16[272,128]{1,0:T(8,128)(2,1)S(1)}, bf16[272,128]{1,0:T(8,128)(2,1)S(1)}, u32[]{:S(2)}, u32[]{:S(2)}) collective-permute-start(bf16[272,128]{1,0:T(8,128)(2,1)S(1)} %get-tuple-element.55), channel_id=1, source_target_pairs={{0,5},{1,4},{2,7},{3,6},{4,1},{5,0},{6,3},{7,2},{8,13},{9,12},{10,... | collective-permute-start | bytes 208904 | tf_op jit(solution)/shard_map/ppermute | solution.py:303
  29.9 8.7 %collective-permute-start.12 = (bf16[272,128]{1,0:T(8,128)(2,1)S(1)}, bf16[272,128]{1,0:T(8,128)(2,1)S(1)}, u32[]{:S(2)}, u32[]{:S(2)}) collective-permute-start(bf16[272,128]{1,0:T(8,128)(2,1)S(1)} %get-tuple-element.56), channel_id=1, source_target_pairs={{0,2},{1,3},{2,0},{3,1},{4,6},{5,7},{6,4},{7,5},{8,10},{9,11},{10,... | collective-permute-start | bytes 208904 | tf_op jit(solution)/shard_map/ppermute | solution.py:303
  31.3 7.4 %collective-permute-start.13 = (bf16[272,128]{1,0:T(8,128)(2,1)S(1)}, bf16[272,128]{1,0:T(8,128)(2,1)S(1)}, u32[]{:S(2)}, u32[]{:S(2)}) collective-permute-start(bf16[272,128]{1,0:T(8,128)(2,1)S(1)} %get-tuple-element.57), channel_id=1, source_target_pairs={{0,3},{1,2},{2,1},{3,0},{4,7},{5,6},{6,5},{7,4},{8,11},{9,10},{10,... | collective-permute-start | bytes 208904 | tf_op jit(solution)/shard_map/ppermute | solution.py:303
  32.4 6.2 %copy-start.1 = (f32[1024]{0:T(1024)S(1)}, f32[1024]{0:T(1024)}, u32[]{:S(2)}) copy-start(f32[1024]{0:T(1024)} %param.10) | copy-start | bytes 12292
  32.4 7.9 %collective-permute-start.14 = (bf16[272,128]{1,0:T(8,128)(2,1)S(1)}, bf16[272,128]{1,0:T(8,128)(2,1)S(1)}, u32[]{:S(2)}, u32[]{:S(2)}) collective-permute-start(bf16[272,128]{1,0:T(8,128)(2,1)S(1)} %get-tuple-element.59), channel_id=1, source_target_pairs={{0,6},{1,7},{2,4},{3,5},{4,2},{5,3},{6,0},{7,1},{8,14},{9,15},{10,... | collective-permute-start | bytes 208904 | tf_op jit(solution)/shard_map/ppermute | solution.py:303
  35.1 6.9 %collective-permute-start.15 = (bf16[272,128]{1,0:T(8,128)(2,1)S(1)}, bf16[272,128]{1,0:T(8,128)(2,1)S(1)}, u32[]{:S(2)}, u32[]{:S(2)}) collective-permute-start(bf16[272,128]{1,0:T(8,128)(2,1)S(1)} %get-tuple-element.60), channel_id=1, source_target_pairs={{0,7},{1,6},{2,5},{3,4},{4,3},{5,2},{6,1},{7,0},{8,15},{9,14},{10,... | collective-permute-start | bytes 208904 | tf_op jit(solution)/shard_map/ppermute | solution.py:303
  36.8 5.3 %collective-permute-start.16 = (bf16[272,128]{1,0:T(8,128)(2,1)S(1)}, bf16[272,128]{1,0:T(8,128)(2,1)S(1)}, u32[]{:S(2)}, u32[]{:S(2)}) collective-permute-start(bf16[272,128]{1,0:T(8,128)(2,1)S(1)} %get-tuple-element.61), channel_id=1, source_target_pairs={{0,1},{1,0},{2,3},{3,2},{4,5},{5,4},{6,7},{7,6},{8,9},{9,8},{10,11... | collective-permute-start | bytes 208904 | tf_op jit(solution)/shard_map/ppermute | solution.py:303

commit v10 on v9

--- a/solution.py
+++ b/solution.py
@@ -173,10 +173,16 @@
     send_results(position, order, acc, back_high, back_low, emit)
 
 
+def code_kernel(size, width, blocks, skip, filter_codes, filter_tails):
+    skip_parts = three_parts(skip[...])
+    for i in range(size):
+        filter_codes[i], scale = encode(blocks[i])
+        filter_tails[i] = tail_tile(0, (scale,) + skip_parts, width)
+
+
 def second_kernel(order, length, places, *refs):
     size = len(order)
-    both, back_high, back_low, pair_spec, blocks, skip = refs[-12:-6]
-    filter_codes, filter_tails, input_codes, input_tails, spec, acc = refs[-6:]
+    both, back_high, back_low, pair_spec, input_codes, input_tails, spec, acc = refs[-8:]
     width = spec.shape[2]
     position = lax.axis_index("ctx")
 
@@ -201,11 +207,6 @@
         return carry
 
     lax.fori_loop(0, length // 8, rows, 0, unroll=2)
-
-    skip_parts = three_parts(skip[...])
-    for i in range(size):
-        filter_codes[i], scale = encode(blocks[i])
-        filter_tails[i] = tail_tile(0, (scale,) + skip_parts, width)
 
     def emit(i, block):
         input_codes[i], scale = encode(block)
@@ -381,25 +382,29 @@
         squares if k == 0 else lax.ppermute(squares, "chan", [(i, i ^ k) for i in range(columns)])
         for k in range(columns)
     ]
-    codes_and_tails = run(
+    coded = [
+        jax.ShapeDtypeStruct((size, length, width), bf16),
+        jax.ShapeDtypeStruct((size, tail_rows, width), f32),
+    ]
+    filter_coded = run(
+        functools.partial(code_kernel, size, width), "filter_codes", vmem_bytes, coded, flops=first_flops
+    )(filter_blocks, skip)
+    pair_spec, *filter_coded = lax.optimization_barrier((pair_spec, *filter_coded))
+    input_coded = run(
         functools.partial(second_kernel, order, length, second_places),
         "input_gradient", vmem_bytes,
-        [
-            jax.ShapeDtypeStruct((size, length, width), bf16),
-            jax.ShapeDtypeStruct((size, tail_rows, width), f32),
-        ]
-        * 2,
+        coded,
         [
             pltpu.VMEM((size, 2 * length, width), f32),
             pltpu.VMEM((size, 2 * length, width), f32),
         ],
         flops=second_flops,
-    )(*second_arrived, both, back_high, back_low, pair_spec, filter_blocks, skip)
+    )(*second_arrived, both, back_high, back_low, pair_spec)
     messages = run(
         functools.partial(message_kernel, size, length, columns),
         "messages", vmem_bytes,
         [jax.ShapeDtypeStruct((2 * length + tail_rows, width), bf16)] * size,
-    )(*codes_and_tails, *all_squares)
+    )(*filter_coded, *input_coded, *all_squares[::-1])
     messages = {k: send(message, k) if k else message for k, message in zip(order, messages)}
     nearer = sorted(chips[:far])
     turns = nearer[: far // 2] + chips[far:-1] + nearer[far // 2 :] + [0]

time: 43.4 us -> 43.4 us (level)
  transfers between devices with their start and end apart: 17 -> 17, of which waited for: 8 -> 8; matrix products, arithmetic and copies ran while one was open for 0% -> 0% of each run, Pallas kernels for 8% -> 9%
where the time goes in v10:
time: 43.4 us; the launch traced here: 43.2 us
  starting transfers between devices  25.3 us (58%)
  waiting for transfers between devices  10.7 us (25%)
  Pallas kernels  5.19 us (12%)
  local copies, waits for them, and re-layouts  1.22 us (3%)
  between operations  0.84 us (2%)
    ppermute x14, starting transfers between devices, send(): return lax.ppermute(block, 'ctx', [(i, i ^ k) for i in range(size)])  21.7 us
    ppermute x14, waiting for transfers between devices, send(): return lax.ppermute(block, 'ctx', [(i, i ^ k) for i in range(size)])  10.2 us
    ppermute x3, starting transfers between devices, per_device(): lax.ppermute(squares, 'chan', [(i, i ^ k) for i in range(columns)])  3.55 us
    pallas_call x1, Pallas kernels, per_device(): run(functools.partial(first_kernel, order, length, first_places), 'filter...  1.54 us
    pallas_call x1, Pallas kernels, per_device(): run(functools.partial(second_kernel, order, length, second_places), 'inpu...  1.52 us
    pallas_call x1, Pallas kernels, per_device(): run(functools.partial(last_kernel, turns, early, length, width, clip_limi...  1.22 us
    dynamic_slice x2, local copies, waits for them, and re-layouts, per_device(): lax.dynamic_slice_in_dim(array, (position // half * half ^ other) * part,...  1.08 us
  transfers between devices with their start and end apart: 17, of which 8 were waited for; matrix products, arithmetic and copies ran while one was open for 0% of the time, Pallas kernels for 9%

profile of v10, /device:TPU:0, one launch (start us, length us, event | category | flops | bytes accessed | tf_op | source)
XLA Modules:
  0.0 43.2 jit_solution(8420100701707234124)
XLA Ops:
  0.7 1.0 %constant_dynamic-slice_fusion.4 = (bf16[128,512]{1,0:T(8,128)(2,1)S(1)}, bf16[128,512]{1,0:T(8,128)(2,1)S(1)}) fusion(bf16[128,1024]{1,0:T(8,128)(2,1)} %refs_10_.1, s32[]{:T(128)S(6)} %select_n.22, s32[]{:T(128)S(6)} %select_n.21), kind=kLoop, calls=%fused_computation.6 | loop fusion | bytes 524296 | tf_op jit(solution)/shard_map/dynamic_slice | solution.py:317
  1.7 0.1 copy-done.6
  1.9 0.2 columns.1
  2.0 0.5 %collective-permute-start.2 = (bf16[1280,128]{1,0:T(8,128)(2,1)S(1)}, bf16[1280,128]{1,0:T(8,128)(2,1)S(1)}, u32[]{:S(2)}, u32[]{:S(2)}) collective-permute-start(bf16[1280,128]{1,0:T(8,128)(2,1)S(1)} %get-tuple-element.41), channel_id=1, source_target_pairs={{0,1},{1,0},{2,3},{3,2},{4,5},{5,4},{6,7},{7,6},{8,9},{9,8},{10,11... | collective-permute-start | bytes 983048 | tf_op jit(solution)/shard_map/ppermute | solution.py:304
  2.5 4.7 %collective-permute-start = (bf16[256,128]{1,0:T(8,128)(2,1)S(1)}, bf16[256,128]{1,0:T(8,128)(2,1)S(1)}, u32[]{:S(2)}, u32[]{:S(2)}) collective-permute-start(bf16[256,128]{1,0:T(8,128)(2,1)S(1)} %get-tuple-element.38), channel_id=1, source_target_pairs={{0,6},{1,7},{2,4},{3,5},{4,2},{5,3},{6,0},{7,1},{8,14},{9,15},{10,... | collective-permute-start | bytes 196616 | tf_op jit(solution)/shard_map/ppermute | solution.py:304
  7.2 0.1 collective-permute-start.1
  7.3 0.0 collective-permute-done.2.sibling.refs_5_.refs_4_
  7.4 0.1 collective-permute-start.4
  7.5 0.0 copy-start.2
  7.5 0.0 copy-start.3
  7.5 0.0 copy-start.4
  7.5 4.1 %collective-permute-start.3 = (bf16[512,128]{1,0:T(8,128)(2,1)S(1)}, bf16[512,128]{1,0:T(8,128)(2,1)S(1)}, u32[]{:S(2)}, u32[]{:S(2)}) collective-permute-start(bf16[512,128]{1,0:T(8,128)(2,1)S(1)} %pad_maximum_fusion.1), channel_id=1, source_target_pairs={{0,4},{1,5},{2,6},{3,7},{4,0},{5,1},{6,2},{7,3},{8,12},{9,13},{10,... | collective-permute-start | bytes 393224 | tf_op jit(solution)/shard_map/ppermute | solution.py:304
  11.6 0.0 collective-permute-done.refs_0_
  11.6 1.6 %collective-permute-done.1.refs_1_ = bf16[256,128]{1,0:T(8,128)(2,1)S(1)} collective-permute-done((bf16[256,128]{1,0:T(8,128)(2,1)S(1)}, bf16[256,128]{1,0:T(8,128)(2,1)S(1)}, u32[]{:S(2)}, u32[]{:S(2)}) %collective-permute-start.1) | collective-permute-done | bytes 65568 | tf_op jit(solution)/shard_map/ppermute | solution.py:304
  13.2 0.0 copy-done.2
  13.3 1.4 %collective-permute-start.5 = (bf16[256,128]{1,0:T(8,128)(2,1)S(1)}, bf16[256,128]{1,0:T(8,128)(2,1)S(1)}, u32[]{:S(2)}, u32[]{:S(2)}) collective-permute-start(bf16[256,128]{1,0:T(8,128)(2,1)S(1)} %get-tuple-element.54), channel_id=1, source_target_pairs={{0,6},{1,7},{2,4},{3,5},{4,2},{5,3},{6,0},{7,1},{8,14},{9,15},{10,... | collective-permute-start | bytes 196616 | tf_op jit(solution)/shard_map/ppermute | solution.py:304
  14.7 0.3 collective-permute-start.6
  15.0 3.2 %collective-permute-done.3.refs_2_ = bf16[512,128]{1,0:T(8,128)(2,1)S(1)} collective-permute-done((bf16[512,128]{1,0:T(8,128)(2,1)S(1)}, bf16[512,128]{1,0:T(8,128)(2,1)S(1)}, u32[]{:S(2)}, u32[]{:S(2)}) %collective-permute-start.3) | collective-permute-done | bytes 131104 | tf_op jit(solution)/shard_map/ppermute | solution.py:304
  18.2 0.4 collective-permute-done.4.refs_3_.refs_2_
  18.6 1.5 %filter_gradient.1 = (f32[8,128,128]{2,1,0:T(8,128)S(1)}, f32[1,128]{1,0:T(1,128)S(1)}, f32[8,256,128]{2,1,0:T(8,128)S(1)}, f32[8,128]{1,0:T(8,128)S(1)}) custom-call(bf16[256,128]{1,0:T(8,128)(2,1)S(1)} %collective-permute-done.refs_0_, bf16[256,128]{1,0:T(8,128)(2,1)S(1)} %collective-permute-done.1.refs_1_, ...), custom_call_target="tpu_custom_call" | custom-call | flops 4000000000 | tf_op jit(solution)/shard_map/filter_gradient/pallas_call | solution.py:366
  20.1 2.6 %collective-permute-start.7 = (f32[8,128]{1,0:T(8,128)S(1)}, f32[8,128]{1,0:T(8,128)S(1)}, u32[]{:S(2)}, u32[]{:S(2)}) collective-permute-start(f32[8,128]{1,0:T(8,128)S(1)} %get-tuple-element.59.refs_7_), channel_id=1, source_target_pairs={{0,24},{8,16},{16,8},{24,0},{1,25},{9,17},{17,9},{25,1},{2,26},{10... | collective-permute-start | bytes 12296 | tf_op jit(solution)/shard_map/ppermute | solution.py:382
  22.8 0.5 %collective-permute-start.8 = (f32[8,128]{1,0:T(8,128)S(1)}, f32[8,128]{1,0:T(8,128)S(1)}, u32[]{:S(2)}, u32[]{:S(2)}) collective-permute-start(f32[8,128]{1,0:T(8,128)S(1)} %get-tuple-element.59.refs_7_), channel_id=1, source_target_pairs={{0,16},{8,24},{16,0},{24,8},{1,17},{9,25},{17,1},{25,9},{2,18},{10... | collective-permute-start | bytes 12296 | tf_op jit(solution)/shard_map/ppermute | solution.py:382
  23.3 0.4 collective-permute-start.9
  23.7 0.3 filter_codes.1
  24.0 0.0 collective-permute-done.5.refs_0_
  24.0 0.9 %collective-permute-done.6.refs_1_ = bf16[256,128]{1,0:T(8,128)(2,1)S(1)} collective-permute-done((bf16[256,128]{1,0:T(8,128)(2,1)S(1)}, bf16[256,128]{1,0:T(8,128)(2,1)S(1)}, u32[]{:S(2)}, u32[]{:S(2)}) %collective-permute-start.6) | collective-permute-done | bytes 65568 | tf_op jit(solution)/shard_map/ppermute | solution.py:304
  24.8 1.5 %input_gradient.1 = (bf16[8,128,128]{2,1,0:T(8,128)(2,1)S(1)}, f32[8,16,128]{2,1,0:T(8,128)S(1)}) custom-call(bf16[256,128]{1,0:T(8,128)(2,1)S(1)} %collective-permute-done.5.refs_0_, bf16[256,128]{1,0:T(8,128)(2,1)S(1)} %collective-permute-done.6.refs_1_, bf16[768,128]{1,0:T(8,128)(2,1)S(1)} %collective-permute-done.4.refs_3_.refs_2_, ...), custom_call_target="tpu_custom_call" | custom-call | flops 20000000000 | tf_op jit(solution)/shard_map/input_gradient/pallas_call | solution.py:393
  26.4 0.0 collective-permute-done.7.refs_4_
  26.4 0.0 collective-permute-done.8.refs_5_
  26.4 0.5 %collective-permute-done.9.refs_6_ = f32[8,128]{1,0:T(8,128)S(1)} collective-permute-done((f32[8,128]{1,0:T(8,128)S(1)}, f32[8,128]{1,0:T(8,128)S(1)}, u32[]{:S(2)}, u32[]{:S(2)}) %collective-permute-start.9) | collective-permute-done | bytes 4128 | tf_op jit(solution)/shard_map/ppermute | solution.py:382
  26.9 0.1 messages.1
  27.0 2.9 %collective-permute-start.10 = (bf16[272,128]{1,0:T(8,128)(2,1)S(1)}, bf16[272,128]{1,0:T(8,128)(2,1)S(1)}, u32[]{:S(2)}, u32[]{:S(2)}) collective-permute-start(bf16[272,128]{1,0:T(8,128)(2,1)S(1)} %get-tuple-element.60), channel_id=1, source_target_pairs={{0,4},{1,5},{2,6},{3,7},{4,0},{5,1},{6,2},{7,3},{8,12},{9,13},{10,... | collective-permute-start | bytes 208904 | tf_op jit(solution)/shard_map/ppermute | solution.py:304
  29.9 0.0 collective-permute-start.11
  29.9 1.4 %collective-permute-start.12 = (bf16[272,128]{1,0:T(8,128)(2,1)S(1)}, bf16[272,128]{1,0:T(8,128)(2,1)S(1)}, u32[]{:S(2)}, u32[]{:S(2)}) collective-permute-start(bf16[272,128]{1,0:T(8,128)(2,1)S(1)} %get-tuple-element.62), channel_id=1, source_target_pairs={{0,2},{1,3},{2,0},{3,1},{4,6},{5,7},{6,4},{7,5},{8,10},{9,11},{10,... | collective-permute-start | bytes 208904 | tf_op jit(solution)/shard_map/ppermute | solution.py:304
  31.3 1.2 %collective-permute-start.13 = (bf16[272,128]{1,0:T(8,128)(2,1)S(1)}, bf16[272,128]{1,0:T(8,128)(2,1)S(1)}, u32[]{:S(2)}, u32[]{:S(2)}) collective-permute-start(bf16[272,128]{1,0:T(8,128)(2,1)S(1)} %get-tuple-element.63), channel_id=1, source_target_pairs={{0,3},{1,2},{2,1},{3,0},{4,7},{5,6},{6,5},{7,4},{8,11},{9,10},{10,... | collective-permute-start | bytes 208904 | tf_op jit(solution)/shard_map/ppermute | solution.py:304
  32.4 2.7 %collective-permute-start.14 = (bf16[272,128]{1,0:T(8,128)(2,1)S(1)}, bf16[272,128]{1,0:T(8,128)(2,1)S(1)}, u32[]{:S(2)}, u32[]{:S(2)}) collective-permute-start(bf16[272,128]{1,0:T(8,128)(2,1)S(1)} %get-tuple-element.65), channel_id=1, source_target_pairs={{0,6},{1,7},{2,4},{3,5},{4,2},{5,3},{6,0},{7,1},{8,14},{9,15},{10,... | collective-permute-start | bytes 208904 | tf_op jit(solution)/shard_map/ppermute | solution.py:304
  35.1 0.0 collective-permute-done.10.refs_0_
  35.1 0.6 %collective-permute-start.15 = (bf16[272,128]{1,0:T(8,128)(2,1)S(1)}, bf16[272,128]{1,0:T(8,128)(2,1)S(1)}, u32[]{:S(2)}, u32[]{:S(2)}) collective-permute-start(bf16[272,128]{1,0:T(8,128)(2,1)S(1)} %get-tuple-element.66), channel_id=1, source_target_pairs={{0,7},{1,6},{2,5},{3,4},{4,3},{5,2},{6,1},{7,0},{8,15},{9,14},{10,... | collective-permute-start | bytes 208904 | tf_op jit(solution)/shard_map/ppermute | solution.py:304
  35.7 1.1 %collective-permute-done.11.refs_1_ = bf16[272,128]{1,0:T(8,128)(2,1)S(1)} collective-permute-done((bf16[272,128]{1,0:T(8,128)(2,1)S(1)}, bf16[272,128]{1,0:T(8,128)(2,1)S(1)}, u32[]{:S(2)}, u32[]{:S(2)}) %collective-permute-start.11) | collective-permute-done | bytes 69664 | tf_op jit(solution)/shard_map/ppermute | solution.py:304
  36.8 1.9 %collective-permute-start.16 = (bf16[272,128]{1,0:T(8,128)(2,1)S(1)}, bf16[272,128]{1,0:T(8,128)(2,1)S(1)}, u32[]{:S(2)}, u32[]{:S(2)}) collective-permute-start(bf16[272,128]{1,0:T(8,128)(2,1)S(1)} %get-tuple-element.67), channel_id=1, source_target_pairs={{0,1},{1,0},{2,3},{3,2},{4,5},{5,4},{6,7},{7,6},{8,9},{9,8},{10,11... | collective-permute-start | bytes 208904 | tf_op jit(solution)/shard_map/ppermute | solution.py:304
  38.7 0.0 collective-permute-done.12.refs_2_
  38.7 0.0 collective-permute-done.13.refs_3_
  38.7 0.0 copy-done
  38.7 0.3 early.1
  39.0 1.3 %collective-permute-done.14.refs_5_ = bf16[272,128]{1,0:T(8,128)(2,1)S(1)} collective-permute-done((bf16[272,128]{1,0:T(8,128)(2,1)S(1)}, bf16[272,128]{1,0:T(8,128)(2,1)S(1)}, u32[]{:S(2)}, u32[]{:S(2)}) %collective-permute-start.14) | collective-permute-done | bytes 69664 | tf_op jit(solution)/shard_map/ppermute | solution.py:304
  40.3 1.7 %collective-permute-done.15.refs_6_ = bf16[272,128]{1,0:T(8,128)(2,1)S(1)} collective-permute-done((bf16[272,128]{1,0:T(8,128)(2,1)S(1)}, bf16[272,128]{1,0:T(8,128)(2,1)S(1)}, u32[]{:S(2)}, u32[]{:S(2)}) %collective-permute-start.15) | collective-permute-done | bytes 69664 | tf_op jit(solution)/shard_map/ppermute | solution.py:304
  42.0 0.0 collective-permute-done.16.refs_7_
  42.0 1.2 %outputs.1 = (f32[128,1024]{1,0:T(8,128)}, f32[128,1024]{1,0:T(8,128)}, f32[1,1024]{1,0:T(1,128)}) custom-call(bf16[272,128]{1,0:T(8,128)(2,1)S(1)} %collective-permute-done.10.refs_0_, bf16[272,128]{1,0:T(8,128)(2,1)S(1)} %collective-permute-done.11.refs_1_, bf16[272,128]{1,0:T(8,128)(2,1)S(1)} %collective-permute-done.12.refs_2_, ...), custom_call_target="tpu_custom_call" | custom-call | flops 1000000000 | tf_op jit(solution)/shard_map/outputs/pallas_call | solution.py:429
  (16 shorter events, 0.1 us)
Async XLA Ops:
  0.7 1.1 %copy-start.5 = (bf16[128,1024]{1,0:T(8,128)(2,1)S(1)}, bf16[128,1024]{1,0:T(8,128)(2,1)}, u32[]{:S(2)}) copy-start(bf16[128,1024]{1,0:T(8,128)(2,1)} %param.8) | copy-start | bytes 786436
  0.7 1.1 %copy-start.6 = (bf16[128,1024]{1,0:T(8,128)(2,1)S(1)}, bf16[128,1024]{1,0:T(8,128)(2,1)}, u32[]{:S(2)}) copy-start(bf16[128,1024]{1,0:T(8,128)(2,1)} %param.7) | copy-start | bytes 786436
  2.0 5.3 %collective-permute-start.2 = (bf16[1280,128]{1,0:T(8,128)(2,1)S(1)}, bf16[1280,128]{1,0:T(8,128)(2,1)S(1)}, u32[]{:S(2)}, u32[]{:S(2)}) collective-permute-start(bf16[1280,128]{1,0:T(8,128)(2,1)S(1)} %get-tuple-element.41), channel_id=1, source_target_pairs={{0,1},{1,0},{2,3},{3,2},{4,5},{5,4},{6,7},{7,6},{8,9},{9,8},{10,11... | collective-permute-start | bytes 983048 | tf_op jit(solution)/shard_map/ppermute | solution.py:304
  2.5 9.1 %collective-permute-start = (bf16[256,128]{1,0:T(8,128)(2,1)S(1)}, bf16[256,128]{1,0:T(8,128)(2,1)S(1)}, u32[]{:S(2)}, u32[]{:S(2)}) collective-permute-start(bf16[256,128]{1,0:T(8,128)(2,1)S(1)} %get-tuple-element.38), channel_id=1, source_target_pairs={{0,6},{1,7},{2,4},{3,5},{4,2},{5,3},{6,0},{7,1},{8,14},{9,15},{10,... | collective-permute-start | bytes 196616 | tf_op jit(solution)/shard_map/ppermute | solution.py:304
  7.2 6.0 %collective-permute-start.1 = (bf16[256,128]{1,0:T(8,128)(2,1)S(1)}, bf16[256,128]{1,0:T(8,128)(2,1)S(1)}, u32[]{:S(2)}, u32[]{:S(2)}) collective-permute-start(bf16[256,128]{1,0:T(8,128)(2,1)S(1)} %get-tuple-element.39), channel_id=1, source_target_pairs={{0,7},{1,6},{2,5},{3,4},{4,3},{5,2},{6,1},{7,0},{8,15},{9,14},{10,... | collective-permute-start | bytes 196616 | tf_op jit(solution)/shard_map/ppermute | solution.py:304
  7.4 11.2 %collective-permute-start.4 = (bf16[768,128]{1,0:T(8,128)(2,1)S(1)}, bf16[768,128]{1,0:T(8,128)(2,1)S(1)}, u32[]{:S(2)}, u32[]{:S(2)}) collective-permute-start(bf16[768,128]{1,0:T(8,128)(2,1)S(1)} %pad_maximum_fusion), channel_id=1, source_target_pairs={{0,2},{1,3},{2,0},{3,1},{4,6},{5,7},{6,4},{7,5},{8,10},{9,11},{10,... | collective-permute-start | bytes 589832 | tf_op jit(solution)/shard_map/ppermute | solution.py:304
  7.5 5.8 %copy-start.2 = (bf16[256,256]{1,0:T(8,128)(2,1)S(1)}, bf16[256,256]{1,0:T(8,128)(2,1)}, u32[]{:S(2)}) copy-start(bf16[256,256]{1,0:T(8,128)(2,1)} %constant.44.clone.refs_0_) | copy-start | bytes 393220
  7.5 5.8 %copy-start.3 = (bf16[128,256]{1,0:T(8,128)(2,1)S(1)}, bf16[128,256]{1,0:T(8,128)(2,1)}, u32[]{:S(2)}) copy-start(bf16[128,256]{1,0:T(8,128)(2,1)} %constant.45.clone.refs_1_) | copy-start | bytes 196612
  7.5 5.8 %copy-start.4 = (bf16[128,256]{1,0:T(8,128)(2,1)S(1)}, bf16[128,256]{1,0:T(8,128)(2,1)}, u32[]{:S(2)}) copy-start(bf16[128,256]{1,0:T(8,128)(2,1)} %constant.46.clone.refs_2_) | copy-start | bytes 196612
  7.5 10.6 %collective-permute-start.3 = (bf16[512,128]{1,0:T(8,128)(2,1)S(1)}, bf16[512,128]{1,0:T(8,128)(2,1)S(1)}, u32[]{:S(2)}, u32[]{:S(2)}) collective-permute-start(bf16[512,128]{1,0:T(8,128)(2,1)S(1)} %pad_maximum_fusion.1), channel_id=1, source_target_pairs={{0,4},{1,5},{2,6},{3,7},{4,0},{5,1},{6,2},{7,3},{8,12},{9,13},{10,... | collective-permute-start | bytes 393224 | tf_op jit(solution)/shard_map/ppermute | solution.py:304
  13.3 10.7 %collective-permute-start.5 = (bf16[256,128]{1,0:T(8,128)(2,1)S(1)}, bf16[256,128]{1,0:T(8,128)(2,1)S(1)}, u32[]{:S(2)}, u32[]{:S(2)}) collective-permute-start(bf16[256,128]{1,0:T(8,128)(2,1)S(1)} %get-tuple-element.54), channel_id=1, source_target_pairs={{0,6},{1,7},{2,4},{3,5},{4,2},{5,3},{6,0},{7,1},{8,14},{9,15},{10,... | collective-permute-start | bytes 196616 | tf_op jit(solution)/shard_map/ppermute | solution.py:304
  14.7 10.1 %collective-permute-start.6 = (bf16[256,128]{1,0:T(8,128)(2,1)S(1)}, bf16[256,128]{1,0:T(8,128)(2,1)S(1)}, u32[]{:S(2)}, u32[]{:S(2)}) collective-permute-start(bf16[256,128]{1,0:T(8,128)(2,1)S(1)} %get-tuple-element.55), channel_id=1, source_target_pairs={{0,4},{1,5},{2,6},{3,7},{4,0},{5,1},{6,2},{7,3},{8,12},{9,13},{10,... | collective-permute-start | bytes 196616 | tf_op jit(solution)/shard_map/ppermute | solution.py:304
  20.1 6.2 %collective-permute-start.7 = (f32[8,128]{1,0:T(8,128)S(1)}, f32[8,128]{1,0:T(8,128)S(1)}, u32[]{:S(2)}, u32[]{:S(2)}) collective-permute-start(f32[8,128]{1,0:T(8,128)S(1)} %get-tuple-element.59.refs_7_), channel_id=1, source_target_pairs={{0,24},{8,16},{16,8},{24,0},{1,25},{9,17},{17,9},{25,1},{2,26},{10... | collective-permute-start | bytes 12296 | tf_op jit(solution)/shard_map/ppermute | solution.py:382
  22.8 3.6 %collective-permute-start.8 = (f32[8,128]{1,0:T(8,128)S(1)}, f32[8,128]{1,0:T(8,128)S(1)}, u32[]{:S(2)}, u32[]{:S(2)}) collective-permute-start(f32[8,128]{1,0:T(8,128)S(1)} %get-tuple-element.59.refs_7_), channel_id=1, source_target_pairs={{0,16},{8,24},{16,0},{24,8},{1,17},{9,25},{17,1},{25,9},{2,18},{10... | collective-permute-start | bytes 12296 | tf_op jit(solution)/shard_map/ppermute | solution.py:382
  23.3 3.6 %collective-permute-start.9 = (f32[8,128]{1,0:T(8,128)S(1)}, f32[8,128]{1,0:T(8,128)S(1)}, u32[]{:S(2)}, u32[]{:S(2)}) collective-permute-start(f32[8,128]{1,0:T(8,128)S(1)} %get-tuple-element.59.refs_7_), channel_id=1, source_target_pairs={{0,8},{8,0},{16,24},{24,16},{1,9},{9,1},{17,25},{25,17},{2,10},{10... | collective-permute-start | bytes 12296 | tf_op jit(solution)/shard_map/ppermute | solution.py:382
  26.9 11.8 %copy-start = (bf16[128,1024]{1,0:T(8,128)(2,1)S(1)}, bf16[128,1024]{1,0:T(8,128)(2,1)}, u32[]{:S(2)}) copy-start(bf16[128,1024]{1,0:T(8,128)(2,1)} %refs_10_.1) | copy-start | bytes 786436
  27.0 8.1 %collective-permute-start.10 = (bf16[272,128]{1,0:T(8,128)(2,1)S(1)}, bf16[272,128]{1,0:T(8,128)(2,1)S(1)}, u32[]{:S(2)}, u32[]{:S(2)}) collective-permute-start(bf16[272,128]{1,0:T(8,128)(2,1)S(1)} %get-tuple-element.60), channel_id=1, source_target_pairs={{0,4},{1,5},{2,6},{3,7},{4,0},{5,1},{6,2},{7,3},{8,12},{9,13},{10,... | collective-permute-start | bytes 208904 | tf_op jit(solution)/shard_map/ppermute | solution.py:304
  29.9 6.8 %collective-permute-start.11 = (bf16[272,128]{1,0:T(8,128)(2,1)S(1)}, bf16[272,128]{1,0:T(8,128)(2,1)S(1)}, u32[]{:S(2)}, u32[]{:S(2)}) collective-permute-start(bf16[272,128]{1,0:T(8,128)(2,1)S(1)} %get-tuple-element.61), channel_id=1, source_target_pairs={{0,5},{1,4},{2,7},{3,6},{4,1},{5,0},{6,3},{7,2},{8,13},{9,12},{10,... | collective-permute-start | bytes 208904 | tf_op jit(solution)/shard_map/ppermute | solution.py:304
  29.9 8.7 %collective-permute-start.12 = (bf16[272,128]{1,0:T(8,128)(2,1)S(1)}, bf16[272,128]{1,0:T(8,128)(2,1)S(1)}, u32[]{:S(2)}, u32[]{:S(2)}) collective-permute-start(bf16[272,128]{1,0:T(8,128)(2,1)S(1)} %get-tuple-element.62), channel_id=1, source_target_pairs={{0,2},{1,3},{2,0},{3,1},{4,6},{5,7},{6,4},{7,5},{8,10},{9,11},{10,... | collective-permute-start | bytes 208904 | tf_op jit(solution)/shard_map/ppermute | solution.py:304
  31.3 7.4 %collective-permute-start.13 = (bf16[272,128]{1,0:T(8,128)(2,1)S(1)}, bf16[272,128]{1,0:T(8,128)(2,1)S(1)}, u32[]{:S(2)}, u32[]{:S(2)}) collective-permute-start(bf16[272,128]{1,0:T(8,128)(2,1)S(1)} %get-tuple-element.63), channel_id=1, source_target_pairs={{0,3},{1,2},{2,1},{3,0},{4,7},{5,6},{6,5},{7,4},{8,11},{9,10},{10,... | collective-permute-start | bytes 208904 | tf_op jit(solution)/shard_map/ppermute | solution.py:304
  32.4 6.2 %copy-start.1 = (f32[1024]{0:T(1024)S(1)}, f32[1024]{0:T(1024)}, u32[]{:S(2)}) copy-start(f32[1024]{0:T(1024)} %param.10) | copy-start | bytes 12292
  32.4 7.9 %collective-permute-start.14 = (bf16[272,128]{1,0:T(8,128)(2,1)S(1)}, bf16[272,128]{1,0:T(8,128)(2,1)S(1)}, u32[]{:S(2)}, u32[]{:S(2)}) collective-permute-start(bf16[272,128]{1,0:T(8,128)(2,1)S(1)} %get-tuple-element.65), channel_id=1, source_target_pairs={{0,6},{1,7},{2,4},{3,5},{4,2},{5,3},{6,0},{7,1},{8,14},{9,15},{10,... | collective-permute-start | bytes 208904 | tf_op jit(solution)/shard_map/ppermute | solution.py:304
  35.1 6.9 %collective-permute-start.15 = (bf16[272,128]{1,0:T(8,128)(2,1)S(1)}, bf16[272,128]{1,0:T(8,128)(2,1)S(1)}, u32[]{:S(2)}, u32[]{:S(2)}) collective-permute-start(bf16[272,128]{1,0:T(8,128)(2,1)S(1)} %get-tuple-element.66), channel_id=1, source_target_pairs={{0,7},{1,6},{2,5},{3,4},{4,3},{5,2},{6,1},{7,0},{8,15},{9,14},{10,... | collective-permute-start | bytes 208904 | tf_op jit(solution)/shard_map/ppermute | solution.py:304
  36.8 5.3 %collective-permute-start.16 = (bf16[272,128]{1,0:T(8,128)(2,1)S(1)}, bf16[272,128]{1,0:T(8,128)(2,1)S(1)}, u32[]{:S(2)}, u32[]{:S(2)}) collective-permute-start(bf16[272,128]{1,0:T(8,128)(2,1)S(1)} %get-tuple-element.67), channel_id=1, source_target_pairs={{0,1},{1,0},{2,3},{3,2},{4,5},{5,4},{6,7},{7,6},{8,9},{9,8},{10,11... | collective-permute-start | bytes 208904 | tf_op jit(solution)/shard_map/ppermute | solution.py:304

commit v11 on v10

--- a/solution.py
+++ b/solution.py
@@ -418,8 +418,8 @@
             a.reshape(a.shape[0], size, part), ((0, 0), (0, 0), (0, width - part))
         ).reshape(a.shape[0], whole)
         grad_rows, gain = spread(grad_rows), spread(gain)
-    turns = turns[: size // 2] + [0] + [k for k in turns[size // 2 :] if k]
-    early = size // 2 + 1
+    early = size // 2 + 2
+    turns = turns[: early - 1] + [0] + [k for k in turns[early - 1 :] if k]
     decoded = run(
         functools.partial(early_kernel, turns[:early], length, width),
         "early", vmem_bytes,

time: 43.4 us -> 43.3 us (level)
  no operation moved by 1% of the time
where the time goes in v11:
time: 43.3 us; the launch traced here: 43.2 us
  starting transfers between devices  25.3 us (58%)
  waiting for transfers between devices  10.6 us (24%)
  Pallas kernels  5.17 us (12%)
  local copies, waits for them, and re-layouts  1.22 us (3%)
  between operations  0.83 us (2%)
    ppermute x14, starting transfers between devices, send(): return lax.ppermute(block, 'ctx', [(i, i ^ k) for i in range(size)])  21.7 us
    ppermute x14, waiting for transfers between devices, send(): return lax.ppermute(block, 'ctx', [(i, i ^ k) for i in range(size)])  10.1 us
    ppermute x3, starting transfers between devices, per_device(): lax.ppermute(squares, 'chan', [(i, i ^ k) for i in range(columns)])  3.55 us
    pallas_call x1, Pallas kernels, per_device(): run(functools.partial(first_kernel, order, length, first_places), 'filter...  1.54 us
    pallas_call x1, Pallas kernels, per_device(): run(functools.partial(second_kernel, order, length, second_places), 'inpu...  1.52 us
    pallas_call x1, Pallas kernels, per_device(): run(functools.partial(last_kernel, turns, early, length, width, clip_limi...  1.15 us
    dynamic_slice x2, local copies, waits for them, and re-layouts, per_device(): lax.dynamic_slice_in_dim(array, (position // half * half ^ other) * part,...  1.08 us
  transfers between devices with their start and end apart: 17, of which 8 were waited for; matrix products, arithmetic and copies ran while one was open for 0% of the time, Pallas kernels for 9%

profile of v11, /device:TPU:0, one launch (start us, length us, event | category | flops | bytes accessed | tf_op | source)
XLA Modules:
  0.0 43.2 jit_solution(16259138363081987338)
XLA Ops:
  0.7 0.0 copy-start.5
  0.7 1.0 %constant_dynamic-slice_fusion.4 = (bf16[128,512]{1,0:T(8,128)(2,1)S(1)}, bf16[128,512]{1,0:T(8,128)(2,1)S(1)}) fusion(bf16[128,1024]{1,0:T(8,128)(2,1)} %refs_10_.1, s32[]{:T(128)S(6)} %select_n.22, s32[]{:T(128)S(6)} %select_n.21), kind=kLoop, calls=%fused_computation.6 | loop fusion | bytes 524296 | tf_op jit(solution)/shard_map/dynamic_slice | solution.py:317
  1.7 0.1 copy-done.6
  1.9 0.2 columns.1
  2.0 0.5 %collective-permute-start.2 = (bf16[1280,128]{1,0:T(8,128)(2,1)S(1)}, bf16[1280,128]{1,0:T(8,128)(2,1)S(1)}, u32[]{:S(2)}, u32[]{:S(2)}) collective-permute-start(bf16[1280,128]{1,0:T(8,128)(2,1)S(1)} %get-tuple-element.41), channel_id=1, source_target_pairs={{0,1},{1,0},{2,3},{3,2},{4,5},{5,4},{6,7},{7,6},{8,9},{9,8},{10,11... | collective-permute-start | bytes 983048 | tf_op jit(solution)/shard_map/ppermute | solution.py:304
  2.5 4.7 %collective-permute-start = (bf16[256,128]{1,0:T(8,128)(2,1)S(1)}, bf16[256,128]{1,0:T(8,128)(2,1)S(1)}, u32[]{:S(2)}, u32[]{:S(2)}) collective-permute-start(bf16[256,128]{1,0:T(8,128)(2,1)S(1)} %get-tuple-element.38), channel_id=1, source_target_pairs={{0,6},{1,7},{2,4},{3,5},{4,2},{5,3},{6,0},{7,1},{8,14},{9,15},{10,... | collective-permute-start | bytes 196616 | tf_op jit(solution)/shard_map/ppermute | solution.py:304
  7.2 0.1 collective-permute-start.1
  7.3 0.0 collective-permute-done.2.sibling.refs_5_.refs_4_
  7.4 0.1 collective-permute-start.4
  7.5 0.0 copy-start.2
  7.5 0.0 copy-start.3
  7.5 0.0 copy-start.4
  7.5 4.1 %collective-permute-start.3 = (bf16[512,128]{1,0:T(8,128)(2,1)S(1)}, bf16[512,128]{1,0:T(8,128)(2,1)S(1)}, u32[]{:S(2)}, u32[]{:S(2)}) collective-permute-start(bf16[512,128]{1,0:T(8,128)(2,1)S(1)} %pad_maximum_fusion.1), channel_id=1, source_target_pairs={{0,4},{1,5},{2,6},{3,7},{4,0},{5,1},{6,2},{7,3},{8,12},{9,13},{10,... | collective-permute-start | bytes 393224 | tf_op jit(solution)/shard_map/ppermute | solution.py:304
  11.6 0.0 collective-permute-done.refs_0_
  11.6 1.6 %collective-permute-done.1.refs_1_ = bf16[256,128]{1,0:T(8,128)(2,1)S(1)} collective-permute-done((bf16[256,128]{1,0:T(8,128)(2,1)S(1)}, bf16[256,128]{1,0:T(8,128)(2,1)S(1)}, u32[]{:S(2)}, u32[]{:S(2)}) %collective-permute-start.1) | collective-permute-done | bytes 65568 | tf_op jit(solution)/shard_map/ppermute | solution.py:304
  13.3 1.4 %collective-permute-start.5 = (bf16[256,128]{1,0:T(8,128)(2,1)S(1)}, bf16[256,128]{1,0:T(8,128)(2,1)S(1)}, u32[]{:S(2)}, u32[]{:S(2)}) collective-permute-start(bf16[256,128]{1,0:T(8,128)(2,1)S(1)} %get-tuple-element.54), channel_id=1, source_target_pairs={{0,6},{1,7},{2,4},{3,5},{4,2},{5,3},{6,0},{7,1},{8,14},{9,15},{10,... | collective-permute-start | bytes 196616 | tf_op jit(solution)/shard_map/ppermute | solution.py:304
  14.7 0.3 collective-permute-start.6
  15.0 3.2 %collective-permute-done.3.refs_2_ = bf16[512,128]{1,0:T(8,128)(2,1)S(1)} collective-permute-done((bf16[512,128]{1,0:T(8,128)(2,1)S(1)}, bf16[512,128]{1,0:T(8,128)(2,1)S(1)}, u32[]{:S(2)}, u32[]{:S(2)}) %collective-permute-start.3) | collective-permute-done | bytes 131104 | tf_op jit(solution)/shard_map/ppermute | solution.py:304
  18.2 0.4 collective-permute-done.4.refs_3_.refs_2_
  18.6 1.5 %filter_gradient.1 = (f32[8,128,128]{2,1,0:T(8,128)S(1)}, f32[1,128]{1,0:T(1,128)S(1)}, f32[8,256,128]{2,1,0:T(8,128)S(1)}, f32[8,128]{1,0:T(8,128)S(1)}) custom-call(bf16[256,128]{1,0:T(8,128)(2,1)S(1)} %collective-permute-done.refs_0_, bf16[256,128]{1,0:T(8,128)(2,1)S(1)} %collective-permute-done.1.refs_1_, ...), custom_call_target="tpu_custom_call" | custom-call | flops 4000000000 | tf_op jit(solution)/shard_map/filter_gradient/pallas_call | solution.py:366
  20.1 2.6 %collective-permute-start.7 = (f32[8,128]{1,0:T(8,128)S(1)}, f32[8,128]{1,0:T(8,128)S(1)}, u32[]{:S(2)}, u32[]{:S(2)}) collective-permute-start(f32[8,128]{1,0:T(8,128)S(1)} %get-tuple-element.59.refs_7_), channel_id=1, source_target_pairs={{0,24},{8,16},{16,8},{24,0},{1,25},{9,17},{17,9},{25,1},{2,26},{10... | collective-permute-start | bytes 12296 | tf_op jit(solution)/shard_map/ppermute | solution.py:382
  22.8 0.5 %collective-permute-start.8 = (f32[8,128]{1,0:T(8,128)S(1)}, f32[8,128]{1,0:T(8,128)S(1)}, u32[]{:S(2)}, u32[]{:S(2)}) collective-permute-start(f32[8,128]{1,0:T(8,128)S(1)} %get-tuple-element.59.refs_7_), channel_id=1, source_target_pairs={{0,16},{8,24},{16,0},{24,8},{1,17},{9,25},{17,1},{25,9},{2,18},{10... | collective-permute-start | bytes 12296 | tf_op jit(solution)/shard_map/ppermute | solution.py:382
  23.3 0.4 collective-permute-start.9
  23.7 0.3 filter_codes.1
  24.0 0.0 collective-permute-done.5.refs_0_
  24.0 0.9 %collective-permute-done.6.refs_1_ = bf16[256,128]{1,0:T(8,128)(2,1)S(1)} collective-permute-done((bf16[256,128]{1,0:T(8,128)(2,1)S(1)}, bf16[256,128]{1,0:T(8,128)(2,1)S(1)}, u32[]{:S(2)}, u32[]{:S(2)}) %collective-permute-start.6) | collective-permute-done | bytes 65568 | tf_op jit(solution)/shard_map/ppermute | solution.py:304
  24.8 1.5 %input_gradient.1 = (bf16[8,128,128]{2,1,0:T(8,128)(2,1)S(1)}, f32[8,16,128]{2,1,0:T(8,128)S(1)}) custom-call(bf16[256,128]{1,0:T(8,128)(2,1)S(1)} %collective-permute-done.5.refs_0_, bf16[256,128]{1,0:T(8,128)(2,1)S(1)} %collective-permute-done.6.refs_1_, bf16[768,128]{1,0:T(8,128)(2,1)S(1)} %collective-permute-done.4.refs_3_.refs_2_, ...), custom_call_target="tpu_custom_call" | custom-call | flops 20000000000 | tf_op jit(solution)/shard_map/input_gradient/pallas_call | solution.py:393
  26.4 0.0 collective-permute-done.7.refs_4_
  26.4 0.0 collective-permute-done.8.refs_5_
  26.4 0.5 %collective-permute-done.9.refs_6_ = f32[8,128]{1,0:T(8,128)S(1)} collective-permute-done((f32[8,128]{1,0:T(8,128)S(1)}, f32[8,128]{1,0:T(8,128)S(1)}, u32[]{:S(2)}, u32[]{:S(2)}) %collective-permute-start.9) | collective-permute-done | bytes 4128 | tf_op jit(solution)/shard_map/ppermute | solution.py:382
  26.9 0.1 messages.1
  27.0 2.9 %collective-permute-start.10 = (bf16[272,128]{1,0:T(8,128)(2,1)S(1)}, bf16[272,128]{1,0:T(8,128)(2,1)S(1)}, u32[]{:S(2)}, u32[]{:S(2)}) collective-permute-start(bf16[272,128]{1,0:T(8,128)(2,1)S(1)} %get-tuple-element.60), channel_id=1, source_target_pairs={{0,4},{1,5},{2,6},{3,7},{4,0},{5,1},{6,2},{7,3},{8,12},{9,13},{10,... | collective-permute-start | bytes 208904 | tf_op jit(solution)/shard_map/ppermute | solution.py:304
  29.9 0.0 collective-permute-start.11
  29.9 1.4 %collective-permute-start.12 = (bf16[272,128]{1,0:T(8,128)(2,1)S(1)}, bf16[272,128]{1,0:T(8,128)(2,1)S(1)}, u32[]{:S(2)}, u32[]{:S(2)}) collective-permute-start(bf16[272,128]{1,0:T(8,128)(2,1)S(1)} %get-tuple-element.62), channel_id=1, source_target_pairs={{0,2},{1,3},{2,0},{3,1},{4,6},{5,7},{6,4},{7,5},{8,10},{9,11},{10,... | collective-permute-start | bytes 208904 | tf_op jit(solution)/shard_map/ppermute | solution.py:304
  31.3 1.2 %collective-permute-start.13 = (bf16[272,128]{1,0:T(8,128)(2,1)S(1)}, bf16[272,128]{1,0:T(8,128)(2,1)S(1)}, u32[]{:S(2)}, u32[]{:S(2)}) collective-permute-start(bf16[272,128]{1,0:T(8,128)(2,1)S(1)} %get-tuple-element.63), channel_id=1, source_target_pairs={{0,3},{1,2},{2,1},{3,0},{4,7},{5,6},{6,5},{7,4},{8,11},{9,10},{10,... | collective-permute-start | bytes 208904 | tf_op jit(solution)/shard_map/ppermute | solution.py:304
  32.4 2.7 %collective-permute-start.14 = (bf16[272,128]{1,0:T(8,128)(2,1)S(1)}, bf16[272,128]{1,0:T(8,128)(2,1)S(1)}, u32[]{:S(2)}, u32[]{:S(2)}) collective-permute-start(bf16[272,128]{1,0:T(8,128)(2,1)S(1)} %get-tuple-element.64), channel_id=1, source_target_pairs={{0,6},{1,7},{2,4},{3,5},{4,2},{5,3},{6,0},{7,1},{8,14},{9,15},{10,... | collective-permute-start | bytes 208904 | tf_op jit(solution)/shard_map/ppermute | solution.py:304
  35.1 0.0 collective-permute-done.10.refs_0_
  35.1 0.6 %collective-permute-start.15 = (bf16[272,128]{1,0:T(8,128)(2,1)S(1)}, bf16[272,128]{1,0:T(8,128)(2,1)S(1)}, u32[]{:S(2)}, u32[]{:S(2)}) collective-permute-start(bf16[272,128]{1,0:T(8,128)(2,1)S(1)} %get-tuple-element.66), channel_id=1, source_target_pairs={{0,7},{1,6},{2,5},{3,4},{4,3},{5,2},{6,1},{7,0},{8,15},{9,14},{10,... | collective-permute-start | bytes 208904 | tf_op jit(solution)/shard_map/ppermute | solution.py:304
  35.7 1.1 %collective-permute-done.11.refs_1_ = bf16[272,128]{1,0:T(8,128)(2,1)S(1)} collective-permute-done((bf16[272,128]{1,0:T(8,128)(2,1)S(1)}, bf16[272,128]{1,0:T(8,128)(2,1)S(1)}, u32[]{:S(2)}, u32[]{:S(2)}) %collective-permute-start.11) | collective-permute-done | bytes 69664 | tf_op jit(solution)/shard_map/ppermute | solution.py:304
  36.8 1.9 %collective-permute-start.16 = (bf16[272,128]{1,0:T(8,128)(2,1)S(1)}, bf16[272,128]{1,0:T(8,128)(2,1)S(1)}, u32[]{:S(2)}, u32[]{:S(2)}) collective-permute-start(bf16[272,128]{1,0:T(8,128)(2,1)S(1)} %get-tuple-element.67), channel_id=1, source_target_pairs={{0,1},{1,0},{2,3},{3,2},{4,5},{5,4},{6,7},{7,6},{8,9},{9,8},{10,11... | collective-permute-start | bytes 208904 | tf_op jit(solution)/shard_map/ppermute | solution.py:304
  38.7 0.0 collective-permute-done.12.refs_2_
  38.7 0.0 collective-permute-done.13.refs_3_
  38.7 1.7 %collective-permute-done.14.refs_4_ = bf16[272,128]{1,0:T(8,128)(2,1)S(1)} collective-permute-done((bf16[272,128]{1,0:T(8,128)(2,1)S(1)}, bf16[272,128]{1,0:T(8,128)(2,1)S(1)}, u32[]{:S(2)}, u32[]{:S(2)}) %collective-permute-start.14) | collective-permute-done | bytes 69664 | tf_op jit(solution)/shard_map/ppermute | solution.py:304
  40.3 0.0 copy-done
  40.3 0.4 early.1
  40.7 1.3 %collective-permute-done.15.refs_6_ = bf16[272,128]{1,0:T(8,128)(2,1)S(1)} collective-permute-done((bf16[272,128]{1,0:T(8,128)(2,1)S(1)}, bf16[272,128]{1,0:T(8,128)(2,1)S(1)}, u32[]{:S(2)}, u32[]{:S(2)}) %collective-permute-start.15) | collective-permute-done | bytes 69664 | tf_op jit(solution)/shard_map/ppermute | solution.py:304
  42.0 0.0 collective-permute-done.16.refs_7_
  42.0 1.1 %outputs.1 = (f32[128,1024]{1,0:T(8,128)}, f32[128,1024]{1,0:T(8,128)}, f32[1,1024]{1,0:T(1,128)}) custom-call(bf16[272,128]{1,0:T(8,128)(2,1)S(1)} %collective-permute-done.10.refs_0_, bf16[272,128]{1,0:T(8,128)(2,1)S(1)} %collective-permute-done.11.refs_1_, bf16[272,128]{1,0:T(8,128)(2,1)S(1)} %collective-permute-done.12.refs_2_, ...), custom_call_target="tpu_custom_call" | custom-call | flops 1000000000 | tf_op jit(solution)/shard_map/outputs/pallas_call | solution.py:429
  (16 shorter events, 0.1 us)
Async XLA Ops:
  0.7 1.1 %copy-start.5 = (bf16[128,1024]{1,0:T(8,128)(2,1)S(1)}, bf16[128,1024]{1,0:T(8,128)(2,1)}, u32[]{:S(2)}) copy-start(bf16[128,1024]{1,0:T(8,128)(2,1)} %param.8) | copy-start | bytes 786436
  0.7 1.1 %copy-start.6 = (bf16[128,1024]{1,0:T(8,128)(2,1)S(1)}, bf16[128,1024]{1,0:T(8,128)(2,1)}, u32[]{:S(2)}) copy-start(bf16[128,1024]{1,0:T(8,128)(2,1)} %param.7) | copy-start | bytes 786436
  2.0 5.3 %collective-permute-start.2 = (bf16[1280,128]{1,0:T(8,128)(2,1)S(1)}, bf16[1280,128]{1,0:T(8,128)(2,1)S(1)}, u32[]{:S(2)}, u32[]{:S(2)}) collective-permute-start(bf16[1280,128]{1,0:T(8,128)(2,1)S(1)} %get-tuple-element.41), channel_id=1, source_target_pairs={{0,1},{1,0},{2,3},{3,2},{4,5},{5,4},{6,7},{7,6},{8,9},{9,8},{10,11... | collective-permute-start | bytes 983048 | tf_op jit(solution)/shard_map/ppermute | solution.py:304
  2.5 9.1 %collective-permute-start = (bf16[256,128]{1,0:T(8,128)(2,1)S(1)}, bf16[256,128]{1,0:T(8,128)(2,1)S(1)}, u32[]{:S(2)}, u32[]{:S(2)}) collective-permute-start(bf16[256,128]{1,0:T(8,128)(2,1)S(1)} %get-tuple-element.38), channel_id=1, source_target_pairs={{0,6},{1,7},{2,4},{3,5},{4,2},{5,3},{6,0},{7,1},{8,14},{9,15},{10,... | collective-permute-start | bytes 196616 | tf_op jit(solution)/shard_map/ppermute | solution.py:304
  7.2 6.0 %collective-permute-start.1 = (bf16[256,128]{1,0:T(8,128)(2,1)S(1)}, bf16[256,128]{1,0:T(8,128)(2,1)S(1)}, u32[]{:S(2)}, u32[]{:S(2)}) collective-permute-start(bf16[256,128]{1,0:T(8,128)(2,1)S(1)} %get-tuple-element.39), channel_id=1, source_target_pairs={{0,7},{1,6},{2,5},{3,4},{4,3},{5,2},{6,1},{7,0},{8,15},{9,14},{10,... | collective-permute-start | bytes 196616 | tf_op jit(solution)/shard_map/ppermute | solution.py:304
  7.4 11.2 %collective-permute-start.4 = (bf16[768,128]{1,0:T(8,128)(2,1)S(1)}, bf16[768,128]{1,0:T(8,128)(2,1)S(1)}, u32[]{:S(2)}, u32[]{:S(2)}) collective-permute-start(bf16[768,128]{1,0:T(8,128)(2,1)S(1)} %pad_maximum_fusion), channel_id=1, source_target_pairs={{0,2},{1,3},{2,0},{3,1},{4,6},{5,7},{6,4},{7,5},{8,10},{9,11},{10,... | collective-permute-start | bytes 589832 | tf_op jit(solution)/shard_map/ppermute | solution.py:304
  7.5 5.8 %copy-start.2 = (bf16[256,256]{1,0:T(8,128)(2,1)S(1)}, bf16[256,256]{1,0:T(8,128)(2,1)}, u32[]{:S(2)}) copy-start(bf16[256,256]{1,0:T(8,128)(2,1)} %constant.44.clone.refs_0_) | copy-start | bytes 393220
  7.5 5.8 %copy-start.3 = (bf16[128,256]{1,0:T(8,128)(2,1)S(1)}, bf16[128,256]{1,0:T(8,128)(2,1)}, u32[]{:S(2)}) copy-start(bf16[128,256]{1,0:T(8,128)(2,1)} %constant.45.clone.refs_1_) | copy-start | bytes 196612
  7.5 5.8 %copy-start.4 = (bf16[128,256]{1,0:T(8,128)(2,1)S(1)}, bf16[128,256]{1,0:T(8,128)(2,1)}, u32[]{:S(2)}) copy-start(bf16[128,256]{1,0:T(8,128)(2,1)} %constant.46.clone.refs_2_) | copy-start | bytes 196612
  7.5 10.6 %collective-permute-start.3 = (bf16[512,128]{1,0:T(8,128)(2,1)S(1)}, bf16[512,128]{1,0:T(8,128)(2,1)S(1)}, u32[]{:S(2)}, u32[]{:S(2)}) collective-permute-start(bf16[512,128]{1,0:T(8,128)(2,1)S(1)} %pad_maximum_fusion.1), channel_id=1, source_target_pairs={{0,4},{1,5},{2,6},{3,7},{4,0},{5,1},{6,2},{7,3},{8,12},{9,13},{10,... | collective-permute-start | bytes 393224 | tf_op jit(solution)/shard_map/ppermute | solution.py:304
  13.3 10.7 %collective-permute-start.5 = (bf16[256,128]{1,0:T(8,128)(2,1)S(1)}, bf16[256,128]{1,0:T(8,128)(2,1)S(1)}, u32[]{:S(2)}, u32[]{:S(2)}) collective-permute-start(bf16[256,128]{1,0:T(8,128)(2,1)S(1)} %get-tuple-element.54), channel_id=1, source_target_pairs={{0,6},{1,7},{2,4},{3,5},{4,2},{5,3},{6,0},{7,1},{8,14},{9,15},{10,... | collective-permute-start | bytes 196616 | tf_op jit(solution)/shard_map/ppermute | solution.py:304
  14.7 10.1 %collective-permute-start.6 = (bf16[256,128]{1,0:T(8,128)(2,1)S(1)}, bf16[256,128]{1,0:T(8,128)(2,1)S(1)}, u32[]{:S(2)}, u32[]{:S(2)}) collective-permute-start(bf16[256,128]{1,0:T(8,128)(2,1)S(1)} %get-tuple-element.55), channel_id=1, source_target_pairs={{0,4},{1,5},{2,6},{3,7},{4,0},{5,1},{6,2},{7,3},{8,12},{9,13},{10,... | collective-permute-start | bytes 196616 | tf_op jit(solution)/shard_map/ppermute | solution.py:304
  20.1 6.2 %collective-permute-start.7 = (f32[8,128]{1,0:T(8,128)S(1)}, f32[8,128]{1,0:T(8,128)S(1)}, u32[]{:S(2)}, u32[]{:S(2)}) collective-permute-start(f32[8,128]{1,0:T(8,128)S(1)} %get-tuple-element.59.refs_7_), channel_id=1, source_target_pairs={{0,24},{8,16},{16,8},{24,0},{1,25},{9,17},{17,9},{25,1},{2,26},{10... | collective-permute-start | bytes 12296 | tf_op jit(solution)/shard_map/ppermute | solution.py:382
  22.8 3.6 %collective-permute-start.8 = (f32[8,128]{1,0:T(8,128)S(1)}, f32[8,128]{1,0:T(8,128)S(1)}, u32[]{:S(2)}, u32[]{:S(2)}) collective-permute-start(f32[8,128]{1,0:T(8,128)S(1)} %get-tuple-element.59.refs_7_), channel_id=1, source_target_pairs={{0,16},{8,24},{16,0},{24,8},{1,17},{9,25},{17,1},{25,9},{2,18},{10... | collective-permute-start | bytes 12296 | tf_op jit(solution)/shard_map/ppermute | solution.py:382
  23.3 3.6 %collective-permute-start.9 = (f32[8,128]{1,0:T(8,128)S(1)}, f32[8,128]{1,0:T(8,128)S(1)}, u32[]{:S(2)}, u32[]{:S(2)}) collective-permute-start(f32[8,128]{1,0:T(8,128)S(1)} %get-tuple-element.59.refs_7_), channel_id=1, source_target_pairs={{0,8},{8,0},{16,24},{24,16},{1,9},{9,1},{17,25},{25,17},{2,10},{10... | collective-permute-start | bytes 12296 | tf_op jit(solution)/shard_map/ppermute | solution.py:382
  26.9 13.5 %copy-start = (bf16[128,1024]{1,0:T(8,128)(2,1)S(1)}, bf16[128,1024]{1,0:T(8,128)(2,1)}, u32[]{:S(2)}) copy-start(bf16[128,1024]{1,0:T(8,128)(2,1)} %refs_10_.1) | copy-start | bytes 786436
  27.0 8.1 %collective-permute-start.10 = (bf16[272,128]{1,0:T(8,128)(2,1)S(1)}, bf16[272,128]{1,0:T(8,128)(2,1)S(1)}, u32[]{:S(2)}, u32[]{:S(2)}) collective-permute-start(bf16[272,128]{1,0:T(8,128)(2,1)S(1)} %get-tuple-element.60), channel_id=1, source_target_pairs={{0,4},{1,5},{2,6},{3,7},{4,0},{5,1},{6,2},{7,3},{8,12},{9,13},{10,... | collective-permute-start | bytes 208904 | tf_op jit(solution)/shard_map/ppermute | solution.py:304
  29.9 6.8 %collective-permute-start.11 = (bf16[272,128]{1,0:T(8,128)(2,1)S(1)}, bf16[272,128]{1,0:T(8,128)(2,1)S(1)}, u32[]{:S(2)}, u32[]{:S(2)}) collective-permute-start(bf16[272,128]{1,0:T(8,128)(2,1)S(1)} %get-tuple-element.61), channel_id=1, source_target_pairs={{0,5},{1,4},{2,7},{3,6},{4,1},{5,0},{6,3},{7,2},{8,13},{9,12},{10,... | collective-permute-start | bytes 208904 | tf_op jit(solution)/shard_map/ppermute | solution.py:304
  29.9 8.7 %collective-permute-start.12 = (bf16[272,128]{1,0:T(8,128)(2,1)S(1)}, bf16[272,128]{1,0:T(8,128)(2,1)S(1)}, u32[]{:S(2)}, u32[]{:S(2)}) collective-permute-start(bf16[272,128]{1,0:T(8,128)(2,1)S(1)} %get-tuple-element.62), channel_id=1, source_target_pairs={{0,2},{1,3},{2,0},{3,1},{4,6},{5,7},{6,4},{7,5},{8,10},{9,11},{10,... | collective-permute-start | bytes 208904 | tf_op jit(solution)/shard_map/ppermute | solution.py:304
  31.3 7.4 %collective-permute-start.13 = (bf16[272,128]{1,0:T(8,128)(2,1)S(1)}, bf16[272,128]{1,0:T(8,128)(2,1)S(1)}, u32[]{:S(2)}, u32[]{:S(2)}) collective-permute-start(bf16[272,128]{1,0:T(8,128)(2,1)S(1)} %get-tuple-element.63), channel_id=1, source_target_pairs={{0,3},{1,2},{2,1},{3,0},{4,7},{5,6},{6,5},{7,4},{8,11},{9,10},{10,... | collective-permute-start | bytes 208904 | tf_op jit(solution)/shard_map/ppermute | solution.py:304
  32.4 7.9 %copy-start.1 = (f32[1024]{0:T(1024)S(1)}, f32[1024]{0:T(1024)}, u32[]{:S(2)}) copy-start(f32[1024]{0:T(1024)} %param.10) | copy-start | bytes 12292
  32.4 7.9 %collective-permute-start.14 = (bf16[272,128]{1,0:T(8,128)(2,1)S(1)}, bf16[272,128]{1,0:T(8,128)(2,1)S(1)}, u32[]{:S(2)}, u32[]{:S(2)}) collective-permute-start(bf16[272,128]{1,0:T(8,128)(2,1)S(1)} %get-tuple-element.64), channel_id=1, source_target_pairs={{0,6},{1,7},{2,4},{3,5},{4,2},{5,3},{6,0},{7,1},{8,14},{9,15},{10,... | collective-permute-start | bytes 208904 | tf_op jit(solution)/shard_map/ppermute | solution.py:304
  35.1 6.9 %collective-permute-start.15 = (bf16[272,128]{1,0:T(8,128)(2,1)S(1)}, bf16[272,128]{1,0:T(8,128)(2,1)S(1)}, u32[]{:S(2)}, u32[]{:S(2)}) collective-permute-start(bf16[272,128]{1,0:T(8,128)(2,1)S(1)} %get-tuple-element.66), channel_id=1, source_target_pairs={{0,7},{1,6},{2,5},{3,4},{4,3},{5,2},{6,1},{7,0},{8,15},{9,14},{10,... | collective-permute-start | bytes 208904 | tf_op jit(solution)/shard_map/ppermute | solution.py:304
  36.8 5.3 %collective-permute-start.16 = (bf16[272,128]{1,0:T(8,128)(2,1)S(1)}, bf16[272,128]{1,0:T(8,128)(2,1)S(1)}, u32[]{:S(2)}, u32[]{:S(2)}) collective-permute-start(bf16[272,128]{1,0:T(8,128)(2,1)S(1)} %get-tuple-element.67), channel_id=1, source_target_pairs={{0,1},{1,0},{2,3},{3,2},{4,5},{5,4},{6,7},{7,6},{8,9},{9,8},{10,11... | collective-permute-start | bytes 208904 | tf_op jit(solution)/shard_map/ppermute | solution.py:304
